TPU v7x, 32 devices: a whole 2x2x4 slice. The times are simulated.
32 devices in a mesh: grp: 4 (over x, core), seq: 2 (over y), dp: 4 (over z).
Axes of the slice: x: 2, y: 2, z: 4, core: 2. Of those that a mesh axis runs over, the one named last changes fastest.
Arguments:
- image: bfloat16 [16, 160, 3072], P(('grp', 'dp'), 'seq'), may hold values from -6 to 6
- noise: bfloat16 [16, 160, 3072], P(('grp', 'dp'), 'seq'), may hold values from -6 to 6
- text: bfloat16 [16, 96, 3072], P(('grp', 'dp'), 'seq'), may hold values from -6 to 6
- timestep: int32 [16], P(('grp', 'dp')), may hold values from 0 to 999
- guidance: float32 [16], P(('grp', 'dp')), may hold values from 1 to 5
- text_token_length: int32 [16], P(('grp', 'dp')), may hold values from 1 to 96
- image_projection_weight: bfloat16 [3072, 6144], P(None, 'seq'), may hold values from -0.109375 to 0.109375
- text_projection_weight: bfloat16 [3072, 4096], P(None, 'seq'), may hold values from -0.109375 to 0.109375
- modulation_weight: bfloat16 [256, 12288], P(None, 'seq'), may hold values from -0.375 to 0.375
- query_key_norm_gain: float32 [3, 128], replicated, may hold values from 0.5 to 1.5
- adapter_down_weight: bfloat16 [3072, 64], replicated, may hold values from -0.109375 to 0.109375
- adapter_up_weight: bfloat16 [64, 6144], P(None, 'seq'), may hold values from -0.75 to 0.75
Outputs:
- direction_a: float32 [3072, 64], replicated
- direction_b: float32 [64, 6144], P(None, 'seq')
- loss_mean: float32 [], replicated
All inputs are finite; a program needn't handle non-finite values.
Results may differ from a plain program's by a relative error of at most 0.0032.
Values may be sent and summed in bfloat16 or wider, within the bound.
No kernel may reach another device: no remote copies, remote signals or barrier semaphores. Data moves between devices by JAX's collectives and lax.ppermute only.
A program may use at most 128 MiB of HBM per device.

v0:
```python
import math

import jax
import jax.numpy as jnp
from jax import lax
from jax.sharding import PartitionSpec as P

HD = 128
HEADS = 16
STEPS = 1000


def timing(value, width):
    count = width // 4
    freqs = jnp.exp(-math.log(10000.0) * jnp.arange(count, dtype=jnp.float32) / count)
    angles = 1000.0 * value * freqs
    return jnp.concatenate([jnp.cos(angles), jnp.sin(angles)])


def modulate(tokens, shift, scale):
    values = tokens.astype(jnp.float32)
    center = values - jnp.mean(values, axis=1, keepdims=True)
    spread = jnp.mean(center * center, axis=1, keepdims=True)
    return (center * lax.rsqrt(spread + 1e-06) * (1.0 + scale) + shift).astype(jnp.bfloat16)


def headnorm(vector, gain):
    return vector * lax.rsqrt(jnp.mean(vector * vector, axis=-1, keepdims=True) + 1e-06) * gain


def attend(kv_txt, qkv_img, query_key_norm_gain, keep):
    count = qkv_img.shape[1] // (3 * HD)
    img = qkv_img.reshape(qkv_img.shape[0], count, 3, HD)
    txt = kv_txt.reshape(kv_txt.shape[0], count, 2, HD)
    queries = headnorm(img[:, :, 0], query_key_norm_gain[0]).astype(jnp.bfloat16)
    keys = jnp.concatenate(
        [
            headnorm(txt[:, :, 0], query_key_norm_gain[2]),
            headnorm(img[:, :, 1], query_key_norm_gain[1]),
        ],
        0,
    ).astype(jnp.bfloat16)
    values = jnp.concatenate([txt[:, :, 1], img[:, :, 2]], 0).astype(jnp.bfloat16)
    scores = jnp.einsum(
        "qhd,khd->hqk", queries, keys, preferred_element_type=jnp.float32
    ) / math.sqrt(HD)
    scores = jnp.where(keep[None, None, :], scores, -1000000000.0)
    weights = jnp.exp(scores)
    probs = (weights / jnp.sum(weights, axis=2, keepdims=True)).astype(jnp.bfloat16)
    out = jnp.einsum("hqk,khd->qhd", probs, values, preferred_element_type=jnp.float32)
    return out.reshape(out.shape[0], count * HD)


def on_device(
    image,
    noise,
    text,
    timestep,
    guidance,
    text_token_length,
    image_projection_weight,
    text_projection_weight,
    modulation_weight,
    query_key_norm_gain,
    adapter_down_weight,
    adapter_up_weight,
):
    width = image.shape[2]
    emb_width = modulation_weight.shape[0]
    samples = lax.axis_size("grp") * lax.axis_size("dp")
    sigma = (timestep[0].astype(jnp.float32) + 1.0) / STEPS
    start = timing(sigma, emb_width)
    emb_t = jax.nn.silu(jnp.concatenate([start, timing(guidance[0], emb_width)])).astype(
        jnp.bfloat16
    )
    emb_s = jax.nn.silu(jnp.concatenate([start, jnp.zeros((emb_width // 2,), jnp.float32)])).astype(
        jnp.bfloat16
    )
    part_t = jnp.dot(emb_t[None], modulation_weight, preferred_element_type=jnp.float32)
    part_s = jnp.dot(emb_s[None], modulation_weight, preferred_element_type=jnp.float32)
    mod_t, mod_s = (
        lax.all_gather(part_t, "seq", axis=1, tiled=True),
        lax.all_gather(part_s, "seq", axis=1, tiled=True),
    )
    mod_t = mod_t[0]
    mod_s = mod_s[0]
    noisy = (
        (1.0 - sigma) * image[0].astype(jnp.float32) + sigma * noise[0].astype(jnp.float32)
    ).astype(jnp.bfloat16)
    words = text[0]
    h_img_s_local = modulate(noisy, mod_s[:width], mod_s[width : 2 * width])
    h_img_t_local = modulate(noisy, mod_t[:width], mod_t[width : 2 * width])
    h_txt_t_local = modulate(words, mod_t[2 * width : 3 * width], mod_t[3 * width :])
    h_txt_s_local = modulate(words, mod_s[2 * width : 3 * width], mod_s[3 * width :])
    h_img_t, student_image_hidden = (
        lax.all_gather(h_img_t_local, "seq", axis=0, tiled=True),
        lax.all_gather(h_img_s_local, "seq", axis=0, tiled=True),
    )
    h_txt_t, h_txt_s = (
        lax.all_gather(h_txt_t_local, "seq", axis=0, tiled=True),
        lax.all_gather(h_txt_s_local, "seq", axis=0, tiled=True),
    )
    adapter_output = jnp.dot(
        student_image_hidden, adapter_down_weight, preferred_element_type=jnp.float32
    ).astype(jnp.bfloat16)
    qkv_t = jnp.dot(h_img_t, image_projection_weight, preferred_element_type=jnp.float32)
    student_base = jnp.dot(
        student_image_hidden, image_projection_weight, preferred_element_type=jnp.float32
    )
    kv_t = jnp.dot(h_txt_t, text_projection_weight, preferred_element_type=jnp.float32)
    kv_s = jnp.dot(h_txt_s, text_projection_weight, preferred_element_type=jnp.float32)
    student_query_key_value = student_base + jnp.dot(
        adapter_output, adapter_up_weight, preferred_element_type=jnp.float32
    )
    txt_rows = kv_t.shape[0]
    img_rows = qkv_t.shape[0]
    position = jnp.arange(txt_rows + img_rows, dtype=jnp.int32)
    keep = jnp.logical_or(position >= txt_rows, position < text_token_length[0])
    target = attend(kv_t, qkv_t, query_key_norm_gain, keep).astype(jnp.bfloat16)
    student, pull = jax.vjp(
        lambda inner: attend(kv_s, inner, query_key_norm_gain, keep), student_query_key_value
    )
    diff = student - target.astype(jnp.float32)
    loss_part = jnp.sum(diff * diff) / samples
    (query_key_value_gradient,) = pull(2.0 * diff / samples)
    query_key_value_gradient = query_key_value_gradient.astype(jnp.bfloat16)
    grad_b_part = jnp.dot(
        adapter_output.T, query_key_value_gradient, preferred_element_type=jnp.float32
    )
    partial_adapter_gradient = jnp.dot(
        query_key_value_gradient, adapter_up_weight.T, preferred_element_type=jnp.float32
    )
    adapter_gradient = lax.psum_scatter(
        partial_adapter_gradient, "seq", scatter_dimension=0, tiled=True
    )
    grad_a_part = jnp.dot(
        h_img_s_local.astype(jnp.float32).T, adapter_gradient, precision=lax.Precision.HIGHEST
    )
    grad_a, loss_total = lax.psum((grad_a_part, loss_part), ("grp", "seq", "dp"))
    grad_b = lax.psum(grad_b_part, ("grp", "dp"))
    squares_b = lax.psum(jnp.sum(grad_b * grad_b), "seq")
    entries_b = grad_b.shape[0] * grad_b.shape[1] * lax.axis_size("seq")
    loss_mean = loss_total / (img_rows * HEADS * HD)
    direction_a = grad_a / jnp.sqrt(jnp.mean(grad_a * grad_a) + 1e-06)
    direction_b = grad_b / jnp.sqrt(squares_b / entries_b + 1e-06)
    return (direction_a, direction_b, loss_mean)


def solution(mesh):
    in_specs = (
        P(("grp", "dp"), "seq", None),
        P(("grp", "dp"), "seq", None),
        P(("grp", "dp"), "seq", None),
        P(("grp", "dp")),
        P(("grp", "dp")),
        P(("grp", "dp")),
        P(None, "seq"),
        P(None, "seq"),
        P(None, "seq"),
        P(),
        P(),
        P(None, "seq"),
    )
    out_specs = (P(), P(None, "seq"), P())
    return jax.shard_map(
        on_device, mesh=mesh, in_specs=in_specs, out_specs=out_specs, check_vma=False
    )
```

profile of v0, /device:TPU:0, one launch (start us, length us, event | category | flops | bytes accessed | tf_op | source)
XLA Modules:
  0.0 383.1 jit_solution(567787852062828447)
XLA Ops:
  13.2 5.4 %all-gather.1 = f32[12288]{0:T(1024)S(1)} all-gather(f32[6144]{0:T(1024)S(1)} %bitcast.172), channel_id=3, replica_groups=mesh['grp'=4,'seq'=2,'dp'=4] {'seq'}, dimensions={0}, use_global_device_ids=true | all-gather | bytes 73728 | tf_op jit(solution)/shard_map/all_gather | solution.py:82
  19.3 4.5 %all-gather = f32[12288]{0:T(1024)S(1)} all-gather(f32[6144]{0:T(1024)S(1)} %bitcast.171), channel_id=2, replica_groups=mesh['grp'=4,'seq'=2,'dp'=4] {'seq'}, dimensions={0}, use_global_device_ids=true | all-gather | bytes 73728 | tf_op jit(solution)/shard_map/all_gather | solution.py:83
  24.6 7.4 %all_gather.22 = bf16[96,3072]{1,0:T(8,128)(2,1)S(1)} all-gather(bf16[48,3072]{1,0:T(8,128)(2,1)S(1)} %get-tuple-element.11), channel_id=1, replica_groups=mesh['grp'=4,'seq'=2,'dp'=4] {'seq'}, dimensions={0}, use_global_device_ids=true | all-gather | bytes 884736 | tf_op jit(solution)/shard_map/all_gather | solution.py:100
  32.1 6.7 %fusion.83 = f32[96,2048]{1,0:T(8,128)S(1)} fusion(bf16[96,3072]{1,0:T(8,128)(2,1)S(1)} %all_gather.22, bf16[3072,2048]{1,0:T(8,128)(2,1)} %param.19), kind=kOutput, calls=%fused_computation.163 | convolution fusion | flops 1207959552 | bytes 13959168 | tf_op jit(solution)/shard_map/dot_general | solution.py:110
  40.9 7.4 %all_gather.19 = bf16[96,3072]{1,0:T(8,128)(2,1)S(1)} all-gather(bf16[48,3072]{1,0:T(8,128)(2,1)S(1)} %get-tuple-element.12), channel_id=1, replica_groups=mesh['grp'=4,'seq'=2,'dp'=4] {'seq'}, dimensions={0}, use_global_device_ids=true | all-gather | bytes 884736 | tf_op jit(solution)/shard_map/all_gather | solution.py:101
  48.3 6.7 %fusion.80 = f32[96,2048]{1,0:T(8,128)S(1)} fusion(bf16[96,3072]{1,0:T(8,128)(2,1)S(1)} %all_gather.19, bf16[3072,2048]{1,0:T(8,128)(2,1)} %param.19), kind=kOutput, calls=%fused_computation.160 | convolution fusion | flops 1207959552 | bytes 13959168 | tf_op jit(solution)/shard_map/dot_general | solution.py:111
  59.6 9.7 %all_gather.20 = bf16[160,3072]{1,0:T(8,128)(2,1)S(1)} all-gather(bf16[80,3072]{1,0:T(8,128)(2,1)S(1)} %get-tuple-element.10), channel_id=1, replica_groups=mesh['grp'=4,'seq'=2,'dp'=4] {'seq'}, dimensions={0}, use_global_device_ids=true | all-gather | bytes 1474560 | tf_op jit(solution)/shard_map/all_gather | solution.py:97
  69.8 8.1 %fusion.81 = f32[160,3072]{1,0:T(8,128)S(1)} fusion(bf16[160,3072]{1,0:T(8,128)(2,1)S(1)} %all_gather.20, bf16[3072,3072]{1,0:T(8,128)(2,1)} %param.18), kind=kOutput, calls=%fused_computation.161 | convolution fusion | flops 3019898880 | bytes 21823488 | tf_op jit(solution)/shard_map/dot_general | solution.py:107
  77.9 1.7 convolution_add_fusion
  79.7 3.2 reshape.184
  82.9 1.5 copy-done.2
  84.4 1.5 slice.107
  85.9 4.8 %fusion.77 = (f32[160,8,1,128]{3,2,1,0:T(1,128)}, f32[160,8,1,128]{3,2,1,0:T(1,128)S(1)}) fusion(f32[160,8,3,128]{3,2,1,0:T(4,128)} %copy-done.2), kind=kLoop, calls=%fused_computation.157 | loop fusion | bytes 2621440 | tf_op jit(solution)/shard_map/jvp()/slice | solution.py:35
  90.7 9.5 %all_gather.23 = bf16[160,3072]{1,0:T(8,128)(2,1)S(1)} all-gather(bf16[80,3072]{1,0:T(8,128)(2,1)S(1)} %copy-done.9), channel_id=1, replica_groups=mesh['grp'=4,'seq'=2,'dp'=4] {'seq'}, dimensions={0}, use_global_device_ids=true | all-gather | bytes 1474560 | tf_op jit(solution)/shard_map/all_gather | solution.py:96
  100.2 8.1 %fusion.84 = f32[160,3072]{1,0:T(8,128)S(1)} fusion(bf16[160,3072]{1,0:T(8,128)(2,1)S(1)} %all_gather.23, bf16[3072,3072]{1,0:T(8,128)(2,1)} %param.18), kind=kOutput, calls=%fused_computation.164 | convolution fusion | flops 3019898880 | bytes 21823488 | tf_op jit(solution)/shard_map/dot_general | solution.py:106
  108.3 2.6 reshape.186
  110.8 2.4 slice.116
  113.3 3.9 %fusion.76 = (f32[160,8,1,128]{3,2,1,0:T(1,128)S(1)}, f32[160,8,1,128]{3,2,1,0:T(1,128)S(1)}) fusion(f32[160,8,3,128]{3,2,1,0:T(4,128)} %reshape.186), kind=kLoop, calls=%fused_computation.156 | loop fusion | bytes 2621440 | tf_op jit(solution)/shard_map/slice | solution.py:35
  124.0 1.6 fusion.78
  125.6 1.6 fusion.1
  127.2 3.2 fusion.15
  130.4 2.1 multiply_reduce_fusion.2
  135.0 1.8 fusion.10
  143.0 41.2 %psum.31 = f32[]{:T(128)} all-reduce(f32[]{:T(128)S(6)} %div.179), channel_id=1, replica_groups=mesh['grp'=4,'seq'=2,'dp'=4] {'grp','seq','dp'}, use_global_device_ids=true, to_apply=%region_22.23 | all-reduce | flops 1 | bytes 8 | tf_op jit(solution)/shard_map/psum | solution.py:139
  184.8 2.2 fusion.86
  187.0 52.7 %all-reduce.8.cloned.1.call-done = f32[64,3072]{1,0:T(8,128)} async-done(((f32[64,3072]{1,0:T(8,128)}), f32[64,3072]{1,0:T(8,128)}) %all-reduce.8.cloned.1.call-update) | async-done | bytes 786448 | tf_op jit(solution)/shard_map/psum | solution.py:140
  239.7 1.9 multiply_reduce_fusion
  241.7 5.6 %psum.30 = f32[]{:T(128)} all-reduce(f32[]{:T(128)} %multiply_reduce_fusion), channel_id=1, replica_groups=mesh['grp'=4,'seq'=2,'dp'=4] {'seq'}, use_global_device_ids=true, to_apply=%region_20.21 | all-reduce | flops 1 | bytes 8 | tf_op jit(solution)/shard_map/psum | solution.py:141
  247.9 2.2 broadcast_divide_fusion
  250.2 119.7 %all-reduce.6.cloned.1.call-done = f32[3072,64]{0,1:T(8,128)} async-done(((f32[3072,64]{0,1:T(8,128)}), f32[3072,64]{0,1:T(8,128)}) %all-reduce.6.cloned.1.call-update) | async-done | bytes 786448 | tf_op jit(solution)/shard_map/psum | solution.py:139
  369.9 1.9 multiply_reduce_fusion.1
  372.5 2.1 broadcast_divide_fusion.1
  (145 shorter events, 26.1 us)
Async XLA Ops:
  8.0 4.2 %copy-start = (bf16[256,6144]{1,0:T(8,128)(2,1)S(1)}, bf16[256,6144]{1,0:T(8,128)(2,1)}, u32[]{:S(2)}) copy-start(bf16[256,6144]{1,0:T(8,128)(2,1)} %param.20) | copy-start | bytes 9437188
  8.0 176.8 %reduce-scatter.4.cloned.1.call-start = ((), (), s32[]{:S(2)}) async-start(), calls=%async_computation.3 | async-start | bytes 122880
  12.7 11.7 %copy-start.7 = (bf16[1,48,3072]{2,1,0:T(8,128)(2,1)S(1)}, bf16[1,48,3072]{2,1,0:T(8,128)(2,1)}, u32[]{:S(2)}) copy-start(bf16[1,48,3072]{2,1,0:T(8,128)(2,1)} %param.14) | copy-start | bytes 884740
  54.9 2.9 copy-start.17
  54.9 2.9 copy-start.18
  56.6 1.8 copy-start.28
  58.5 10.8 %copy-start.19 = (bf16[3072,64]{0,1:T(8,128)(2,1)S(1)}, bf16[3072,64]{0,1:T(8,128)(2,1)}, u32[]{:S(2)}) copy-start(bf16[3072,64]{0,1:T(8,128)(2,1)} %param.22) | copy-start | bytes 1179652
  59.6 9.7 %copy-start.4 = (bf16[80,3072]{1,0:T(8,128)(2,1)}, bf16[80,3072]{1,0:T(8,128)(2,1)S(1)}, u32[]{:S(2)}) copy-start(bf16[80,3072]{1,0:T(8,128)(2,1)S(1)} %get-tuple-element.10) | copy-start | bytes 1474564
  69.7 8.2 %copy-start.20 = (bf16[160,64]{0,1:T(8,128)(2,1)}, bf16[160,64]{0,1:T(8,128)(2,1)S(1)}, u32[]{:S(2)}) copy-start(bf16[160,64]{0,1:T(8,128)(2,1)S(1)} %convolution_convert_fusion.5) | copy-start | bytes 61444
  69.8 8.2 %copy-start.10 = (bf16[64,3072]{1,0:T(8,128)(2,1)S(1)}, bf16[64,3072]{1,0:T(8,128)(2,1)}, u32[]{:S(2)}) copy-start(bf16[64,3072]{1,0:T(8,128)(2,1)} %param.23) | copy-start | bytes 1179652
  85.9 4.8 %copy-start.9 = (bf16[80,3072]{1,0:T(8,128)(2,1)S(1)}, bf16[80,3072]{1,0:T(8,128)(2,1)}, u32[]{:S(2)}) copy-start(bf16[80,3072]{1,0:T(8,128)(2,1)} %get-tuple-element.9) | copy-start | bytes 1474564
  113.3 4.8 %copy-start.33 = (f32[3,128]{1,0:T(4,128)S(1)}, f32[3,128]{1,0:T(4,128)}, u32[]{:S(2)}) copy-start(f32[3,128]{1,0:T(4,128)} %param.21) | copy-start | bytes 4612
  113.3 4.8 %copy-start.12 = (bf16[96,8,1,128]{3,2,1,0:T(2,128)(2,1)S(1)}, bf16[96,8,1,128]{3,2,1,0:T(2,128)(2,1)}, u32[]{:S(2)}) copy-start(bf16[96,8,1,128]{3,2,1,0:T(2,128)(2,1)} %slice.115) | copy-start | bytes 589828
  113.3 5.8 %copy-start.13 = (bf16[96,8,1,128]{3,2,1,0:T(2,128)(2,1)S(1)}, bf16[96,8,1,128]{3,2,1,0:T(2,128)(2,1)}, u32[]{:S(2)}) copy-start(bf16[96,8,1,128]{3,2,1,0:T(2,128)(2,1)} %slice.106) | copy-start | bytes 589828
  117.2 2.6 copy-start.6
  117.2 2.8 copy-start.8
  118.0 7.6 %copy-start.36 = (pred[256]{0:T(512)(128)(4,1)}, pred[256]{0:T(512)(128)(4,1)S(1)}, u32[]{:S(2)}) copy-start(pred[256]{0:T(512)(128)(4,1)S(1)} %compare_or_fusion) | copy-start | bytes 772
  118.0 5.6 %copy-start.31 = (f32[128]{0:T(128)}, f32[128]{0:T(128)S(1)}, u32[]{:S(2)}) copy-start(f32[128]{0:T(128)S(1)} %get-tuple-element.22) | copy-start | bytes 1540
  118.1 7.5 %copy-start.34 = (f32[128]{0:T(128)}, f32[128]{0:T(128)S(1)}, u32[]{:S(2)}) copy-start(f32[128]{0:T(128)S(1)} %get-tuple-element.21) | copy-start | bytes 1540
  119.1 2.2 copy-start.3
  121.7 1.9 copy-start.24
  121.7 2.3 copy-start.29
  123.6 2.0 copy-start.22
  127.2 3.2 copy-start.14
  127.2 3.2 copy-start.15
  127.2 3.2 copy-start.16
  134.9 1.8 copy-start.25
  134.9 1.8 copy-start.32
  141.0 43.8 %copy-start.5 = (bf16[80,3072]{1,0:T(8,128)(2,1)S(1)}, bf16[80,3072]{1,0:T(8,128)(2,1)}, u32[]{:S(2)}) copy-start(bf16[80,3072]{1,0:T(8,128)(2,1)} %copy-done.4) | copy-start | bytes 1474564
  141.0 98.7 %all-reduce.8.cloned.1.call-start = ((), (), s32[]{:S(2)}) async-start(), calls=%async_computation.2 | async-start | bytes 1572864 | tf_op jit(solution)/shard_map/psum | solution.py:140
  142.3 227.6 %all-reduce.6.cloned.1.call-start = ((), (), s32[]{:S(2)}) async-start(), calls=%async_computation.1 | async-start | bytes 1572864 | tf_op jit(solution)/shard_map/psum | solution.py:139
  247.9 126.6 %copy-start.1 = (bf16[256,6144]{1,0:T(8,128)(2,1)S(1)}, bf16[256,6144]{1,0:T(8,128)(2,1)}, u32[]{:S(2)}) copy-start(bf16[256,6144]{1,0:T(8,128)(2,1)} %param.20) | copy-start | bytes 9437188
  (9 other events, 10.8 us)
Sparse Core Ops, SparseCore 0:
  141.1 11.6 reduce-scatter.3
  241.8 128.0 all-reduce.5
Sparse Core Ops, SparseCore 1:
  145.9 93.8 all-reduce.7
where the time goes:
time: 384 us; the launch traced here: 383 us
  waiting for transfers between devices  172 us (45%)
  blocking collectives  90.7 us (24%)
  matrix products  49.5 us (13%)
  local copies, waits for them, and re-layouts  30.4 us (8%)
  between operations  22.3 us (6%)
  other arithmetic  17.8 us (5%)
    psum x1, waiting for transfers between devices, on_device(): lax.psum((grad_a_part, loss_part), ('grp', 'seq', 'dp'))  120 us
    psum x1, waiting for transfers between devices, on_device(): grad_b = lax.psum(grad_b_part, ('grp', 'dp'))  52.7 us
    psum x1, blocking collectives, on_device(): lax.psum((grad_a_part, loss_part), ('grp', 'seq', 'dp'))  41.2 us
    all_gather x1, blocking collectives, on_device(): lax.all_gather(h_img_s_local, 'seq', axis=0, tiled=True)  9.68 us
    all_gather x1, blocking collectives, on_device(): lax.all_gather(h_img_t_local, 'seq', axis=0, tiled=True)  9.49 us
    slice x2, local copies, waits for them, and re-layouts, attend(): img[:, :, 0]  8.71 us
    dot_general x1, matrix products, on_device(): jnp.dot(student_image_hidden, image_projection_weight, preferred_element_...  8.13 us
    dot_general x1, matrix products, on_device(): jnp.dot(h_img_t, image_projection_weight, preferred_element_type=jnp.floa...  8.1 us
  transfers between devices with their start and end apart: 3, of which 2 were waited for; matrix products, arithmetic and copies ran while one was open for 1% of the time, Pallas kernels for 0%

commit v1 on v0

v1 whole, which is shorter than its diff:
```python
import functools
import math

import jax
import jax.numpy as jnp
from jax import lax
from jax.experimental import pallas as pl
from jax.experimental.pallas import tpu as pltpu
from jax.sharding import PartitionSpec as P

HD = 128
HEADS = 16
STEPS = 1000
EPS = 1e-06
F32 = jnp.float32
BF16 = jnp.bfloat16
ROOT = 1.0 / math.sqrt(HD)


def timing(value, width):
    count = width // 4
    freqs = jnp.exp(-math.log(10000.0) * jnp.arange(count, dtype=F32) / count)
    angles = 1000.0 * value * freqs
    return jnp.concatenate([jnp.cos(angles), jnp.sin(angles)])


def nn(a, b):
    return lax.dot_general(a, b, (((1,), (0,)), ((), ())), preferred_element_type=F32)


def nt(a, b):
    return lax.dot_general(a, b, (((1,), (1,)), ((), ())), preferred_element_type=F32)


def tn(a, b):
    return lax.dot_general(a, b, (((0,), (0,)), ((), ())), preferred_element_type=F32)


def over(total, size, body):
    if total == size:
        body(0)
    else:

        @pl.loop(0, total // size)
        def _(i):
            body(pl.multiple_of(i * size, size))


def inverse_rms(x):
    return lax.rsqrt(jnp.mean(x * x, axis=-1, keepdims=True) + EPS)


def norm_pull(x, gain, dy):
    r = inverse_rms(x)
    u = gain * dy
    return r * (u - x * (r * r * jnp.mean(x * u, axis=-1, keepdims=True)))


def middle_kernel(
    n, steps, pair, samples, where_ref, mod_ref, bias_ref, gain_ref, down_ref, up_ref, wi_ref, wt_ref, *refs
):
    noisy, text = refs[:n], refs[n : 2 * n]
    send_a, keep_a, send_b, keep_b, loss_ref = refs[2 * n : 2 * n + 5]
    hi, ht, low, lowt, glt, qkv, kv, q_s, k_s, v_s, dk_s, dv_s, gq, whole = refs[2 * n + 5 :]
    step = pl.program_id(0)
    core = where_ref[0]
    img_part, txt_part = noisy[0].shape[0], text[0].shape[0]
    rows, trows = n * img_part, n * txt_part
    block = min(rows, 160)
    grp_rows = send_a.shape[1]

    def modulated(parts, dest, size, total, base):
        for k in range(n):

            @pl.loop(0, size // 16)
            def _(i, k=k):
                v = parts[k][pl.ds(pl.multiple_of(i * 16, 16), 16), :].astype(F32)
                center = v - jnp.mean(v, axis=1, keepdims=True)
                spread = jnp.mean(center * center, axis=1, keepdims=True)
                unit = center * lax.rsqrt(spread + EPS)
                for m in range(2):
                    row = 4 * m + base
                    h = unit * (1.0 + mod_ref[row + 1 : row + 2, :]) + mod_ref[row : row + 1, :]
                    at = pl.multiple_of(m * total + k * size + i * 16, 16)
                    dest[pl.ds(at, 16), :] = h.astype(BF16)

    @pl.when(step == 0)
    def _():
        modulated(noisy, hi, img_part, rows, 0)
        modulated(text, ht, txt_part, trows, 2)

        def adapter(start):
            low[pl.ds(start, block), :] = nn(hi[pl.ds(rows + start, block), :], down_ref[...]).astype(BF16)

        over(rows, block, adapter)
        lowt[...] = low[...].astype(F32).T.astype(BF16)
        glt[...] = jnp.zeros_like(glt)
        loss_ref[...] = jnp.zeros_like(loss_ref)

    def project_image(start):
        qkv[pl.ds(start, 2 * block), :] = nn(hi[pl.ds(start, 2 * block), :], wi_ref[...])

    def project_text(start):
        size = min(2 * trows, 192)
        kv[pl.ds(start, size), :] = nn(ht[pl.ds(start, size), :], wt_ref[...])

    def add_adapter(start):
        at = pl.ds(rows + start, block)
        qkv[at, :] = qkv[at, :] + nn(low[pl.ds(start, block), :], up_ref[...])

    over(2 * rows, 2 * block, project_image)
    over(2 * trows, min(2 * trows, 192), project_text)
    over(rows, block, add_adapter)

    gain_q, gain_k, gain_t = gain_ref[0:1, :], gain_ref[1:2, :], gain_ref[2:3, :]
    for j in range(pair):
        ic, tc = j * 3 * HD, j * 2 * HD
        for m in range(2):
            slot = 2 * j + m

            def image_part(start, m=m, slot=slot):
                src = pl.ds(m * rows + start, block)
                dst = pl.ds(start, block)
                q = qkv[src, ic : ic + HD]
                k = qkv[src, ic + HD : ic + 2 * HD]
                q_s[slot, dst, :] = (q * inverse_rms(q) * gain_q).astype(BF16)
                k_s[slot, dst, :] = (k * inverse_rms(k) * gain_k).astype(BF16)
                v_s[slot, dst, :] = qkv[src, ic + 2 * HD : ic + 3 * HD].astype(BF16)

            def text_part(start, m=m, slot=slot):
                size = min(trows, 96)
                src = pl.ds(m * trows + start, size)
                dst = pl.ds(rows + start, size)
                k = kv[src, tc : tc + HD]
                k_s[slot, dst, :] = (k * inverse_rms(k) * gain_t).astype(BF16)
                v_s[slot, dst, :] = kv[src, tc + HD : tc + 2 * HD].astype(BF16)

            over(rows, block, image_part)
            over(trows, min(trows, 96), text_part)

        teacher, student = 2 * j, 2 * j + 1
        if rows > block:
            dk_s[j] = jnp.zeros(dk_s.shape[1:], F32)
            dv_s[j] = jnp.zeros(dv_s.shape[1:], F32)

        def attend(start, j=j, ic=ic, teacher=teacher, student=student):
            at = pl.ds(start, block)

            def forward(slot):
                scores = nt(q_s[slot, at, :], k_s[slot]) * ROOT + bias_ref[...]
                weights = jnp.exp(scores)
                probs = weights * (1.0 / jnp.sum(weights, axis=1, keepdims=True))
                rounded = probs.astype(BF16)
                return probs, rounded, nn(rounded, v_s[slot])

            _, _, target = forward(teacher)
            probs, rounded, out = forward(student)
            diff = out - target.astype(BF16).astype(F32)
            loss_ref[...] += jnp.sum((diff * diff).reshape(block // 8, 8, HD), axis=0)
            dout = (diff * (2.0 / samples)).astype(BF16)
            dprobs = nt(dout, v_s[student]).astype(BF16).astype(F32)
            dscores = probs * (dprobs - jnp.sum(dprobs * probs, axis=1, keepdims=True))
            dscores = (dscores * ROOT).astype(BF16)
            dq = nn(dscores, k_s[student]).astype(BF16).astype(F32)
            q = qkv[pl.ds(rows + start, block), ic : ic + HD]
            gq[at, ic : ic + HD] = norm_pull(q, gain_q, dq).astype(BF16)
            dk = tn(dscores, q_s[student, at, :])[:rows]
            dv = tn(rounded, dout)[:rows]
            if rows > block:
                dk_s[j] += dk
                dv_s[j] += dv
            else:
                dk_s[j] = dk
                dv_s[j] = dv

        over(rows, block, attend)

        def finish(start, j=j, ic=ic):
            at = pl.ds(start, block)
            k = qkv[pl.ds(rows + start, block), ic + HD : ic + 2 * HD]
            dk = dk_s[j, at, :].astype(BF16).astype(F32)
            gq[at, ic + HD : ic + 2 * HD] = norm_pull(k, gain_k, dk).astype(BF16)
            gq[at, ic + 2 * HD : ic + 3 * HD] = dv_s[j, at, :].astype(BF16)

        over(rows, block, finish)

    def share(value, columns, send, keep):
        whole[:, columns] = value
        for x in range(2):
            keep[x] = whole[pl.ds(pl.multiple_of((2 * x + core) * grp_rows, 8), grp_rows), columns]
            send[x] = whole[pl.ds(pl.multiple_of((2 * x + 1 - core) * grp_rows, 8), grp_rows), columns]

    share(nn(lowt[...], gq[...]), slice(0, gq.shape[1]), send_b, keep_b)
    glt[...] += nt(up_ref[...], gq[...])

    @pl.when(step == steps - 1)
    def _():
        g = glt[...]
        g1 = g.astype(BF16)
        rest = g - g1.astype(F32)
        g2 = rest.astype(BF16)
        g3 = (rest - g2.astype(F32)).astype(BF16)
        stack = jnp.concatenate([g1, g2, g3], 0)
        rank = g.shape[0]
        full = nn(stack, hi[rows : 2 * rows, :])
        share(
            full[:rank] + full[rank : 2 * rank] + full[2 * rank :],
            slice(0, full.shape[1]),
            send_a,
            keep_a,
        )


def middle(n, where, mod, bias, gain, down, up, wi, wt, noisy, text):
    rank, img_cols = up.shape
    width = wi.shape[0]
    count = img_cols // (3 * HD)
    pair = 2 if count % 2 == 0 else 1
    steps = count // pair
    rows, trows = n * noisy[0].shape[0], n * text[0].shape[0]
    groups = rank // 4
    samples = lax.axis_size("grp") * lax.axis_size("dp")
    ic, tc = pair * 3 * HD, pair * 2 * HD

    def fixed(x):
        return pl.BlockSpec(x.shape, lambda s: (0,) * x.ndim, pipeline_mode=pl.Buffered(1))

    def columns(height, cols):
        if steps == 1:
            return pl.BlockSpec((height, cols), lambda s: (0, s), pipeline_mode=pl.Buffered(1))
        return pl.BlockSpec((height, cols), lambda s: (0, s))

    out_a = jax.ShapeDtypeStruct((2, groups, width), F32)
    out_b = jax.ShapeDtypeStruct((2, groups, img_cols), F32)
    spec_a = pl.BlockSpec(out_a.shape, lambda s: (0, 0, 0))
    spec_b = pl.BlockSpec((2, groups, ic), lambda s: (0, 0, s))
    flops = 4 * rows * width * img_cols + 4 * trows * width * wt.shape[1]
    return pl.pallas_call(
        functools.partial(middle_kernel, n, steps, pair, samples),
        grid=(steps,),
        in_specs=[pl.BlockSpec(memory_space=pltpu.SMEM)]
        + [fixed(mod), fixed(bias), fixed(gain), fixed(down)]
        + [columns(rank, ic), columns(width, ic), columns(width, tc)]
        + [fixed(x) for x in (*noisy, *text)],
        out_specs=[spec_a, spec_a, spec_b, spec_b, pl.BlockSpec((8, HD), lambda s: (0, 0))],
        out_shape=[out_a, out_a, out_b, out_b, jax.ShapeDtypeStruct((8, HD), F32)],
        scratch_shapes=[
            pltpu.VMEM((2 * rows, width), BF16),
            pltpu.VMEM((2 * trows, width), BF16),
            pltpu.VMEM((rows, rank), BF16),
            pltpu.VMEM((rank, rows), BF16),
            pltpu.VMEM((rank, rows), F32),
            pltpu.VMEM((2 * rows, ic), F32),
            pltpu.VMEM((2 * trows, tc), F32),
            pltpu.VMEM((2 * pair, rows, HD), BF16),
            pltpu.VMEM((2 * pair, rows + trows, HD), BF16),
            pltpu.VMEM((2 * pair, rows + trows, HD), BF16),
            pltpu.VMEM((pair, rows, HD), F32),
            pltpu.VMEM((pair, rows, HD), F32),
            pltpu.VMEM((rows, ic), BF16),
            pltpu.VMEM((rank, max(width, ic)), F32),
        ],
        compiler_params=pltpu.CompilerParams(
            dimension_semantics=("arbitrary",), vmem_limit_bytes=58 * 1024 * 1024
        ),
        cost_estimate=pl.CostEstimate(
            flops=flops,
            bytes_accessed=2 * (wi.size + wt.size),
            transcendentals=2 * count * rows * (rows + trows),
        ),
        name="middle",
    )(where, mod, bias, gain, down, up, wi, wt, *noisy, *text)


def swap(x, bit):
    size = lax.axis_size("grp")
    return lax.ppermute(x, "grp", [(i, i ^ bit) for i in range(size)])


def shifted(x, axis, k):
    size = lax.axis_size(axis)
    return lax.ppermute(x, axis, [(i, (i + k) % size) for i in range(size)])


def scatter_sum(x, axis, dim):
    size, me = lax.axis_size(axis), lax.axis_index(axis)
    each = x.shape[dim] // size
    block = lambda k: lax.dynamic_slice_in_dim(x, lax.rem(me + k, size) * each, each, dim)
    total = block(0)
    for k in range(1, size):
        total = total + shifted(block(k), axis, k)
    return total


def half_sum(x, bit):
    side = lax.div(lax.axis_index("grp"), bit)
    keep = lax.dynamic_index_in_dim(x, side, 0, keepdims=False)
    send = lax.dynamic_index_in_dim(x, 1 - side, 0, keepdims=False)
    return keep + swap(send, bit)


def pieces(value):
    first = lax.reduce_precision(value, 8, 7)
    second = lax.reduce_precision(value - first, 8, 7)
    return [first, second, value - first - second]


def on_device(
    image,
    noise,
    text,
    timestep,
    guidance,
    text_token_length,
    image_projection_weight,
    text_projection_weight,
    modulation_weight,
    query_key_norm_gain,
    adapter_down_weight,
    adapter_up_weight,
):
    width = image.shape[2]
    emb_width = modulation_weight.shape[0]
    n, me = lax.axis_size("seq"), lax.axis_index("seq")
    samples = lax.axis_size("grp") * lax.axis_size("dp")
    sigma = (timestep[0].astype(F32) + 1.0) / STEPS
    start = timing(sigma, emb_width)
    emb = jnp.stack(
        [
            jnp.concatenate([start, timing(guidance[0], emb_width)]),
            jnp.concatenate([start, jnp.zeros((emb_width // 2,), F32)]),
        ]
    )
    emb = jax.nn.silu(emb).astype(BF16)
    part = jnp.dot(emb, modulation_weight, preferred_element_type=F32)
    mods = [part] + [shifted(part, "seq", k) for k in range(1, n)]
    noisy = ((1.0 - sigma) * image[0].astype(F32) + sigma * noise[0].astype(F32)).astype(BF16)
    noisy_parts = [noisy] + [shifted(noisy, "seq", k) for k in range(1, n)]
    words = text[0]
    text_parts = [words] + [shifted(words, "seq", k) for k in range(1, n)]
    origin = [lax.rem(me + n - k, n) for k in range(n)]
    ordered = [
        functools.reduce(
            lambda so_far, k: jnp.where(origin[k] == j, mods[k], so_far), range(1, n), mods[0]
        )
        for j in range(n)
    ]
    mod = jnp.concatenate(ordered, 1).reshape(8, width)
    img_part, txt_part = noisy.shape[0], words.shape[0]
    place = jnp.concatenate(
        [jnp.zeros((n * img_part,), jnp.int32)]
        + [origin[k] * txt_part + jnp.arange(txt_part, dtype=jnp.int32) for k in range(n)]
    )
    bias = jnp.where(place < text_token_length[0], 0.0, -1000000000.0).astype(F32)[None]
    core = lax.rem(lax.axis_index("grp"), 2).astype(jnp.int32)
    send_a, keep_a, send_b, keep_b, loss = middle(
        n,
        core[None],
        mod,
        bias,
        query_key_norm_gain,
        adapter_down_weight,
        adapter_up_weight,
        image_projection_weight,
        text_projection_weight,
        noisy_parts,
        text_parts,
    )
    sum_a = keep_a + swap(send_a, 1)
    sum_b = keep_b + swap(send_b, 1)
    sum_a = scatter_sum(sum_a, "seq", 1)
    sum_b = half_sum(sum_b, 2)
    sum_a = half_sum(sum_a, 2)
    sum_b = scatter_sum(sum_b, "dp", 1)
    sum_a = scatter_sum(sum_a, "dp", 1)
    scalars = jnp.stack(pieces(jnp.sum(loss)) + pieces(jnp.sum(sum_b * sum_b)))
    extra = jnp.broadcast_to(jnp.pad(scalars, (0, HD - 6))[None], (sum_a.shape[0], HD))
    all_a = lax.all_gather(
        jnp.concatenate([sum_a, extra], 1).astype(BF16), ("grp", "seq", "dp")
    ).astype(F32)
    all_b = lax.all_gather(sum_b.astype(BF16), ("grp", "dp")).astype(F32)
    grps, dps = lax.axis_size("grp"), lax.axis_size("dp")
    scalars = jnp.sum(all_a[:, 0, -HD:], 0)
    loss_mean = jnp.sum(scalars[:3]) / samples / (n * img_part * HEADS * HD)
    squares_b = jnp.sum(scalars[3:6])
    grad_a = all_a[:, :, :-HD].reshape(grps * n, dps, sum_a.shape[0], sum_a.shape[1])
    grad_a = grad_a.transpose(1, 3, 0, 2).reshape(width, -1)
    grad_b = all_b.reshape(grps, dps, *sum_b.shape).transpose(0, 2, 1, 3)
    grad_b = grad_b.reshape(adapter_up_weight.shape)
    direction_a = grad_a * lax.rsqrt(jnp.mean(grad_a * grad_a) + EPS)
    direction_b = grad_b * lax.rsqrt(squares_b / (grad_b.size * n) + EPS)
    return (direction_a, direction_b, loss_mean)


def solution(mesh):
    in_specs = (
        P(("grp", "dp"), "seq", None),
        P(("grp", "dp"), "seq", None),
        P(("grp", "dp"), "seq", None),
        P(("grp", "dp")),
        P(("grp", "dp")),
        P(("grp", "dp")),
        P(None, "seq"),
        P(None, "seq"),
        P(None, "seq"),
        P(),
        P(),
        P(None, "seq"),
    )
    out_specs = (P(), P(None, "seq"), P())
    return jax.shard_map(
        on_device, mesh=mesh, in_specs=in_specs, out_specs=out_specs, check_vma=False
    )
```

time: 384 us -> 207 us (0.54)
  waiting for transfers between devices: 172 us -> 19.3 us
  matrix products: 49.5 us -> 1.14 us
  Pallas kernels: 0 us -> 29.2 us
  local copies, waits for them, and re-layouts: 30.4 us -> 8.49 us
  starting transfers between devices: 0.12 us -> 18.6 us
  blocking collectives: 90.7 us -> 103 us
  between operations: 22.3 us -> 13.8 us
  other arithmetic: 17.8 us -> 13.4 us
    psum x2 -> x0, waiting for transfers between devices: 172 us -> none  [the longest x1 120 us: on_device(): lax.psum((grad_a_part, loss_part), ('grp', 'seq', 'dp'))]
    all_gather x6 -> x2, blocking collectives: 43.9 us -> 103 us  [the longest x1 69.4 us: on_device(): lax.all_gather(jnp.concatenate([sum_a, extra], 1).astype(BF16), ('grp', '...]
    dot_general x18 -> x1, matrix products: 48.4 us -> 1.14 us  [on_device(): part = jnp.dot(emb, modulation_weight, preferred_element_type=F32)]
    psum x2 -> x0, blocking collectives: 46.8 us -> none  [the longest x1 41.2 us: on_device(): lax.psum((grad_a_part, loss_part), ('grp', 'seq', 'dp'))]
    pallas_call x0 -> x1, Pallas kernels: none -> 29.2 us  [middle(): pl.pallas_call(functools.partial(middle_kernel, n, steps, pair, samples),...]
    ppermute x0 -> x14, waiting for transfers between devices: none -> 19.3 us  [the longest x10 15.5 us: shifted(): return lax.ppermute(x, axis, [(i, (i + k) % size) for i in range(size)])]
    ppermute x0 -> x14, starting transfers between devices: none -> 18.6 us  [the longest x10 15 us: shifted(): return lax.ppermute(x, axis, [(i, (i + k) % size) for i in range(size)])]
    slice x8 -> x0, local copies, waits for them, and re-layouts: 16.3 us -> none  [the longest x2 8.71 us: attend(): img[:, :, 0]]
  transfers between devices with their start and end apart: 3 -> 14, of which waited for: 2 -> 4; matrix products, arithmetic and copies ran while one was open for 1% -> 7% of each run, Pallas kernels for 0% -> 0%
where the time goes in v1:
time: 207 us
  blocking collectives  103 us (50%)
  Pallas kernels  29.2 us (14%)
  waiting for transfers between devices  19.3 us (9%)
  starting transfers between devices  18.6 us (9%)
  between operations  13.8 us (7%)
  other arithmetic  13.4 us (6%)
  local copies, waits for them, and re-layouts  8.49 us (4%)
    all_gather x1, blocking collectives, on_device(): lax.all_gather(jnp.concatenate([sum_a, extra], 1).astype(BF16), ('grp', '...  69.4 us
    all_gather x1, blocking collectives, on_device(): all_b = lax.all_gather(sum_b.astype(BF16), ('grp', 'dp')).astype(F32)  33.4 us
    pallas_call x1, Pallas kernels, middle(): pl.pallas_call(functools.partial(middle_kernel, n, steps, pair, samples),...  29.2 us
    ppermute x10, waiting for transfers between devices, shifted(): return lax.ppermute(x, axis, [(i, (i + k) % size) for i in range(size)])  15.5 us
    ppermute x10, starting transfers between devices, shifted(): return lax.ppermute(x, axis, [(i, (i + k) % size) for i in range(size)])  15 us
  transfers between devices with their start and end apart: 14, of which 4 were waited for; matrix products, arithmetic and copies ran while one was open for 7% of the time, Pallas kernels for 0%

profile of v1, /device:TPU:0, one launch (start us, length us, event | category | flops | bytes accessed | tf_op | source)
XLA Modules:
  0.0 206.8 jit_solution(13006104766243122900)
XLA Ops:
  2.5 1.1 fusion.3
  3.7 3.0 %collective-permute-start = (f32[2,6144]{1,0:T(2,128)}, f32[2,6144]{1,0:T(2,128)}, u32[]{:S(2)}, u32[]{:S(2)}) collective-permute-start(f32[2,6144]{1,0:T(2,128)} %fusion.3), channel_id=1, source_target_pairs={{0,4},{4,0},{1,5},{5,1},{2,6},{6,2},{3,7},{7,3},{8,12},{12,8},{9,1... | collective-permute-start | bytes 147464 | tf_op jit(solution)/shard_map/ppermute | solution.py:282
  6.7 2.1 %fusion.refs_0_ = bf16[80,3072]{1,0:T(8,128)(2,1)} fusion(bf16[1,80,3072]{2,1,0:T(8,128)(2,1)} %param.13, bf16[1,80,3072]{2,1,0:T(8,128)(2,1)} %param.12, f32[]{:T(128)S(6)} %div.36, f32[]{:T(128)S(6)} %sub.25), kind=kLoop, calls=%fused_computation.4 | loop fusion | flops 1474560 | bytes 1474568 | tf_op jit(solution)/shard_map/convert_element_type | solution.py:337
  8.8 2.0 collective-permute-start.2
  11.5 0.7 compare_select_fusion.bias_ref
  12.2 1.2 copy.19.down_ref
  13.3 0.9 broadcast_select_fusion.1
  14.2 0.7 reshape.106.mod_ref
  15.0 13.1 %collective-permute-done.2.refs_3_ = bf16[48,3072]{1,0:T(8,128)(2,1)} collective-permute-done((bf16[48,3072]{1,0:T(8,128)(2,1)}, bf16[48,3072]{1,0:T(8,128)(2,1)}, u32[]{:S(2)}, u32[]{:S(2)}) %collective-permute-start.2) | collective-permute-done | bytes 294944 | tf_op jit(solution)/shard_map/ppermute | solution.py:282
  28.1 29.2 %middle.1 = (f32[2,16,3072]{2,1,0:T(8,128)}, f32[2,16,3072]{2,1,0:T(8,128)}, f32[2,16,3072]{2,1,0:T(8,128)}, f32[2,16,3072]{2,1,0:T(8,128)}, f32[8,128]{1,0:T(8,128)}) custom-call(s32[1]{0:T(128)} %bitcast.where_ref, f32[8,3072]{1,0:T(8,128)} %reshape.106.mod_ref, f32[1,256]{1,0:T(1,128)} %compare_select_fusion.bias_ref, f32[3,128]{1,0:T(4,128)} %gain_ref.1, ...), custom_call_target="tpu_custom_call" | custom-call | flops 8455716864 | bytes 31457280 | tf_op jit(solution)/shard_map/middle/pallas_call | solution.py:238
  57.9 1.3 reduce_sum.54
  62.8 1.2 add.158
  64.0 1.6 collective-permute-start.10
  65.5 1.0 add.141
  67.2 3.7 %collective-permute-done.10 = f32[16,3072]{1,0:T(8,128)S(1)} collective-permute-done((f32[16,3072]{1,0:T(8,128)S(1)}, f32[16,3072]{1,0:T(8,128)S(1)}, u32[]{:S(2)}, u32[]{:S(2)}) %collective-permute-start.10) | collective-permute-done | bytes 196640 | tf_op jit(solution)/shard_map/ppermute | solution.py:277
  71.0 1.6 collective-permute-start.11
  72.6 2.6 %collective-permute-start.12 = (f32[16,768]{1,0:T(8,128)S(1)}, f32[16,768]{1,0:T(8,128)S(1)}, u32[]{:S(2)}, u32[]{:S(2)}) collective-permute-start(f32[16,768]{1,0:T(8,128)S(1)} %get-tuple-element.19), channel_id=1, source_target_pairs={{0,2},{1,3},{2,0},{3,1},{4,6},{5,7},{6,4},{7,5},{8,10},{9,11},{10,... | collective-permute-start | bytes 147464 | tf_op jit(solution)/shard_map/ppermute | solution.py:282
  75.2 1.4 collective-permute-start.13
  77.9 1.5 collective-permute-start.5
  80.1 0.7 multiply_reduce_fusion.1
  84.7 2.7 %stack.39 = bf16[6]{0:T(256)(128)(2,1)S(1)} concatenate(f32[1]{0:T(128)} %bitcast.13, f32[1]{0:T(128)} %bitcast.14, bf16[1]{0:T(256)(128)(2,1)} %bitcast.15, f32[1]{0:T(128)} %bitcast.18, f32[1]{0:T(128)} %bitcast.19, bf16[1]{0:T(256)(128)(2,1)} %bitcast.20), dimensions={0} | concatenate | bytes 32 | tf_op jit(solution)/shard_map/stack | solution.py:376
  87.4 33.4 %all-gather = bf16[256,768]{1,0:T(8,128)(2,1)S(1)} all-gather(bf16[16,768]{1,0:T(8,128)(2,1)} %get-tuple-element.15), channel_id=2, replica_groups=mesh['grp'=4,'seq'=2,'dp'=4] {'grp','dp'}, dimensions={0}, use_global_device_ids=true | all-gather | bytes 417792 | tf_op jit(solution)/shard_map/all_gather | solution.py:381
  120.8 1.0 bitcast_add_fusion.1
  121.8 0.7 collective-permute-start.6
  122.5 3.2 %collective-permute-start.8 = (f32[8,768]{1,0:T(8,128)S(1)}, f32[8,768]{1,0:T(8,128)S(1)}, u32[]{:S(2)}, u32[]{:S(2)}) collective-permute-start(f32[8,768]{1,0:T(8,128)S(1)} %get-tuple-element.21), channel_id=1, source_target_pairs={{0,3},{1,0},{2,1},{3,2},{4,7},{5,4},{6,5},{7,6},{8,11},{9,8},{10,9... | collective-permute-start | bytes 73736 | tf_op jit(solution)/shard_map/ppermute | solution.py:282
  125.7 1.8 collective-permute-done.6
  128.1 69.4 %all_gather.10 = bf16[32,8,896]{2,1,0:T(8,128)(2,1)S(1)} all-gather(bf16[1,8,896]{2,1,0:T(8,128)(2,1)S(1)} %pad_maximum_fusion.1), channel_id=1, replica_groups=mesh['grp'=4,'seq'=2,'dp'=4] {'grp','seq','dp'}, dimensions={0}, use_global_device_ids=true | all-gather | bytes 473088 | tf_op jit(solution)/shard_map/all_gather | solution.py:378
  197.6 0.9 copy-done.1
  198.5 0.8 multiply_reduce_fusion
  199.3 0.7 slice_reduce_fusion.1
  201.2 1.0 copy.21
  203.0 2.1 slice_multiply_fusion
  (47 shorter events, 4.8 us)
Async XLA Ops:
  0.6 1.9 copy-start
  0.6 11.5 %copy-start.3 = (bf16[3072,64]{0,1:T(8,128)(2,1)S(1)}, bf16[3072,64]{0,1:T(8,128)(2,1)}, u32[]{:S(2)}) copy-start(bf16[3072,64]{0,1:T(8,128)(2,1)} %param.22) | copy-start | bytes 1179652
  3.7 9.6 %collective-permute-start = (f32[2,6144]{1,0:T(2,128)}, f32[2,6144]{1,0:T(2,128)}, u32[]{:S(2)}, u32[]{:S(2)}) collective-permute-start(f32[2,6144]{1,0:T(2,128)} %fusion.3), channel_id=1, source_target_pairs={{0,4},{4,0},{1,5},{5,1},{2,6},{6,2},{3,7},{7,3},{8,12},{12,8},{9,1... | collective-permute-start | bytes 147464 | tf_op jit(solution)/shard_map/ppermute | solution.py:282
  8.8 19.3 %collective-permute-start.1 = (bf16[80,3072]{1,0:T(8,128)(2,1)}, bf16[80,3072]{1,0:T(8,128)(2,1)}, u32[]{:S(2)}, u32[]{:S(2)}) collective-permute-start(bf16[80,3072]{1,0:T(8,128)(2,1)} %fusion.refs_0_), channel_id=1, source_target_pairs={{0,4},{4,0},{1,5},{5,1},{2,6},{6,2},{3,7},{7,3},{8,12},{12,8},{9,1... | collective-permute-start | bytes 1474568 | tf_op jit(solution)/shard_map/ppermute | solution.py:282
  8.8 19.3 %collective-permute-start.2 = (bf16[48,3072]{1,0:T(8,128)(2,1)}, bf16[48,3072]{1,0:T(8,128)(2,1)}, u32[]{:S(2)}, u32[]{:S(2)}) collective-permute-start(bf16[48,3072]{1,0:T(8,128)(2,1)} %bitcast.47), channel_id=1, source_target_pairs={{0,4},{4,0},{1,5},{5,1},{2,6},{6,2},{3,7},{7,3},{8,12},{12,8},{9,1... | collective-permute-start | bytes 884744 | tf_op jit(solution)/shard_map/ppermute | solution.py:282
  57.3 5.5 %collective-permute-start.9 = (f32[2,16,3072]{2,1,0:T(8,128)}, f32[2,16,3072]{2,1,0:T(8,128)}, u32[]{:S(2)}, u32[]{:S(2)}) collective-permute-start(f32[2,16,3072]{2,1,0:T(8,128)} %get-tuple-element.12), channel_id=1, source_target_pairs={{0,8},{8,0},{16,24},{24,16},{1,9},{9,1},{17,25},{25,17},{2,10},{10... | collective-permute-start | bytes 1179656 | tf_op jit(solution)/shard_map/ppermute | solution.py:277
  57.4 8.1 %collective-permute-start.3 = (f32[2,16,3072]{2,1,0:T(8,128)}, f32[2,16,3072]{2,1,0:T(8,128)S(1)}, u32[]{:S(2)}, u32[]{:S(2)}) collective-permute-start(f32[2,16,3072]{2,1,0:T(8,128)} %get-tuple-element.9), channel_id=1, source_target_pairs={{0,8},{8,0},{16,24},{24,16},{1,9},{9,1},{17,25},{25,17},{2,10},{10... | collective-permute-start | bytes 1179656 | tf_op jit(solution)/shard_map/ppermute | solution.py:277
  64.0 7.0 %collective-permute-start.10 = (f32[16,3072]{1,0:T(8,128)S(1)}, f32[16,3072]{1,0:T(8,128)S(1)}, u32[]{:S(2)}, u32[]{:S(2)}) collective-permute-start(f32[16,3072]{1,0:T(8,128)S(1)} %dynamic-slice_bitcast_fusion), channel_id=1, source_target_pairs={{0,16},{8,24},{16,0},{24,8},{1,17},{9,25},{17,1},{25,9},{2,18},{10... | collective-permute-start | bytes 589832 | tf_op jit(solution)/shard_map/ppermute | solution.py:277
  66.6 10.0 %collective-permute-start.4 = (f32[2,8,3072]{2,1,0:T(8,128)S(1)}, f32[2,8,3072]{2,1,0:T(8,128)S(1)}, u32[]{:S(2)}, u32[]{:S(2)}) collective-permute-start(f32[2,8,3072]{2,1,0:T(8,128)S(1)} %constant_dynamic-slice_fusion.6), channel_id=1, source_target_pairs={{0,4},{4,0},{1,5},{5,1},{2,6},{6,2},{3,7},{7,3},{8,12},{12,8},{9,1... | collective-permute-start | bytes 589832 | tf_op jit(solution)/shard_map/ppermute | solution.py:282
  71.0 8.4 %collective-permute-start.11 = (f32[16,768]{1,0:T(8,128)S(1)}, f32[16,768]{1,0:T(8,128)S(1)}, u32[]{:S(2)}, u32[]{:S(2)}) collective-permute-start(f32[16,768]{1,0:T(8,128)S(1)} %get-tuple-element.17), channel_id=1, source_target_pairs={{0,1},{1,2},{2,3},{3,0},{4,5},{5,6},{6,7},{7,4},{8,9},{9,10},{10,1... | collective-permute-start | bytes 147464 | tf_op jit(solution)/shard_map/ppermute | solution.py:282
  72.6 6.8 %collective-permute-start.12 = (f32[16,768]{1,0:T(8,128)S(1)}, f32[16,768]{1,0:T(8,128)S(1)}, u32[]{:S(2)}, u32[]{:S(2)}) collective-permute-start(f32[16,768]{1,0:T(8,128)S(1)} %get-tuple-element.19), channel_id=1, source_target_pairs={{0,2},{1,3},{2,0},{3,1},{4,6},{5,7},{6,4},{7,5},{8,10},{9,11},{10,... | collective-permute-start | bytes 147464 | tf_op jit(solution)/shard_map/ppermute | solution.py:282
  75.2 4.2 %collective-permute-start.13 = (f32[16,768]{1,0:T(8,128)S(1)}, f32[16,768]{1,0:T(8,128)S(1)}, u32[]{:S(2)}, u32[]{:S(2)}) collective-permute-start(f32[16,768]{1,0:T(8,128)S(1)} %get-tuple-element.18), channel_id=1, source_target_pairs={{0,3},{1,0},{2,1},{3,2},{4,7},{5,4},{6,5},{7,6},{8,11},{9,8},{10,9... | collective-permute-start | bytes 147464 | tf_op jit(solution)/shard_map/ppermute | solution.py:282
  76.6 0.7 copy-start.2
  77.9 42.9 %collective-permute-start.5 = (f32[8,3072]{1,0:T(8,128)}, f32[8,3072]{1,0:T(8,128)}, u32[]{:S(2)}, u32[]{:S(2)}) collective-permute-start(f32[8,3072]{1,0:T(8,128)} %dynamic-slice_bitcast_fusion.1), channel_id=1, source_target_pairs={{0,16},{8,24},{16,0},{24,8},{1,17},{9,25},{17,1},{25,9},{2,18},{10... | collective-permute-start | bytes 294920 | tf_op jit(solution)/shard_map/ppermute | solution.py:277
  121.8 5.7 %collective-permute-start.6 = (f32[8,768]{1,0:T(8,128)S(1)}, f32[8,768]{1,0:T(8,128)S(1)}, u32[]{:S(2)}, u32[]{:S(2)}) collective-permute-start(f32[8,768]{1,0:T(8,128)S(1)} %get-tuple-element.20), channel_id=1, source_target_pairs={{0,1},{1,2},{2,3},{3,0},{4,5},{5,6},{6,7},{7,4},{8,9},{9,10},{10,1... | collective-permute-start | bytes 73736 | tf_op jit(solution)/shard_map/ppermute | solution.py:282
  122.5 5.0 %collective-permute-start.7 = (f32[8,768]{1,0:T(8,128)S(1)}, f32[8,768]{1,0:T(8,128)S(1)}, u32[]{:S(2)}, u32[]{:S(2)}) collective-permute-start(f32[8,768]{1,0:T(8,128)S(1)} %get-tuple-element.22), channel_id=1, source_target_pairs={{0,2},{1,3},{2,0},{3,1},{4,6},{5,7},{6,4},{7,5},{8,10},{9,11},{10,... | collective-permute-start | bytes 73736 | tf_op jit(solution)/shard_map/ppermute | solution.py:282
  122.5 5.5 %collective-permute-start.8 = (f32[8,768]{1,0:T(8,128)S(1)}, f32[8,768]{1,0:T(8,128)S(1)}, u32[]{:S(2)}, u32[]{:S(2)}) collective-permute-start(f32[8,768]{1,0:T(8,128)S(1)} %get-tuple-element.21), channel_id=1, source_target_pairs={{0,3},{1,0},{2,1},{3,2},{4,7},{5,4},{6,5},{7,6},{8,11},{9,8},{10,9... | collective-permute-start | bytes 73736 | tf_op jit(solution)/shard_map/ppermute | solution.py:282
  197.6 0.9 copy-start.1

commit v2 on v1

--- a/solution.py
+++ b/solution.py
@@ -67,7 +67,7 @@
     img_part, txt_part = noisy[0].shape[0], text[0].shape[0]
     rows, trows = n * img_part, n * txt_part
     block = min(rows, 160)
-    grp_rows = send_a.shape[1]
+    half = send_a.shape[0]
 
     def modulated(parts, dest, size, total, base):
         for k in range(n):
@@ -186,9 +186,8 @@
 
     def share(value, columns, send, keep):
         whole[:, columns] = value
-        for x in range(2):
-            keep[x] = whole[pl.ds(pl.multiple_of((2 * x + core) * grp_rows, 8), grp_rows), columns]
-            send[x] = whole[pl.ds(pl.multiple_of((2 * x + 1 - core) * grp_rows, 8), grp_rows), columns]
+        keep[...] = whole[pl.ds(pl.multiple_of(core * half, 8), half), columns]
+        send[...] = whole[pl.ds(pl.multiple_of((1 - core) * half, 8), half), columns].astype(send.dtype)
 
     share(nn(lowt[...], gq[...]), slice(0, gq.shape[1]), send_b, keep_b)
     glt[...] += nt(up_ref[...], gq[...])
@@ -218,7 +217,7 @@
     pair = 2 if count % 2 == 0 else 1
     steps = count // pair
     rows, trows = n * noisy[0].shape[0], n * text[0].shape[0]
-    groups = rank // 4
+    half = rank // 2
     samples = lax.axis_size("grp") * lax.axis_size("dp")
     ic, tc = pair * 3 * HD, pair * 2 * HD
 
@@ -230,10 +229,9 @@
             return pl.BlockSpec((height, cols), lambda s: (0, s), pipeline_mode=pl.Buffered(1))
         return pl.BlockSpec((height, cols), lambda s: (0, s))
 
-    out_a = jax.ShapeDtypeStruct((2, groups, width), F32)
-    out_b = jax.ShapeDtypeStruct((2, groups, img_cols), F32)
-    spec_a = pl.BlockSpec(out_a.shape, lambda s: (0, 0, 0))
-    spec_b = pl.BlockSpec((2, groups, ic), lambda s: (0, 0, s))
+    out_a, out_b = (half, width), (half, img_cols)
+    spec_a = pl.BlockSpec(out_a, lambda s: (0, 0))
+    spec_b = pl.BlockSpec((half, ic), lambda s: (0, s))
     flops = 4 * rows * width * img_cols + 4 * trows * width * wt.shape[1]
     return pl.pallas_call(
         functools.partial(middle_kernel, n, steps, pair, samples),
@@ -243,7 +241,13 @@
         + [columns(rank, ic), columns(width, ic), columns(width, tc)]
         + [fixed(x) for x in (*noisy, *text)],
         out_specs=[spec_a, spec_a, spec_b, spec_b, pl.BlockSpec((8, HD), lambda s: (0, 0))],
-        out_shape=[out_a, out_a, out_b, out_b, jax.ShapeDtypeStruct((8, HD), F32)],
+        out_shape=[
+            jax.ShapeDtypeStruct(out_a, BF16),
+            jax.ShapeDtypeStruct(out_a, F32),
+            jax.ShapeDtypeStruct(out_b, BF16),
+            jax.ShapeDtypeStruct(out_b, F32),
+            jax.ShapeDtypeStruct((8, HD), F32),
+        ],
         scratch_shapes=[
             pltpu.VMEM((2 * rows, width), BF16),
             pltpu.VMEM((2 * trows, width), BF16),
@@ -272,9 +276,67 @@
     )(where, mod, bias, gain, down, up, wi, wt, *noisy, *text)
 
 
-def swap(x, bit):
-    size = lax.axis_size("grp")
-    return lax.ppermute(x, "grp", [(i, i ^ bit) for i in range(size)])
+def start_kernel(sigma_ref, image_ref, noise_ref, emb_ref, weight_ref, noisy_ref, part_ref):
+    sigma = sigma_ref[0]
+    clean, noise = image_ref[...].astype(F32), noise_ref[...].astype(F32)
+    noisy_ref[...] = ((1.0 - sigma) * clean + sigma * noise).astype(BF16)
+    part_ref[...] = nn(emb_ref[...], weight_ref[...])[: part_ref.shape[0]]
+
+
+def start(sigma, image, noise, emb, weight):
+    rows, width = image.shape
+    depth, cols = weight.shape
+    steps = 4 if width % 512 == 0 and cols % 512 == 0 else 1
+    tokens = pl.BlockSpec((rows, width // steps), lambda s: (0, s))
+    return pl.pallas_call(
+        start_kernel,
+        grid=(steps,),
+        in_specs=[
+            pl.BlockSpec(memory_space=pltpu.SMEM),
+            tokens,
+            tokens,
+            pl.BlockSpec(emb.shape, lambda s: (0, 0)),
+            pl.BlockSpec((depth, cols // steps), lambda s: (0, s)),
+        ],
+        out_specs=[tokens, pl.BlockSpec((2, cols // steps), lambda s: (0, s))],
+        out_shape=[
+            jax.ShapeDtypeStruct((rows, width), BF16),
+            jax.ShapeDtypeStruct((2, cols), F32),
+        ],
+        compiler_params=pltpu.CompilerParams(
+            dimension_semantics=("arbitrary",), vmem_limit_bytes=16 * 1024 * 1024
+        ),
+        cost_estimate=pl.CostEstimate(
+            flops=4 * depth * cols, bytes_accessed=30_000_000, transcendentals=0
+        ),
+        name="start",
+    )(sigma, image, noise, emb, weight)
+
+
+def finish_kernel(scale_a, scale_b, scale_loss, a_ref, b_ref, sums_ref, out_a, out_b, loss_ref):
+    half = HD // 2
+    total = jnp.sum(sums_ref[...], axis=0, keepdims=True)
+    loss_ref[...] = jnp.sum(total[:, :half], axis=1, keepdims=True) * scale_loss
+    squares_b = jnp.sum(total[:, half:], axis=1, keepdims=True) * scale_b
+    grad_a = a_ref[...].astype(F32)
+    squares = jnp.sum(jnp.sum(grad_a * grad_a, axis=0, keepdims=True), axis=1, keepdims=True)
+    unit_a = lax.rsqrt(squares * scale_a + EPS)
+    out_b[...] = b_ref[...].astype(F32) * lax.rsqrt(squares_b + EPS)
+    for c in range(0, a_ref.shape[1], HD):
+        out_a[c : c + HD, :] = (a_ref[:, c : c + HD].astype(F32) * unit_a).T
+
+
+def finish(grad_a, grad_b, sums, n, entries):
+    (rank, width), cols = grad_a.shape, grad_b.shape[1]
+    return pl.pallas_call(
+        functools.partial(finish_kernel, 1.0 / (rank * width), 1.0 / (rank * cols * n), 1.0 / entries),
+        out_shape=[
+            jax.ShapeDtypeStruct((width, rank), F32),
+            jax.ShapeDtypeStruct((rank, cols), F32),
+            jax.ShapeDtypeStruct((1, 1), F32),
+        ],
+        name="finish",
+    )(grad_a, grad_b, sums)
 
 
 def shifted(x, axis, k):
@@ -282,27 +344,75 @@
     return lax.ppermute(x, axis, [(i, (i + k) % size) for i in range(size)])
 
 
-def scatter_sum(x, axis, dim):
-    size, me = lax.axis_size(axis), lax.axis_index(axis)
-    each = x.shape[dim] // size
-    block = lambda k: lax.dynamic_slice_in_dim(x, lax.rem(me + k, size) * each, each, dim)
-    total = block(0)
-    for k in range(1, size):
-        total = total + shifted(block(k), axis, k)
-    return total
-
-
-def half_sum(x, bit):
-    side = lax.div(lax.axis_index("grp"), bit)
-    keep = lax.dynamic_index_in_dim(x, side, 0, keepdims=False)
-    send = lax.dynamic_index_in_dim(x, 1 - side, 0, keepdims=False)
-    return keep + swap(send, bit)
+def side_of(axis, bit):
+    return lax.rem(lax.div(lax.axis_index(axis), bit), 2)
+
+
+def swap(arrays, axis, bit):
+    pairs = [(i, i ^ bit) for i in range(lax.axis_size(axis))]
+    if len(arrays) == 1 or any(x.shape[0] % 8 or x.shape[1] % HD for x in arrays):
+        return [lax.ppermute(x, axis, pairs) for x in arrays]
+    rows = [x[r : r + 8] for x in arrays for r in range(0, x.shape[0], 8)]
+    got = lax.ppermute(jnp.concatenate(rows, 1), axis, pairs)
+    out, at = [], 0
+    for x in arrays:
+        blocks = []
+        for _ in range(0, x.shape[0], 8):
+            blocks.append(got[:, at : at + x.shape[1]])
+            at += x.shape[1]
+        out.append(blocks[0] if len(blocks) == 1 else jnp.concatenate(blocks, 0))
+    return out
+
+
+def cut_of(x):
+    if x.shape[0] % 16 == 0:
+        return 0
+    return 1 if x.shape[1] % (2 * HD) == 0 else 0
+
+
+def halve(arrays, axis, bit, dtype):
+    side = side_of(axis, bit)
+    keep, send = [], []
+    for x in arrays:
+        dim = cut_of(x)
+        first, second = jnp.split(x, 2, dim)
+        keep.append(jnp.where(side == 0, first, second))
+        send.append(jnp.where(side == 0, second, first).astype(dtype))
+    got = swap(send, axis, bit)
+    return [k + g.astype(F32) for k, g in zip(keep, got)]
+
+
+def join(mine, theirs, side, dim):
+    return jnp.concatenate(
+        [jnp.where(side == 0, mine, theirs), jnp.where(side == 0, theirs, mine)], dim
+    )
 
 
 def pieces(value):
     first = lax.reduce_precision(value, 8, 7)
-    second = lax.reduce_precision(value - first, 8, 7)
-    return [first, second, value - first - second]
+    rest = value - first
+    second = lax.reduce_precision(rest, 8, 7)
+    return jnp.concatenate([first, second, rest - second], 1).astype(BF16)
+
+
+def rejoin(arrays, dims, sums, axis, bit):
+    side = side_of(axis, bit)
+    *got, other = swap([*arrays, pieces(sums)], axis, bit)
+    other = other.astype(F32)
+    sums = sums + (other[:, :HD] + other[:, HD : 2 * HD] + other[:, 2 * HD :])
+    return [join(x, g, side, d) for x, g, d in zip(arrays, got, dims)], sums
+
+
+def bits(axis):
+    size = lax.axis_size(axis)
+    return [1 << i for i in range(size.bit_length() - 1)]
+
+
+def fold(x):
+    half = HD // 2
+    return functools.reduce(
+        lambda total, c: total + x[:, c : c + half], range(half, x.shape[1], half), x[:, :half]
+    )
 
 
 def on_device(
@@ -324,17 +434,16 @@
     n, me = lax.axis_size("seq"), lax.axis_index("seq")
     samples = lax.axis_size("grp") * lax.axis_size("dp")
     sigma = (timestep[0].astype(F32) + 1.0) / STEPS
-    start = timing(sigma, emb_width)
+    time = timing(sigma, emb_width)
     emb = jnp.stack(
         [
-            jnp.concatenate([start, timing(guidance[0], emb_width)]),
-            jnp.concatenate([start, jnp.zeros((emb_width // 2,), F32)]),
+            jnp.concatenate([time, timing(guidance[0], emb_width)]),
+            jnp.concatenate([time, jnp.zeros((emb_width // 2,), F32)]),
         ]
     )
-    emb = jax.nn.silu(emb).astype(BF16)
-    part = jnp.dot(emb, modulation_weight, preferred_element_type=F32)
+    emb = jnp.pad(jax.nn.silu(emb).astype(BF16), ((0, 14), (0, 0)))
+    noisy, part = start(sigma[None], image[0], noise[0], emb, modulation_weight)
     mods = [part] + [shifted(part, "seq", k) for k in range(1, n)]
-    noisy = ((1.0 - sigma) * image[0].astype(F32) + sigma * noise[0].astype(F32)).astype(BF16)
     noisy_parts = [noisy] + [shifted(noisy, "seq", k) for k in range(1, n)]
     words = text[0]
     text_parts = [words] + [shifted(words, "seq", k) for k in range(1, n)]
@@ -366,30 +475,32 @@
         noisy_parts,
         text_parts,
     )
-    sum_a = keep_a + swap(send_a, 1)
-    sum_b = keep_b + swap(send_b, 1)
-    sum_a = scatter_sum(sum_a, "seq", 1)
-    sum_b = half_sum(sum_b, 2)
-    sum_a = half_sum(sum_a, 2)
-    sum_b = scatter_sum(sum_b, "dp", 1)
-    sum_a = scatter_sum(sum_a, "dp", 1)
-    scalars = jnp.stack(pieces(jnp.sum(loss)) + pieces(jnp.sum(sum_b * sum_b)))
-    extra = jnp.broadcast_to(jnp.pad(scalars, (0, HD - 6))[None], (sum_a.shape[0], HD))
-    all_a = lax.all_gather(
-        jnp.concatenate([sum_a, extra], 1).astype(BF16), ("grp", "seq", "dp")
-    ).astype(F32)
-    all_b = lax.all_gather(sum_b.astype(BF16), ("grp", "dp")).astype(F32)
-    grps, dps = lax.axis_size("grp"), lax.axis_size("dp")
-    scalars = jnp.sum(all_a[:, 0, -HD:], 0)
-    loss_mean = jnp.sum(scalars[:3]) / samples / (n * img_part * HEADS * HD)
-    squares_b = jnp.sum(scalars[3:6])
-    grad_a = all_a[:, :, :-HD].reshape(grps * n, dps, sum_a.shape[0], sum_a.shape[1])
-    grad_a = grad_a.transpose(1, 3, 0, 2).reshape(width, -1)
-    grad_b = all_b.reshape(grps, dps, *sum_b.shape).transpose(0, 2, 1, 3)
-    grad_b = grad_b.reshape(adapter_up_weight.shape)
-    direction_a = grad_a * lax.rsqrt(jnp.mean(grad_a * grad_a) + EPS)
-    direction_b = grad_b * lax.rsqrt(squares_b / (grad_b.size * n) + EPS)
-    return (direction_a, direction_b, loss_mean)
+    (got_a,), (got_b,) = swap([send_a], "grp", 1), swap([send_b], "grp", 1)
+    grad_a, grad_b = keep_a + got_a.astype(F32), keep_b + got_b.astype(F32)
+    seq_dims, dp_dims = [], []
+    for bit in reversed(bits("seq")):
+        seq_dims.append(cut_of(grad_a))
+        (grad_a,) = halve([grad_a], "seq", bit, BF16)
+    x_dims = [cut_of(grad_a), cut_of(grad_b)]
+    (grad_b,) = halve([grad_b], "grp", 2, BF16)
+    (grad_a,) = halve([grad_a], "grp", 2, BF16)
+    for bit in reversed(bits("dp")):
+        dp_dims.append([cut_of(grad_a), cut_of(grad_b)])
+        grad_a, grad_b = halve([grad_a, grad_b], "dp", bit, F32)
+    squares = fold(grad_b * grad_b)
+    squares = jnp.pad(squares, ((0, 8 - squares.shape[0]), (0, 0)))
+    sums = jnp.concatenate([fold(loss), squares], 1)
+    grads = [grad_a.astype(BF16), grad_b.astype(BF16)]
+    for bit in bits("dp"):
+        grads, sums = rejoin(grads, dp_dims.pop(), sums, "dp", bit)
+    grads, sums = rejoin(grads, x_dims, sums, "grp", 2)
+    for bit in bits("seq"):
+        (grads[0],), sums = rejoin(grads[:1], [seq_dims.pop()], sums, "seq", bit)
+    grads, sums = rejoin(grads, [0, 0], sums, "grp", 1)
+    direction_a, direction_b, loss_mean = finish(
+        *grads, sums, n, samples * n * img_part * HEADS * HD
+    )
+    return (direction_a, direction_b, loss_mean[0, 0])
 
 
 def solution(mesh):

time: 207 us -> 116 us (0.56)
  blocking collectives: 103 us -> 0 us
  waiting for transfers between devices: 19.3 us -> 43.2 us
  between operations: 13.8 us -> 3.01 us
  other arithmetic: 13.4 us -> 6.93 us
  Pallas kernels: 29.2 us -> 33.3 us
  local copies, waits for them, and re-layouts: 8.49 us -> 10.6 us
    all_gather x2 -> x0, blocking collectives: 103 us -> none  [the longest x1 69.4 us: on_device(): lax.all_gather(jnp.concatenate([sum_a, extra], 1).astype(BF16), ('grp', '...]
    ppermute x4 -> x12, waiting for transfers between devices: 3.76 us -> 30.6 us  [the longest x7 26.4 us: swap(): got = lax.ppermute(jnp.concatenate(rows, 1), axis, pairs)]
    ppermute x4 -> x12, starting transfers between devices: 3.6 us -> 13.7 us  [the longest x7 8.28 us: swap(): got = lax.ppermute(jnp.concatenate(rows, 1), axis, pairs)]
    ppermute x10 -> x3, starting transfers between devices: 15 us -> 5.05 us  [shifted(): return lax.ppermute(x, axis, [(i, (i + k) % size) for i in range(size)])]
    unnamed x10 -> x23, local copies, waits for them, and re-layouts: 3.77 us -> 9.78 us
    pallas_call x0 -> x2, Pallas kernels: none -> 4.25 us  [the longest x1 2.93 us: finish(): pl.pallas_call(functools.partial(finish_kernel, 1.0 / (rank * width), 1.0...]
    reduce_sum x5 -> x0, other arithmetic: 3.49 us -> none  [the longest x2 1.97 us: on_device(): scalars = jnp.stack(pieces(jnp.sum(loss)) + pieces(jnp.sum(sum_b * sum_b)))]
    ppermute x10 -> x3, waiting for transfers between devices: 15.5 us -> 12.7 us  [shifted(): return lax.ppermute(x, axis, [(i, (i + k) % size) for i in range(size)])]
  transfers between devices with their start and end apart: 14 -> 15, of which waited for: 4 -> 12; matrix products, arithmetic and copies ran while one was open for 7% -> 6% of each run, Pallas kernels for 0% -> 0%
where the time goes in v2:
time: 116 us
  waiting for transfers between devices  43.2 us (37%)
  Pallas kernels  33.3 us (29%)
  starting transfers between devices  18.8 us (16%)
  local copies, waits for them, and re-layouts  10.6 us (9%)
  other arithmetic  6.93 us (6%)
  between operations  3.01 us (3%)
    pallas_call x1, Pallas kernels, middle(): pl.pallas_call(functools.partial(middle_kernel, n, steps, pair, samples),...  29.1 us
    ppermute x7, waiting for transfers between devices, swap(): got = lax.ppermute(jnp.concatenate(rows, 1), axis, pairs)  26.4 us
    ppermute x3, waiting for transfers between devices, shifted(): return lax.ppermute(x, axis, [(i, (i + k) % size) for i in range(size)])  12.7 us
    unnamed x23, local copies, waits for them, and re-layouts  9.78 us
    ppermute x7, starting transfers between devices, swap(): got = lax.ppermute(jnp.concatenate(rows, 1), axis, pairs)  8.28 us
    ppermute x5, starting transfers between devices, swap(): return [lax.ppermute(x, axis, pairs) for x in arrays]  5.45 us
    ppermute x3, starting transfers between devices, shifted(): return lax.ppermute(x, axis, [(i, (i + k) % size) for i in range(size)])  5.05 us
    ppermute x5, waiting for transfers between devices, swap(): return [lax.ppermute(x, axis, pairs) for x in arrays]  4.15 us
  transfers between devices with their start and end apart: 15, of which 12 were waited for; matrix products, arithmetic and copies ran while one was open for 6% of the time, Pallas kernels for 0%

profile of v2, /device:TPU:0, one launch (start us, length us, event | category | flops | bytes accessed | tf_op | source)
XLA Modules:
  0.0 115.9 jit_solution(13616122785471793856)
XLA Ops:
  2.2 1.9 %copy-done = bf16[256,6144]{1,0:T(8,128)(2,1)S(1)} copy-done((bf16[256,6144]{1,0:T(8,128)(2,1)S(1)}, bf16[256,6144]{1,0:T(8,128)(2,1)}, u32[]{:S(2)}) %copy-start) | copy-done | bytes 3145752
  4.1 1.0 copy-done.2
  5.1 1.0 copy-done.3
  6.1 1.3 %start.1 = (bf16[80,3072]{1,0:T(8,128)(2,1)S(1)}, f32[2,6144]{1,0:T(2,128)S(1)}) custom-call(f32[1]{0:T(128)} %bitcast.2.sigma_ref, bf16[80,3072]{1,0:T(8,128)(2,1)S(1)} %bitcast.17, bf16[80,3072]{1,0:T(8,128)(2,1)S(1)} %bitcast.18, bf16[16,256]{1,0:T(8,128)(2,1)S(1)} %pad.4.emb_ref, bf16[256,6144]{1,0:T(8,128)(2,1)S(1)} %copy-done), custom_call_target="tpu_custom_call" | custom-call | flops 6291456 | bytes 30000000 | tf_op jit(solution)/shard_map/start/pallas_call | solution.py:291
  7.4 3.0 %collective-permute-start = (f32[2,6144]{1,0:T(2,128)S(1)}, f32[2,6144]{1,0:T(2,128)S(1)}, u32[]{:S(2)}, u32[]{:S(2)}) collective-permute-start(f32[2,6144]{1,0:T(2,128)S(1)} %get-tuple-element.13), channel_id=1, source_target_pairs={{0,4},{4,0},{1,5},{5,1},{2,6},{6,2},{3,7},{7,3},{8,12},{12,8},{9,1... | collective-permute-start | bytes 147464 | tf_op jit(solution)/shard_map/ppermute | solution.py:344
  10.6 1.9 %collective-permute-start.2 = (bf16[48,3072]{1,0:T(8,128)(2,1)}, bf16[48,3072]{1,0:T(8,128)(2,1)S(1)}, u32[]{:S(2)}, u32[]{:S(2)}) collective-permute-start(bf16[48,3072]{1,0:T(8,128)(2,1)} %bitcast.19), channel_id=1, source_target_pairs={{0,4},{4,0},{1,5},{5,1},{2,6},{6,2},{3,7},{7,3},{8,12},{12,8},{9,1... | collective-permute-start | bytes 884744 | tf_op jit(solution)/shard_map/ppermute | solution.py:344
  13.8 2.2 %copy.15.down_ref = bf16[3072,64]{1,0:T(8,128)(2,1)} copy(bf16[3072,64]{0,1:T(8,128)(2,1)} %param.22) | data formatting | bytes 786432 | tf_op args[10]
  16.8 12.7 %collective-permute-done.2.refs_3_ = bf16[48,3072]{1,0:T(8,128)(2,1)S(1)} collective-permute-done((bf16[48,3072]{1,0:T(8,128)(2,1)}, bf16[48,3072]{1,0:T(8,128)(2,1)S(1)}, u32[]{:S(2)}, u32[]{:S(2)}) %collective-permute-start.2) | collective-permute-done | bytes 294944 | tf_op jit(solution)/shard_map/ppermute | solution.py:344
  30.4 29.1 %middle.1 = (bf16[32,3072]{1,0:T(8,128)(2,1)}, f32[32,3072]{1,0:T(8,128)}, bf16[32,3072]{1,0:T(8,128)(2,1)}, f32[32,3072]{1,0:T(8,128)}, f32[8,128]{1,0:T(8,128)}) custom-call(s32[1]{0:T(128)} %bitcast.where_ref, f32[8,3072]{1,0:T(8,128)} %reshape.47.mod_ref, f32[1,256]{1,0:T(1,128)} %compare_select_fusion.bias_ref, f32[3,128]{1,0:T(4,128)} %gain_ref.1, ...), custom_call_target="tpu_custom_call" | custom-call | flops 8455716864 | bytes 31457280 | tf_op jit(solution)/shard_map/middle/pallas_call | solution.py:236
  60.0 1.1 collective-permute-done.3
  61.2 1.0 convert_add_fusion.1
  62.2 1.4 %collective-permute-start.4 = (bf16[16,3072]{1,0:T(8,128)(2,1)S(1)}, bf16[16,3072]{1,0:T(8,128)(2,1)S(1)}, u32[]{:S(2)}, u32[]{:S(2)}) collective-permute-start(bf16[16,3072]{1,0:T(8,128)(2,1)S(1)} %select_convert_fusion.1), channel_id=1, source_target_pairs={{0,4},{4,0},{1,5},{5,1},{2,6},{6,2},{3,7},{7,3},{8,12},{12,8},{9,1... | collective-permute-start | bytes 294920 | tf_op jit(solution)/shard_map/ppermute | solution.py:354
  63.6 1.0 convert_add_fusion
  64.7 1.6 %collective-permute-start.7 = (bf16[16,3072]{1,0:T(8,128)(2,1)S(1)}, bf16[16,3072]{1,0:T(8,128)(2,1)S(1)}, u32[]{:S(2)}, u32[]{:S(2)}) collective-permute-start(bf16[16,3072]{1,0:T(8,128)(2,1)S(1)} %select_convert_fusion), channel_id=1, source_target_pairs={{0,16},{8,24},{16,0},{24,8},{1,17},{9,25},{17,1},{25,9},{2,18},{10... | collective-permute-start | bytes 294920 | tf_op jit(solution)/shard_map/ppermute | solution.py:354
  66.3 0.9 collective-permute-done.4
  67.2 2.0 %collective-permute-start.5 = (bf16[8,3072]{1,0:T(8,128)(2,1)S(1)}, bf16[8,3072]{1,0:T(8,128)(2,1)S(1)}, u32[]{:S(2)}, u32[]{:S(2)}) collective-permute-start(bf16[8,3072]{1,0:T(8,128)(2,1)S(1)} %select_convert_fusion.2), channel_id=1, source_target_pairs={{0,16},{8,24},{16,0},{24,8},{1,17},{9,25},{17,1},{25,9},{2,18},{10... | collective-permute-start | bytes 147464 | tf_op jit(solution)/shard_map/ppermute | solution.py:354
  69.5 1.8 %collective-permute-done.5 = bf16[8,3072]{1,0:T(8,128)(2,1)S(1)} collective-permute-done((bf16[8,3072]{1,0:T(8,128)(2,1)S(1)}, bf16[8,3072]{1,0:T(8,128)(2,1)S(1)}, u32[]{:S(2)}, u32[]{:S(2)}) %collective-permute-start.5) | collective-permute-done | bytes 49184 | tf_op jit(solution)/shard_map/ppermute | solution.py:354
  71.4 3.1 %collective-permute-start.8 = (f32[8,4608]{1,0:T(8,128)S(1)}, f32[8,4608]{1,0:T(8,128)S(1)}, u32[]{:S(2)}, u32[]{:S(2)}) collective-permute-start(f32[8,4608]{1,0:T(8,128)S(1)} %pad_maximum_fusion.6), channel_id=1, source_target_pairs={{0,2},{1,3},{2,0},{3,1},{4,6},{5,7},{6,4},{7,5},{8,10},{9,11},{10,... | collective-permute-start | bytes 442376 | tf_op jit(solution)/shard_map/ppermute | solution.py:356
  74.5 5.3 %collective-permute-done.8 = f32[8,4608]{1,0:T(8,128)S(1)} collective-permute-done((f32[8,4608]{1,0:T(8,128)S(1)}, f32[8,4608]{1,0:T(8,128)S(1)}, u32[]{:S(2)}, u32[]{:S(2)}) %collective-permute-start.8) | collective-permute-done | bytes 147488 | tf_op jit(solution)/shard_map/ppermute | solution.py:356
  79.9 0.8 collective-permute-start.9
  80.7 0.8 slice_add_fusion.37
  81.5 3.3 %collective-permute-done.9 = f32[8,2304]{1,0:T(8,128)S(1)} collective-permute-done((f32[8,2304]{1,0:T(8,128)S(1)}, f32[8,2304]{1,0:T(8,128)S(1)}, u32[]{:S(2)}, u32[]{:S(2)}) %collective-permute-start.9) | collective-permute-done | bytes 73760 | tf_op jit(solution)/shard_map/ppermute | solution.py:356
  85.3 4.4 %collective-permute-done.10 = bf16[8,2688]{1,0:T(8,128)(2,1)S(1)} collective-permute-done((bf16[8,2688]{1,0:T(8,128)(2,1)S(1)}, bf16[8,2688]{1,0:T(8,128)(2,1)S(1)}, u32[]{:S(2)}, u32[]{:S(2)}) %collective-permute-start.10) | collective-permute-done | bytes 43040 | tf_op jit(solution)/shard_map/ppermute | solution.py:356
  89.9 1.5 %collective-permute-start.11 = (bf16[8,4992]{1,0:T(8,128)(2,1)S(1)}, bf16[8,4992]{1,0:T(8,128)(2,1)S(1)}, u32[]{:S(2)}, u32[]{:S(2)}) collective-permute-start(bf16[8,4992]{1,0:T(8,128)(2,1)S(1)} %constant_dynamic-update-slice_fusion.5), channel_id=1, source_target_pairs={{0,2},{1,3},{2,0},{3,1},{4,6},{5,7},{6,4},{7,5},{8,10},{9,11},{10,... | collective-permute-start | bytes 239624 | tf_op jit(solution)/shard_map/ppermute | solution.py:356
  91.3 4.3 %collective-permute-done.11 = bf16[8,4992]{1,0:T(8,128)(2,1)S(1)} collective-permute-done((bf16[8,4992]{1,0:T(8,128)(2,1)S(1)}, bf16[8,4992]{1,0:T(8,128)(2,1)S(1)}, u32[]{:S(2)}, u32[]{:S(2)}) %collective-permute-start.11) | collective-permute-done | bytes 79904 | tf_op jit(solution)/shard_map/ppermute | solution.py:356
  95.7 1.6 %collective-permute-start.12 = (bf16[8,9600]{1,0:T(8,128)(2,1)S(1)}, bf16[8,9600]{1,0:T(8,128)(2,1)S(1)}, u32[]{:S(2)}, u32[]{:S(2)}) collective-permute-start(bf16[8,9600]{1,0:T(8,128)(2,1)S(1)} %constant_dynamic-update-slice_fusion.12), channel_id=1, source_target_pairs={{0,16},{8,24},{16,0},{24,8},{1,17},{9,25},{17,1},{25,9},{2,18},{10... | collective-permute-start | bytes 460808 | tf_op jit(solution)/shard_map/ppermute | solution.py:356
  97.3 3.7 %collective-permute-done.12 = bf16[8,9600]{1,0:T(8,128)(2,1)S(1)} collective-permute-done((bf16[8,9600]{1,0:T(8,128)(2,1)S(1)}, bf16[8,9600]{1,0:T(8,128)(2,1)S(1)}, u32[]{:S(2)}, u32[]{:S(2)}) %collective-permute-start.12) | collective-permute-done | bytes 153632 | tf_op jit(solution)/shard_map/ppermute | solution.py:356
  101.1 1.0 collective-permute-start.13
  102.1 3.7 %collective-permute-done.13 = bf16[8,6528]{1,0:T(8,128)(2,1)S(1)} collective-permute-done((bf16[8,6528]{1,0:T(8,128)(2,1)S(1)}, bf16[8,6528]{1,0:T(8,128)(2,1)S(1)}, u32[]{:S(2)}, u32[]{:S(2)}) %collective-permute-start.13) | collective-permute-done | bytes 104480 | tf_op jit(solution)/shard_map/ppermute | solution.py:356
  106.1 1.7 %collective-permute-done.14 = bf16[8,24960]{1,0:T(8,128)(2,1)S(1)} collective-permute-done((bf16[8,24960]{1,0:T(8,128)(2,1)S(1)}, bf16[8,24960]{1,0:T(8,128)(2,1)S(1)}, u32[]{:S(2)}, u32[]{:S(2)}) %collective-permute-start.14) | collective-permute-done | bytes 399392 | tf_op jit(solution)/shard_map/ppermute | solution.py:356
  110.2 2.9 %finish.1 = (f32[3072,64]{1,0:T(8,128)}, f32[64,3072]{1,0:T(8,128)}, f32[1,1]{1,0:T(1,128)}) custom-call(bf16[64,3072]{1,0:T(8,128)(2,1)} %pad_maximum_fusion.a_ref, bf16[64,3072]{1,0:T(8,128)(2,1)} %pad_maximum_fusion.1.b_ref, f32[8,128]{1,0:T(8,128)} %fusion.6.sums_ref), custom_call_target="tpu_custom_call" | custom-call | tf_op jit(solution)/shard_map/finish/pallas_call | solution.py:331
  113.1 2.7 %copy.16 = f32[3072,64]{0,1:T(8,128)} copy(f32[3072,64]{1,0:T(8,128)} %get-tuple-element.23) | data formatting | bytes 1572864
  (96 shorter events, 7.1 us)
Async XLA Ops:
  2.2 1.9 %copy-start = (bf16[256,6144]{1,0:T(8,128)(2,1)S(1)}, bf16[256,6144]{1,0:T(8,128)(2,1)}, u32[]{:S(2)}) copy-start(bf16[256,6144]{1,0:T(8,128)(2,1)} %weight_ref.1) | copy-start | bytes 9437188
  4.1 1.0 copy-start.2
  5.1 1.0 copy-start.3
  7.4 22.0 %copy-start.1 = (bf16[80,3072]{1,0:T(8,128)(2,1)}, bf16[80,3072]{1,0:T(8,128)(2,1)S(1)}, u32[]{:S(2)}) copy-start(bf16[80,3072]{1,0:T(8,128)(2,1)S(1)} %get-tuple-element.14.refs_0_) | copy-start | bytes 1474564
  7.4 8.5 %collective-permute-start = (f32[2,6144]{1,0:T(2,128)S(1)}, f32[2,6144]{1,0:T(2,128)S(1)}, u32[]{:S(2)}, u32[]{:S(2)}) collective-permute-start(f32[2,6144]{1,0:T(2,128)S(1)} %get-tuple-element.13), channel_id=1, source_target_pairs={{0,4},{4,0},{1,5},{5,1},{2,6},{6,2},{3,7},{7,3},{8,12},{12,8},{9,1... | collective-permute-start | bytes 147464 | tf_op jit(solution)/shard_map/ppermute | solution.py:344
  10.5 19.0 %collective-permute-start.1 = (bf16[80,3072]{1,0:T(8,128)(2,1)S(1)}, bf16[80,3072]{1,0:T(8,128)(2,1)S(1)}, u32[]{:S(2)}, u32[]{:S(2)}) collective-permute-start(bf16[80,3072]{1,0:T(8,128)(2,1)S(1)} %get-tuple-element.14.refs_0_), channel_id=1, source_target_pairs={{0,4},{4,0},{1,5},{5,1},{2,6},{6,2},{3,7},{7,3},{8,12},{12,8},{9,1... | collective-permute-start | bytes 1474568 | tf_op jit(solution)/shard_map/ppermute | solution.py:344
  10.6 18.9 %collective-permute-start.2 = (bf16[48,3072]{1,0:T(8,128)(2,1)}, bf16[48,3072]{1,0:T(8,128)(2,1)S(1)}, u32[]{:S(2)}, u32[]{:S(2)}) collective-permute-start(bf16[48,3072]{1,0:T(8,128)(2,1)} %bitcast.19), channel_id=1, source_target_pairs={{0,4},{4,0},{1,5},{5,1},{2,6},{6,2},{3,7},{7,3},{8,12},{12,8},{9,1... | collective-permute-start | bytes 884744 | tf_op jit(solution)/shard_map/ppermute | solution.py:344
  29.5 0.8 copy-start.5
  29.5 0.9 copy-start.4
  59.5 1.7 %collective-permute-start.3 = (bf16[32,3072]{1,0:T(8,128)(2,1)}, bf16[32,3072]{1,0:T(8,128)(2,1)S(1)}, u32[]{:S(2)}, u32[]{:S(2)}) collective-permute-start(bf16[32,3072]{1,0:T(8,128)(2,1)} %get-tuple-element.16), channel_id=1, source_target_pairs={{0,8},{8,0},{16,24},{24,16},{1,9},{9,1},{17,25},{25,17},{2,10},{10... | collective-permute-start | bytes 589832 | tf_op jit(solution)/shard_map/ppermute | solution.py:354
  59.6 4.1 %collective-permute-start.6 = (bf16[32,3072]{1,0:T(8,128)(2,1)}, bf16[32,3072]{1,0:T(8,128)(2,1)S(1)}, u32[]{:S(2)}, u32[]{:S(2)}) collective-permute-start(bf16[32,3072]{1,0:T(8,128)(2,1)} %get-tuple-element.18), channel_id=1, source_target_pairs={{0,8},{8,0},{16,24},{24,16},{1,9},{9,1},{17,25},{25,17},{2,10},{10... | collective-permute-start | bytes 589832 | tf_op jit(solution)/shard_map/ppermute | solution.py:354
  62.2 4.9 %collective-permute-start.4 = (bf16[16,3072]{1,0:T(8,128)(2,1)S(1)}, bf16[16,3072]{1,0:T(8,128)(2,1)S(1)}, u32[]{:S(2)}, u32[]{:S(2)}) collective-permute-start(bf16[16,3072]{1,0:T(8,128)(2,1)S(1)} %select_convert_fusion.1), channel_id=1, source_target_pairs={{0,4},{4,0},{1,5},{5,1},{2,6},{6,2},{3,7},{7,3},{8,12},{12,8},{9,1... | collective-permute-start | bytes 294920 | tf_op jit(solution)/shard_map/ppermute | solution.py:354
  64.7 4.7 %collective-permute-start.7 = (bf16[16,3072]{1,0:T(8,128)(2,1)S(1)}, bf16[16,3072]{1,0:T(8,128)(2,1)S(1)}, u32[]{:S(2)}, u32[]{:S(2)}) collective-permute-start(bf16[16,3072]{1,0:T(8,128)(2,1)S(1)} %select_convert_fusion), channel_id=1, source_target_pairs={{0,16},{8,24},{16,0},{24,8},{1,17},{9,25},{17,1},{25,9},{2,18},{10... | collective-permute-start | bytes 294920 | tf_op jit(solution)/shard_map/ppermute | solution.py:354
  67.2 4.2 %collective-permute-start.5 = (bf16[8,3072]{1,0:T(8,128)(2,1)S(1)}, bf16[8,3072]{1,0:T(8,128)(2,1)S(1)}, u32[]{:S(2)}, u32[]{:S(2)}) collective-permute-start(bf16[8,3072]{1,0:T(8,128)(2,1)S(1)} %select_convert_fusion.2), channel_id=1, source_target_pairs={{0,16},{8,24},{16,0},{24,8},{1,17},{9,25},{17,1},{25,9},{2,18},{10... | collective-permute-start | bytes 147464 | tf_op jit(solution)/shard_map/ppermute | solution.py:354
  71.4 8.4 %collective-permute-start.8 = (f32[8,4608]{1,0:T(8,128)S(1)}, f32[8,4608]{1,0:T(8,128)S(1)}, u32[]{:S(2)}, u32[]{:S(2)}) collective-permute-start(f32[8,4608]{1,0:T(8,128)S(1)} %pad_maximum_fusion.6), channel_id=1, source_target_pairs={{0,2},{1,3},{2,0},{3,1},{4,6},{5,7},{6,4},{7,5},{8,10},{9,11},{10,... | collective-permute-start | bytes 442376 | tf_op jit(solution)/shard_map/ppermute | solution.py:356
  79.9 4.9 %collective-permute-start.9 = (f32[8,2304]{1,0:T(8,128)S(1)}, f32[8,2304]{1,0:T(8,128)S(1)}, u32[]{:S(2)}, u32[]{:S(2)}) collective-permute-start(f32[8,2304]{1,0:T(8,128)S(1)} %pad_maximum_fusion.12), channel_id=1, source_target_pairs={{0,1},{1,0},{2,3},{3,2},{4,5},{5,4},{6,7},{7,6},{8,9},{9,8},{10,11... | collective-permute-start | bytes 221192 | tf_op jit(solution)/shard_map/ppermute | solution.py:356
  85.0 4.7 %collective-permute-start.10 = (bf16[8,2688]{1,0:T(8,128)(2,1)S(1)}, bf16[8,2688]{1,0:T(8,128)(2,1)S(1)}, u32[]{:S(2)}, u32[]{:S(2)}) collective-permute-start(bf16[8,2688]{1,0:T(8,128)(2,1)S(1)} %constant_dynamic-update-slice_fusion), channel_id=1, source_target_pairs={{0,1},{1,0},{2,3},{3,2},{4,5},{5,4},{6,7},{7,6},{8,9},{9,8},{10,11... | collective-permute-start | bytes 129032 | tf_op jit(solution)/shard_map/ppermute | solution.py:356
  89.9 5.7 %collective-permute-start.11 = (bf16[8,4992]{1,0:T(8,128)(2,1)S(1)}, bf16[8,4992]{1,0:T(8,128)(2,1)S(1)}, u32[]{:S(2)}, u32[]{:S(2)}) collective-permute-start(bf16[8,4992]{1,0:T(8,128)(2,1)S(1)} %constant_dynamic-update-slice_fusion.5), channel_id=1, source_target_pairs={{0,2},{1,3},{2,0},{3,1},{4,6},{5,7},{6,4},{7,5},{8,10},{9,11},{10,... | collective-permute-start | bytes 239624 | tf_op jit(solution)/shard_map/ppermute | solution.py:356
  95.7 5.3 %collective-permute-start.12 = (bf16[8,9600]{1,0:T(8,128)(2,1)S(1)}, bf16[8,9600]{1,0:T(8,128)(2,1)S(1)}, u32[]{:S(2)}, u32[]{:S(2)}) collective-permute-start(bf16[8,9600]{1,0:T(8,128)(2,1)S(1)} %constant_dynamic-update-slice_fusion.12), channel_id=1, source_target_pairs={{0,16},{8,24},{16,0},{24,8},{1,17},{9,25},{17,1},{25,9},{2,18},{10... | collective-permute-start | bytes 460808 | tf_op jit(solution)/shard_map/ppermute | solution.py:356
  101.1 4.7 %collective-permute-start.13 = (bf16[8,6528]{1,0:T(8,128)(2,1)S(1)}, bf16[8,6528]{1,0:T(8,128)(2,1)S(1)}, u32[]{:S(2)}, u32[]{:S(2)}) collective-permute-start(bf16[8,6528]{1,0:T(8,128)(2,1)S(1)} %constant_dynamic-update-slice_fusion.19), channel_id=1, source_target_pairs={{0,4},{4,0},{1,5},{5,1},{2,6},{6,2},{3,7},{7,3},{8,12},{12,8},{9,1... | collective-permute-start | bytes 313352 | tf_op jit(solution)/shard_map/ppermute | solution.py:356
  106.1 1.8 %collective-permute-start.14 = (bf16[8,24960]{1,0:T(8,128)(2,1)S(1)}, bf16[8,24960]{1,0:T(8,128)(2,1)S(1)}, u32[]{:S(2)}, u32[]{:S(2)}) collective-permute-start(bf16[8,24960]{1,0:T(8,128)(2,1)S(1)} %constant_dynamic-update-slice_fusion.24), channel_id=1, source_target_pairs={{0,8},{8,0},{16,24},{24,16},{1,9},{9,1},{17,25},{25,17},{2,10},{10... | collective-permute-start | bytes 1198088 | tf_op jit(solution)/shard_map/ppermute | solution.py:356

commit v3 on v2

v3 whole, which is shorter than its diff:
```python
import functools
import math

import jax
import jax.numpy as jnp
from jax import lax
from jax.experimental import pallas as pl
from jax.experimental.pallas import tpu as pltpu
from jax.sharding import PartitionSpec as P

HD = 128
HEADS = 16
STEPS = 1000
EPS = 1e-06
F32 = jnp.float32
BF16 = jnp.bfloat16
ROOT = 1.0 / math.sqrt(HD)
LOG2E = 1.0 / math.log(2.0)


def timing(value, width):
    count = width // 4
    freqs = jnp.exp(-math.log(10000.0) * jnp.arange(count, dtype=F32) / count)
    angles = 1000.0 * value * freqs
    return jnp.concatenate([jnp.cos(angles), jnp.sin(angles)])


def nn(a, b):
    return lax.dot_general(a, b, (((1,), (0,)), ((), ())), preferred_element_type=F32)


def nt(a, b):
    return lax.dot_general(a, b, (((1,), (1,)), ((), ())), preferred_element_type=F32)


def tn(a, b):
    return lax.dot_general(a, b, (((0,), (0,)), ((), ())), preferred_element_type=F32)


def over(total, size, body):
    if total == size:
        body(0)
    else:

        @pl.loop(0, total // size)
        def _(i):
            body(pl.multiple_of(i * size, size))


def inverse_rms(x):
    return lax.rsqrt(jnp.mean(x * x, axis=-1, keepdims=True) + EPS)


def norm_pull(x, gain, dy):
    r = inverse_rms(x)
    u = gain * dy
    return r * (u - x * (r * r * jnp.mean(x * u, axis=-1, keepdims=True)))


def modulate(tokens, mod_ref, kind, width, dest, rows, base):
    size = tokens.shape[0]

    @pl.loop(0, size // 16)
    def _(i):
        v = tokens[pl.ds(pl.multiple_of(i * 16, 16), 16), :].astype(F32)
        center = v - jnp.mean(v, axis=1, keepdims=True)
        spread = jnp.mean(center * center, axis=1, keepdims=True)
        unit = center * lax.rsqrt(spread + EPS)
        for m in range(2):
            shift = mod_ref[m : m + 1, kind * width : (kind + 1) * width]
            scale = mod_ref[m : m + 1, (kind + 1) * width : (kind + 2) * width]
            at = pl.multiple_of(m * rows + base + i * 16, 16)
            dest[pl.ds(at, 16), :] = (unit * (1.0 + scale) + shift).astype(BF16)


def normed(x, gain):
    return (x * inverse_rms(x) * gain).astype(BF16)


def text_kernel(n, pair, mod_ref, gain_ref, w_ref, *refs):
    parts, (k_ref, v_ref, ht, kv) = refs[:n], refs[n:]
    rows = n * parts[0].shape[0]

    @pl.when(pl.program_id(0) == 0)
    def _():
        for k in range(n):
            modulate(parts[k], mod_ref, 2, w_ref.shape[0], ht, rows, k * parts[0].shape[0])

    size = min(2 * rows, 192)

    def project(start):
        kv[pl.ds(start, size), :] = nn(ht[pl.ds(start, size), :], w_ref[...])

    over(2 * rows, size, project)
    gain = gain_ref[2:3, :]
    for j in range(pair):
        for m in range(2):
            at = slice(m * rows, (m + 1) * rows)
            c = j * 2 * HD
            k_ref[j, m] = normed(kv[at, c : c + HD], gain)
            v_ref[j, m] = kv[at, c + HD : c + 2 * HD].astype(BF16)


def fixed(x):
    return pl.BlockSpec(x.shape, lambda s: (0,) * x.ndim, pipeline_mode=pl.Buffered(1))


def split(count):
    pair = 2 if count % 2 == 0 else 1
    return pair, count // pair


def params(mib):
    return pltpu.CompilerParams(
        dimension_semantics=("arbitrary",), vmem_limit_bytes=mib * 1024 * 1024
    )


def project_text(mod, gain, w, parts):
    n, width = len(parts), w.shape[0]
    pair, steps = split(w.shape[1] // (2 * HD))
    rows = n * parts[0].shape[0]
    out = jax.ShapeDtypeStruct((pair * steps, 2, rows, HD), BF16)
    spec = pl.BlockSpec((pair, 2, rows, HD), lambda s: (s, 0, 0, 0))
    cols = pair * 2 * HD
    return pl.pallas_call(
        functools.partial(text_kernel, n, pair),
        grid=(steps,),
        in_specs=[fixed(mod), fixed(gain), pl.BlockSpec((width, cols), lambda s: (0, s))]
        + [fixed(x) for x in parts],
        out_specs=[spec, spec],
        out_shape=[out, out],
        scratch_shapes=[pltpu.VMEM((2 * rows, width), BF16), pltpu.VMEM((2 * rows, cols), F32)],
        compiler_params=params(58),
        cost_estimate=pl.CostEstimate(
            flops=4 * rows * w.size, bytes_accessed=2 * w.size, transcendentals=0
        ),
        name="project_text",
    )(mod, gain, w, *parts)


def image_kernel(pair, past, mod_ref, gain_ref, down_ref, up_ref, w_ref, tokens, *refs):
    q_ref, k_ref, v_ref, x_ref, low_ref, hs_ref, hi, qkv = refs[past:]
    rows = tokens.shape[0]

    @pl.when(pl.program_id(0) == 0)
    def _():
        modulate(tokens, mod_ref, 0, w_ref.shape[0], hi, rows, 0)
        hs_ref[...] = hi[rows:, :]
        low_ref[...] = nt(hi[rows:, :], down_ref[...]).astype(BF16)

    qkv[...] = nn(hi[...], w_ref[...])
    qkv[rows:, :] = qkv[rows:, :] + nn(low_ref[...], up_ref[...])
    for j in range(pair):
        c = j * 3 * HD
        for m in range(2):
            at = slice(m * rows, (m + 1) * rows)
            q, k = qkv[at, c : c + HD], qkv[at, c + HD : c + 2 * HD]
            q_ref[j, m] = normed(q, gain_ref[0:1, :])
            k_ref[j, m] = normed(k, gain_ref[1:2, :])
            v_ref[j, m] = qkv[at, c + 2 * HD : c + 3 * HD].astype(BF16)
            if m == 1:
                x_ref[j, 0] = q
                x_ref[j, 1] = k


def project_image(part, n, before, mod, gain, down, up, w, tokens):
    (rows, width), rank = tokens.shape, up.shape[0]
    pair, steps = split(w.shape[1] // (3 * HD))
    cols = pair * 3 * HD
    heads = (pair * steps, 2, n * rows, HD)
    spec = pl.BlockSpec((pair, 2, rows, HD), lambda s: (s, 0, part, 0))
    whole = lambda s: (part, 0)
    shapes = [jax.ShapeDtypeStruct(heads, BF16)] * 3 + [
        jax.ShapeDtypeStruct(heads, F32),
        jax.ShapeDtypeStruct((n * rows, rank), BF16),
        jax.ShapeDtypeStruct((n * rows, width), BF16),
    ]
    return pl.pallas_call(
        functools.partial(image_kernel, pair, len(before)),
        grid=(steps,),
        in_specs=[fixed(mod), fixed(gain), fixed(down)]
        + [
            pl.BlockSpec((rank, cols), lambda s: (0, s)),
            pl.BlockSpec((width, cols), lambda s: (0, s)),
            fixed(tokens),
        ]
        + [pl.BlockSpec(memory_space=pl.ANY)] * len(before),
        out_specs=[spec] * 4 + [pl.BlockSpec((rows, rank), whole), pl.BlockSpec((rows, width), whole)],
        out_shape=shapes,
        input_output_aliases={6 + i: i for i in range(len(before))},
        scratch_shapes=[pltpu.VMEM((2 * rows, width), BF16), pltpu.VMEM((2 * rows, cols), F32)],
        compiler_params=params(58),
        cost_estimate=pl.CostEstimate(
            flops=4 * rows * w.size, bytes_accessed=2 * w.size, transcendentals=0
        ),
        name="project_image",
    )(mod, gain, down, up, w, tokens, *before)


def attend_kernel(
    steps, pair, samples, where_ref, bias_ref, gain_ref, up_ref, q_ref, k_ref, v_ref, x_ref, kt_ref, vt_ref,
    low_ref, hs_ref, send_a, keep_a, send_b, keep_b, loss_ref, lowt, glt, k_s, v_s, dk_s, dv_s, gq, whole
):
    step = pl.program_id(0)
    core = where_ref[0]
    rows, trows = q_ref.shape[2], kt_ref.shape[2]
    block = min(rows, 160)
    half = send_a.shape[0]
    heads = range(pair)

    @pl.when(step == 0)
    def _():
        lowt[...] = low_ref[...].astype(F32).T.astype(BF16)
        glt[...] = jnp.zeros_like(glt)
        loss_ref[...] = jnp.zeros_like(loss_ref)

    for j in heads:
        for m in range(2):
            k_s[j, m, :rows, :] = k_ref[j, m]
            k_s[j, m, rows:, :] = kt_ref[j, m]
            v_s[j, m, :rows, :] = v_ref[j, m]
            v_s[j, m, rows:, :] = vt_ref[j, m]
    if rows > block:
        dk_s[...] = jnp.zeros_like(dk_s)
        dv_s[...] = jnp.zeros_like(dv_s)
    gain_q, gain_k = gain_ref[0:1, :], gain_ref[1:2, :]

    def attend(start):
        at = pl.ds(start, block)
        both = [(j, m) for j in heads for m in range(2)]
        scores = {(j, m): nt(q_ref[j, m, at, :], k_s[j, m]) for j, m in both}
        weights = {i: jnp.exp2(scores[i] * (ROOT * LOG2E) + bias_ref[...]) for i in both}
        scale = {i: 1.0 / jnp.sum(weights[i], axis=1, keepdims=True) for i in both}
        probs = {i: weights[i] * scale[i] for i in both}
        rounded = {i: probs[i].astype(BF16) for i in both}
        out = {(j, m): nn(rounded[j, m], v_s[j, m]) for j, m in both}
        diff = [out[j, 1] - out[j, 0].astype(BF16).astype(F32) for j in heads]
        total = diff[0] * diff[0]
        for d in diff[1:]:
            total = total + d * d
        loss_ref[...] += jnp.sum(total.reshape(block // 8, 8, HD), axis=0)
        dout = [(d * (2.0 / samples)).astype(BF16) for d in diff]
        dprobs = [nt(dout[j], v_s[j, 1]).astype(BF16).astype(F32) for j in heads]
        dv = [tn(rounded[j, 1], dout[j]) for j in heads]
        inner = [jnp.sum(dprobs[j] * probs[j, 1], axis=1, keepdims=True) for j in heads]
        dscores = [(probs[j, 1] * (dprobs[j] - inner[j]) * ROOT).astype(BF16) for j in heads]
        dq = [nn(dscores[j], k_s[j, 1]).astype(BF16).astype(F32) for j in heads]
        dk = [tn(dscores[j], q_ref[j, 1, at, :]) for j in heads]
        for j in heads:
            c = j * 3 * HD
            gq[at, c : c + HD] = norm_pull(x_ref[j, 0, at, :], gain_q, dq[j]).astype(BF16)
            if rows > block:
                dk_s[j] += dk[j][:rows]
                dv_s[j] += dv[j][:rows]
            else:
                dk_s[j] = dk[j][:rows]
                dv_s[j] = dv[j][:rows]

    over(rows, block, attend)

    def rest(start):
        at = pl.ds(start, block)
        for j in heads:
            c = j * 3 * HD
            dk = dk_s[j, at, :].astype(BF16).astype(F32)
            gq[at, c + HD : c + 2 * HD] = norm_pull(x_ref[j, 1, at, :], gain_k, dk).astype(BF16)
            gq[at, c + 2 * HD : c + 3 * HD] = dv_s[j, at, :].astype(BF16)

    over(rows, block, rest)

    def share(value, columns, send, keep):
        whole[:, columns] = value
        keep[...] = whole[pl.ds(pl.multiple_of(core * half, 8), half), columns]
        send[...] = whole[pl.ds(pl.multiple_of((1 - core) * half, 8), half), columns].astype(send.dtype)

    share(nn(lowt[...], gq[...]), slice(0, gq.shape[1]), send_b, keep_b)
    glt[...] += nt(up_ref[...], gq[...])

    @pl.when(step == steps - 1)
    def _():
        g = glt[...]
        g1 = g.astype(BF16)
        rest = g - g1.astype(F32)
        g2 = rest.astype(BF16)
        g3 = (rest - g2.astype(F32)).astype(BF16)
        stack = jnp.concatenate([g1, g2, g3], 0)
        rank = g.shape[0]
        full = nn(stack, hs_ref[...])
        share(
            full[:rank] + full[rank : 2 * rank] + full[2 * rank :],
            slice(0, full.shape[1]),
            send_a,
            keep_a,
        )


def attend(where, bias, gain, up, image, text):
    q, k, v, x, low, hs = image
    kt, vt = text
    (rank, img_cols), width = up.shape, hs.shape[1]
    count, _, rows, _ = q.shape
    trows = kt.shape[2]
    pair, steps = split(count)
    half, ic = rank // 2, pair * 3 * HD
    samples = lax.axis_size("grp") * lax.axis_size("dp")
    out_a, out_b = (half, width), (half, img_cols)
    spec_a = pl.BlockSpec(out_a, lambda s: (0, 0))
    spec_b = pl.BlockSpec((half, ic), lambda s: (0, s))
    by_head = lambda a: pl.BlockSpec((pair, *a.shape[1:]), lambda s: (s, 0, 0, 0))
    return pl.pallas_call(
        functools.partial(attend_kernel, steps, pair, samples),
        grid=(steps,),
        in_specs=[pl.BlockSpec(memory_space=pltpu.SMEM), fixed(bias), fixed(gain)]
        + [pl.BlockSpec((rank, ic), lambda s: (0, s))]
        + [by_head(a) for a in (q, k, v, x, kt, vt)]
        + [fixed(low), fixed(hs)],
        out_specs=[spec_a, spec_a, spec_b, spec_b, pl.BlockSpec((8, HD), lambda s: (0, 0))],
        out_shape=[
            jax.ShapeDtypeStruct(out_a, BF16),
            jax.ShapeDtypeStruct(out_a, F32),
            jax.ShapeDtypeStruct(out_b, BF16),
            jax.ShapeDtypeStruct(out_b, F32),
            jax.ShapeDtypeStruct((8, HD), F32),
        ],
        scratch_shapes=[
            pltpu.VMEM((rank, rows), BF16),
            pltpu.VMEM((rank, rows), F32),
            pltpu.VMEM((pair, 2, rows + trows, HD), BF16),
            pltpu.VMEM((pair, 2, rows + trows, HD), BF16),
            pltpu.VMEM((pair, rows, HD), F32),
            pltpu.VMEM((pair, rows, HD), F32),
            pltpu.VMEM((rows, ic), BF16),
            pltpu.VMEM((rank, max(width, ic)), F32),
        ],
        compiler_params=params(40),
        cost_estimate=pl.CostEstimate(
            flops=16 * count * rows * (rows + trows) * HD,
            bytes_accessed=8_000_000,
            transcendentals=2 * count * rows * (rows + trows),
        ),
        name="attend",
    )(where, bias, gain, up, q, k, v, x, kt, vt, low, hs)


def start_kernel(sigma_ref, image_ref, noise_ref, emb_ref, weight_ref, noisy_ref, part_ref):
    sigma = sigma_ref[0]
    clean, noise = image_ref[...].astype(F32), noise_ref[...].astype(F32)
    noisy_ref[...] = ((1.0 - sigma) * clean + sigma * noise).astype(BF16)
    part_ref[...] = nn(emb_ref[...], weight_ref[...])[: part_ref.shape[0]]


def start(sigma, image, noise, emb, weight):
    rows, width = image.shape
    depth, cols = weight.shape
    steps = 4 if width % 512 == 0 and cols % 512 == 0 else 1
    tokens = pl.BlockSpec((rows, width // steps), lambda s: (0, s))
    return pl.pallas_call(
        start_kernel,
        grid=(steps,),
        in_specs=[
            pl.BlockSpec(memory_space=pltpu.SMEM),
            tokens,
            tokens,
            pl.BlockSpec(emb.shape, lambda s: (0, 0)),
            pl.BlockSpec((depth, cols // steps), lambda s: (0, s)),
        ],
        out_specs=[tokens, pl.BlockSpec((2, cols // steps), lambda s: (0, s))],
        out_shape=[
            jax.ShapeDtypeStruct((rows, width), BF16),
            jax.ShapeDtypeStruct((2, cols), F32),
        ],
        compiler_params=params(60),
        cost_estimate=pl.CostEstimate(
            flops=4 * depth * cols, bytes_accessed=2 * weight.size + 6 * image.size, transcendentals=0
        ),
        name="start",
    )(sigma, image, noise, emb, weight)


def finish_kernel(scale_a, scale_b, scale_loss, a_ref, b_ref, sums_ref, out_a, out_b, loss_ref):
    half = HD // 2
    total = jnp.sum(sums_ref[...], axis=0, keepdims=True)
    loss_ref[...] = jnp.sum(total[:, :half], axis=1, keepdims=True) * scale_loss
    squares_b = jnp.sum(total[:, half:], axis=1, keepdims=True) * scale_b
    grad_a = a_ref[...].astype(F32)
    squares = jnp.sum(jnp.sum(grad_a * grad_a, axis=0, keepdims=True), axis=1, keepdims=True)
    unit_a = lax.rsqrt(squares * scale_a + EPS)
    out_b[...] = b_ref[...].astype(F32) * lax.rsqrt(squares_b + EPS)
    out_a[...] = grad_a * unit_a


def finish(grad_a, grad_b, sums, n, entries):
    (rank, width), cols = grad_a.shape, grad_b.shape[1]
    return pl.pallas_call(
        functools.partial(finish_kernel, 1.0 / (rank * width), 1.0 / (rank * cols * n), 1.0 / entries),
        out_shape=[
            jax.ShapeDtypeStruct((rank, width), F32),
            jax.ShapeDtypeStruct((rank, cols), F32),
            jax.ShapeDtypeStruct((1, 1), F32),
        ],
        name="finish",
    )(grad_a, grad_b, sums)


def shifted(x, axis, k):
    size = lax.axis_size(axis)
    return lax.ppermute(x, axis, [(i, (i + k) % size) for i in range(size)])


def side_of(axis, bit):
    return lax.rem(lax.div(lax.axis_index(axis), bit), 2)


def swap(arrays, axis, bit):
    pairs = [(i, i ^ bit) for i in range(lax.axis_size(axis))]
    if len(arrays) == 1 or any(x.shape[0] % 8 or x.shape[1] % HD for x in arrays):
        return [lax.ppermute(x, axis, pairs) for x in arrays]
    rows = [x[r : r + 8] for x in arrays for r in range(0, x.shape[0], 8)]
    got = lax.ppermute(jnp.concatenate(rows, 1), axis, pairs)
    out, at = [], 0
    for x in arrays:
        blocks = []
        for _ in range(0, x.shape[0], 8):
            blocks.append(got[:, at : at + x.shape[1]])
            at += x.shape[1]
        out.append(blocks[0] if len(blocks) == 1 else jnp.concatenate(blocks, 0))
    return out


def cut_of(x):
    if x.shape[0] % 16 == 0:
        return 0
    return 1 if x.shape[1] % (2 * HD) == 0 else 0


def halve(arrays, axis, bit, dtype):
    side = side_of(axis, bit)
    keep, send = [], []
    for x in arrays:
        dim = cut_of(x)
        first, second = jnp.split(x, 2, dim)
        keep.append(jnp.where(side == 0, first, second))
        send.append(jnp.where(side == 0, second, first).astype(dtype))
    got = swap(send, axis, bit)
    return [k + g.astype(F32) for k, g in zip(keep, got)]


def join(mine, theirs, side, dim):
    return jnp.concatenate(
        [jnp.where(side == 0, mine, theirs), jnp.where(side == 0, theirs, mine)], dim
    )


def pieces(value):
    first = lax.reduce_precision(value, 8, 7)
    rest = value - first
    second = lax.reduce_precision(rest, 8, 7)
    return jnp.concatenate([first, second, rest - second], 1).astype(BF16)


def rejoin(arrays, dims, sums, axis, bit):
    side = side_of(axis, bit)
    *got, other = swap([*arrays, pieces(sums)], axis, bit)
    other = other.astype(F32)
    sums = sums + (other[:, :HD] + other[:, HD : 2 * HD] + other[:, 2 * HD :])
    return [join(x, g, side, d) for x, g, d in zip(arrays, got, dims)], sums


def bits(axis):
    size = lax.axis_size(axis)
    return [1 << i for i in range(size.bit_length() - 1)]


def fold(x):
    half = HD // 2
    return functools.reduce(
        lambda total, c: total + x[:, c : c + half], range(half, x.shape[1], half), x[:, :half]
    )


def on_device(
    image,
    noise,
    text,
    timestep,
    guidance,
    text_token_length,
    image_projection_weight,
    text_projection_weight,
    modulation_weight,
    query_key_norm_gain,
    adapter_down_weight,
    adapter_up_weight,
):
    emb_width = modulation_weight.shape[0]
    n, me = lax.axis_size("seq"), lax.axis_index("seq")
    samples = lax.axis_size("grp") * lax.axis_size("dp")
    sigma = (timestep[0].astype(F32) + 1.0) / STEPS
    time = timing(sigma, emb_width)
    emb = jnp.stack(
        [
            jnp.concatenate([time, timing(guidance[0], emb_width)]),
            jnp.concatenate([time, jnp.zeros((emb_width // 2,), F32)]),
        ]
    )
    emb = jnp.pad(jax.nn.silu(emb).astype(BF16), ((0, 14), (0, 0)))
    noisy, part = start(sigma[None], image[0], noise[0], emb, modulation_weight)
    mods = [part] + [shifted(part, "seq", k) for k in range(1, n)]
    noisy_parts = [noisy] + [shifted(noisy, "seq", k) for k in range(1, n)]
    words = text[0]
    text_parts = [words] + [shifted(words, "seq", k) for k in range(1, n)]
    origin = [lax.rem(me + n - k, n) for k in range(n)]
    ordered = [
        functools.reduce(
            lambda so_far, k: jnp.where(origin[k] == j, mods[k], so_far), range(1, n), mods[0]
        )
        for j in range(n)
    ]
    mod = jnp.concatenate(ordered, 1)
    img_part, txt_part = noisy.shape[0], words.shape[0]
    place = jnp.concatenate(
        [jnp.zeros((n * img_part,), jnp.int32)]
        + [origin[k] * txt_part + jnp.arange(txt_part, dtype=jnp.int32) for k in range(n)]
    )
    bias = jnp.where(place < text_token_length[0], 0.0, -1000000000.0).astype(F32)[None]
    core = lax.rem(lax.axis_index("grp"), 2).astype(jnp.int32)
    gain = query_key_norm_gain
    text_heads = project_text(mod, gain, text_projection_weight, text_parts)
    image_heads = []
    for k in range(n):
        image_heads = project_image(
            k,
            n,
            image_heads,
            mod,
            gain,
            adapter_down_weight.T,
            adapter_up_weight,
            image_projection_weight,
            noisy_parts[k],
        )
    send_a, keep_a, send_b, keep_b, loss = attend(
        core[None], bias, gain, adapter_up_weight, image_heads, text_heads
    )
    (got_a,), (got_b,) = swap([send_a], "grp", 1), swap([send_b], "grp", 1)
    grad_a, grad_b = keep_a + got_a.astype(F32), keep_b + got_b.astype(F32)
    seq_dims, dp_dims = [], []
    for bit in reversed(bits("seq")):
        seq_dims.append(cut_of(grad_a))
        (grad_a,) = halve([grad_a], "seq", bit, BF16)
    x_dims = [cut_of(grad_a), cut_of(grad_b)]
    (grad_b,) = halve([grad_b], "grp", 2, BF16)
    (grad_a,) = halve([grad_a], "grp", 2, BF16)
    for bit in bits("dp"):
        dp_dims.append([cut_of(grad_a), cut_of(grad_b)])
        grad_a, grad_b = halve([grad_a, grad_b], "dp", bit, F32)
    squares = fold(grad_b * grad_b)
    squares = jnp.pad(squares, ((0, 8 - squares.shape[0]), (0, 0)))
    sums = jnp.concatenate([fold(loss), squares], 1)
    grads = [grad_a.astype(BF16), grad_b.astype(BF16)]
    for bit in reversed(bits("dp")):
        grads, sums = rejoin(grads, dp_dims.pop(), sums, "dp", bit)
    grads, sums = rejoin(grads, x_dims, sums, "grp", 2)
    for bit in bits("seq"):
        (grads[0],), sums = rejoin(grads[:1], [seq_dims.pop()], sums, "seq", bit)
    grads, sums = rejoin(grads, [0, 0], sums, "grp", 1)
    direction_a, direction_b, loss_mean = finish(
        *grads, sums, n, samples * n * img_part * HEADS * HD
    )
    return (direction_a.T, direction_b, loss_mean[0, 0])


def solution(mesh):
    in_specs = (
        P(("grp", "dp"), "seq", None),
        P(("grp", "dp"), "seq", None),
        P(("grp", "dp"), "seq", None),
        P(("grp", "dp")),
        P(("grp", "dp")),
        P(("grp", "dp")),
        P(None, "seq"),
        P(None, "seq"),
        P(None, "seq"),
        P(),
        P(),
        P(None, "seq"),
    )
    out_specs = (P(), P(None, "seq"), P())
    return jax.shard_map(
        on_device, mesh=mesh, in_specs=in_specs, out_specs=out_specs, check_vma=False
    )
```

time: 116 us -> 115 us (level)
  waiting for transfers between devices: 43.2 us -> 28.9 us
  Pallas kernels: 33.3 us -> 45.7 us
  starting transfers between devices: 18.8 us -> 22.9 us
  other arithmetic: 6.93 us -> 5.1 us
  local copies, waits for them, and re-layouts: 10.6 us -> 8.78 us
    pallas_call x1 -> x4, Pallas kernels: 29.1 us -> 38.9 us  [the longest x2 23.7 us: project_image(): pl.pallas_call(functools.partial(image_kernel, pair, len(before)), grid=(...]
    ppermute x3, waiting for transfers between devices: 12.7 us -> 3.1 us  [shifted(): return lax.ppermute(x, axis, [(i, (i + k) % size) for i in range(size)])]
    ppermute x7, waiting for transfers between devices: 26.4 us -> 20.9 us  [swap(): got = lax.ppermute(jnp.concatenate(rows, 1), axis, pairs)]
    ppermute x7, starting transfers between devices: 8.28 us -> 12.4 us  [swap(): got = lax.ppermute(jnp.concatenate(rows, 1), axis, pairs)]
    pallas_call x1, Pallas kernels: 1.32 us -> 4.32 us  [start(): pl.pallas_call(start_kernel, grid=(steps,), in_specs=[pl.BlockSpec(memory...]
    add x2, other arithmetic: 2.07 us -> 0.09 us  [on_device(): grad_a, grad_b = (keep_a + got_a.astype(F32), keep_b + got_b.astype(F32))]
    unnamed x23 -> x35, local copies, waits for them, and re-layouts: 9.78 us -> 8.12 us
  transfers between devices with their start and end apart: 15 -> 15, of which waited for: 12 -> 11; matrix products, arithmetic and copies ran while one was open for 6% -> 2% of each run, Pallas kernels for 0% -> 18%
where the time goes in v3:
time: 115 us; the launch traced here: 114 us
  Pallas kernels  45.7 us (40%)
  waiting for transfers between devices  28.9 us (25%)
  starting transfers between devices  22.9 us (20%)
  local copies, waits for them, and re-layouts  8.78 us (8%)
  other arithmetic  5.1 us (4%)
  between operations  3.1 us (3%)
    pallas_call x2, Pallas kernels, project_image(): pl.pallas_call(functools.partial(image_kernel, pair, len(before)), grid=(...  23.7 us
    ppermute x7, waiting for transfers between devices, swap(): got = lax.ppermute(jnp.concatenate(rows, 1), axis, pairs)  20.9 us
    ppermute x7, starting transfers between devices, swap(): got = lax.ppermute(jnp.concatenate(rows, 1), axis, pairs)  12.4 us
    pallas_call x1, Pallas kernels, project_text(): pl.pallas_call(functools.partial(text_kernel, n, pair), grid=(steps,), in...  9.28 us
    unnamed x35, local copies, waits for them, and re-layouts  8.12 us
    pallas_call x1, Pallas kernels, attend(): pl.pallas_call(functools.partial(attend_kernel, steps, pair, samples), gr...  5.95 us
    ppermute x5, starting transfers between devices, swap(): return [lax.ppermute(x, axis, pairs) for x in arrays]  5.5 us
    ppermute x3, starting transfers between devices, shifted(): return lax.ppermute(x, axis, [(i, (i + k) % size) for i in range(size)])  4.99 us
  transfers between devices with their start and end apart: 15, of which 11 were waited for; matrix products, arithmetic and copies ran while one was open for 2% of the time, Pallas kernels for 18%

profile of v3, /device:TPU:0, one launch (start us, length us, event | category | flops | bytes accessed | tf_op | source)
XLA Modules:
  0.0 114.5 jit_solution(17126970278459220171)
XLA Ops:
  2.8 4.3 %start.1 = (bf16[80,3072]{1,0:T(8,128)(2,1)}, f32[2,6144]{1,0:T(2,128)}) custom-call(f32[1]{0:T(128)} %bitcast.5.sigma_ref, bf16[80,3072]{1,0:T(8,128)(2,1)} %bitcast.21, bf16[80,3072]{1,0:T(8,128)(2,1)} %bitcast.22, bf16[16,256]{1,0:T(8,128)(2,1)} %pad.4.emb_ref, bf16[256,6144]{1,0:T(8,128)(2,1)} %weight_ref.1), custom_call_target="tpu_custom_call" | custom-call | flops 6291456 | bytes 4620288 | tf_op jit(solution)/shard_map/start/pallas_call | solution.py:358
  7.1 3.0 %collective-permute-start = (f32[2,6144]{1,0:T(2,128)}, f32[2,6144]{1,0:T(2,128)S(1)}, u32[]{:S(2)}, u32[]{:S(2)}) collective-permute-start(f32[2,6144]{1,0:T(2,128)} %get-tuple-element.27), channel_id=1, source_target_pairs={{0,4},{4,0},{1,5},{5,1},{2,6},{6,2},{3,7},{7,3},{8,12},{12,8},{9,1... | collective-permute-start | bytes 147464 | tf_op jit(solution)/shard_map/ppermute | solution.py:408
  10.2 2.0 %collective-permute-start.2 = (bf16[48,3072]{1,0:T(8,128)(2,1)S(1)}, bf16[48,3072]{1,0:T(8,128)(2,1)S(1)}, u32[]{:S(2)}, u32[]{:S(2)}) collective-permute-start(bf16[48,3072]{1,0:T(8,128)(2,1)S(1)} %bitcast.24), channel_id=1, source_target_pairs={{0,4},{4,0},{1,5},{5,1},{2,6},{6,2},{3,7},{7,3},{8,12},{12,8},{9,1... | collective-permute-start | bytes 884744 | tf_op jit(solution)/shard_map/ppermute | solution.py:408
  14.4 11.8 %project_image.2 = (bf16[8,2,160,128]{3,2,1,0:T(8,128)(2,1)}, bf16[8,2,160,128]{3,2,1,0:T(8,128)(2,1)}, bf16[8,2,160,128]{3,2,1,0:T(8,128)(2,1)}, f32[8,2,160,12...) custom-call(f32[2,12288]{1,0:T(2,128)} %pad_maximum_fusion.7.mod_ref, f32[3,128]{1,0:T(4,128)} %gain_ref.7, ...), custom_call_target="tpu_custom_call" | custom-call | flops 3019898880 | bytes 18874368 | tf_op jit(solution)/shard_map/project_image/pallas_call | solution.py:179
  26.2 3.1 %collective-permute-done.2.refs_1_ = bf16[48,3072]{1,0:T(8,128)(2,1)S(1)} collective-permute-done((bf16[48,3072]{1,0:T(8,128)(2,1)S(1)}, bf16[48,3072]{1,0:T(8,128)(2,1)S(1)}, u32[]{:S(2)}, u32[]{:S(2)}) %collective-permute-start.2) | collective-permute-done | bytes 294944 | tf_op jit(solution)/shard_map/ppermute | solution.py:408
  30.0 9.3 %project_text.1 = (bf16[8,2,96,128]{3,2,1,0:T(8,128)(2,1)}, bf16[8,2,96,128]{3,2,1,0:T(8,128)(2,1)}) custom-call(f32[2,12288]{1,0:T(2,128)} %pad_maximum_fusion.7.mod_ref, f32[3,128]{1,0:T(4,128)} %gain_ref.7, bf16[3072,2048]{1,0:T(8,128)(2,1)} %w_ref.5, bf16[48,3072]{1,0:T(8,128)(2,1)} %bitcast.23, bf16[48,3072]{1,0:T(8,128)(2,1)} %copy-done.12), custom_call_target="tpu_custom_call" | custom-call | flops 2415919104 | bytes 12582912 | tf_op jit(solution)/shard_map/project_text/pallas_call | solution.py:126
  40.1 11.9 %project_image.3 = (bf16[8,2,160,128]{3,2,1,0:T(8,128)(2,1)}, bf16[8,2,160,128]{3,2,1,0:T(8,128)(2,1)}, bf16[8,2,160,128]{3,2,1,0:T(8,128)(2,1)}, f32[8,2,160,12...) custom-call(f32[2,12288]{1,0:T(2,128)} %pad_maximum_fusion.7.mod_ref, ...), custom_call_target="tpu_custom_call", output_to_operand_aliasing={{0}: (6, {}), {1}: (7, {}), {2}: (8, {}), {3}: (9, {}), {4}... | custom-call | flops 3019898880 | bytes 18874368 | tf_op jit(solution)/shard_map/project_image/pallas_call | solution.py:179
  52.1 1.3 %copy-done = f32[8,2,160,128]{3,2,1,0:T(8,128)S(1)} copy-done((f32[8,2,160,128]{3,2,1,0:T(8,128)S(1)}, f32[8,2,160,128]{3,2,1,0:T(8,128)}, u32[]{:S(2)}) %copy-start) | copy-done | bytes 1310744
  53.4 1.2 %copy-done.1 = bf16[160,3072]{1,0:T(8,128)(2,1)S(1)} copy-done((bf16[160,3072]{1,0:T(8,128)(2,1)S(1)}, bf16[160,3072]{1,0:T(8,128)(2,1)}, u32[]{:S(2)}) %copy-start.1) | copy-done | bytes 983064
  54.6 1.1 copy-done.3
  55.7 1.1 copy-done.4
  56.8 1.1 copy-done.5
  58.6 6.0 %attend.1 = (bf16[32,3072]{1,0:T(8,128)(2,1)S(1)}, f32[32,3072]{1,0:T(8,128)S(1)}, bf16[32,3072]{1,0:T(8,128)(2,1)S(1)}, f32[32,3072]{1,0:T(8,128)S(1)}, f32[8,128]{1,0:T(8,128)S(1)}) custom-call(s32[1]{0:T(128)} %bitcast.where_ref, f32[1,256]{1,0:T(1,128)S(1)} %compare_select_fusion.bias_ref, f32[3,128]{1,0:T(4,128)S(1)} %copy-done.9, ...), custom_call_target="tpu_custom_call" | custom-call | flops 671088640 | bytes 8000000 | tf_op jit(solution)/shard_map/attend/pallas_call | solution.py:311
  66.2 1.4 %collective-permute-start.4 = (bf16[16,3072]{1,0:T(8,128)(2,1)S(1)}, bf16[16,3072]{1,0:T(8,128)(2,1)S(1)}, u32[]{:S(2)}, u32[]{:S(2)}) collective-permute-start(bf16[16,3072]{1,0:T(8,128)(2,1)S(1)} %select_convert_fusion.1), channel_id=1, source_target_pairs={{0,4},{4,0},{1,5},{5,1},{2,6},{6,2},{3,7},{7,3},{8,12},{12,8},{9,1... | collective-permute-start | bytes 294920 | tf_op jit(solution)/shard_map/ppermute | solution.py:418
  67.7 1.6 %collective-permute-start.7 = (bf16[16,3072]{1,0:T(8,128)(2,1)S(1)}, bf16[16,3072]{1,0:T(8,128)(2,1)S(1)}, u32[]{:S(2)}, u32[]{:S(2)}) collective-permute-start(bf16[16,3072]{1,0:T(8,128)(2,1)S(1)} %select_convert_fusion), channel_id=1, source_target_pairs={{0,16},{8,24},{16,0},{24,8},{1,17},{9,25},{17,1},{25,9},{2,18},{10... | collective-permute-start | bytes 294920 | tf_op jit(solution)/shard_map/ppermute | solution.py:418
  69.2 1.9 %collective-permute-done.4 = bf16[16,3072]{1,0:T(8,128)(2,1)S(1)} collective-permute-done((bf16[16,3072]{1,0:T(8,128)(2,1)S(1)}, bf16[16,3072]{1,0:T(8,128)(2,1)S(1)}, u32[]{:S(2)}, u32[]{:S(2)}) %collective-permute-start.4) | collective-permute-done | bytes 98336 | tf_op jit(solution)/shard_map/ppermute | solution.py:418
  71.1 2.0 %collective-permute-start.5 = (bf16[8,3072]{1,0:T(8,128)(2,1)S(1)}, bf16[8,3072]{1,0:T(8,128)(2,1)S(1)}, u32[]{:S(2)}, u32[]{:S(2)}) collective-permute-start(bf16[8,3072]{1,0:T(8,128)(2,1)S(1)} %select_convert_fusion.2), channel_id=1, source_target_pairs={{0,16},{8,24},{16,0},{24,8},{1,17},{9,25},{17,1},{25,9},{2,18},{10... | collective-permute-start | bytes 147464 | tf_op jit(solution)/shard_map/ppermute | solution.py:418
  73.2 2.1 %collective-permute-done.5 = bf16[8,3072]{1,0:T(8,128)(2,1)S(1)} collective-permute-done((bf16[8,3072]{1,0:T(8,128)(2,1)S(1)}, bf16[8,3072]{1,0:T(8,128)(2,1)S(1)}, u32[]{:S(2)}, u32[]{:S(2)}) %collective-permute-start.5) | collective-permute-done | bytes 49184 | tf_op jit(solution)/shard_map/ppermute | solution.py:418
  75.3 2.1 %collective-permute-start.8 = (f32[8,4608]{1,0:T(8,128)S(1)}, f32[8,4608]{1,0:T(8,128)S(1)}, u32[]{:S(2)}, u32[]{:S(2)}) collective-permute-start(f32[8,4608]{1,0:T(8,128)S(1)} %pad_maximum_fusion.6), channel_id=1, source_target_pairs={{0,1},{1,0},{2,3},{3,2},{4,5},{5,4},{6,7},{7,6},{8,9},{9,8},{10,11... | collective-permute-start | bytes 442376 | tf_op jit(solution)/shard_map/ppermute | solution.py:420
  77.4 3.1 %collective-permute-done.8 = f32[8,4608]{1,0:T(8,128)S(1)} collective-permute-done((f32[8,4608]{1,0:T(8,128)S(1)}, f32[8,4608]{1,0:T(8,128)S(1)}, u32[]{:S(2)}, u32[]{:S(2)}) %collective-permute-start.8) | collective-permute-done | bytes 147488 | tf_op jit(solution)/shard_map/ppermute | solution.py:420
  80.6 3.4 %collective-permute-start.9 = (f32[8,2304]{1,0:T(8,128)S(1)}, f32[8,2304]{1,0:T(8,128)S(1)}, u32[]{:S(2)}, u32[]{:S(2)}) collective-permute-start(f32[8,2304]{1,0:T(8,128)S(1)} %pad_maximum_fusion.12), channel_id=1, source_target_pairs={{0,2},{1,3},{2,0},{3,1},{4,6},{5,7},{6,4},{7,5},{8,10},{9,11},{10,... | collective-permute-start | bytes 221192 | tf_op jit(solution)/shard_map/ppermute | solution.py:420
  84.1 3.5 %collective-permute-done.9 = f32[8,2304]{1,0:T(8,128)S(1)} collective-permute-done((f32[8,2304]{1,0:T(8,128)S(1)}, f32[8,2304]{1,0:T(8,128)S(1)}, u32[]{:S(2)}, u32[]{:S(2)}) %collective-permute-start.9) | collective-permute-done | bytes 73760 | tf_op jit(solution)/shard_map/ppermute | solution.py:420
  87.8 2.3 %collective-permute-start.10 = (bf16[8,2688]{1,0:T(8,128)(2,1)S(1)}, bf16[8,2688]{1,0:T(8,128)(2,1)S(1)}, u32[]{:S(2)}, u32[]{:S(2)}) collective-permute-start(bf16[8,2688]{1,0:T(8,128)(2,1)S(1)} %constant_dynamic-update-slice_fusion), channel_id=1, source_target_pairs={{0,2},{1,3},{2,0},{3,1},{4,6},{5,7},{6,4},{7,5},{8,10},{9,11},{10,... | collective-permute-start | bytes 129032 | tf_op jit(solution)/shard_map/ppermute | solution.py:420
  90.2 2.6 %collective-permute-done.10 = bf16[8,2688]{1,0:T(8,128)(2,1)S(1)} collective-permute-done((bf16[8,2688]{1,0:T(8,128)(2,1)S(1)}, bf16[8,2688]{1,0:T(8,128)(2,1)S(1)}, u32[]{:S(2)}, u32[]{:S(2)}) %collective-permute-start.10) | collective-permute-done | bytes 43040 | tf_op jit(solution)/shard_map/ppermute | solution.py:420
  92.9 2.0 %collective-permute-start.11 = (bf16[8,4992]{1,0:T(8,128)(2,1)S(1)}, bf16[8,4992]{1,0:T(8,128)(2,1)S(1)}, u32[]{:S(2)}, u32[]{:S(2)}) collective-permute-start(bf16[8,4992]{1,0:T(8,128)(2,1)S(1)} %constant_dynamic-update-slice_fusion.5), channel_id=1, source_target_pairs={{0,1},{1,0},{2,3},{3,2},{4,5},{5,4},{6,7},{7,6},{8,9},{9,8},{10,11... | collective-permute-start | bytes 239624 | tf_op jit(solution)/shard_map/ppermute | solution.py:420
  94.9 2.5 %collective-permute-done.11 = bf16[8,4992]{1,0:T(8,128)(2,1)S(1)} collective-permute-done((bf16[8,4992]{1,0:T(8,128)(2,1)S(1)}, bf16[8,4992]{1,0:T(8,128)(2,1)S(1)}, u32[]{:S(2)}, u32[]{:S(2)}) %collective-permute-start.11) | collective-permute-done | bytes 79904 | tf_op jit(solution)/shard_map/ppermute | solution.py:420
  97.5 1.6 %collective-permute-start.12 = (bf16[8,9600]{1,0:T(8,128)(2,1)S(1)}, bf16[8,9600]{1,0:T(8,128)(2,1)S(1)}, u32[]{:S(2)}, u32[]{:S(2)}) collective-permute-start(bf16[8,9600]{1,0:T(8,128)(2,1)S(1)} %constant_dynamic-update-slice_fusion.12), channel_id=1, source_target_pairs={{0,16},{8,24},{16,0},{24,8},{1,17},{9,25},{17,1},{25,9},{2,18},{10... | collective-permute-start | bytes 460808 | tf_op jit(solution)/shard_map/ppermute | solution.py:420
  99.1 3.7 %collective-permute-done.12 = bf16[8,9600]{1,0:T(8,128)(2,1)S(1)} collective-permute-done((bf16[8,9600]{1,0:T(8,128)(2,1)S(1)}, bf16[8,9600]{1,0:T(8,128)(2,1)S(1)}, u32[]{:S(2)}, u32[]{:S(2)}) %collective-permute-start.12) | collective-permute-done | bytes 153632 | tf_op jit(solution)/shard_map/ppermute | solution.py:420
  102.9 1.0 collective-permute-start.13
  103.9 3.7 %collective-permute-done.13 = bf16[8,6528]{1,0:T(8,128)(2,1)S(1)} collective-permute-done((bf16[8,6528]{1,0:T(8,128)(2,1)S(1)}, bf16[8,6528]{1,0:T(8,128)(2,1)S(1)}, u32[]{:S(2)}, u32[]{:S(2)}) %collective-permute-start.13) | collective-permute-done | bytes 104480 | tf_op jit(solution)/shard_map/ppermute | solution.py:420
  107.9 1.7 %collective-permute-done.14 = bf16[8,24960]{1,0:T(8,128)(2,1)S(1)} collective-permute-done((bf16[8,24960]{1,0:T(8,128)(2,1)S(1)}, bf16[8,24960]{1,0:T(8,128)(2,1)S(1)}, u32[]{:S(2)}, u32[]{:S(2)}) %collective-permute-start.14) | collective-permute-done | bytes 399392 | tf_op jit(solution)/shard_map/ppermute | solution.py:420
  112.0 2.5 %finish.1 = (f32[64,3072]{1,0:T(8,128)}, f32[64,3072]{1,0:T(8,128)}, f32[1,1]{1,0:T(1,128)}) custom-call(bf16[64,3072]{1,0:T(8,128)(2,1)} %pad_maximum_fusion.a_ref, bf16[64,3072]{1,0:T(8,128)(2,1)} %pad_maximum_fusion.1.b_ref, f32[8,128]{1,0:T(8,128)} %fusion.6.sums_ref), custom_call_target="tpu_custom_call" | custom-call | tf_op jit(solution)/shard_map/finish/pallas_call | solution.py:395
  (110 shorter events, 9.8 us)
Async XLA Ops:
  0.6 9.6 %copy-start.11 = (bf16[1,48,3072]{2,1,0:T(8,128)(2,1)S(1)}, bf16[1,48,3072]{2,1,0:T(8,128)(2,1)}, u32[]{:S(2)}) copy-start(bf16[1,48,3072]{2,1,0:T(8,128)(2,1)} %param.14) | copy-start | bytes 884740
  7.1 5.8 %collective-permute-start = (f32[2,6144]{1,0:T(2,128)}, f32[2,6144]{1,0:T(2,128)S(1)}, u32[]{:S(2)}, u32[]{:S(2)}) collective-permute-start(f32[2,6144]{1,0:T(2,128)} %get-tuple-element.27), channel_id=1, source_target_pairs={{0,4},{4,0},{1,5},{5,1},{2,6},{6,2},{3,7},{7,3},{8,12},{12,8},{9,1... | collective-permute-start | bytes 147464 | tf_op jit(solution)/shard_map/ppermute | solution.py:408
  10.1 29.2 %collective-permute-start.1 = (bf16[80,3072]{1,0:T(8,128)(2,1)}, bf16[80,3072]{1,0:T(8,128)(2,1)S(1)}, u32[]{:S(2)}, u32[]{:S(2)}) collective-permute-start(bf16[80,3072]{1,0:T(8,128)(2,1)} %get-tuple-element.28.tokens), channel_id=1, source_target_pairs={{0,4},{4,0},{1,5},{5,1},{2,6},{6,2},{3,7},{7,3},{8,12},{12,8},{9,1... | collective-permute-start | bytes 1474568 | tf_op jit(solution)/shard_map/ppermute | solution.py:408
  10.2 19.1 %collective-permute-start.2 = (bf16[48,3072]{1,0:T(8,128)(2,1)S(1)}, bf16[48,3072]{1,0:T(8,128)(2,1)S(1)}, u32[]{:S(2)}, u32[]{:S(2)}) collective-permute-start(bf16[48,3072]{1,0:T(8,128)(2,1)S(1)} %bitcast.24), channel_id=1, source_target_pairs={{0,4},{4,0},{1,5},{5,1},{2,6},{6,2},{3,7},{7,3},{8,12},{12,8},{9,1... | collective-permute-start | bytes 884744 | tf_op jit(solution)/shard_map/ppermute | solution.py:408
  29.3 0.7 copy-start.12
  39.3 0.8 copy-start.10
  40.1 11.9 %copy-start.2 = (bf16[64,3072]{1,0:T(8,128)(2,1)S(1)}, bf16[64,3072]{1,0:T(8,128)(2,1)}, u32[]{:S(2)}) copy-start(bf16[64,3072]{1,0:T(8,128)(2,1)} %up_ref.5) | copy-start | bytes 1179652
  40.1 11.9 %copy-start.6 = (bf16[8,2,96,128]{3,2,1,0:T(8,128)(2,1)S(1)}, bf16[8,2,96,128]{3,2,1,0:T(8,128)(2,1)}, u32[]{:S(2)}) copy-start(bf16[8,2,96,128]{3,2,1,0:T(8,128)(2,1)} %get-tuple-element.39.kt_ref) | copy-start | bytes 1179652
  40.1 11.9 %copy-start.7 = (bf16[8,2,96,128]{3,2,1,0:T(8,128)(2,1)S(1)}, bf16[8,2,96,128]{3,2,1,0:T(8,128)(2,1)}, u32[]{:S(2)}) copy-start(bf16[8,2,96,128]{3,2,1,0:T(8,128)(2,1)} %get-tuple-element.40.vt_ref) | copy-start | bytes 1179652
  40.1 11.9 %copy-start.9 = (f32[3,128]{1,0:T(4,128)S(1)}, f32[3,128]{1,0:T(4,128)}, u32[]{:S(2)}) copy-start(f32[3,128]{1,0:T(4,128)} %gain_ref.7) | copy-start | bytes 4612
  52.1 1.3 %copy-start = (f32[8,2,160,128]{3,2,1,0:T(8,128)S(1)}, f32[8,2,160,128]{3,2,1,0:T(8,128)}, u32[]{:S(2)}) copy-start(f32[8,2,160,128]{3,2,1,0:T(8,128)} %get-tuple-element.38.x_ref) | copy-start | bytes 3932164
  53.4 1.2 %copy-start.1 = (bf16[160,3072]{1,0:T(8,128)(2,1)S(1)}, bf16[160,3072]{1,0:T(8,128)(2,1)}, u32[]{:S(2)}) copy-start(bf16[160,3072]{1,0:T(8,128)(2,1)} %get-tuple-element.42.hs_ref) | copy-start | bytes 2949124
  54.6 1.1 copy-start.3
  55.7 1.1 copy-start.4
  56.8 1.1 copy-start.5
  57.9 0.8 copy-start.8
  64.6 1.5 %collective-permute-start.3 = (bf16[32,3072]{1,0:T(8,128)(2,1)S(1)}, bf16[32,3072]{1,0:T(8,128)(2,1)S(1)}, u32[]{:S(2)}, u32[]{:S(2)}) collective-permute-start(bf16[32,3072]{1,0:T(8,128)(2,1)S(1)} %get-tuple-element.44), channel_id=1, source_target_pairs={{0,8},{8,0},{16,24},{24,16},{1,9},{9,1},{17,25},{25,17},{2,10},{10... | collective-permute-start | bytes 589832 | tf_op jit(solution)/shard_map/ppermute | solution.py:418
  64.7 2.9 %collective-permute-start.6 = (bf16[32,3072]{1,0:T(8,128)(2,1)S(1)}, bf16[32,3072]{1,0:T(8,128)(2,1)S(1)}, u32[]{:S(2)}, u32[]{:S(2)}) collective-permute-start(bf16[32,3072]{1,0:T(8,128)(2,1)S(1)} %get-tuple-element.46), channel_id=1, source_target_pairs={{0,8},{8,0},{16,24},{24,16},{1,9},{9,1},{17,25},{25,17},{2,10},{10... | collective-permute-start | bytes 589832 | tf_op jit(solution)/shard_map/ppermute | solution.py:418
  66.2 4.9 %collective-permute-start.4 = (bf16[16,3072]{1,0:T(8,128)(2,1)S(1)}, bf16[16,3072]{1,0:T(8,128)(2,1)S(1)}, u32[]{:S(2)}, u32[]{:S(2)}) collective-permute-start(bf16[16,3072]{1,0:T(8,128)(2,1)S(1)} %select_convert_fusion.1), channel_id=1, source_target_pairs={{0,4},{4,0},{1,5},{5,1},{2,6},{6,2},{3,7},{7,3},{8,12},{12,8},{9,1... | collective-permute-start | bytes 294920 | tf_op jit(solution)/shard_map/ppermute | solution.py:418
  67.7 5.5 %collective-permute-start.7 = (bf16[16,3072]{1,0:T(8,128)(2,1)S(1)}, bf16[16,3072]{1,0:T(8,128)(2,1)S(1)}, u32[]{:S(2)}, u32[]{:S(2)}) collective-permute-start(bf16[16,3072]{1,0:T(8,128)(2,1)S(1)} %select_convert_fusion), channel_id=1, source_target_pairs={{0,16},{8,24},{16,0},{24,8},{1,17},{9,25},{17,1},{25,9},{2,18},{10... | collective-permute-start | bytes 294920 | tf_op jit(solution)/shard_map/ppermute | solution.py:418
  71.1 4.2 %collective-permute-start.5 = (bf16[8,3072]{1,0:T(8,128)(2,1)S(1)}, bf16[8,3072]{1,0:T(8,128)(2,1)S(1)}, u32[]{:S(2)}, u32[]{:S(2)}) collective-permute-start(bf16[8,3072]{1,0:T(8,128)(2,1)S(1)} %select_convert_fusion.2), channel_id=1, source_target_pairs={{0,16},{8,24},{16,0},{24,8},{1,17},{9,25},{17,1},{25,9},{2,18},{10... | collective-permute-start | bytes 147464 | tf_op jit(solution)/shard_map/ppermute | solution.py:418
  75.3 5.2 %collective-permute-start.8 = (f32[8,4608]{1,0:T(8,128)S(1)}, f32[8,4608]{1,0:T(8,128)S(1)}, u32[]{:S(2)}, u32[]{:S(2)}) collective-permute-start(f32[8,4608]{1,0:T(8,128)S(1)} %pad_maximum_fusion.6), channel_id=1, source_target_pairs={{0,1},{1,0},{2,3},{3,2},{4,5},{5,4},{6,7},{7,6},{8,9},{9,8},{10,11... | collective-permute-start | bytes 442376 | tf_op jit(solution)/shard_map/ppermute | solution.py:420
  80.6 6.9 %collective-permute-start.9 = (f32[8,2304]{1,0:T(8,128)S(1)}, f32[8,2304]{1,0:T(8,128)S(1)}, u32[]{:S(2)}, u32[]{:S(2)}) collective-permute-start(f32[8,2304]{1,0:T(8,128)S(1)} %pad_maximum_fusion.12), channel_id=1, source_target_pairs={{0,2},{1,3},{2,0},{3,1},{4,6},{5,7},{6,4},{7,5},{8,10},{9,11},{10,... | collective-permute-start | bytes 221192 | tf_op jit(solution)/shard_map/ppermute | solution.py:420
  87.8 5.0 %collective-permute-start.10 = (bf16[8,2688]{1,0:T(8,128)(2,1)S(1)}, bf16[8,2688]{1,0:T(8,128)(2,1)S(1)}, u32[]{:S(2)}, u32[]{:S(2)}) collective-permute-start(bf16[8,2688]{1,0:T(8,128)(2,1)S(1)} %constant_dynamic-update-slice_fusion), channel_id=1, source_target_pairs={{0,2},{1,3},{2,0},{3,1},{4,6},{5,7},{6,4},{7,5},{8,10},{9,11},{10,... | collective-permute-start | bytes 129032 | tf_op jit(solution)/shard_map/ppermute | solution.py:420
  92.9 4.5 %collective-permute-start.11 = (bf16[8,4992]{1,0:T(8,128)(2,1)S(1)}, bf16[8,4992]{1,0:T(8,128)(2,1)S(1)}, u32[]{:S(2)}, u32[]{:S(2)}) collective-permute-start(bf16[8,4992]{1,0:T(8,128)(2,1)S(1)} %constant_dynamic-update-slice_fusion.5), channel_id=1, source_target_pairs={{0,1},{1,0},{2,3},{3,2},{4,5},{5,4},{6,7},{7,6},{8,9},{9,8},{10,11... | collective-permute-start | bytes 239624 | tf_op jit(solution)/shard_map/ppermute | solution.py:420
  97.5 5.3 %collective-permute-start.12 = (bf16[8,9600]{1,0:T(8,128)(2,1)S(1)}, bf16[8,9600]{1,0:T(8,128)(2,1)S(1)}, u32[]{:S(2)}, u32[]{:S(2)}) collective-permute-start(bf16[8,9600]{1,0:T(8,128)(2,1)S(1)} %constant_dynamic-update-slice_fusion.12), channel_id=1, source_target_pairs={{0,16},{8,24},{16,0},{24,8},{1,17},{9,25},{17,1},{25,9},{2,18},{10... | collective-permute-start | bytes 460808 | tf_op jit(solution)/shard_map/ppermute | solution.py:420
  102.9 4.7 %collective-permute-start.13 = (bf16[8,6528]{1,0:T(8,128)(2,1)S(1)}, bf16[8,6528]{1,0:T(8,128)(2,1)S(1)}, u32[]{:S(2)}, u32[]{:S(2)}) collective-permute-start(bf16[8,6528]{1,0:T(8,128)(2,1)S(1)} %constant_dynamic-update-slice_fusion.19), channel_id=1, source_target_pairs={{0,4},{4,0},{1,5},{5,1},{2,6},{6,2},{3,7},{7,3},{8,12},{12,8},{9,1... | collective-permute-start | bytes 313352 | tf_op jit(solution)/shard_map/ppermute | solution.py:420
  107.8 1.8 %collective-permute-start.14 = (bf16[8,24960]{1,0:T(8,128)(2,1)S(1)}, bf16[8,24960]{1,0:T(8,128)(2,1)S(1)}, u32[]{:S(2)}, u32[]{:S(2)}) collective-permute-start(bf16[8,24960]{1,0:T(8,128)(2,1)S(1)} %constant_dynamic-update-slice_fusion.24), channel_id=1, source_target_pairs={{0,8},{8,0},{16,24},{24,16},{1,9},{9,1},{17,25},{25,17},{2,10},{10... | collective-permute-start | bytes 1198088 | tf_op jit(solution)/shard_map/ppermute | solution.py:420

commit v4 on v3

--- a/solution.py
+++ b/solution.py
@@ -16,6 +16,7 @@
 BF16 = jnp.bfloat16
 ROOT = 1.0 / math.sqrt(HD)
 LOG2E = 1.0 / math.log(2.0)
+SMALL = 10 * 1024 * 1024
 
 
 def timing(value, width):
@@ -77,28 +78,22 @@
     return (x * inverse_rms(x) * gain).astype(BF16)
 
 
-def text_kernel(n, pair, mod_ref, gain_ref, w_ref, *refs):
-    parts, (k_ref, v_ref, ht, kv) = refs[:n], refs[n:]
-    rows = n * parts[0].shape[0]
-
-    @pl.when(pl.program_id(0) == 0)
-    def _():
-        for k in range(n):
-            modulate(parts[k], mod_ref, 2, w_ref.shape[0], ht, rows, k * parts[0].shape[0])
-
-    size = min(2 * rows, 192)
-
-    def project(start):
-        kv[pl.ds(start, size), :] = nn(ht[pl.ds(start, size), :], w_ref[...])
-
-    over(2 * rows, size, project)
-    gain = gain_ref[2:3, :]
-    for j in range(pair):
-        for m in range(2):
-            at = slice(m * rows, (m + 1) * rows)
-            c = j * 2 * HD
-            k_ref[j, m] = normed(kv[at, c : c + HD], gain)
-            v_ref[j, m] = kv[at, c + HD : c + 2 * HD].astype(BF16)
+def text_kernel(pair, index, past, mod_ref, gain_ref, w_ref, tokens, *refs):
+    k_ref, v_ref, ht = refs[past + min(index, 1) :]
+    rows = tokens.shape[0]
+    part = slice(index * rows, (index + 1) * rows)
+    modulate(tokens, mod_ref, 2, w_ref.shape[0], ht, rows, 0)
+    cols = pair * 2 * HD
+
+    @pl.loop(0, w_ref.shape[1] // cols)
+    def _(step):
+        kv = nn(ht[...], w_ref[:, pl.ds(pl.multiple_of(step * cols, cols), cols)])
+        for j in range(pair):
+            head, c = step * pair + j, j * 2 * HD
+            for m in range(2):
+                at = slice(m * rows, (m + 1) * rows)
+                k_ref[head, m, part, :] = normed(kv[at, c : c + HD], gain_ref[2:3, :])
+                v_ref[head, m, part, :] = kv[at, c + HD : c + 2 * HD].astype(BF16)
 
 
 def fixed(x):
@@ -116,105 +111,184 @@
     )
 
 
-def project_text(mod, gain, w, parts):
-    n, width = len(parts), w.shape[0]
+VMEM = pl.BlockSpec(memory_space=pltpu.VMEM)
+HELD = pl.BlockSpec(memory_space=pltpu.HBM)
+
+
+def project_text(part, n, before, mod, gain, w, tokens, after):
+    after = [after] * min(part, 1)
+    rows, width = tokens.shape
     pair, steps = split(w.shape[1] // (2 * HD))
-    rows = n * parts[0].shape[0]
-    out = jax.ShapeDtypeStruct((pair * steps, 2, rows, HD), BF16)
-    spec = pl.BlockSpec((pair, 2, rows, HD), lambda s: (s, 0, 0, 0))
-    cols = pair * 2 * HD
+    out = pltpu.VMEM((pair * steps, 2, n * rows, HD), BF16)
     return pl.pallas_call(
-        functools.partial(text_kernel, n, pair),
-        grid=(steps,),
-        in_specs=[fixed(mod), fixed(gain), pl.BlockSpec((width, cols), lambda s: (0, s))]
-        + [fixed(x) for x in parts],
-        out_specs=[spec, spec],
+        functools.partial(text_kernel, pair, part, len(before)),
+        in_specs=[VMEM] * (4 + len(before)) + [pl.BlockSpec(memory_space=pl.ANY)] * len(after),
+        out_specs=[VMEM] * 2,
         out_shape=[out, out],
-        scratch_shapes=[pltpu.VMEM((2 * rows, width), BF16), pltpu.VMEM((2 * rows, cols), F32)],
-        compiler_params=params(58),
+        input_output_aliases={4 + i: i for i in range(len(before))},
+        scratch_shapes=[pltpu.VMEM((2 * rows, width), BF16)],
+        compiler_params=pltpu.CompilerParams(vmem_limit_bytes=SMALL),
         cost_estimate=pl.CostEstimate(
             flops=4 * rows * w.size, bytes_accessed=2 * w.size, transcendentals=0
         ),
         name="project_text",
-    )(mod, gain, w, *parts)
-
-
-def image_kernel(pair, past, mod_ref, gain_ref, down_ref, up_ref, w_ref, tokens, *refs):
-    q_ref, k_ref, v_ref, x_ref, low_ref, hs_ref, hi, qkv = refs[past:]
+    )(mod, gain, w, tokens, *before, *after)
+
+
+def fetch_kernel(after_ref, w_ref, out_ref, sems):
+    for copy in fetches(w_ref, out_ref, sems):
+        copy.start()
+    for copy in fetches(w_ref, out_ref, sems):
+        copy.wait()
+
+
+def fetches(w_ref, out_ref, sems):
+    cols = w_ref.shape[1] // sems.shape[0]
+    return [
+        pltpu.make_async_copy(
+            w_ref.at[:, i * cols : (i + 1) * cols], out_ref.at[:, i * cols : (i + 1) * cols], sems.at[i]
+        )
+        for i in range(sems.shape[0])
+    ]
+
+
+def held(x):
+    return pltpu.with_memory_space_constraint(x, pltpu.HBM)
+
+
+def fetch(w, steps, after):
+    return pl.pallas_call(
+        fetch_kernel,
+        in_specs=[pl.BlockSpec(memory_space=pl.ANY), HELD],
+        out_specs=VMEM,
+        out_shape=pltpu.VMEM(w.shape, w.dtype),
+        scratch_shapes=[pltpu.SemaphoreType.DMA((steps,))],
+        compiler_params=pltpu.CompilerParams(vmem_limit_bytes=SMALL),
+        cost_estimate=pl.CostEstimate(flops=0, bytes_accessed=4 * w.size, transcendentals=0),
+        name="fetch",
+    )(after, w)
+
+
+def image_kernel(pair, index, past, mod_ref, gain_ref, down_ref, up_ref, w_ref, tokens, *refs):
+    first = past == 0
+    q_ref, k_ref, v_ref, x_ref, low_ref, hs_ref, *rest = refs[past + first :]
+    weights, copies = w_ref, None
+    if first:
+        weights, hi, sems = rest
+        copies = fetches(w_ref, weights, sems)
+        for copy in copies:
+            copy.start()
+    else:
+        (hi,) = rest
     rows = tokens.shape[0]
-
-    @pl.when(pl.program_id(0) == 0)
-    def _():
-        modulate(tokens, mod_ref, 0, w_ref.shape[0], hi, rows, 0)
-        hs_ref[...] = hi[rows:, :]
-        low_ref[...] = nt(hi[rows:, :], down_ref[...]).astype(BF16)
-
-    qkv[...] = nn(hi[...], w_ref[...])
-    qkv[rows:, :] = qkv[rows:, :] + nn(low_ref[...], up_ref[...])
-    for j in range(pair):
-        c = j * 3 * HD
-        for m in range(2):
-            at = slice(m * rows, (m + 1) * rows)
-            q, k = qkv[at, c : c + HD], qkv[at, c + HD : c + 2 * HD]
-            q_ref[j, m] = normed(q, gain_ref[0:1, :])
-            k_ref[j, m] = normed(k, gain_ref[1:2, :])
-            v_ref[j, m] = qkv[at, c + 2 * HD : c + 3 * HD].astype(BF16)
-            if m == 1:
-                x_ref[j, 0] = q
-                x_ref[j, 1] = k
-
-
-def project_image(part, n, before, mod, gain, down, up, w, tokens):
+    part = slice(index * rows, (index + 1) * rows)
+    modulate(tokens, mod_ref, 0, w_ref.shape[0], hi, rows, 0)
+    hs_ref[part, :] = hi[rows:, :]
+    low_ref[part, :] = nt(hi[rows:, :], down_ref[...]).astype(BF16)
+    cols = pair * 3 * HD
+
+    def project(step):
+        columns = pl.ds(step * cols, cols)
+        if not isinstance(step, int):
+            columns = pl.ds(pl.multiple_of(step * cols, cols), cols)
+        qkv = nn(hi[...], weights[:, columns])
+        student = qkv[rows:] + nn(low_ref[part, :], up_ref[:, columns])
+        for j in range(pair):
+            head, c = step * pair + j, j * 3 * HD
+            for m, own in enumerate((qkv[:rows], student)):
+                q, k = own[:, c : c + HD], own[:, c + HD : c + 2 * HD]
+                q_ref[head, m, part, :] = normed(q, gain_ref[0:1, :])
+                k_ref[head, m, part, :] = normed(k, gain_ref[1:2, :])
+                v_ref[head, m, part, :] = own[:, c + 2 * HD : c + 3 * HD].astype(BF16)
+                if m == 1:
+                    x_ref[head, 0, part, :] = q
+                    x_ref[head, 1, part, :] = k
+
+    if copies is None:
+        pl.loop(0, w_ref.shape[1] // cols)(project)
+    else:
+        for step, copy in enumerate(copies):
+            copy.wait()
+            project(step)
+
+
+def project_image(part, n, before, mod, gain, down, up, w, tokens, after):
+    after = [] if before else [after]
     (rows, width), rank = tokens.shape, up.shape[0]
     pair, steps = split(w.shape[1] // (3 * HD))
-    cols = pair * 3 * HD
     heads = (pair * steps, 2, n * rows, HD)
-    spec = pl.BlockSpec((pair, 2, rows, HD), lambda s: (s, 0, part, 0))
-    whole = lambda s: (part, 0)
-    shapes = [jax.ShapeDtypeStruct(heads, BF16)] * 3 + [
-        jax.ShapeDtypeStruct(heads, F32),
-        jax.ShapeDtypeStruct((n * rows, rank), BF16),
-        jax.ShapeDtypeStruct((n * rows, width), BF16),
+    shapes = [pltpu.VMEM(heads, BF16)] * 3 + [
+        pltpu.VMEM(heads, F32),
+        pltpu.VMEM((n * rows, rank), BF16),
+        pltpu.VMEM((n * rows, width), BF16),
     ]
+    scratch = [pltpu.VMEM((2 * rows, width), BF16)]
+    if not before:
+        shapes.append(pltpu.VMEM(w.shape, w.dtype))
+        scratch.append(pltpu.SemaphoreType.DMA((steps,)))
     return pl.pallas_call(
-        functools.partial(image_kernel, pair, len(before)),
-        grid=(steps,),
-        in_specs=[fixed(mod), fixed(gain), fixed(down)]
-        + [
-            pl.BlockSpec((rank, cols), lambda s: (0, s)),
-            pl.BlockSpec((width, cols), lambda s: (0, s)),
-            fixed(tokens),
-        ]
-        + [pl.BlockSpec(memory_space=pl.ANY)] * len(before),
-        out_specs=[spec] * 4 + [pl.BlockSpec((rows, rank), whole), pl.BlockSpec((rows, width), whole)],
+        functools.partial(image_kernel, pair, part, len(before)),
+        in_specs=[VMEM] * 4
+        + [VMEM if before else HELD]
+        + [VMEM] * (1 + len(before))
+        + [pl.BlockSpec(memory_space=pl.ANY)] * len(after),
+        out_specs=[VMEM] * len(shapes),
         out_shape=shapes,
         input_output_aliases={6 + i: i for i in range(len(before))},
-        scratch_shapes=[pltpu.VMEM((2 * rows, width), BF16), pltpu.VMEM((2 * rows, cols), F32)],
-        compiler_params=params(58),
+        scratch_shapes=scratch,
+        compiler_params=pltpu.CompilerParams(vmem_limit_bytes=SMALL),
         cost_estimate=pl.CostEstimate(
             flops=4 * rows * w.size, bytes_accessed=2 * w.size, transcendentals=0
         ),
         name="project_image",
-    )(mod, gain, down, up, w, tokens, *before)
+    )(mod, gain, down, up, w, tokens, *before, *after)
 
 
 def attend_kernel(
     steps, pair, samples, where_ref, bias_ref, gain_ref, up_ref, q_ref, k_ref, v_ref, x_ref, kt_ref, vt_ref,
     low_ref, hs_ref, send_a, keep_a, send_b, keep_b, loss_ref, lowt, glt, k_s, v_s, dk_s, dv_s, gq, whole
 ):
-    step = pl.program_id(0)
     core = where_ref[0]
-    rows, trows = q_ref.shape[2], kt_ref.shape[2]
+    half = send_a.shape[0]
+    lowt[...] = low_ref[...].astype(F32).T.astype(BF16)
+    glt[...] = jnp.zeros_like(glt)
+    loss_ref[...] = jnp.zeros_like(loss_ref)
+
+    def share(value, columns, send, keep):
+        whole[:, : value.shape[1]] = value
+        mine = pl.ds(pl.multiple_of(core * half, 8), half)
+        other = pl.ds(pl.multiple_of((1 - core) * half, 8), half)
+        keep[:, columns] = whole[mine, : value.shape[1]]
+        send[:, columns] = whole[other, : value.shape[1]].astype(send.dtype)
+
+    @pl.loop(0, steps)
+    def _(step):
+        columns = pl.ds(pl.multiple_of(step * gq.shape[1], HD), gq.shape[1])
+        group = pl.ds(step * pair, pair)
+        attend_heads(
+            pair, samples, bias_ref, gain_ref, *[r.at[group] for r in (q_ref, k_ref, v_ref, x_ref, kt_ref, vt_ref)],
+            loss_ref, k_s, v_s, dk_s, dv_s, gq,
+        )
+        share(nn(lowt[...], gq[...]), columns, send_b, keep_b)
+        glt[...] += nt(up_ref[:, columns], gq[...])
+
+    g = glt[...]
+    g1 = g.astype(BF16)
+    rest = g - g1.astype(F32)
+    g2 = rest.astype(BF16)
+    g3 = (rest - g2.astype(F32)).astype(BF16)
+    stack = jnp.concatenate([g1, g2, g3], 0)
+    rank = g.shape[0]
+    full = nn(stack, hs_ref[...])
+    share(full[:rank] + full[rank : 2 * rank] + full[2 * rank :], slice(0, full.shape[1]), send_a, keep_a)
+
+
+def attend_heads(
+    pair, samples, bias_ref, gain_ref, q_ref, k_ref, v_ref, x_ref, kt_ref, vt_ref, loss_ref, k_s, v_s, dk_s, dv_s, gq
+):
+    rows = q_ref.shape[2]
     block = min(rows, 160)
-    half = send_a.shape[0]
     heads = range(pair)
-
-    @pl.when(step == 0)
-    def _():
-        lowt[...] = low_ref[...].astype(F32).T.astype(BF16)
-        glt[...] = jnp.zeros_like(glt)
-        loss_ref[...] = jnp.zeros_like(loss_ref)
-
     for j in heads:
         for m in range(2):
             k_s[j, m, :rows, :] = k_ref[j, m]
@@ -269,31 +343,6 @@
 
     over(rows, block, rest)
 
-    def share(value, columns, send, keep):
-        whole[:, columns] = value
-        keep[...] = whole[pl.ds(pl.multiple_of(core * half, 8), half), columns]
-        send[...] = whole[pl.ds(pl.multiple_of((1 - core) * half, 8), half), columns].astype(send.dtype)
-
-    share(nn(lowt[...], gq[...]), slice(0, gq.shape[1]), send_b, keep_b)
-    glt[...] += nt(up_ref[...], gq[...])
-
-    @pl.when(step == steps - 1)
-    def _():
-        g = glt[...]
-        g1 = g.astype(BF16)
-        rest = g - g1.astype(F32)
-        g2 = rest.astype(BF16)
-        g3 = (rest - g2.astype(F32)).astype(BF16)
-        stack = jnp.concatenate([g1, g2, g3], 0)
-        rank = g.shape[0]
-        full = nn(stack, hs_ref[...])
-        share(
-            full[:rank] + full[rank : 2 * rank] + full[2 * rank :],
-            slice(0, full.shape[1]),
-            send_a,
-            keep_a,
-        )
-
 
 def attend(where, bias, gain, up, image, text):
     q, k, v, x, low, hs = image
@@ -305,17 +354,10 @@
     half, ic = rank // 2, pair * 3 * HD
     samples = lax.axis_size("grp") * lax.axis_size("dp")
     out_a, out_b = (half, width), (half, img_cols)
-    spec_a = pl.BlockSpec(out_a, lambda s: (0, 0))
-    spec_b = pl.BlockSpec((half, ic), lambda s: (0, s))
-    by_head = lambda a: pl.BlockSpec((pair, *a.shape[1:]), lambda s: (s, 0, 0, 0))
     return pl.pallas_call(
         functools.partial(attend_kernel, steps, pair, samples),
-        grid=(steps,),
-        in_specs=[pl.BlockSpec(memory_space=pltpu.SMEM), fixed(bias), fixed(gain)]
-        + [pl.BlockSpec((rank, ic), lambda s: (0, s))]
-        + [by_head(a) for a in (q, k, v, x, kt, vt)]
-        + [fixed(low), fixed(hs)],
-        out_specs=[spec_a, spec_a, spec_b, spec_b, pl.BlockSpec((8, HD), lambda s: (0, 0))],
+        in_specs=[pl.BlockSpec(memory_space=pltpu.SMEM)] + [VMEM] * 11,
+        out_specs=[VMEM] * 5,
         out_shape=[
             jax.ShapeDtypeStruct(out_a, BF16),
             jax.ShapeDtypeStruct(out_a, F32),
@@ -333,7 +375,7 @@
             pltpu.VMEM((rows, ic), BF16),
             pltpu.VMEM((rank, max(width, ic)), F32),
         ],
-        compiler_params=params(40),
+        compiler_params=pltpu.CompilerParams(vmem_limit_bytes=2 * SMALL),
         cost_estimate=pl.CostEstimate(
             flops=16 * count * rows * (rows + trows) * HD,
             bytes_accessed=8_000_000,
@@ -353,7 +395,7 @@
 def start(sigma, image, noise, emb, weight):
     rows, width = image.shape
     depth, cols = weight.shape
-    steps = 4 if width % 512 == 0 and cols % 512 == 0 else 1
+    steps = 2 if width % 256 == 0 and cols % 256 == 0 else 1
     tokens = pl.BlockSpec((rows, width // steps), lambda s: (0, s))
     return pl.pallas_call(
         start_kernel,
@@ -370,12 +412,12 @@
             jax.ShapeDtypeStruct((rows, width), BF16),
             jax.ShapeDtypeStruct((2, cols), F32),
         ],
-        compiler_params=params(60),
+        compiler_params=params(10),
         cost_estimate=pl.CostEstimate(
             flops=4 * depth * cols, bytes_accessed=2 * weight.size + 6 * image.size, transcendentals=0
         ),
         name="start",
-    )(sigma, image, noise, emb, weight)
+    )(sigma, held(image), held(noise), emb, held(weight))
 
 
 def finish_kernel(scale_a, scale_b, scale_loss, a_ref, b_ref, sums_ref, out_a, out_b, loss_ref):
@@ -498,13 +540,9 @@
     samples = lax.axis_size("grp") * lax.axis_size("dp")
     sigma = (timestep[0].astype(F32) + 1.0) / STEPS
     time = timing(sigma, emb_width)
-    emb = jnp.stack(
-        [
-            jnp.concatenate([time, timing(guidance[0], emb_width)]),
-            jnp.concatenate([time, jnp.zeros((emb_width // 2,), F32)]),
-        ]
-    )
-    emb = jnp.pad(jax.nn.silu(emb).astype(BF16), ((0, 14), (0, 0)))
+    guide = jnp.where(jnp.arange(16)[:, None] == 0, timing(guidance[0], emb_width)[None], 0.0)
+    emb = jnp.concatenate([jnp.broadcast_to(time[None], guide.shape), guide], 1)
+    emb = jax.nn.silu(emb).astype(BF16)
     noisy, part = start(sigma[None], image[0], noise[0], emb, modulation_weight)
     mods = [part] + [shifted(part, "seq", k) for k in range(1, n)]
     noisy_parts = [noisy] + [shifted(noisy, "seq", k) for k in range(1, n)]
@@ -526,20 +564,25 @@
     bias = jnp.where(place < text_token_length[0], 0.0, -1000000000.0).astype(F32)[None]
     core = lax.rem(lax.axis_index("grp"), 2).astype(jnp.int32)
     gain = query_key_norm_gain
-    text_heads = project_text(mod, gain, text_projection_weight, text_parts)
-    image_heads = []
-    for k in range(n):
-        image_heads = project_image(
-            k,
-            n,
-            image_heads,
-            mod,
-            gain,
-            adapter_down_weight.T,
-            adapter_up_weight,
-            image_projection_weight,
-            noisy_parts[k],
+    image_weight = held(image_projection_weight)
+    text_steps = split(text_projection_weight.shape[1] // (2 * HD))[1]
+    text_weight = fetch(held(text_projection_weight), text_steps, part)
+    down = adapter_down_weight.T
+
+    def text_part(k, after):
+        return project_text(k, n, text_heads, mod, gain, text_weight, text_parts[k], after)
+
+    def image_part(k, after):
+        return project_image(
+            k, n, image_heads, mod, gain, down, adapter_up_weight, image_weight, noisy_parts[k], after
         )
+
+    text_heads, image_heads = [], []
+    text_heads = text_part(0, None)
+    *image_heads, image_weight = image_part(0, text_heads[0])
+    for k in range(1, n):
+        image_heads = image_part(k, None)
+        text_heads = text_part(k, image_heads[0])
     send_a, keep_a, send_b, keep_b, loss = attend(
         core[None], bias, gain, adapter_up_weight, image_heads, text_heads
     )

time: 115 us -> 107 us (0.930)
  Pallas kernels: 45.7 us -> 41 us
  starting transfers between devices: 22.9 us -> 20.2 us
  local copies, waits for them, and re-layouts: 8.78 us -> 10.2 us
  other arithmetic: 5.1 us -> 3.79 us
    pallas_call x4 -> x6, Pallas kernels: 38.9 us -> 35.1 us  [the longest x2 16.1 us: project_image(): pl.pallas_call(functools.partial(image_kernel, pair, part, len(before)),...]
    ppermute x3, waiting for transfers between devices: 3.1 us -> 0.01 us  [shifted(): return lax.ppermute(x, axis, [(i, (i + k) % size) for i in range(size)])]
    unnamed x35 -> x27, local copies, waits for them, and re-layouts: 8.12 us -> 10.2 us
    ppermute x5, waiting for transfers between devices: 4.9 us -> 6.26 us  [swap(): return [lax.ppermute(x, axis, pairs) for x in arrays]]
    ppermute x5, starting transfers between devices: 5.5 us -> 4.14 us  [swap(): return [lax.ppermute(x, axis, pairs) for x in arrays]]
    ppermute x7, starting transfers between devices: 12.4 us -> 11.1 us  [swap(): got = lax.ppermute(jnp.concatenate(rows, 1), axis, pairs)]
  transfers between devices with their start and end apart: 15 -> 15, of which waited for: 11 -> 11; matrix products, arithmetic and copies ran while one was open for 2% -> 0% of each run, Pallas kernels for 18% -> 23%
where the time goes in v4:
time: 107 us; the launch traced here: 106 us
  Pallas kernels  41 us (38%)
  waiting for transfers between devices  28 us (26%)
  starting transfers between devices  20.2 us (19%)
  local copies, waits for them, and re-layouts  10.2 us (10%)
  other arithmetic  3.79 us (4%)
  between operations  3.15 us (3%)
    ppermute x7, waiting for transfers between devices, swap(): got = lax.ppermute(jnp.concatenate(rows, 1), axis, pairs)  21.8 us
    pallas_call x2, Pallas kernels, project_image(): pl.pallas_call(functools.partial(image_kernel, pair, part, len(before)),...  16.1 us
    ppermute x7, starting transfers between devices, swap(): got = lax.ppermute(jnp.concatenate(rows, 1), axis, pairs)  11.1 us
    unnamed x27, local copies, waits for them, and re-layouts  10.2 us
    pallas_call x2, Pallas kernels, project_text(): pl.pallas_call(functools.partial(text_kernel, pair, part, len(before)), i...  8.43 us
    ppermute x5, waiting for transfers between devices, swap(): return [lax.ppermute(x, axis, pairs) for x in arrays]  6.26 us
    pallas_call x1, Pallas kernels, attend(): pl.pallas_call(functools.partial(attend_kernel, steps, pair, samples), in...  5.75 us
    ppermute x3, starting transfers between devices, shifted(): return lax.ppermute(x, axis, [(i, (i + k) % size) for i in range(size)])  4.99 us
  transfers between devices with their start and end apart: 15, of which 11 were waited for; matrix products, arithmetic and copies ran while one was open for 0% of the time, Pallas kernels for 23%

profile of v4, /device:TPU:0, one launch (start us, length us, event | category | flops | bytes accessed | tf_op | source)
XLA Modules:
  0.0 106.4 jit_solution(5074530527099960837)
XLA Ops:
  2.3 3.4 %start.1 = (bf16[80,3072]{1,0:T(8,128)(2,1)}, f32[2,6144]{1,0:T(2,128)S(1)}) custom-call(f32[1]{0:T(128)} %bitcast.5.sigma_ref, bf16[80,3072]{1,0:T(8,128)(2,1)} %bitcast.23, bf16[80,3072]{1,0:T(8,128)(2,1)} %bitcast.24, bf16[16,256]{1,0:T(8,128)(2,1)S(1)} %fusion.6.emb_ref, bf16[256,6144]{1,0:T(8,128)(2,1)} %weight_ref.1), custom_call_target="tpu_custom_call" | custom-call | flops 6291456 | bytes 4620288 | tf_op jit(solution)/shard_map/start/pallas_call | solution.py:400
  5.7 3.0 %collective-permute-start = (f32[2,6144]{1,0:T(2,128)S(1)}, f32[2,6144]{1,0:T(2,128)S(1)}, u32[]{:S(2)}, u32[]{:S(2)}) collective-permute-start(f32[2,6144]{1,0:T(2,128)S(1)} %get-tuple-element.30.after_ref), channel_id=1, source_target_pairs={{0,4},{4,0},{1,5},{5,1},{2,6},{6,2},{3,7},{7,3},{8,12},{12,8},{9,1... | collective-permute-start | bytes 147464 | tf_op jit(solution)/shard_map/ppermute | solution.py:450
  8.7 2.0 %collective-permute-start.2 = (bf16[48,3072]{1,0:T(8,128)(2,1)}, bf16[48,3072]{1,0:T(8,128)(2,1)}, u32[]{:S(2)}, u32[]{:S(2)}) collective-permute-start(bf16[48,3072]{1,0:T(8,128)(2,1)} %bitcast.21), channel_id=1, source_target_pairs={{0,4},{4,0},{1,5},{5,1},{2,6},{6,2},{3,7},{7,3},{8,12},{12,8},{9,1... | collective-permute-start | bytes 884744 | tf_op jit(solution)/shard_map/ppermute | solution.py:450
  11.5 4.8 %fetch.1.w_ref = bf16[3072,2048]{1,0:T(8,128)(2,1)S(1)} custom-call(f32[2,6144]{1,0:T(2,128)S(1)} %get-tuple-element.30.after_ref, bf16[3072,2048]{1,0:T(8,128)(2,1)} %w_ref.2), custom_call_target="tpu_custom_call" | custom-call | bytes 25165824 | tf_op jit(solution)/shard_map/fetch/pallas_call | solution.py:160
  16.3 4.6 %copy-done = bf16[3072,2048]{1,0:T(8,128)(2,1)} copy-done((bf16[3072,2048]{1,0:T(8,128)(2,1)}, bf16[3072,2048]{1,0:T(8,128)(2,1)S(1)}, u32[]{:S(2)}) %copy-start) | copy-done | bytes 12582936
  21.0 4.6 %copy-done.1 = bf16[3072,2048]{1,0:T(8,128)(2,1)S(1)} copy-done((bf16[3072,2048]{1,0:T(8,128)(2,1)S(1)}, bf16[3072,2048]{1,0:T(8,128)(2,1)}, u32[]{:S(2)}) %copy-start.1) | copy-done | bytes 12582936
  25.5 3.7 %project_text.2 = (bf16[8,2,96,128]{3,2,1,0:T(8,128)(2,1)S(1)}, bf16[8,2,96,128]{3,2,1,0:T(8,128)(2,1)S(1)}) custom-call(f32[2,12288]{1,0:T(2,128)S(1)} %pad_maximum_fusion.7.mod_ref, f32[3,128]{1,0:T(4,128)S(1)} %copy-done.5, bf16[3072,2048]{1,0:T(8,128)(2,1)S(1)} %copy-done.1, bf16[48,3072]{1,0:T(8,128)(2,1)S(1)} %bitcast.22), custom_call_target="tpu_custom_call" | custom-call | flops 1207959552 | bytes 12582912 | tf_op jit(solution)/shard_map/project_text/pallas_call | solution.py:123
  29.3 1.0 copy-done.3
  30.3 8.9 %project_image.2 = (bf16[8,2,160,128]{3,2,1,0:T(8,128)(2,1)S(1)}, bf16[8,2,160,128]{3,2,1,0:T(8,128)(2,1)S(1)}, bf16[8,2,160,128]{3,2,1,0:T(8,128)(2,1)S(1)}, f3...) custom-call(f32[2,12288]{1,0:T(2,128)S(1)} %pad_maximum_fusion.7.mod, ...), custom_call_target="tpu_custom_call" | custom-call | flops 3019898880 | bytes 18874368 | tf_op jit(solution)/shard_map/project_image/pallas_call | solution.py:229
  39.2 7.2 %project_image.3 = (bf16[8,2,160,128]{3,2,1,0:T(8,128)(2,1)S(1)}, bf16[8,2,160,128]{3,2,1,0:T(8,128)(2,1)S(1)}, bf16[8,2,160,128]{3,2,1,0:T(8,128)(2,1)S(1)}, f3...) custom-call(f32[2,12288]{1,0:T(2,128)S(1)} %pad_maximum_fusion.7.mod, ...), custom_call_target="tpu_custom_call", output_to_operand_aliasing={{0}: (6, {}), {1}: (7, {}), {2}: (8, {}), {3}: (9, {}), {4}... | custom-call | flops 3019898880 | bytes 18874368 | tf_op jit(solution)/shard_map/project_image/pallas_call | solution.py:229
  46.5 4.7 %project_text.3 = (bf16[8,2,96,128]{3,2,1,0:T(8,128)(2,1)S(1)}, bf16[8,2,96,128]{3,2,1,0:T(8,128)(2,1)S(1)}) custom-call(f32[2,12288]{1,0:T(2,128)S(1)} %pad_maximum_fusion.7.mod_ref, f32[3,128]{1,0:T(4,128)S(1)} %copy-done.5, bf16[3072,2048]{1,0:T(8,128)(2,1)S(1)} %bitcast.18, ...), custom_call_target="tpu_custom_call", output_to_operand_aliasing={{0}: (4, {}), {1}: (5, {})} | custom-call | flops 1207959552 | bytes 12582912 | tf_op jit(solution)/shard_map/project_text/pallas_call | solution.py:123
  51.2 5.8 %attend.1 = (bf16[32,3072]{1,0:T(8,128)(2,1)S(1)}, f32[32,3072]{1,0:T(8,128)S(1)}, bf16[32,3072]{1,0:T(8,128)(2,1)S(1)}, f32[32,3072]{1,0:T(8,128)S(1)}, f32[8,128]{1,0:T(8,128)S(1)}) custom-call(s32[1]{0:T(128)} %bitcast.where_ref, f32[1,256]{1,0:T(1,128)S(1)} %compare_select_fusion.bias_ref, f32[3,128]{1,0:T(4,128)S(1)} %copy-done.5, ...), custom_call_target="tpu_custom_call" | custom-call | flops 671088640 | bytes 8000000 | tf_op jit(solution)/shard_map/attend/pallas_call | solution.py:357
  57.6 0.9 collective-permute-done.3
  58.9 1.9 %collective-permute-start.7 = (bf16[16,3072]{1,0:T(8,128)(2,1)S(1)}, bf16[16,3072]{1,0:T(8,128)(2,1)S(1)}, u32[]{:S(2)}, u32[]{:S(2)}) collective-permute-start(bf16[16,3072]{1,0:T(8,128)(2,1)S(1)} %select_convert_fusion), channel_id=1, source_target_pairs={{0,16},{8,24},{16,0},{24,8},{1,17},{9,25},{17,1},{25,9},{2,18},{10... | collective-permute-start | bytes 294920 | tf_op jit(solution)/shard_map/ppermute | solution.py:460
  60.8 2.7 %collective-permute-done.4 = bf16[16,3072]{1,0:T(8,128)(2,1)S(1)} collective-permute-done((bf16[16,3072]{1,0:T(8,128)(2,1)S(1)}, bf16[16,3072]{1,0:T(8,128)(2,1)S(1)}, u32[]{:S(2)}, u32[]{:S(2)}) %collective-permute-start.4) | collective-permute-done | bytes 98336 | tf_op jit(solution)/shard_map/ppermute | solution.py:460
  63.5 1.6 %collective-permute-start.5 = (bf16[8,3072]{1,0:T(8,128)(2,1)S(1)}, bf16[8,3072]{1,0:T(8,128)(2,1)S(1)}, u32[]{:S(2)}, u32[]{:S(2)}) collective-permute-start(bf16[8,3072]{1,0:T(8,128)(2,1)S(1)} %select_convert_fusion.2), channel_id=1, source_target_pairs={{0,16},{8,24},{16,0},{24,8},{1,17},{9,25},{17,1},{25,9},{2,18},{10... | collective-permute-start | bytes 147464 | tf_op jit(solution)/shard_map/ppermute | solution.py:460
  65.2 2.5 %collective-permute-done.5 = bf16[8,3072]{1,0:T(8,128)(2,1)S(1)} collective-permute-done((bf16[8,3072]{1,0:T(8,128)(2,1)S(1)}, bf16[8,3072]{1,0:T(8,128)(2,1)S(1)}, u32[]{:S(2)}, u32[]{:S(2)}) %collective-permute-start.5) | collective-permute-done | bytes 49184 | tf_op jit(solution)/shard_map/ppermute | solution.py:460
  67.8 1.6 %collective-permute-start.8 = (f32[8,4608]{1,0:T(8,128)S(1)}, f32[8,4608]{1,0:T(8,128)S(1)}, u32[]{:S(2)}, u32[]{:S(2)}) collective-permute-start(f32[8,4608]{1,0:T(8,128)S(1)} %pad_maximum_fusion.6), channel_id=1, source_target_pairs={{0,1},{1,0},{2,3},{3,2},{4,5},{5,4},{6,7},{7,6},{8,9},{9,8},{10,11... | collective-permute-start | bytes 442376 | tf_op jit(solution)/shard_map/ppermute | solution.py:462
  69.4 3.6 %collective-permute-done.8 = f32[8,4608]{1,0:T(8,128)S(1)} collective-permute-done((f32[8,4608]{1,0:T(8,128)S(1)}, f32[8,4608]{1,0:T(8,128)S(1)}, u32[]{:S(2)}, u32[]{:S(2)}) %collective-permute-start.8) | collective-permute-done | bytes 147488 | tf_op jit(solution)/shard_map/ppermute | solution.py:462
  73.0 3.0 %collective-permute-start.9 = (f32[8,2304]{1,0:T(8,128)S(1)}, f32[8,2304]{1,0:T(8,128)S(1)}, u32[]{:S(2)}, u32[]{:S(2)}) collective-permute-start(f32[8,2304]{1,0:T(8,128)S(1)} %pad_maximum_fusion.12), channel_id=1, source_target_pairs={{0,2},{1,3},{2,0},{3,1},{4,6},{5,7},{6,4},{7,5},{8,10},{9,11},{10,... | collective-permute-start | bytes 221192 | tf_op jit(solution)/shard_map/ppermute | solution.py:462
  76.1 3.5 %collective-permute-done.9 = f32[8,2304]{1,0:T(8,128)S(1)} collective-permute-done((f32[8,2304]{1,0:T(8,128)S(1)}, f32[8,2304]{1,0:T(8,128)S(1)}, u32[]{:S(2)}, u32[]{:S(2)}) %collective-permute-start.9) | collective-permute-done | bytes 73760 | tf_op jit(solution)/shard_map/ppermute | solution.py:462
  79.8 2.3 %collective-permute-start.10 = (bf16[8,2688]{1,0:T(8,128)(2,1)S(1)}, bf16[8,2688]{1,0:T(8,128)(2,1)S(1)}, u32[]{:S(2)}, u32[]{:S(2)}) collective-permute-start(bf16[8,2688]{1,0:T(8,128)(2,1)S(1)} %constant_dynamic-update-slice_fusion), channel_id=1, source_target_pairs={{0,2},{1,3},{2,0},{3,1},{4,6},{5,7},{6,4},{7,5},{8,10},{9,11},{10,... | collective-permute-start | bytes 129032 | tf_op jit(solution)/shard_map/ppermute | solution.py:462
  82.1 2.6 %collective-permute-done.10 = bf16[8,2688]{1,0:T(8,128)(2,1)S(1)} collective-permute-done((bf16[8,2688]{1,0:T(8,128)(2,1)S(1)}, bf16[8,2688]{1,0:T(8,128)(2,1)S(1)}, u32[]{:S(2)}, u32[]{:S(2)}) %collective-permute-start.10) | collective-permute-done | bytes 43040 | tf_op jit(solution)/shard_map/ppermute | solution.py:462
  84.9 2.0 %collective-permute-start.11 = (bf16[8,4992]{1,0:T(8,128)(2,1)S(1)}, bf16[8,4992]{1,0:T(8,128)(2,1)S(1)}, u32[]{:S(2)}, u32[]{:S(2)}) collective-permute-start(bf16[8,4992]{1,0:T(8,128)(2,1)S(1)} %constant_dynamic-update-slice_fusion.5), channel_id=1, source_target_pairs={{0,1},{1,0},{2,3},{3,2},{4,5},{5,4},{6,7},{7,6},{8,9},{9,8},{10,11... | collective-permute-start | bytes 239624 | tf_op jit(solution)/shard_map/ppermute | solution.py:462
  86.9 2.5 %collective-permute-done.11 = bf16[8,4992]{1,0:T(8,128)(2,1)S(1)} collective-permute-done((bf16[8,4992]{1,0:T(8,128)(2,1)S(1)}, bf16[8,4992]{1,0:T(8,128)(2,1)S(1)}, u32[]{:S(2)}, u32[]{:S(2)}) %collective-permute-start.11) | collective-permute-done | bytes 79904 | tf_op jit(solution)/shard_map/ppermute | solution.py:462
  89.5 1.6 %collective-permute-start.12 = (bf16[8,9600]{1,0:T(8,128)(2,1)S(1)}, bf16[8,9600]{1,0:T(8,128)(2,1)S(1)}, u32[]{:S(2)}, u32[]{:S(2)}) collective-permute-start(bf16[8,9600]{1,0:T(8,128)(2,1)S(1)} %constant_dynamic-update-slice_fusion.12), channel_id=1, source_target_pairs={{0,16},{8,24},{16,0},{24,8},{1,17},{9,25},{17,1},{25,9},{2,18},{10... | collective-permute-start | bytes 460808 | tf_op jit(solution)/shard_map/ppermute | solution.py:462
  91.1 3.7 %collective-permute-done.12 = bf16[8,9600]{1,0:T(8,128)(2,1)S(1)} collective-permute-done((bf16[8,9600]{1,0:T(8,128)(2,1)S(1)}, bf16[8,9600]{1,0:T(8,128)(2,1)S(1)}, u32[]{:S(2)}, u32[]{:S(2)}) %collective-permute-start.12) | collective-permute-done | bytes 153632 | tf_op jit(solution)/shard_map/ppermute | solution.py:462
  95.4 4.2 %collective-permute-done.13 = bf16[8,6528]{1,0:T(8,128)(2,1)S(1)} collective-permute-done((bf16[8,6528]{1,0:T(8,128)(2,1)S(1)}, bf16[8,6528]{1,0:T(8,128)(2,1)S(1)}, u32[]{:S(2)}, u32[]{:S(2)}) %collective-permute-start.13) | collective-permute-done | bytes 104480 | tf_op jit(solution)/shard_map/ppermute | solution.py:462
  99.9 1.7 %collective-permute-done.14 = bf16[8,24960]{1,0:T(8,128)(2,1)S(1)} collective-permute-done((bf16[8,24960]{1,0:T(8,128)(2,1)S(1)}, bf16[8,24960]{1,0:T(8,128)(2,1)S(1)}, u32[]{:S(2)}, u32[]{:S(2)}) %collective-permute-start.14) | collective-permute-done | bytes 399392 | tf_op jit(solution)/shard_map/ppermute | solution.py:462
  102.3 0.8 pad_maximum_fusion.1.b_ref
  103.2 0.8 pad_maximum_fusion.a_ref
  104.0 2.5 %finish.1 = (f32[64,3072]{1,0:T(8,128)}, f32[64,3072]{1,0:T(8,128)}, f32[1,1]{1,0:T(1,128)}) custom-call(bf16[64,3072]{1,0:T(8,128)(2,1)} %pad_maximum_fusion.a_ref, bf16[64,3072]{1,0:T(8,128)(2,1)} %pad_maximum_fusion.1.b_ref, f32[8,128]{1,0:T(8,128)} %fusion.12.sums_ref), custom_call_target="tpu_custom_call" | custom-call | tf_op jit(solution)/shard_map/finish/pallas_call | solution.py:437
  (106 shorter events, 3.7 us)
Async XLA Ops:
  5.7 15.1 %collective-permute-start = (f32[2,6144]{1,0:T(2,128)S(1)}, f32[2,6144]{1,0:T(2,128)S(1)}, u32[]{:S(2)}, u32[]{:S(2)}) collective-permute-start(f32[2,6144]{1,0:T(2,128)S(1)} %get-tuple-element.30.after_ref), channel_id=1, source_target_pairs={{0,4},{4,0},{1,5},{5,1},{2,6},{6,2},{3,7},{7,3},{8,12},{12,8},{9,1... | collective-permute-start | bytes 147464 | tf_op jit(solution)/shard_map/ppermute | solution.py:450
  8.7 30.5 %collective-permute-start.1 = (bf16[80,3072]{1,0:T(8,128)(2,1)}, bf16[80,3072]{1,0:T(8,128)(2,1)}, u32[]{:S(2)}, u32[]{:S(2)}) collective-permute-start(bf16[80,3072]{1,0:T(8,128)(2,1)} %get-tuple-element.31.tokens), channel_id=1, source_target_pairs={{0,4},{4,0},{1,5},{5,1},{2,6},{6,2},{3,7},{7,3},{8,12},{12,8},{9,1... | collective-permute-start | bytes 1474568 | tf_op jit(solution)/shard_map/ppermute | solution.py:450
  8.7 37.7 %collective-permute-start.2 = (bf16[48,3072]{1,0:T(8,128)(2,1)}, bf16[48,3072]{1,0:T(8,128)(2,1)}, u32[]{:S(2)}, u32[]{:S(2)}) collective-permute-start(bf16[48,3072]{1,0:T(8,128)(2,1)} %bitcast.21), channel_id=1, source_target_pairs={{0,4},{4,0},{1,5},{5,1},{2,6},{6,2},{3,7},{7,3},{8,12},{12,8},{9,1... | collective-permute-start | bytes 884744 | tf_op jit(solution)/shard_map/ppermute | solution.py:450
  11.5 9.5 %copy-start.4 = (bf16[1,48,3072]{2,1,0:T(8,128)(2,1)S(1)}, bf16[1,48,3072]{2,1,0:T(8,128)(2,1)}, u32[]{:S(2)}) copy-start(bf16[1,48,3072]{2,1,0:T(8,128)(2,1)} %param.14) | copy-start | bytes 884740
  11.5 9.5 %copy-start.5 = (f32[3,128]{1,0:T(4,128)S(1)}, f32[3,128]{1,0:T(4,128)}, u32[]{:S(2)}) copy-start(f32[3,128]{1,0:T(4,128)} %gain_ref.9) | copy-start | bytes 4612
  16.3 4.6 %copy-start = (bf16[3072,2048]{1,0:T(8,128)(2,1)}, bf16[3072,2048]{1,0:T(8,128)(2,1)S(1)}, u32[]{:S(2)}) copy-start(bf16[3072,2048]{1,0:T(8,128)(2,1)S(1)} %fetch.1.w_ref) | copy-start | bytes 37748740
  20.8 8.4 %copy-start.2 = (bf16[64,3072]{1,0:T(8,128)(2,1)S(1)}, bf16[64,3072]{1,0:T(8,128)(2,1)}, u32[]{:S(2)}) copy-start(bf16[64,3072]{1,0:T(8,128)(2,1)} %up_ref.5) | copy-start | bytes 1179652
  21.0 4.6 %copy-start.1 = (bf16[3072,2048]{1,0:T(8,128)(2,1)S(1)}, bf16[3072,2048]{1,0:T(8,128)(2,1)}, u32[]{:S(2)}) copy-start(bf16[3072,2048]{1,0:T(8,128)(2,1)} %copy-done) | copy-start | bytes 37748740
  29.3 1.0 copy-start.3
  39.2 7.3 %slice-start = ((s8[12582912]{0:T(1024)(128)(4,1)}), s8[4194304]{0:T(1024)(128)(4,1)S(1)}, s32[]{:S(2)}) async-start(s8[12582912]{0:T(1024)(128)(4,1)} %bitcast.17), calls=%async_computation | async-start | bytes 8388608
  39.2 7.3 %slice-start.1 = ((s8[12582912]{0:T(1024)(128)(4,1)}), s8[4194304]{0:T(1024)(128)(4,1)S(1)}, s32[]{:S(2)}) async-start(s8[12582912]{0:T(1024)(128)(4,1)} %bitcast.17), calls=%async_computation.1 | async-start | bytes 8388608
  39.2 7.3 %slice-start.2 = ((s8[12582912]{0:T(1024)(128)(4,1)}), s8[4194304]{0:T(1024)(128)(4,1)S(1)}, s32[]{:S(2)}) async-start(s8[12582912]{0:T(1024)(128)(4,1)} %bitcast.17), calls=%async_computation.2 | async-start | bytes 8388608
  57.0 1.5 %collective-permute-start.3 = (bf16[32,3072]{1,0:T(8,128)(2,1)S(1)}, bf16[32,3072]{1,0:T(8,128)(2,1)S(1)}, u32[]{:S(2)}, u32[]{:S(2)}) collective-permute-start(bf16[32,3072]{1,0:T(8,128)(2,1)S(1)} %get-tuple-element.50), channel_id=1, source_target_pairs={{0,8},{8,0},{16,24},{24,16},{1,9},{9,1},{17,25},{25,17},{2,10},{10... | collective-permute-start | bytes 589832 | tf_op jit(solution)/shard_map/ppermute | solution.py:460
  57.1 1.7 %collective-permute-start.6 = (bf16[32,3072]{1,0:T(8,128)(2,1)S(1)}, bf16[32,3072]{1,0:T(8,128)(2,1)S(1)}, u32[]{:S(2)}, u32[]{:S(2)}) collective-permute-start(bf16[32,3072]{1,0:T(8,128)(2,1)S(1)} %get-tuple-element.52), channel_id=1, source_target_pairs={{0,8},{8,0},{16,24},{24,16},{1,9},{9,1},{17,25},{25,17},{2,10},{10... | collective-permute-start | bytes 589832 | tf_op jit(solution)/shard_map/ppermute | solution.py:460
  58.6 4.9 %collective-permute-start.4 = (bf16[16,3072]{1,0:T(8,128)(2,1)S(1)}, bf16[16,3072]{1,0:T(8,128)(2,1)S(1)}, u32[]{:S(2)}, u32[]{:S(2)}) collective-permute-start(bf16[16,3072]{1,0:T(8,128)(2,1)S(1)} %select_convert_fusion.1), channel_id=1, source_target_pairs={{0,4},{4,0},{1,5},{5,1},{2,6},{6,2},{3,7},{7,3},{8,12},{12,8},{9,1... | collective-permute-start | bytes 294920 | tf_op jit(solution)/shard_map/ppermute | solution.py:460
  58.9 6.2 %collective-permute-start.7 = (bf16[16,3072]{1,0:T(8,128)(2,1)S(1)}, bf16[16,3072]{1,0:T(8,128)(2,1)S(1)}, u32[]{:S(2)}, u32[]{:S(2)}) collective-permute-start(bf16[16,3072]{1,0:T(8,128)(2,1)S(1)} %select_convert_fusion), channel_id=1, source_target_pairs={{0,16},{8,24},{16,0},{24,8},{1,17},{9,25},{17,1},{25,9},{2,18},{10... | collective-permute-start | bytes 294920 | tf_op jit(solution)/shard_map/ppermute | solution.py:460
  63.5 4.2 %collective-permute-start.5 = (bf16[8,3072]{1,0:T(8,128)(2,1)S(1)}, bf16[8,3072]{1,0:T(8,128)(2,1)S(1)}, u32[]{:S(2)}, u32[]{:S(2)}) collective-permute-start(bf16[8,3072]{1,0:T(8,128)(2,1)S(1)} %select_convert_fusion.2), channel_id=1, source_target_pairs={{0,16},{8,24},{16,0},{24,8},{1,17},{9,25},{17,1},{25,9},{2,18},{10... | collective-permute-start | bytes 147464 | tf_op jit(solution)/shard_map/ppermute | solution.py:460
  67.8 5.2 %collective-permute-start.8 = (f32[8,4608]{1,0:T(8,128)S(1)}, f32[8,4608]{1,0:T(8,128)S(1)}, u32[]{:S(2)}, u32[]{:S(2)}) collective-permute-start(f32[8,4608]{1,0:T(8,128)S(1)} %pad_maximum_fusion.6), channel_id=1, source_target_pairs={{0,1},{1,0},{2,3},{3,2},{4,5},{5,4},{6,7},{7,6},{8,9},{9,8},{10,11... | collective-permute-start | bytes 442376 | tf_op jit(solution)/shard_map/ppermute | solution.py:462
  73.0 6.5 %collective-permute-start.9 = (f32[8,2304]{1,0:T(8,128)S(1)}, f32[8,2304]{1,0:T(8,128)S(1)}, u32[]{:S(2)}, u32[]{:S(2)}) collective-permute-start(f32[8,2304]{1,0:T(8,128)S(1)} %pad_maximum_fusion.12), channel_id=1, source_target_pairs={{0,2},{1,3},{2,0},{3,1},{4,6},{5,7},{6,4},{7,5},{8,10},{9,11},{10,... | collective-permute-start | bytes 221192 | tf_op jit(solution)/shard_map/ppermute | solution.py:462
  79.8 5.0 %collective-permute-start.10 = (bf16[8,2688]{1,0:T(8,128)(2,1)S(1)}, bf16[8,2688]{1,0:T(8,128)(2,1)S(1)}, u32[]{:S(2)}, u32[]{:S(2)}) collective-permute-start(bf16[8,2688]{1,0:T(8,128)(2,1)S(1)} %constant_dynamic-update-slice_fusion), channel_id=1, source_target_pairs={{0,2},{1,3},{2,0},{3,1},{4,6},{5,7},{6,4},{7,5},{8,10},{9,11},{10,... | collective-permute-start | bytes 129032 | tf_op jit(solution)/shard_map/ppermute | solution.py:462
  84.9 4.5 %collective-permute-start.11 = (bf16[8,4992]{1,0:T(8,128)(2,1)S(1)}, bf16[8,4992]{1,0:T(8,128)(2,1)S(1)}, u32[]{:S(2)}, u32[]{:S(2)}) collective-permute-start(bf16[8,4992]{1,0:T(8,128)(2,1)S(1)} %constant_dynamic-update-slice_fusion.5), channel_id=1, source_target_pairs={{0,1},{1,0},{2,3},{3,2},{4,5},{5,4},{6,7},{7,6},{8,9},{9,8},{10,11... | collective-permute-start | bytes 239624 | tf_op jit(solution)/shard_map/ppermute | solution.py:462
  89.5 5.3 %collective-permute-start.12 = (bf16[8,9600]{1,0:T(8,128)(2,1)S(1)}, bf16[8,9600]{1,0:T(8,128)(2,1)S(1)}, u32[]{:S(2)}, u32[]{:S(2)}) collective-permute-start(bf16[8,9600]{1,0:T(8,128)(2,1)S(1)} %constant_dynamic-update-slice_fusion.12), channel_id=1, source_target_pairs={{0,16},{8,24},{16,0},{24,8},{1,17},{9,25},{17,1},{25,9},{2,18},{10... | collective-permute-start | bytes 460808 | tf_op jit(solution)/shard_map/ppermute | solution.py:462
  94.9 4.7 %collective-permute-start.13 = (bf16[8,6528]{1,0:T(8,128)(2,1)S(1)}, bf16[8,6528]{1,0:T(8,128)(2,1)S(1)}, u32[]{:S(2)}, u32[]{:S(2)}) collective-permute-start(bf16[8,6528]{1,0:T(8,128)(2,1)S(1)} %constant_dynamic-update-slice_fusion.19), channel_id=1, source_target_pairs={{0,4},{4,0},{1,5},{5,1},{2,6},{6,2},{3,7},{7,3},{8,12},{12,8},{9,1... | collective-permute-start | bytes 313352 | tf_op jit(solution)/shard_map/ppermute | solution.py:462
  99.8 1.8 %collective-permute-start.14 = (bf16[8,24960]{1,0:T(8,128)(2,1)S(1)}, bf16[8,24960]{1,0:T(8,128)(2,1)S(1)}, u32[]{:S(2)}, u32[]{:S(2)}) collective-permute-start(bf16[8,24960]{1,0:T(8,128)(2,1)S(1)} %constant_dynamic-update-slice_fusion.24), channel_id=1, source_target_pairs={{0,8},{8,0},{16,24},{24,16},{1,9},{9,1},{17,25},{25,17},{2,10},{10... | collective-permute-start | bytes 1198088 | tf_op jit(solution)/shard_map/ppermute | solution.py:462

commit v5 on v4

--- a/solution.py
+++ b/solution.py
@@ -78,70 +78,6 @@
     return (x * inverse_rms(x) * gain).astype(BF16)
 
 
-def text_kernel(pair, index, past, mod_ref, gain_ref, w_ref, tokens, *refs):
-    k_ref, v_ref, ht = refs[past + min(index, 1) :]
-    rows = tokens.shape[0]
-    part = slice(index * rows, (index + 1) * rows)
-    modulate(tokens, mod_ref, 2, w_ref.shape[0], ht, rows, 0)
-    cols = pair * 2 * HD
-
-    @pl.loop(0, w_ref.shape[1] // cols)
-    def _(step):
-        kv = nn(ht[...], w_ref[:, pl.ds(pl.multiple_of(step * cols, cols), cols)])
-        for j in range(pair):
-            head, c = step * pair + j, j * 2 * HD
-            for m in range(2):
-                at = slice(m * rows, (m + 1) * rows)
-                k_ref[head, m, part, :] = normed(kv[at, c : c + HD], gain_ref[2:3, :])
-                v_ref[head, m, part, :] = kv[at, c + HD : c + 2 * HD].astype(BF16)
-
-
-def fixed(x):
-    return pl.BlockSpec(x.shape, lambda s: (0,) * x.ndim, pipeline_mode=pl.Buffered(1))
-
-
-def split(count):
-    pair = 2 if count % 2 == 0 else 1
-    return pair, count // pair
-
-
-def params(mib):
-    return pltpu.CompilerParams(
-        dimension_semantics=("arbitrary",), vmem_limit_bytes=mib * 1024 * 1024
-    )
-
-
-VMEM = pl.BlockSpec(memory_space=pltpu.VMEM)
-HELD = pl.BlockSpec(memory_space=pltpu.HBM)
-
-
-def project_text(part, n, before, mod, gain, w, tokens, after):
-    after = [after] * min(part, 1)
-    rows, width = tokens.shape
-    pair, steps = split(w.shape[1] // (2 * HD))
-    out = pltpu.VMEM((pair * steps, 2, n * rows, HD), BF16)
-    return pl.pallas_call(
-        functools.partial(text_kernel, pair, part, len(before)),
-        in_specs=[VMEM] * (4 + len(before)) + [pl.BlockSpec(memory_space=pl.ANY)] * len(after),
-        out_specs=[VMEM] * 2,
-        out_shape=[out, out],
-        input_output_aliases={4 + i: i for i in range(len(before))},
-        scratch_shapes=[pltpu.VMEM((2 * rows, width), BF16)],
-        compiler_params=pltpu.CompilerParams(vmem_limit_bytes=SMALL),
-        cost_estimate=pl.CostEstimate(
-            flops=4 * rows * w.size, bytes_accessed=2 * w.size, transcendentals=0
-        ),
-        name="project_text",
-    )(mod, gain, w, tokens, *before, *after)
-
-
-def fetch_kernel(after_ref, w_ref, out_ref, sems):
-    for copy in fetches(w_ref, out_ref, sems):
-        copy.start()
-    for copy in fetches(w_ref, out_ref, sems):
-        copy.wait()
-
-
 def fetches(w_ref, out_ref, sems):
     cols = w_ref.shape[1] // sems.shape[0]
     return [
@@ -156,22 +92,75 @@
     return pltpu.with_memory_space_constraint(x, pltpu.HBM)
 
 
-def fetch(w, steps, after):
+def text_kernel(n, pair, mod_ref, gain_ref, w_ref, after_ref, *refs):
+    parts, (k_ref, v_ref, ht, weights, sems) = refs[:n], refs[n:]
+    copies = fetches(w_ref, weights, sems)
+    for copy in copies:
+        copy.start()
+    rows = n * parts[0].shape[0]
+    for k in range(n):
+        modulate(parts[k], mod_ref, 2, w_ref.shape[0], ht, rows, k * parts[0].shape[0])
+    cols = pair * 2 * HD
+    size = min(rows, 96)
+    for step, copy in enumerate(copies):
+        copy.wait()
+
+        def project(start, step=step):
+            w = weights[:, step * cols : (step + 1) * cols]
+            if size == rows:
+                both = nn(ht[...], w)
+                own = [both[:rows], both[rows:]]
+            else:
+                own = [nn(ht[pl.ds(m * rows + start, size), :], w) for m in range(2)]
+            for m, kv in enumerate(own):
+                for j in range(pair):
+                    head, c = step * pair + j, j * 2 * HD
+                    k_ref[head, m, pl.ds(start, size), :] = normed(kv[:, c : c + HD], gain_ref[2:3, :])
+                    v_ref[head, m, pl.ds(start, size), :] = kv[:, c + HD : c + 2 * HD].astype(BF16)
+
+        over(rows, size, project)
+
+
+def split(count):
+    pair = 2 if count % 2 == 0 else 1
+    return pair, count // pair
+
+
+def params(mib):
+    return pltpu.CompilerParams(
+        dimension_semantics=("arbitrary",), vmem_limit_bytes=mib * 1024 * 1024
+    )
+
+
+VMEM = pl.BlockSpec(memory_space=pltpu.VMEM)
+HELD = pl.BlockSpec(memory_space=pltpu.HBM)
+
+
+def project_text(mod, gain, w, after, parts):
+    n, (part, width) = len(parts), parts[0].shape
+    pair, steps = split(w.shape[1] // (2 * HD))
+    out = pltpu.VMEM((pair * steps, 2, n * part, HD), BF16)
     return pl.pallas_call(
-        fetch_kernel,
-        in_specs=[pl.BlockSpec(memory_space=pl.ANY), HELD],
-        out_specs=VMEM,
-        out_shape=pltpu.VMEM(w.shape, w.dtype),
-        scratch_shapes=[pltpu.SemaphoreType.DMA((steps,))],
-        compiler_params=pltpu.CompilerParams(vmem_limit_bytes=SMALL),
-        cost_estimate=pl.CostEstimate(flops=0, bytes_accessed=4 * w.size, transcendentals=0),
-        name="fetch",
-    )(after, w)
+        functools.partial(text_kernel, n, pair),
+        in_specs=[VMEM, VMEM, HELD, pl.BlockSpec(memory_space=pl.ANY)] + [VMEM] * n,
+        out_specs=[VMEM] * 2,
+        out_shape=[out, out],
+        scratch_shapes=[
+            pltpu.VMEM((2 * n * part, width), BF16),
+            pltpu.VMEM(w.shape, w.dtype),
+            pltpu.SemaphoreType.DMA((steps,)),
+        ],
+        compiler_params=pltpu.CompilerParams(vmem_limit_bytes=2 * SMALL),
+        cost_estimate=pl.CostEstimate(
+            flops=4 * n * part * w.size, bytes_accessed=2 * w.size, transcendentals=0
+        ),
+        name="project_text",
+    )(mod, gain, w, after, *parts)
 
 
 def image_kernel(pair, index, past, mod_ref, gain_ref, down_ref, up_ref, w_ref, tokens, *refs):
     first = past == 0
-    q_ref, k_ref, v_ref, x_ref, low_ref, hs_ref, *rest = refs[past + first :]
+    q_ref, k_ref, v_ref, x_ref, low_ref, hs_ref, *rest = refs[past:]
     weights, copies = w_ref, None
     if first:
         weights, hi, sems = rest
@@ -212,8 +201,7 @@
             project(step)
 
 
-def project_image(part, n, before, mod, gain, down, up, w, tokens, after):
-    after = [] if before else [after]
+def project_image(part, n, before, mod, gain, down, up, w, tokens):
     (rows, width), rank = tokens.shape, up.shape[0]
     pair, steps = split(w.shape[1] // (3 * HD))
     heads = (pair * steps, 2, n * rows, HD)
@@ -230,8 +218,7 @@
         functools.partial(image_kernel, pair, part, len(before)),
         in_specs=[VMEM] * 4
         + [VMEM if before else HELD]
-        + [VMEM] * (1 + len(before))
-        + [pl.BlockSpec(memory_space=pl.ANY)] * len(after),
+        + [VMEM] * (1 + len(before)),
         out_specs=[VMEM] * len(shapes),
         out_shape=shapes,
         input_output_aliases={6 + i: i for i in range(len(before))},
@@ -241,7 +228,7 @@
             flops=4 * rows * w.size, bytes_accessed=2 * w.size, transcendentals=0
         ),
         name="project_image",
-    )(mod, gain, down, up, w, tokens, *before, *after)
+    )(mod, gain, down, up, w, tokens, *before)
 
 
 def attend_kernel(
@@ -420,29 +407,48 @@
     )(sigma, held(image), held(noise), emb, held(weight))
 
 
-def finish_kernel(scale_a, scale_b, scale_loss, a_ref, b_ref, sums_ref, out_a, out_b, loss_ref):
+def finish_kernel(scale_a, scale_b, scale_loss, side_ref, a_ref, b_ref, sums_ref, got_ref, out_a, out_b, loss_ref):
     half = HD // 2
-    total = jnp.sum(sums_ref[...], axis=0, keepdims=True)
+    rows, width, cols = a_ref.shape[0], a_ref.shape[1], b_ref.shape[1]
+    at = rows // 8 * (width + cols)
+    other = [got_ref[:, at + i * HD : at + (i + 1) * HD].astype(F32) for i in range(3)]
+    total = jnp.sum(sums_ref[...] + (other[0] + other[1] + other[2]), axis=0, keepdims=True)
     loss_ref[...] = jnp.sum(total[:, :half], axis=1, keepdims=True) * scale_loss
     squares_b = jnp.sum(total[:, half:], axis=1, keepdims=True) * scale_b
-    grad_a = a_ref[...].astype(F32)
-    squares = jnp.sum(jnp.sum(grad_a * grad_a, axis=0, keepdims=True), axis=1, keepdims=True)
-    unit_a = lax.rsqrt(squares * scale_a + EPS)
-    out_b[...] = b_ref[...].astype(F32) * lax.rsqrt(squares_b + EPS)
-    out_a[...] = grad_a * unit_a
-
-
-def finish(grad_a, grad_b, sums, n, entries):
-    (rank, width), cols = grad_a.shape, grad_b.shape[1]
+    unit_b = lax.rsqrt(squares_b + EPS)
+    blocks = range(rows // 8)
+    mine = [lambda b=b: a_ref[8 * b : 8 * b + 8, :].astype(F32) for b in blocks]
+    theirs = [lambda b=b: got_ref[:, b * width : (b + 1) * width].astype(F32) for b in blocks]
+
+    def squares(parts):
+        each = functools.reduce(lambda x, y: x + y, [p() * p() for p in parts])
+        return jnp.sum(jnp.sum(each, axis=0, keepdims=True), axis=1, keepdims=True)
+
+    unit_a = lax.rsqrt((squares(mine) + squares(theirs)) * scale_a + EPS)
+    side = side_ref[0]
+    at = rows // 8 * width
+    for b in blocks:
+        own = pl.ds(pl.multiple_of(side * rows + 8 * b, 8), 8)
+        far = pl.ds(pl.multiple_of((1 - side) * rows + 8 * b, 8), 8)
+        out_a[own, :] = mine[b]() * unit_a
+        out_a[far, :] = theirs[b]() * unit_a
+        out_b[own, :] = b_ref[8 * b : 8 * b + 8, :].astype(F32) * unit_b
+        out_b[far, :] = got_ref[:, at + b * cols : at + (b + 1) * cols].astype(F32) * unit_b
+
+
+def finish(side, grad_a, grad_b, sums, got, n, entries):
+    (half, width), cols = grad_a.shape, grad_b.shape[1]
+    rank = 2 * half
     return pl.pallas_call(
         functools.partial(finish_kernel, 1.0 / (rank * width), 1.0 / (rank * cols * n), 1.0 / entries),
+        in_specs=[pl.BlockSpec(memory_space=pltpu.SMEM)] + [VMEM] * 4,
         out_shape=[
             jax.ShapeDtypeStruct((rank, width), F32),
             jax.ShapeDtypeStruct((rank, cols), F32),
             jax.ShapeDtypeStruct((1, 1), F32),
         ],
         name="finish",
-    )(grad_a, grad_b, sums)
+    )(side, grad_a, grad_b, sums, got)
 
 
 def shifted(x, axis, k):
@@ -450,48 +456,108 @@
     return lax.ppermute(x, axis, [(i, (i + k) % size) for i in range(size)])
 
 
-def side_of(axis, bit):
-    return lax.rem(lax.div(lax.axis_index(axis), bit), 2)
-
-
-def swap(arrays, axis, bit):
-    pairs = [(i, i ^ bit) for i in range(lax.axis_size(axis))]
-    if len(arrays) == 1 or any(x.shape[0] % 8 or x.shape[1] % HD for x in arrays):
-        return [lax.ppermute(x, axis, pairs) for x in arrays]
-    rows = [x[r : r + 8] for x in arrays for r in range(0, x.shape[0], 8)]
-    got = lax.ppermute(jnp.concatenate(rows, 1), axis, pairs)
+def packed(arrays):
+    return len(arrays) > 1 and all(x.shape[0] % 8 == 0 and x.shape[1] % HD == 0 for x in arrays)
+
+
+def pack(arrays):
+    return jnp.concatenate([x[r : r + 8] for x in arrays for r in range(0, x.shape[0], 8)], 1)
+
+
+def unpack(message, arrays):
     out, at = [], 0
     for x in arrays:
         blocks = []
         for _ in range(0, x.shape[0], 8):
-            blocks.append(got[:, at : at + x.shape[1]])
+            blocks.append(message[:, at : at + x.shape[1]])
             at += x.shape[1]
         out.append(blocks[0] if len(blocks) == 1 else jnp.concatenate(blocks, 0))
     return out
 
 
-def cut_of(x):
-    if x.shape[0] % 16 == 0:
+def send(arrays, group, hop):
+    pairs = [(i, i ^ group.mask(hop)) for i in range(group.size)]
+    if not packed(arrays):
+        return [lax.ppermute(x, group.axes, pairs) for x in arrays]
+    return unpack(lax.ppermute(pack(arrays), group.axes, pairs), arrays)
+
+
+class Group:
+    def __init__(self, *places):
+        self.axes = tuple(a for a in ("grp", "seq", "dp") if any(a == p[0] for p in places))
+        self.size = math.prod(lax.axis_size(a) for a in self.axes)
+        self.places = places
+        self.count = 1 << len(places)
+        sides = [lax.rem(lax.div(lax.axis_index(a), bit), 2) for a, bit in places]
+        self.me = functools.reduce(lambda total, side: 2 * total + side, sides, 0)
+
+    def mask(self, hop):
+        total = 0
+        for i, (axis, bit) in enumerate(reversed(self.places)):
+            if hop >> i & 1:
+                below = self.axes[self.axes.index(axis) + 1 :]
+                total ^= bit * math.prod(lax.axis_size(a) for a in below)
+        return total
+
+
+def cut_of(x, count):
+    if x.shape[0] % (8 * count) == 0:
         return 0
-    return 1 if x.shape[1] % (2 * HD) == 0 else 0
-
-
-def halve(arrays, axis, bit, dtype):
-    side = side_of(axis, bit)
-    keep, send = [], []
-    for x in arrays:
-        dim = cut_of(x)
-        first, second = jnp.split(x, 2, dim)
-        keep.append(jnp.where(side == 0, first, second))
-        send.append(jnp.where(side == 0, second, first).astype(dtype))
-    got = swap(send, axis, bit)
-    return [k + g.astype(F32) for k, g in zip(keep, got)]
-
-
-def join(mine, theirs, side, dim):
-    return jnp.concatenate(
-        [jnp.where(side == 0, mine, theirs), jnp.where(side == 0, theirs, mine)], dim
-    )
+    return 1 if x.shape[1] % (count * HD) == 0 else 0
+
+
+def block(x, dim, count, index):
+    each = x.shape[dim] // count
+    return lax.dynamic_slice_in_dim(x, index * each, each, dim)
+
+
+def scatter(wide, narrow=()):
+    arrays, group = wide
+    more, part = narrow or ([], None)
+    dims = [cut_of(x, group.count) for x in arrays]
+    more_dims = [cut_of(x, part.count) for x in more]
+    sums = [block(x, d, group.count, group.me) for x, d in zip(arrays, dims)]
+    more_sums = [block(x, d, part.count, part.me) for x, d in zip(more, more_dims)]
+    for hop in range(1, group.count):
+        out = [block(x, d, group.count, group.me ^ hop).astype(BF16) for x, d in zip(arrays, dims)]
+        join = part is not None and hop < part.count
+        if join:
+            out += [block(x, d, part.count, part.me ^ hop).astype(BF16) for x, d in zip(more, more_dims)]
+        got = [g.astype(F32) for g in send(out, group, hop)]
+        sums = [t + g for t, g in zip(sums, got)]
+        if join:
+            more_sums = [t + g for t, g in zip(more_sums, got[len(sums) :])]
+    return sums, dims, more_sums, more_dims
+
+
+def ordered(parts, me):
+    return [
+        functools.reduce(
+            lambda so_far, hop: jnp.where(me == j ^ hop, parts[hop], so_far), range(1, len(parts)), parts[0]
+        )
+        for j in range(len(parts))
+    ]
+
+
+def gather(wide, sums, narrow=()):
+    arrays, dims, group = wide
+    more, more_dims, part = narrow or ([], [], None)
+    parts = [[x] for x in arrays]
+    more_parts = [[x] for x in more]
+    totals = [sums]
+    for hop in range(1, group.count):
+        join = part is not None and hop < part.count
+        out = [*arrays, *(more if join else []), pieces(sums)]
+        *got, other = send(out, group, hop)
+        other = other.astype(F32)
+        totals.append(other[:, :HD] + other[:, HD : 2 * HD] + other[:, 2 * HD :])
+        for so_far, g in zip(parts + (more_parts if join else []), got):
+            so_far.append(g)
+    totals = ordered(totals, group.me)
+    sums = functools.reduce(lambda x, y: x + y, totals)
+    whole = [jnp.concatenate(ordered(p, group.me), d) for p, d in zip(parts, dims)]
+    more_whole = [jnp.concatenate(ordered(p, part.me), d) for p, d in zip(more_parts, more_dims)]
+    return whole, more_whole, sums
 
 
 def pieces(value):
@@ -499,14 +565,6 @@
     rest = value - first
     second = lax.reduce_precision(rest, 8, 7)
     return jnp.concatenate([first, second, rest - second], 1).astype(BF16)
-
-
-def rejoin(arrays, dims, sums, axis, bit):
-    side = side_of(axis, bit)
-    *got, other = swap([*arrays, pieces(sums)], axis, bit)
-    other = other.astype(F32)
-    sums = sums + (other[:, :HD] + other[:, HD : 2 * HD] + other[:, 2 * HD :])
-    return [join(x, g, side, d) for x, g, d in zip(arrays, got, dims)], sums
 
 
 def bits(axis):
@@ -564,52 +622,42 @@
     bias = jnp.where(place < text_token_length[0], 0.0, -1000000000.0).astype(F32)[None]
     core = lax.rem(lax.axis_index("grp"), 2).astype(jnp.int32)
     gain = query_key_norm_gain
-    image_weight = held(image_projection_weight)
-    text_steps = split(text_projection_weight.shape[1] // (2 * HD))[1]
-    text_weight = fetch(held(text_projection_weight), text_steps, part)
     down = adapter_down_weight.T
-
-    def text_part(k, after):
-        return project_text(k, n, text_heads, mod, gain, text_weight, text_parts[k], after)
-
-    def image_part(k, after):
-        return project_image(
-            k, n, image_heads, mod, gain, down, adapter_up_weight, image_weight, noisy_parts[k], after
+    image_weight, image_heads = held(image_projection_weight), []
+    for k in range(n):
+        image_heads = project_image(
+            k, n, image_heads, mod, gain, down, adapter_up_weight, image_weight, noisy_parts[k]
         )
-
-    text_heads, image_heads = [], []
-    text_heads = text_part(0, None)
-    *image_heads, image_weight = image_part(0, text_heads[0])
-    for k in range(1, n):
-        image_heads = image_part(k, None)
-        text_heads = text_part(k, image_heads[0])
+        if k == 0:
+            *image_heads, image_weight = image_heads
+    text_heads = project_text(mod, gain, held(text_projection_weight), image_heads[0], text_parts)
     send_a, keep_a, send_b, keep_b, loss = attend(
         core[None], bias, gain, adapter_up_weight, image_heads, text_heads
     )
-    (got_a,), (got_b,) = swap([send_a], "grp", 1), swap([send_b], "grp", 1)
+    cores = Group(("grp", 1))
+    (got_a,), (got_b,) = send([send_a], cores, 1), send([send_b], cores, 1)
     grad_a, grad_b = keep_a + got_a.astype(F32), keep_b + got_b.astype(F32)
-    seq_dims, dp_dims = [], []
-    for bit in reversed(bits("seq")):
-        seq_dims.append(cut_of(grad_a))
-        (grad_a,) = halve([grad_a], "seq", bit, BF16)
-    x_dims = [cut_of(grad_a), cut_of(grad_b)]
-    (grad_b,) = halve([grad_b], "grp", 2, BF16)
-    (grad_a,) = halve([grad_a], "grp", 2, BF16)
-    for bit in bits("dp"):
-        dp_dims.append([cut_of(grad_a), cut_of(grad_b)])
-        grad_a, grad_b = halve([grad_a, grad_b], "dp", bit, F32)
-    squares = fold(grad_b * grad_b)
+    last, *far = bits("seq")
+    far = [(Group(("seq", bit)), []) for bit in reversed(far)]
+    for group, dims in far:
+        (grad_a,), dims[:], _, _ = scatter(([grad_a], group))
+    near, across = Group(("seq", last), ("grp", 2)), Group(("grp", 2))
+    (grad_a,), dims_a, (grad_b,), dims_b = scatter(([grad_a], near), ([grad_b], across))
+    line = Group(*[("dp", bit) for bit in reversed(bits("dp"))])
+    (grad_a, grad_b), dims_z, _, _ = scatter(([grad_a, grad_b], line))
+    squares = fold(jnp.sum(grad_b.reshape(-1, min(grad_b.shape[0], 8), grad_b.shape[1]) ** 2, 0))
     squares = jnp.pad(squares, ((0, 8 - squares.shape[0]), (0, 0)))
     sums = jnp.concatenate([fold(loss), squares], 1)
-    grads = [grad_a.astype(BF16), grad_b.astype(BF16)]
-    for bit in reversed(bits("dp")):
-        grads, sums = rejoin(grads, dp_dims.pop(), sums, "dp", bit)
-    grads, sums = rejoin(grads, x_dims, sums, "grp", 2)
-    for bit in bits("seq"):
-        (grads[0],), sums = rejoin(grads[:1], [seq_dims.pop()], sums, "seq", bit)
-    grads, sums = rejoin(grads, [0, 0], sums, "grp", 1)
+    grads, _, sums = gather(([grad_a.astype(BF16), grad_b.astype(BF16)], dims_z, line), sums)
+    (grad_a,), (grad_b,), sums = gather(
+        (grads[:1], dims_a, near), sums, (grads[1:], dims_b, across)
+    )
+    for group, dims in reversed(far):
+        (grad_a,), _, sums = gather(([grad_a], dims, group), sums)
+    pairs = [(i, i ^ 1) for i in range(cores.size)]
+    got = lax.ppermute(pack([grad_a, grad_b, pieces(sums)]), "grp", pairs)
     direction_a, direction_b, loss_mean = finish(
-        *grads, sums, n, samples * n * img_part * HEADS * HD
+        core[None], grad_a, grad_b, sums, got, n, samples * n * img_part * HEADS * HD
     )
     return (direction_a.T, direction_b, loss_mean[0, 0])
 

time: 107 us -> 79.7 us (0.74)
  waiting for transfers between devices: 28 us -> 17.5 us
  Pallas kernels: 41 us -> 30.9 us
  local copies, waits for them, and re-layouts: 10.2 us -> 3.62 us
  starting transfers between devices: 20.2 us -> 21.5 us
    ppermute x12 -> x15, waiting for transfers between devices: 28 us -> 16.8 us  [the longest x10 14.3 us: send(): return unpack(lax.ppermute(pack(arrays), group.axes, pairs), arrays)]
    pallas_call x3 -> x1, Pallas kernels: 13.2 us -> 5.65 us  [project_text(): pl.pallas_call(functools.partial(text_kernel, n, pair), in_specs=[VMEM, V...]
    unnamed x27 -> x26, local copies, waits for them, and re-layouts: 10.2 us -> 3.5 us
    pallas_call x2, Pallas kernels: 16.1 us -> 13.9 us  [project_image(): pl.pallas_call(functools.partial(image_kernel, pair, part, len(before)),...]
    ppermute x12 -> x15, starting transfers between devices: 15.3 us -> 16.5 us  [the longest x10 13.9 us: send(): return unpack(lax.ppermute(pack(arrays), group.axes, pairs), arrays)]
  transfers between devices with their start and end apart: 15 -> 18, of which waited for: 11 -> 12; matrix products, arithmetic and copies ran while one was open for 0% -> 2% of each run, Pallas kernels for 23% -> 18%
where the time goes in v5:
time: 79.7 us; the launch traced here: 79.5 us
  Pallas kernels  30.9 us (39%)
  starting transfers between devices  21.5 us (27%)
  waiting for transfers between devices  17.5 us (22%)
  local copies, waits for them, and re-layouts  3.62 us (5%)
  between operations  3.11 us (4%)
  other arithmetic  2.83 us (4%)
    ppermute x10, waiting for transfers between devices, send(): return unpack(lax.ppermute(pack(arrays), group.axes, pairs), arrays)  14.3 us
    pallas_call x2, Pallas kernels, project_image(): pl.pallas_call(functools.partial(image_kernel, pair, part, len(before)),...  13.9 us
    ppermute x10, starting transfers between devices, send(): return unpack(lax.ppermute(pack(arrays), group.axes, pairs), arrays)  13.9 us
    pallas_call x1, Pallas kernels, attend(): pl.pallas_call(functools.partial(attend_kernel, steps, pair, samples), in...  5.93 us
    pallas_call x1, Pallas kernels, project_text(): pl.pallas_call(functools.partial(text_kernel, n, pair), in_specs=[VMEM, V...  5.65 us
    ppermute x3, starting transfers between devices, shifted(): return lax.ppermute(x, axis, [(i, (i + k) % size) for i in range(size)])  5.06 us
    unnamed x26, local copies, waits for them, and re-layouts  3.5 us
    pallas_call x1, Pallas kernels, start(): pl.pallas_call(start_kernel, grid=(steps,), in_specs=[pl.BlockSpec(memory...  2.8 us
  transfers between devices with their start and end apart: 18, of which 12 were waited for; matrix products, arithmetic and copies ran while one was open for 2% of the time, Pallas kernels for 18%

profile of v5, /device:TPU:0, one launch (start us, length us, event | category | flops | bytes accessed | tf_op | source)
XLA Modules:
  0.0 79.5 jit_solution(14862019678613388639)
XLA Ops:
  2.3 2.8 %start.1 = (bf16[80,3072]{1,0:T(8,128)(2,1)S(1)}, f32[2,6144]{1,0:T(2,128)S(1)}) custom-call(f32[1]{0:T(128)} %bitcast.5.sigma_ref, bf16[80,3072]{1,0:T(8,128)(2,1)} %bitcast.23, bf16[80,3072]{1,0:T(8,128)(2,1)} %bitcast.24, bf16[16,256]{1,0:T(8,128)(2,1)S(1)} %fusion.5.emb_ref, bf16[256,6144]{1,0:T(8,128)(2,1)} %weight_ref.1), custom_call_target="tpu_custom_call" | custom-call | flops 6291456 | bytes 4620288 | tf_op jit(solution)/shard_map/start/pallas_call | solution.py:387
  5.1 3.0 %collective-permute-start = (f32[2,6144]{1,0:T(2,128)S(1)}, f32[2,6144]{1,0:T(2,128)S(1)}, u32[]{:S(2)}, u32[]{:S(2)}) collective-permute-start(f32[2,6144]{1,0:T(2,128)S(1)} %get-tuple-element.28), channel_id=1, source_target_pairs={{0,4},{4,0},{1,5},{5,1},{2,6},{6,2},{3,7},{7,3},{8,12},{12,8},{9,1... | collective-permute-start | bytes 147464 | tf_op jit(solution)/shard_map/ppermute | solution.py:456
  8.2 1.9 %collective-permute-start.2 = (bf16[48,3072]{1,0:T(8,128)(2,1)}, bf16[48,3072]{1,0:T(8,128)(2,1)S(1)}, u32[]{:S(2)}, u32[]{:S(2)}) collective-permute-start(bf16[48,3072]{1,0:T(8,128)(2,1)} %bitcast.21), channel_id=1, source_target_pairs={{0,4},{4,0},{1,5},{5,1},{2,6},{6,2},{3,7},{7,3},{8,12},{12,8},{9,1... | collective-permute-start | bytes 884744 | tf_op jit(solution)/shard_map/ppermute | solution.py:456
  11.0 1.0 %copy-done = bf16[64,3072]{1,0:T(8,128)(2,1)S(1)} copy-done((bf16[64,3072]{1,0:T(8,128)(2,1)S(1)}, bf16[64,3072]{1,0:T(8,128)(2,1)}, u32[]{:S(2)}) %copy-start) | copy-done | bytes 393240
  12.0 1.0 %copy-done.2 = bf16[3072,64]{0,1:T(8,128)(2,1)S(1)} copy-done((bf16[3072,64]{0,1:T(8,128)(2,1)S(1)}, bf16[3072,64]{0,1:T(8,128)(2,1)}, u32[]{:S(2)}) %copy-start.2) | copy-done | bytes 393240
  13.0 0.7 copy-done.4
  13.7 7.9 %project_image.2 = (bf16[8,2,160,128]{3,2,1,0:T(8,128)(2,1)S(1)}, bf16[8,2,160,128]{3,2,1,0:T(8,128)(2,1)S(1)}, bf16[8,2,160,128]{3,2,1,0:T(8,128)(2,1)S(1)}, f3...) custom-call(f32[2,12288]{1,0:T(2,128)S(1)} %pad_maximum_fusion.3.mod, ...), custom_call_target="tpu_custom_call" | custom-call | flops 3019898880 | bytes 18874368 | tf_op jit(solution)/shard_map/project_image/pallas_call | solution.py:217
  21.6 0.7 collective-permute-done.1.tokens
  22.3 6.0 %project_image.3 = (bf16[8,2,160,128]{3,2,1,0:T(8,128)(2,1)S(1)}, bf16[8,2,160,128]{3,2,1,0:T(8,128)(2,1)S(1)}, bf16[8,2,160,128]{3,2,1,0:T(8,128)(2,1)S(1)}, f3...) custom-call(f32[2,12288]{1,0:T(2,128)S(1)} %pad_maximum_fusion.3.mod, ...), custom_call_target="tpu_custom_call", output_to_operand_aliasing={{0}: (6, {}), {1}: (7, {}), {2}: (8, {}), {3}: (9, {}), {4}... | custom-call | flops 3019898880 | bytes 18874368 | tf_op jit(solution)/shard_map/project_image/pallas_call | solution.py:217
  28.4 5.7 %project_text.1 = (bf16[8,2,96,128]{3,2,1,0:T(8,128)(2,1)S(1)}, bf16[8,2,96,128]{3,2,1,0:T(8,128)(2,1)S(1)}) custom-call(f32[2,12288]{1,0:T(2,128)S(1)} %pad_maximum_fusion.3.mod_ref, f32[3,128]{1,0:T(4,128)S(1)} %copy-done.4, bf16[3072,2048]{1,0:T(8,128)(2,1)} %w_ref.3, bf16[8,2,160,128]{3,2,1,0:T(8,128)(2,1)S(1)} %get-tuple-element.37.after_ref.q_ref, ...), custom_call_target="tpu_custom_call" | custom-call | flops 2415919104 | bytes 12582912 | tf_op jit(solution)/shard_map/project_text/pallas_call | solution.py:143
  34.0 5.9 %attend.1 = (bf16[32,3072]{1,0:T(8,128)(2,1)S(1)}, f32[32,3072]{1,0:T(8,128)S(1)}, bf16[32,3072]{1,0:T(8,128)(2,1)S(1)}, f32[32,3072]{1,0:T(8,128)S(1)}, f32[8,128]{1,0:T(8,128)S(1)}) custom-call(s32[1]{0:T(128)} %bitcast.where_ref.side_ref, f32[1,256]{1,0:T(1,128)S(1)} %compare_select_fusion.bias_ref, f32[3,128]{1,0:T(4,128)S(1)} %copy-done.4, ...), custom_call_target="tpu_custom_call" | custom-call | flops 671088640 | bytes 8000000 | tf_op jit(solution)/shard_map/attend/pallas_call | solution.py:344
  40.6 0.9 %collective-permute-done.4 = bf16[32,3072]{1,0:T(8,128)(2,1)S(1)} collective-permute-done((bf16[32,3072]{1,0:T(8,128)(2,1)S(1)}, bf16[32,3072]{1,0:T(8,128)(2,1)S(1)}, u32[]{:S(2)}, u32[]{:S(2)}) %collective-permute-start.4) | collective-permute-done | bytes 196640 | tf_op jit(solution)/shard_map/ppermute | solution.py:481
  41.9 1.6 %collective-permute-start.5 = (bf16[8,9216]{1,0:T(8,128)(2,1)S(1)}, bf16[8,9216]{1,0:T(8,128)(2,1)S(1)}, u32[]{:S(2)}, u32[]{:S(2)}) collective-permute-start(bf16[8,9216]{1,0:T(8,128)(2,1)S(1)} %pad_maximum_fusion.2), channel_id=1, source_target_pairs={{0,16},{4,20},{8,24},{12,28},{16,0},{20,4},{24,8},{28,12},{1,17},{... | collective-permute-start | bytes 442376 | tf_op jit(solution)/shard_map/ppermute | solution.py:482
  43.4 1.2 %collective-permute-start.6 = (bf16[8,3072]{1,0:T(8,128)(2,1)S(1)}, bf16[8,3072]{1,0:T(8,128)(2,1)S(1)}, u32[]{:S(2)}, u32[]{:S(2)}) collective-permute-start(bf16[8,3072]{1,0:T(8,128)(2,1)S(1)} %get-tuple-element.77), channel_id=1, source_target_pairs={{0,4},{4,0},{8,12},{12,8},{16,20},{20,16},{24,28},{28,24},{1,5},{5... | collective-permute-start | bytes 147464 | tf_op jit(solution)/shard_map/ppermute | solution.py:481
  44.6 0.8 %collective-permute-start.7 = (bf16[8,3072]{1,0:T(8,128)(2,1)S(1)}, bf16[8,3072]{1,0:T(8,128)(2,1)S(1)}, u32[]{:S(2)}, u32[]{:S(2)}) collective-permute-start(bf16[8,3072]{1,0:T(8,128)(2,1)S(1)} %get-tuple-element.78), channel_id=1, source_target_pairs={{0,20},{4,16},{8,28},{12,24},{16,4},{20,0},{24,12},{28,8},{1,21},{... | collective-permute-start | bytes 147464 | tf_op jit(solution)/shard_map/ppermute | solution.py:481
  45.4 3.0 %collective-permute-done.5 = bf16[8,9216]{1,0:T(8,128)(2,1)S(1)} collective-permute-done((bf16[8,9216]{1,0:T(8,128)(2,1)S(1)}, bf16[8,9216]{1,0:T(8,128)(2,1)S(1)}, u32[]{:S(2)}, u32[]{:S(2)}) %collective-permute-start.5) | collective-permute-done | bytes 147488 | tf_op jit(solution)/shard_map/ppermute | solution.py:482
  48.5 1.1 %collective-permute-done.7 = bf16[8,3072]{1,0:T(8,128)(2,1)S(1)} collective-permute-done((bf16[8,3072]{1,0:T(8,128)(2,1)S(1)}, bf16[8,3072]{1,0:T(8,128)(2,1)S(1)}, u32[]{:S(2)}, u32[]{:S(2)}) %collective-permute-start.7) | collective-permute-done | bytes 49184 | tf_op jit(solution)/shard_map/ppermute | solution.py:481
  49.7 2.7 %collective-permute-start.9 = (bf16[8,2304]{1,0:T(8,128)(2,1)S(1)}, bf16[8,2304]{1,0:T(8,128)(2,1)S(1)}, u32[]{:S(2)}, u32[]{:S(2)}) collective-permute-start(bf16[8,2304]{1,0:T(8,128)(2,1)S(1)} %pad_maximum_fusion.8), channel_id=1, source_target_pairs={{0,2},{1,3},{2,0},{3,1},{4,6},{5,7},{6,4},{7,5},{8,10},{9,11},{10,... | collective-permute-start | bytes 110600 | tf_op jit(solution)/shard_map/ppermute | solution.py:482
  52.4 1.3 %collective-permute-start.10 = (bf16[8,2304]{1,0:T(8,128)(2,1)S(1)}, bf16[8,2304]{1,0:T(8,128)(2,1)S(1)}, u32[]{:S(2)}, u32[]{:S(2)}) collective-permute-start(bf16[8,2304]{1,0:T(8,128)(2,1)S(1)} %pad_maximum_fusion.9), channel_id=1, source_target_pairs={{0,3},{1,2},{2,1},{3,0},{4,7},{5,6},{6,5},{7,4},{8,11},{9,10},{10,... | collective-permute-start | bytes 110600 | tf_op jit(solution)/shard_map/ppermute | solution.py:482
  54.6 3.5 %collective-permute-done.10 = bf16[8,2304]{1,0:T(8,128)(2,1)S(1)} collective-permute-done((bf16[8,2304]{1,0:T(8,128)(2,1)S(1)}, bf16[8,2304]{1,0:T(8,128)(2,1)S(1)}, u32[]{:S(2)}, u32[]{:S(2)}) %collective-permute-start.10) | collective-permute-done | bytes 36896 | tf_op jit(solution)/shard_map/ppermute | solution.py:482
  58.4 2.1 %collective-permute-start.11 = (bf16[8,2688]{1,0:T(8,128)(2,1)S(1)}, bf16[8,2688]{1,0:T(8,128)(2,1)S(1)}, u32[]{:S(2)}, u32[]{:S(2)}) collective-permute-start(bf16[8,2688]{1,0:T(8,128)(2,1)S(1)} %constant_dynamic-update-slice_fusion), channel_id=1, source_target_pairs={{0,3},{1,2},{2,1},{3,0},{4,7},{5,6},{6,5},{7,4},{8,11},{9,10},{10,... | collective-permute-start | bytes 129032 | tf_op jit(solution)/shard_map/ppermute | solution.py:482
  60.5 2.4 %collective-permute-start.13 = (bf16[8,2688]{1,0:T(8,128)(2,1)S(1)}, bf16[8,2688]{1,0:T(8,128)(2,1)S(1)}, u32[]{:S(2)}, u32[]{:S(2)}) collective-permute-start(bf16[8,2688]{1,0:T(8,128)(2,1)S(1)} %constant_dynamic-update-slice_fusion), channel_id=1, source_target_pairs={{0,1},{1,0},{2,3},{3,2},{4,5},{5,4},{6,7},{7,6},{8,9},{9,8},{10,11... | collective-permute-start | bytes 129032 | tf_op jit(solution)/shard_map/ppermute | solution.py:482
  62.9 1.4 %collective-permute-done.11 = bf16[8,2688]{1,0:T(8,128)(2,1)S(1)} collective-permute-done((bf16[8,2688]{1,0:T(8,128)(2,1)S(1)}, bf16[8,2688]{1,0:T(8,128)(2,1)S(1)}, u32[]{:S(2)}, u32[]{:S(2)}) %collective-permute-start.11) | collective-permute-done | bytes 43040 | tf_op jit(solution)/shard_map/ppermute | solution.py:482
  64.3 1.1 %collective-permute-done.12 = bf16[8,2688]{1,0:T(8,128)(2,1)S(1)} collective-permute-done((bf16[8,2688]{1,0:T(8,128)(2,1)S(1)}, bf16[8,2688]{1,0:T(8,128)(2,1)S(1)}, u32[]{:S(2)}, u32[]{:S(2)}) %collective-permute-start.12) | collective-permute-done | bytes 43040 | tf_op jit(solution)/shard_map/ppermute | solution.py:482
  65.8 1.8 %collective-permute-start.14 = (bf16[8,3456]{1,0:T(8,128)(2,1)S(1)}, bf16[8,3456]{1,0:T(8,128)(2,1)S(1)}, u32[]{:S(2)}, u32[]{:S(2)}) collective-permute-start(bf16[8,3456]{1,0:T(8,128)(2,1)S(1)} %get-tuple-element.120), channel_id=1, source_target_pairs={{0,20},{4,16},{8,28},{12,24},{16,4},{20,0},{24,12},{28,8},{1,21},{... | collective-permute-start | bytes 165896 | tf_op jit(solution)/shard_map/ppermute | solution.py:482
  67.6 1.2 %collective-permute-start.15 = (bf16[8,3456]{1,0:T(8,128)(2,1)S(1)}, bf16[8,3456]{1,0:T(8,128)(2,1)S(1)}, u32[]{:S(2)}, u32[]{:S(2)}) collective-permute-start(bf16[8,3456]{1,0:T(8,128)(2,1)S(1)} %get-tuple-element.120), channel_id=1, source_target_pairs={{0,4},{4,0},{8,12},{12,8},{16,20},{20,16},{24,28},{28,24},{1,5},{5... | collective-permute-start | bytes 165896 | tf_op jit(solution)/shard_map/ppermute | solution.py:482
  69.3 2.4 %collective-permute-done.15 = bf16[8,3456]{1,0:T(8,128)(2,1)S(1)} collective-permute-done((bf16[8,3456]{1,0:T(8,128)(2,1)S(1)}, bf16[8,3456]{1,0:T(8,128)(2,1)S(1)}, u32[]{:S(2)}, u32[]{:S(2)}) %collective-permute-start.15) | collective-permute-done | bytes 55328 | tf_op jit(solution)/shard_map/ppermute | solution.py:482
  71.8 2.2 %collective-permute-done.16 = bf16[8,9600]{1,0:T(8,128)(2,1)S(1)} collective-permute-done((bf16[8,9600]{1,0:T(8,128)(2,1)S(1)}, bf16[8,9600]{1,0:T(8,128)(2,1)S(1)}, u32[]{:S(2)}, u32[]{:S(2)}) %collective-permute-start.16) | collective-permute-done | bytes 153632 | tf_op jit(solution)/shard_map/ppermute | solution.py:482
  74.4 0.7 pad_maximum_fusion.1.b_ref
  75.1 0.7 pad_maximum_fusion.a_ref
  76.1 0.8 copy-done.5
  76.9 2.6 %finish.1 = (f32[64,3072]{1,0:T(8,128)}, f32[64,3072]{1,0:T(8,128)}, f32[1,1]{1,0:T(1,128)}) custom-call(s32[1]{0:T(128)} %bitcast.where_ref.side_ref, bf16[32,3072]{1,0:T(8,128)(2,1)} %pad_maximum_fusion.a_ref, bf16[32,3072]{1,0:T(8,128)(2,1)} %pad_maximum_fusion.1.b_ref, f32[8,128]{1,0:T(8,128)} %copy-done.6, bf16[8,24960]{1,0:T(8,128)(2,1)} %copy-done.5), custom_call_target="tpu_custom_call" | custom-call | tf_op jit(solution)/shard_map/finish/pallas_call | solution.py:442
  (101 shorter events, 4.2 us)
Async XLA Ops:
  5.1 5.8 %collective-permute-start = (f32[2,6144]{1,0:T(2,128)S(1)}, f32[2,6144]{1,0:T(2,128)S(1)}, u32[]{:S(2)}, u32[]{:S(2)}) collective-permute-start(f32[2,6144]{1,0:T(2,128)S(1)} %get-tuple-element.28), channel_id=1, source_target_pairs={{0,4},{4,0},{1,5},{5,1},{2,6},{6,2},{3,7},{7,3},{8,12},{12,8},{9,1... | collective-permute-start | bytes 147464 | tf_op jit(solution)/shard_map/ppermute | solution.py:456
  8.1 14.1 %collective-permute-start.1 = (bf16[80,3072]{1,0:T(8,128)(2,1)S(1)}, bf16[80,3072]{1,0:T(8,128)(2,1)S(1)}, u32[]{:S(2)}, u32[]{:S(2)}) collective-permute-start(bf16[80,3072]{1,0:T(8,128)(2,1)S(1)} %get-tuple-element.29.tokens), channel_id=1, source_target_pairs={{0,4},{4,0},{1,5},{5,1},{2,6},{6,2},{3,7},{7,3},{8,12},{12,8},{9,1... | collective-permute-start | bytes 1474568 | tf_op jit(solution)/shard_map/ppermute | solution.py:456
  8.2 20.1 %collective-permute-start.2 = (bf16[48,3072]{1,0:T(8,128)(2,1)}, bf16[48,3072]{1,0:T(8,128)(2,1)S(1)}, u32[]{:S(2)}, u32[]{:S(2)}) collective-permute-start(bf16[48,3072]{1,0:T(8,128)(2,1)} %bitcast.21), channel_id=1, source_target_pairs={{0,4},{4,0},{1,5},{5,1},{2,6},{6,2},{3,7},{7,3},{8,12},{12,8},{9,1... | collective-permute-start | bytes 884744 | tf_op jit(solution)/shard_map/ppermute | solution.py:456
  11.0 1.0 %copy-start = (bf16[64,3072]{1,0:T(8,128)(2,1)S(1)}, bf16[64,3072]{1,0:T(8,128)(2,1)}, u32[]{:S(2)}) copy-start(bf16[64,3072]{1,0:T(8,128)(2,1)} %up_ref.5) | copy-start | bytes 1179652
  12.0 1.0 %copy-start.2 = (bf16[3072,64]{0,1:T(8,128)(2,1)S(1)}, bf16[3072,64]{0,1:T(8,128)(2,1)}, u32[]{:S(2)}) copy-start(bf16[3072,64]{0,1:T(8,128)(2,1)} %param.22) | copy-start | bytes 1179652
  13.0 0.7 copy-start.4
  21.6 6.8 %copy-start.3 = (bf16[1,48,3072]{2,1,0:T(8,128)(2,1)S(1)}, bf16[1,48,3072]{2,1,0:T(8,128)(2,1)}, u32[]{:S(2)}) copy-start(bf16[1,48,3072]{2,1,0:T(8,128)(2,1)} %param.14) | copy-start | bytes 884740
  28.3 5.7 %copy-start.1 = (bf16[64,3072]{1,0:T(8,128)(2,1)S(1)}, bf16[64,3072]{1,0:T(8,128)(2,1)}, u32[]{:S(2)}) copy-start(bf16[64,3072]{1,0:T(8,128)(2,1)} %up_ref.5) | copy-start | bytes 1179652
  40.0 1.5 %collective-permute-start.4 = (bf16[32,3072]{1,0:T(8,128)(2,1)S(1)}, bf16[32,3072]{1,0:T(8,128)(2,1)S(1)}, u32[]{:S(2)}, u32[]{:S(2)}) collective-permute-start(bf16[32,3072]{1,0:T(8,128)(2,1)S(1)} %get-tuple-element.48), channel_id=1, source_target_pairs={{0,8},{8,0},{16,24},{24,16},{1,9},{9,1},{17,25},{25,17},{2,10},{10... | collective-permute-start | bytes 589832 | tf_op jit(solution)/shard_map/ppermute | solution.py:481
  40.1 1.7 %collective-permute-start.3 = (bf16[32,3072]{1,0:T(8,128)(2,1)S(1)}, bf16[32,3072]{1,0:T(8,128)(2,1)S(1)}, u32[]{:S(2)}, u32[]{:S(2)}) collective-permute-start(bf16[32,3072]{1,0:T(8,128)(2,1)S(1)} %get-tuple-element.46), channel_id=1, source_target_pairs={{0,8},{8,0},{16,24},{24,16},{1,9},{9,1},{17,25},{25,17},{2,10},{10... | collective-permute-start | bytes 589832 | tf_op jit(solution)/shard_map/ppermute | solution.py:481
  41.9 6.6 %collective-permute-start.5 = (bf16[8,9216]{1,0:T(8,128)(2,1)S(1)}, bf16[8,9216]{1,0:T(8,128)(2,1)S(1)}, u32[]{:S(2)}, u32[]{:S(2)}) collective-permute-start(bf16[8,9216]{1,0:T(8,128)(2,1)S(1)} %pad_maximum_fusion.2), channel_id=1, source_target_pairs={{0,16},{4,20},{8,24},{12,28},{16,0},{20,4},{24,8},{28,12},{1,17},{... | collective-permute-start | bytes 442376 | tf_op jit(solution)/shard_map/ppermute | solution.py:482
  43.4 5.0 %collective-permute-start.6 = (bf16[8,3072]{1,0:T(8,128)(2,1)S(1)}, bf16[8,3072]{1,0:T(8,128)(2,1)S(1)}, u32[]{:S(2)}, u32[]{:S(2)}) collective-permute-start(bf16[8,3072]{1,0:T(8,128)(2,1)S(1)} %get-tuple-element.77), channel_id=1, source_target_pairs={{0,4},{4,0},{8,12},{12,8},{16,20},{20,16},{24,28},{28,24},{1,5},{5... | collective-permute-start | bytes 147464 | tf_op jit(solution)/shard_map/ppermute | solution.py:481
  44.6 5.0 %collective-permute-start.7 = (bf16[8,3072]{1,0:T(8,128)(2,1)S(1)}, bf16[8,3072]{1,0:T(8,128)(2,1)S(1)}, u32[]{:S(2)}, u32[]{:S(2)}) collective-permute-start(bf16[8,3072]{1,0:T(8,128)(2,1)S(1)} %get-tuple-element.78), channel_id=1, source_target_pairs={{0,20},{4,16},{8,28},{12,24},{16,4},{20,0},{24,12},{28,8},{1,21},{... | collective-permute-start | bytes 147464 | tf_op jit(solution)/shard_map/ppermute | solution.py:481
  49.7 4.9 %collective-permute-start.9 = (bf16[8,2304]{1,0:T(8,128)(2,1)S(1)}, bf16[8,2304]{1,0:T(8,128)(2,1)S(1)}, u32[]{:S(2)}, u32[]{:S(2)}) collective-permute-start(bf16[8,2304]{1,0:T(8,128)(2,1)S(1)} %pad_maximum_fusion.8), channel_id=1, source_target_pairs={{0,2},{1,3},{2,0},{3,1},{4,6},{5,7},{6,4},{7,5},{8,10},{9,11},{10,... | collective-permute-start | bytes 110600 | tf_op jit(solution)/shard_map/ppermute | solution.py:482
  52.4 5.8 %collective-permute-start.10 = (bf16[8,2304]{1,0:T(8,128)(2,1)S(1)}, bf16[8,2304]{1,0:T(8,128)(2,1)S(1)}, u32[]{:S(2)}, u32[]{:S(2)}) collective-permute-start(bf16[8,2304]{1,0:T(8,128)(2,1)S(1)} %pad_maximum_fusion.9), channel_id=1, source_target_pairs={{0,3},{1,2},{2,1},{3,0},{4,7},{5,6},{6,5},{7,4},{8,11},{9,10},{10,... | collective-permute-start | bytes 110600 | tf_op jit(solution)/shard_map/ppermute | solution.py:482
  53.7 4.4 %collective-permute-start.8 = (bf16[8,2304]{1,0:T(8,128)(2,1)S(1)}, bf16[8,2304]{1,0:T(8,128)(2,1)S(1)}, u32[]{:S(2)}, u32[]{:S(2)}) collective-permute-start(bf16[8,2304]{1,0:T(8,128)(2,1)S(1)} %pad_maximum_fusion.7), channel_id=1, source_target_pairs={{0,1},{1,0},{2,3},{3,2},{4,5},{5,4},{6,7},{7,6},{8,9},{9,8},{10,11... | collective-permute-start | bytes 110600 | tf_op jit(solution)/shard_map/ppermute | solution.py:482
  58.4 5.9 %collective-permute-start.11 = (bf16[8,2688]{1,0:T(8,128)(2,1)S(1)}, bf16[8,2688]{1,0:T(8,128)(2,1)S(1)}, u32[]{:S(2)}, u32[]{:S(2)}) collective-permute-start(bf16[8,2688]{1,0:T(8,128)(2,1)S(1)} %constant_dynamic-update-slice_fusion), channel_id=1, source_target_pairs={{0,3},{1,2},{2,1},{3,0},{4,7},{5,6},{6,5},{7,4},{8,11},{9,10},{10,... | collective-permute-start | bytes 129032 | tf_op jit(solution)/shard_map/ppermute | solution.py:482
  60.5 4.9 %collective-permute-start.12 = (bf16[8,2688]{1,0:T(8,128)(2,1)S(1)}, bf16[8,2688]{1,0:T(8,128)(2,1)S(1)}, u32[]{:S(2)}, u32[]{:S(2)}) collective-permute-start(bf16[8,2688]{1,0:T(8,128)(2,1)S(1)} %constant_dynamic-update-slice_fusion), channel_id=1, source_target_pairs={{0,2},{1,3},{2,0},{3,1},{4,6},{5,7},{6,4},{7,5},{8,10},{9,11},{10,... | collective-permute-start | bytes 129032 | tf_op jit(solution)/shard_map/ppermute | solution.py:482
  60.5 4.9 %collective-permute-start.13 = (bf16[8,2688]{1,0:T(8,128)(2,1)S(1)}, bf16[8,2688]{1,0:T(8,128)(2,1)S(1)}, u32[]{:S(2)}, u32[]{:S(2)}) collective-permute-start(bf16[8,2688]{1,0:T(8,128)(2,1)S(1)} %constant_dynamic-update-slice_fusion), channel_id=1, source_target_pairs={{0,1},{1,0},{2,3},{3,2},{4,5},{5,4},{6,7},{7,6},{8,9},{9,8},{10,11... | collective-permute-start | bytes 129032 | tf_op jit(solution)/shard_map/ppermute | solution.py:482
  65.8 6.0 %collective-permute-start.14 = (bf16[8,3456]{1,0:T(8,128)(2,1)S(1)}, bf16[8,3456]{1,0:T(8,128)(2,1)S(1)}, u32[]{:S(2)}, u32[]{:S(2)}) collective-permute-start(bf16[8,3456]{1,0:T(8,128)(2,1)S(1)} %get-tuple-element.120), channel_id=1, source_target_pairs={{0,20},{4,16},{8,28},{12,24},{16,4},{20,0},{24,12},{28,8},{1,21},{... | collective-permute-start | bytes 165896 | tf_op jit(solution)/shard_map/ppermute | solution.py:482
  67.6 4.2 %collective-permute-start.15 = (bf16[8,3456]{1,0:T(8,128)(2,1)S(1)}, bf16[8,3456]{1,0:T(8,128)(2,1)S(1)}, u32[]{:S(2)}, u32[]{:S(2)}) collective-permute-start(bf16[8,3456]{1,0:T(8,128)(2,1)S(1)} %get-tuple-element.120), channel_id=1, source_target_pairs={{0,4},{4,0},{8,12},{12,8},{16,20},{20,16},{24,28},{28,24},{1,5},{5... | collective-permute-start | bytes 165896 | tf_op jit(solution)/shard_map/ppermute | solution.py:482
  68.8 5.2 %collective-permute-start.16 = (bf16[8,9600]{1,0:T(8,128)(2,1)S(1)}, bf16[8,9600]{1,0:T(8,128)(2,1)S(1)}, u32[]{:S(2)}, u32[]{:S(2)}) collective-permute-start(bf16[8,9600]{1,0:T(8,128)(2,1)S(1)} %constant_dynamic-update-slice_fusion.13), channel_id=1, source_target_pairs={{0,16},{4,20},{8,24},{12,28},{16,0},{20,4},{24,8},{28,12},{1,17},{... | collective-permute-start | bytes 460808 | tf_op jit(solution)/shard_map/ppermute | solution.py:482
  74.3 1.8 %copy-start.6 = (f32[8,128]{1,0:T(8,128)}, f32[8,128]{1,0:T(8,128)S(1)}, u32[]{:S(2)}) copy-start(f32[8,128]{1,0:T(8,128)S(1)} %get-tuple-element.54.sums_ref) | copy-start | bytes 12292
  74.3 1.8 %collective-permute-start.17 = (bf16[8,24960]{1,0:T(8,128)(2,1)S(1)}, bf16[8,24960]{1,0:T(8,128)(2,1)S(1)}, u32[]{:S(2)}, u32[]{:S(2)}) collective-permute-start(bf16[8,24960]{1,0:T(8,128)(2,1)S(1)} %constant_dynamic-update-slice_fusion.22), channel_id=1, source_target_pairs={{0,8},{8,0},{16,24},{24,16},{1,9},{9,1},{17,25},{25,17},{2,10},{10... | collective-permute-start | bytes 1198088 | tf_op jit(solution)/shard_map/ppermute | solution.py:658
  76.1 0.8 copy-start.5

commit v6 on v5

--- a/solution.py
+++ b/solution.py
@@ -106,17 +106,17 @@
         copy.wait()
 
         def project(start, step=step):
-            w = weights[:, step * cols : (step + 1) * cols]
-            if size == rows:
-                both = nn(ht[...], w)
-                own = [both[:rows], both[rows:]]
-            else:
-                own = [nn(ht[pl.ds(m * rows + start, size), :], w) for m in range(2)]
-            for m, kv in enumerate(own):
-                for j in range(pair):
-                    head, c = step * pair + j, j * 2 * HD
-                    k_ref[head, m, pl.ds(start, size), :] = normed(kv[:, c : c + HD], gain_ref[2:3, :])
-                    v_ref[head, m, pl.ds(start, size), :] = kv[:, c + HD : c + 2 * HD].astype(BF16)
+            for j in range(pair):
+                head, c = step * pair + j, step * cols + j * 2 * HD
+                w = weights[:, c : c + 2 * HD]
+                if size == rows:
+                    both = nn(ht[...], w)
+                    own = [both[:rows], both[rows:]]
+                else:
+                    own = [nn(ht[pl.ds(m * rows + start, size), :], w) for m in range(2)]
+                for m, kv in enumerate(own):
+                    k_ref[head, m, pl.ds(start, size), :] = normed(kv[:, :HD], gain_ref[2:3, :])
+                    v_ref[head, m, pl.ds(start, size), :] = kv[:, HD:].astype(BF16)
 
         over(rows, size, project)
 
@@ -163,35 +163,46 @@
     q_ref, k_ref, v_ref, x_ref, low_ref, hs_ref, *rest = refs[past:]
     weights, copies = w_ref, None
     if first:
-        weights, hi, sems = rest
+        weights, *small, hi, sems, small_sems = rest
+        given = (gain_ref, down_ref, up_ref)
+        fetched = [
+            pltpu.make_async_copy(g, s, small_sems.at[i]) for i, (g, s) in enumerate(zip(given, small))
+        ]
+        gain_ref, down_ref, up_ref = small
         copies = fetches(w_ref, weights, sems)
-        for copy in copies:
+        for copy in fetched + copies:
             copy.start()
     else:
         (hi,) = rest
     rows = tokens.shape[0]
     part = slice(index * rows, (index + 1) * rows)
     modulate(tokens, mod_ref, 0, w_ref.shape[0], hi, rows, 0)
+    if first:
+        for copy in fetched:
+            copy.wait()
     hs_ref[part, :] = hi[rows:, :]
     low_ref[part, :] = nt(hi[rows:, :], down_ref[...]).astype(BF16)
     cols = pair * 3 * HD
+    piece = 2 * HD if cols % (2 * HD) == 0 else HD
 
     def project(step):
-        columns = pl.ds(step * cols, cols)
-        if not isinstance(step, int):
-            columns = pl.ds(pl.multiple_of(step * cols, cols), cols)
-        qkv = nn(hi[...], weights[:, columns])
-        student = qkv[rows:] + nn(low_ref[part, :], up_ref[:, columns])
-        for j in range(pair):
-            head, c = step * pair + j, j * 3 * HD
-            for m, own in enumerate((qkv[:rows], student)):
-                q, k = own[:, c : c + HD], own[:, c + HD : c + 2 * HD]
-                q_ref[head, m, part, :] = normed(q, gain_ref[0:1, :])
-                k_ref[head, m, part, :] = normed(k, gain_ref[1:2, :])
-                v_ref[head, m, part, :] = own[:, c + 2 * HD : c + 3 * HD].astype(BF16)
-                if m == 1:
-                    x_ref[head, 0, part, :] = q
-                    x_ref[head, 1, part, :] = k
+        for at in range(0, cols, piece):
+            columns = pl.ds(step * cols + at, piece)
+            if not isinstance(step, int):
+                columns = pl.ds(pl.multiple_of(step * cols + at, HD), piece)
+            out = nn(hi[...], weights[:, columns])
+            student = out[rows:] + nn(low_ref[part, :], up_ref[:, columns])
+            for c in range(at, at + piece, HD):
+                head, kind = step * pair + c // (3 * HD), c // HD % 3
+                for m, own in enumerate((out[:rows], student)):
+                    x = own[:, c - at : c - at + HD]
+                    if kind == 2:
+                        v_ref[head, m, part, :] = x.astype(BF16)
+                    else:
+                        dest = (q_ref, k_ref)[kind]
+                        dest[head, m, part, :] = normed(x, gain_ref[kind : kind + 1, :])
+                        if m == 1:
+                            x_ref[head, kind, part, :] = x
 
     if copies is None:
         pl.loop(0, w_ref.shape[1] // cols)(project)
@@ -212,13 +223,11 @@
     ]
     scratch = [pltpu.VMEM((2 * rows, width), BF16)]
     if not before:
-        shapes.append(pltpu.VMEM(w.shape, w.dtype))
-        scratch.append(pltpu.SemaphoreType.DMA((steps,)))
+        shapes += [pltpu.VMEM(x.shape, x.dtype) for x in (w, gain, down, up)]
+        scratch += [pltpu.SemaphoreType.DMA((steps,)), pltpu.SemaphoreType.DMA((3,))]
     return pl.pallas_call(
         functools.partial(image_kernel, pair, part, len(before)),
-        in_specs=[VMEM] * 4
-        + [VMEM if before else HELD]
-        + [VMEM] * (1 + len(before)),
+        in_specs=[VMEM] + [VMEM if before else HELD] * 4 + [VMEM] * (1 + len(before)),
         out_specs=[VMEM] * len(shapes),
         out_shape=shapes,
         input_output_aliases={6 + i: i for i in range(len(before))},
@@ -372,39 +381,55 @@
     )(where, bias, gain, up, q, k, v, x, kt, vt, low, hs)
 
 
-def start_kernel(sigma_ref, image_ref, noise_ref, emb_ref, weight_ref, noisy_ref, part_ref):
+def modulation_kernel(emb_ref, weight_ref, part_ref):
+    part_ref[...] = nn(emb_ref[...], weight_ref[...])[: part_ref.shape[0]]
+
+
+def modulation(emb, weight):
+    depth, cols = weight.shape
+    steps = 2 if cols % 256 == 0 else 1
+    return pl.pallas_call(
+        modulation_kernel,
+        grid=(steps,),
+        in_specs=[
+            pl.BlockSpec(emb.shape, lambda s: (0, 0)),
+            pl.BlockSpec((depth, cols // steps), lambda s: (0, s)),
+        ],
+        out_specs=pl.BlockSpec((2, cols // steps), lambda s: (0, s)),
+        out_shape=jax.ShapeDtypeStruct((2, cols), F32),
+        compiler_params=params(10),
+        cost_estimate=pl.CostEstimate(
+            flops=4 * depth * cols, bytes_accessed=2 * weight.size, transcendentals=0
+        ),
+        name="modulation",
+    )(emb, held(weight))
+
+
+def noisy_kernel(sigma_ref, image_ref, noise_ref, after_ref, noisy_ref):
     sigma = sigma_ref[0]
     clean, noise = image_ref[...].astype(F32), noise_ref[...].astype(F32)
     noisy_ref[...] = ((1.0 - sigma) * clean + sigma * noise).astype(BF16)
-    part_ref[...] = nn(emb_ref[...], weight_ref[...])[: part_ref.shape[0]]
-
-
-def start(sigma, image, noise, emb, weight):
+
+
+def mix(sigma, image, noise, after):
     rows, width = image.shape
-    depth, cols = weight.shape
-    steps = 2 if width % 256 == 0 and cols % 256 == 0 else 1
+    steps = 2 if width % 256 == 0 else 1
     tokens = pl.BlockSpec((rows, width // steps), lambda s: (0, s))
     return pl.pallas_call(
-        start_kernel,
+        noisy_kernel,
         grid=(steps,),
         in_specs=[
             pl.BlockSpec(memory_space=pltpu.SMEM),
             tokens,
             tokens,
-            pl.BlockSpec(emb.shape, lambda s: (0, 0)),
-            pl.BlockSpec((depth, cols // steps), lambda s: (0, s)),
+            pl.BlockSpec(memory_space=pl.ANY),
         ],
-        out_specs=[tokens, pl.BlockSpec((2, cols // steps), lambda s: (0, s))],
-        out_shape=[
-            jax.ShapeDtypeStruct((rows, width), BF16),
-            jax.ShapeDtypeStruct((2, cols), F32),
-        ],
+        out_specs=tokens,
+        out_shape=jax.ShapeDtypeStruct((rows, width), BF16),
         compiler_params=params(10),
-        cost_estimate=pl.CostEstimate(
-            flops=4 * depth * cols, bytes_accessed=2 * weight.size + 6 * image.size, transcendentals=0
-        ),
-        name="start",
-    )(sigma, held(image), held(noise), emb, held(weight))
+        cost_estimate=pl.CostEstimate(flops=0, bytes_accessed=6 * image.size, transcendentals=0),
+        name="noisy",
+    )(sigma, held(image), held(noise), after)
 
 
 def finish_kernel(scale_a, scale_b, scale_loss, side_ref, a_ref, b_ref, sums_ref, got_ref, out_a, out_b, loss_ref):
@@ -442,6 +467,7 @@
     return pl.pallas_call(
         functools.partial(finish_kernel, 1.0 / (rank * width), 1.0 / (rank * cols * n), 1.0 / entries),
         in_specs=[pl.BlockSpec(memory_space=pltpu.SMEM)] + [VMEM] * 4,
+        compiler_params=pltpu.CompilerParams(vmem_limit_bytes=SMALL),
         out_shape=[
             jax.ShapeDtypeStruct((rank, width), F32),
             jax.ShapeDtypeStruct((rank, cols), F32),
@@ -528,6 +554,35 @@
         if join:
             more_sums = [t + g for t, g in zip(more_sums, got[len(sums) :])]
     return sums, dims, more_sums, more_dims
+
+
+def to_all(blocks, axis):
+    if packed(blocks[0]):
+        got = lax.all_to_all(jnp.stack([pack(b) for b in blocks]), axis, 0, 0)
+        return [unpack(got[j], blocks[0]) for j in range(len(blocks))]
+    got = [lax.all_to_all(jnp.stack(x), axis, 0, 0) for x in zip(*blocks)]
+    return [[x[j] for x in got] for j in range(len(blocks))]
+
+
+def scatter_axis(arrays, axis):
+    count, me = lax.axis_size(axis), lax.axis_index(axis)
+    dims = [cut_of(x, count) for x in arrays]
+    blocks = [[block(x, d, count, j).astype(BF16) for x, d in zip(arrays, dims)] for j in range(count)]
+    sums = [block(x, d, count, me) for x, d in zip(arrays, dims)]
+    for j, got in enumerate(to_all(blocks, axis)):
+        sums = [t + jnp.where(me == j, 0.0, g.astype(F32)) for t, g in zip(sums, got)]
+    return sums, dims
+
+
+def gather_axis(arrays, dims, sums, axis):
+    blocks = [[*arrays, pieces(sums)]] * lax.axis_size(axis)
+    *parts, others = zip(*to_all(blocks, axis))
+    others = [o.astype(F32) for o in others]
+    totals = [o[:, :HD] + o[:, HD : 2 * HD] + o[:, 2 * HD :] for o in others]
+    return (
+        [jnp.concatenate(p, d) for p, d in zip(parts, dims)],
+        functools.reduce(lambda x, y: x + y, totals),
+    )
 
 
 def ordered(parts, me):
@@ -601,7 +656,8 @@
     guide = jnp.where(jnp.arange(16)[:, None] == 0, timing(guidance[0], emb_width)[None], 0.0)
     emb = jnp.concatenate([jnp.broadcast_to(time[None], guide.shape), guide], 1)
     emb = jax.nn.silu(emb).astype(BF16)
-    noisy, part = start(sigma[None], image[0], noise[0], emb, modulation_weight)
+    part = modulation(emb, modulation_weight)
+    noisy = mix(sigma[None], image[0], noise[0], part)
     mods = [part] + [shifted(part, "seq", k) for k in range(1, n)]
     noisy_parts = [noisy] + [shifted(noisy, "seq", k) for k in range(1, n)]
     words = text[0]
@@ -622,17 +678,17 @@
     bias = jnp.where(place < text_token_length[0], 0.0, -1000000000.0).astype(F32)[None]
     core = lax.rem(lax.axis_index("grp"), 2).astype(jnp.int32)
     gain = query_key_norm_gain
-    down = adapter_down_weight.T
-    image_weight, image_heads = held(image_projection_weight), []
+    down, up = adapter_down_weight.T, adapter_up_weight
+    weights, image_heads = [held(x) for x in (image_projection_weight, gain, down, up)], []
     for k in range(n):
-        image_heads = project_image(
-            k, n, image_heads, mod, gain, down, adapter_up_weight, image_weight, noisy_parts[k]
-        )
+        weight, gain, down, up = weights
+        image_heads = project_image(k, n, image_heads, mod, gain, down, up, weight, noisy_parts[k])
         if k == 0:
-            *image_heads, image_weight = image_heads
+            image_heads, weights = image_heads[:6], image_heads[6:]
+    _, gain, _, up = weights
     text_heads = project_text(mod, gain, held(text_projection_weight), image_heads[0], text_parts)
     send_a, keep_a, send_b, keep_b, loss = attend(
-        core[None], bias, gain, adapter_up_weight, image_heads, text_heads
+        core[None], bias, gain, up, image_heads, text_heads
     )
     cores = Group(("grp", 1))
     (got_a,), (got_b,) = send([send_a], cores, 1), send([send_b], cores, 1)
@@ -643,12 +699,11 @@
         (grad_a,), dims[:], _, _ = scatter(([grad_a], group))
     near, across = Group(("seq", last), ("grp", 2)), Group(("grp", 2))
     (grad_a,), dims_a, (grad_b,), dims_b = scatter(([grad_a], near), ([grad_b], across))
-    line = Group(*[("dp", bit) for bit in reversed(bits("dp"))])
-    (grad_a, grad_b), dims_z, _, _ = scatter(([grad_a, grad_b], line))
+    (grad_a, grad_b), dims_z = scatter_axis([grad_a, grad_b], "dp")
     squares = fold(jnp.sum(grad_b.reshape(-1, min(grad_b.shape[0], 8), grad_b.shape[1]) ** 2, 0))
     squares = jnp.pad(squares, ((0, 8 - squares.shape[0]), (0, 0)))
     sums = jnp.concatenate([fold(loss), squares], 1)
-    grads, _, sums = gather(([grad_a.astype(BF16), grad_b.astype(BF16)], dims_z, line), sums)
+    grads, sums = gather_axis([grad_a.astype(BF16), grad_b.astype(BF16)], dims_z, sums, "dp")
     (grad_a,), (grad_b,), sums = gather(
         (grads[:1], dims_a, near), sums, (grads[1:], dims_b, across)
     )

time: 79.7 us -> 84.3 us (1.058)
  waiting for transfers between devices: 17.5 us -> 22.8 us
  Pallas kernels: 30.9 us -> 33.8 us
  local copies, waits for them, and re-layouts: 3.62 us -> 0.88 us
    all_to_all x0 -> x2, waiting for transfers between devices: none -> 11.9 us  [to_all(): got = lax.all_to_all(jnp.stack([pack(b) for b in blocks]), axis, 0, 0)]
    ppermute x10 -> x4, waiting for transfers between devices: 14.3 us -> 4.66 us  [send(): return unpack(lax.ppermute(pack(arrays), group.axes, pairs), arrays)]
    ppermute x10 -> x4, starting transfers between devices: 13.9 us -> 5.1 us  [send(): return unpack(lax.ppermute(pack(arrays), group.axes, pairs), arrays)]
    all_to_all x0 -> x2, starting transfers between devices: none -> 8.22 us  [to_all(): got = lax.all_to_all(jnp.stack([pack(b) for b in blocks]), axis, 0, 0)]
    pallas_call x2, Pallas kernels: 13.9 us -> 17.4 us  [project_image(): pl.pallas_call(functools.partial(image_kernel, pair, part, len(before)),...]
    unnamed x26 -> x14, local copies, waits for them, and re-layouts: 3.5 us -> 0.08 us
    ppermute x4, waiting for transfers between devices: 2.22 us -> 4.62 us  [send(): return [lax.ppermute(x, group.axes, pairs) for x in arrays]]
    ppermute x1, waiting for transfers between devices: 0.33 us -> 1.67 us  [on_device(): got = lax.ppermute(pack([grad_a, grad_b, pieces(sums)]), 'grp', pairs)]
  transfers between devices with their start and end apart: 18 -> 14, of which waited for: 12 -> 9; matrix products, arithmetic and copies ran while one was open for 2% -> 0% of each run, Pallas kernels for 18% -> 22%
where the time goes in v6:
time: 84.3 us; the launch traced here: 83.9 us
  Pallas kernels  33.8 us (40%)
  waiting for transfers between devices  22.8 us (27%)
  starting transfers between devices  21 us (25%)
  between operations  3.11 us (4%)
  other arithmetic  2.21 us (3%)
  local copies, waits for them, and re-layouts  0.88 us (1%)
    pallas_call x2, Pallas kernels, project_image(): pl.pallas_call(functools.partial(image_kernel, pair, part, len(before)),...  17.4 us
    all_to_all x2, waiting for transfers between devices, to_all(): got = lax.all_to_all(jnp.stack([pack(b) for b in blocks]), axis, 0, 0)  11.9 us
    all_to_all x2, starting transfers between devices, to_all(): got = lax.all_to_all(jnp.stack([pack(b) for b in blocks]), axis, 0, 0)  8.22 us
    pallas_call x1, Pallas kernels, attend(): pl.pallas_call(functools.partial(attend_kernel, steps, pair, samples), in...  5.77 us
    pallas_call x1, Pallas kernels, project_text(): pl.pallas_call(functools.partial(text_kernel, n, pair), in_specs=[VMEM, V...  5.61 us
    ppermute x3, starting transfers between devices, shifted(): return lax.ppermute(x, axis, [(i, (i + k) % size) for i in range(size)])  5.11 us
    ppermute x4, starting transfers between devices, send(): return unpack(lax.ppermute(pack(arrays), group.axes, pairs), arrays)  5.1 us
    ppermute x4, waiting for transfers between devices, send(): return unpack(lax.ppermute(pack(arrays), group.axes, pairs), arrays)  4.66 us
  transfers between devices with their start and end apart: 14, of which 9 were waited for; matrix products, arithmetic and copies ran while one was open for 0% of the time, Pallas kernels for 22%

profile of v6, /device:TPU:0, one launch (start us, length us, event | category | flops | bytes accessed | tf_op | source)
XLA Modules:
  0.0 83.9 jit_solution(14352772569215685211)
XLA Ops:
  2.3 2.2 %modulation.1.after_ref = f32[2,6144]{1,0:T(2,128)S(1)} custom-call(bf16[16,256]{1,0:T(8,128)(2,1)S(1)} %fusion.5.emb_ref, bf16[256,6144]{1,0:T(8,128)(2,1)} %weight_ref.1), custom_call_target="tpu_custom_call" | custom-call | flops 6291456 | bytes 3145728 | tf_op jit(solution)/shard_map/modulation/pallas_call | solution.py:391
  4.5 3.0 %collective-permute-start = (f32[2,6144]{1,0:T(2,128)S(1)}, f32[2,6144]{1,0:T(2,128)S(1)}, u32[]{:S(2)}, u32[]{:S(2)}) collective-permute-start(f32[2,6144]{1,0:T(2,128)S(1)} %modulation.1.after_ref), channel_id=1, source_target_pairs={{0,4},{4,0},{1,5},{5,1},{2,6},{6,2},{3,7},{7,3},{8,12},{12,8},{9,1... | collective-permute-start | bytes 147464 | tf_op jit(solution)/shard_map/ppermute | solution.py:482
  7.5 1.4 %noisy.1.tokens = bf16[80,3072]{1,0:T(8,128)(2,1)S(1)} custom-call(f32[1]{0:T(128)} %bitcast.7.sigma_ref, bf16[80,3072]{1,0:T(8,128)(2,1)} %bitcast.45, bf16[80,3072]{1,0:T(8,128)(2,1)} %bitcast.46, f32[2,6144]{1,0:T(2,128)S(1)} %modulation.1.after_ref), custom_call_target="tpu_custom_call" | custom-call | bytes 1474560 | tf_op jit(solution)/shard_map/noisy/pallas_call | solution.py:418
  9.0 0.1 collective-permute-start.1
  9.1 2.0 %collective-permute-start.2 = (bf16[48,3072]{1,0:T(8,128)(2,1)}, bf16[48,3072]{1,0:T(8,128)(2,1)S(1)}, u32[]{:S(2)}, u32[]{:S(2)}) collective-permute-start(bf16[48,3072]{1,0:T(8,128)(2,1)} %bitcast.43), channel_id=1, source_target_pairs={{0,4},{4,0},{1,5},{5,1},{2,6},{6,2},{3,7},{7,3},{8,12},{12,8},{9,1... | collective-permute-start | bytes 884744 | tf_op jit(solution)/shard_map/ppermute | solution.py:482
  11.9 11.3 %project_image.2 = (bf16[8,2,160,128]{3,2,1,0:T(8,128)(2,1)S(1)}, bf16[8,2,160,128]{3,2,1,0:T(8,128)(2,1)S(1)}, bf16[8,2,160,128]{3,2,1,0:T(8,128)(2,1)S(1)}, f3...) custom-call(f32[2,12288]{1,0:T(2,128)S(1)} %pad_maximum_fusion.4.mod, ...), custom_call_target="tpu_custom_call" | custom-call | flops 3019898880 | bytes 18874368 | tf_op jit(solution)/shard_map/project_image/pallas_call | solution.py:228
  23.3 6.1 %project_image.3 = (bf16[8,2,160,128]{3,2,1,0:T(8,128)(2,1)S(1)}, bf16[8,2,160,128]{3,2,1,0:T(8,128)(2,1)S(1)}, bf16[8,2,160,128]{3,2,1,0:T(8,128)(2,1)S(1)}, f3...) custom-call(f32[2,12288]{1,0:T(2,128)S(1)} %pad_maximum_fusion.4.mod, ...), custom_call_target="tpu_custom_call", output_to_operand_aliasing={{0}: (6, {}), {1}: (7, {}), {2}: (8, {}), {3}: (9, {}), {4}... | custom-call | flops 3019898880 | bytes 18874368 | tf_op jit(solution)/shard_map/project_image/pallas_call | solution.py:228
  29.4 5.6 %project_text.1 = (bf16[8,2,96,128]{3,2,1,0:T(8,128)(2,1)S(1)}, bf16[8,2,96,128]{3,2,1,0:T(8,128)(2,1)S(1)}) custom-call(f32[2,12288]{1,0:T(2,128)S(1)} %pad_maximum_fusion.4.mod_ref, f32[3,128]{1,0:T(4,128)S(1)} %get-tuple-element.29.gain_ref, bf16[3072,2048]{1,0:T(8,128)(2,1)} %w_ref.3, bf16[8,2,160,128]{3,2,1,0:T(8,128)(2,1)S(1)} %get-tuple-element.39.after_ref.q_ref, ...), custom_call_target="tpu_custom_call" | custom-call | flops 2415919104 | bytes 12582912 | tf_op jit(solution)/shard_map/project_text/pallas_call | solution.py:143
  35.0 5.8 %attend.1 = (bf16[32,3072]{1,0:T(8,128)(2,1)S(1)}, f32[32,3072]{1,0:T(8,128)S(1)}, bf16[32,3072]{1,0:T(8,128)(2,1)S(1)}, f32[32,3072]{1,0:T(8,128)S(1)}, f32[8,128]{1,0:T(8,128)S(1)}) custom-call(s32[1]{0:T(128)} %bitcast.where_ref.side_ref, f32[1,256]{1,0:T(1,128)S(1)} %compare_select_fusion.bias_ref, f32[3,128]{1,0:T(4,128)S(1)} %get-tuple-element.29.gain_ref, ...), custom_call_target="tpu_custom_call" | custom-call | flops 671088640 | bytes 8000000 | tf_op jit(solution)/shard_map/attend/pallas_call | solution.py:353
  40.9 0.5 collective-permute-start.3
  41.4 0.9 %collective-permute-done.4 = bf16[32,3072]{1,0:T(8,128)(2,1)S(1)} collective-permute-done((bf16[32,3072]{1,0:T(8,128)(2,1)S(1)}, bf16[32,3072]{1,0:T(8,128)(2,1)S(1)}, u32[]{:S(2)}, u32[]{:S(2)}) %collective-permute-start.4) | collective-permute-done | bytes 196640 | tf_op jit(solution)/shard_map/ppermute | solution.py:507
  42.4 0.2 collective-permute-done.3
  42.7 1.5 %collective-permute-start.5 = (bf16[8,9216]{1,0:T(8,128)(2,1)S(1)}, bf16[8,9216]{1,0:T(8,128)(2,1)S(1)}, u32[]{:S(2)}, u32[]{:S(2)}) collective-permute-start(bf16[8,9216]{1,0:T(8,128)(2,1)S(1)} %pad_maximum_fusion.2), channel_id=1, source_target_pairs={{0,16},{4,20},{8,24},{12,28},{16,0},{20,4},{24,8},{28,12},{1,17},{... | collective-permute-start | bytes 442376 | tf_op jit(solution)/shard_map/ppermute | solution.py:508
  44.2 0.5 collective-permute-start.6
  44.7 1.5 %collective-permute-start.7 = (bf16[8,3072]{1,0:T(8,128)(2,1)S(1)}, bf16[8,3072]{1,0:T(8,128)(2,1)S(1)}, u32[]{:S(2)}, u32[]{:S(2)}) collective-permute-start(bf16[8,3072]{1,0:T(8,128)(2,1)S(1)} %get-tuple-element.74), channel_id=1, source_target_pairs={{0,20},{4,16},{8,28},{12,24},{16,4},{20,0},{24,12},{28,8},{1,21},{... | collective-permute-start | bytes 147464 | tf_op jit(solution)/shard_map/ppermute | solution.py:507
  46.2 2.5 %collective-permute-done.6 = bf16[8,3072]{1,0:T(8,128)(2,1)S(1)} collective-permute-done((bf16[8,3072]{1,0:T(8,128)(2,1)S(1)}, bf16[8,3072]{1,0:T(8,128)(2,1)S(1)}, u32[]{:S(2)}, u32[]{:S(2)}) %collective-permute-start.6) | collective-permute-done | bytes 49184 | tf_op jit(solution)/shard_map/ppermute | solution.py:507
  48.7 1.0 %collective-permute-done.7 = bf16[8,3072]{1,0:T(8,128)(2,1)S(1)} collective-permute-done((bf16[8,3072]{1,0:T(8,128)(2,1)S(1)}, bf16[8,3072]{1,0:T(8,128)(2,1)S(1)}, u32[]{:S(2)}, u32[]{:S(2)}) %collective-permute-start.7) | collective-permute-done | bytes 49184 | tf_op jit(solution)/shard_map/ppermute | solution.py:507
  49.9 0.7 pad_maximum_fusion.3
  50.6 4.9 %all-to-all-start = ((bf16[4,8,2304]{2,1,0:T(8,128)(2,1)}), bf16[4,8,2304]{2,1,0:T(8,128)(2,1)S(1)}, u32[]{:S(2)}, u32[]{:S(2)}) async-start(bf16[4,8,2304]{2,1,0:T(8,128)(2,1)} %pad_maximum_fusion.3), calls=%async_computation | async-start | bytes 294912 | tf_op jit(solution)/shard_map/all_to_all | solution.py:561
  55.5 5.9 %all-to-all-done = bf16[4,8,2304]{2,1,0:T(8,128)(2,1)S(1)} async-done(((bf16[4,8,2304]{2,1,0:T(8,128)(2,1)}), bf16[4,8,2304]{2,1,0:T(8,128)(2,1)S(1)}, u32[]{:S(2)}, u32[]{:S(2)}) %all-to-all-start) | async-done | bytes 147488 | tf_op jit(solution)/shard_map/all_to_all | solution.py:561
  61.6 0.1 constant_dynamic-update-slice_fusion.2
  61.8 0.1 constant_dynamic-update-slice_fusion
  61.9 0.7 stack.27
  62.6 3.4 %all-to-all-start.1 = ((bf16[4,8,2688]{2,1,0:T(8,128)(2,1)}), bf16[4,8,2688]{2,1,0:T(8,128)(2,1)S(1)}, u32[]{:S(2)}, u32[]{:S(2)}) async-start(bf16[4,8,2688]{2,1,0:T(8,128)(2,1)} %stack.27), calls=%async_computation.1 | async-start | bytes 344064 | tf_op jit(solution)/shard_map/all_to_all | solution.py:561
  65.9 6.0 %all-to-all-done.1 = bf16[4,8,2688]{2,1,0:T(8,128)(2,1)S(1)} async-done(((bf16[4,8,2688]{2,1,0:T(8,128)(2,1)}), bf16[4,8,2688]{2,1,0:T(8,128)(2,1)S(1)}, u32[]{:S(2)}, u32[]{:S(2)}) %all-to-all-start.1) | async-done | bytes 172064 | tf_op jit(solution)/shard_map/all_to_all | solution.py:561
  72.2 2.5 %collective-permute-start.8 = (bf16[8,3456]{1,0:T(8,128)(2,1)S(1)}, bf16[8,3456]{1,0:T(8,128)(2,1)S(1)}, u32[]{:S(2)}, u32[]{:S(2)}) collective-permute-start(bf16[8,3456]{1,0:T(8,128)(2,1)S(1)} %get-tuple-element.135), channel_id=1, source_target_pairs={{0,20},{4,16},{8,28},{12,24},{16,4},{20,0},{24,12},{28,8},{1,21},{... | collective-permute-start | bytes 165896 | tf_op jit(solution)/shard_map/ppermute | solution.py:508
  74.7 0.5 collective-permute-start.9
  75.2 0.5 collective-permute-start.10
  75.7 3.1 %collective-permute-done.9 = bf16[8,3456]{1,0:T(8,128)(2,1)S(1)} collective-permute-done((bf16[8,3456]{1,0:T(8,128)(2,1)S(1)}, bf16[8,3456]{1,0:T(8,128)(2,1)S(1)}, u32[]{:S(2)}, u32[]{:S(2)}) %collective-permute-start.9) | collective-permute-done | bytes 55328 | tf_op jit(solution)/shard_map/ppermute | solution.py:508
  78.8 1.6 %collective-permute-done.10 = bf16[8,9600]{1,0:T(8,128)(2,1)S(1)} collective-permute-done((bf16[8,9600]{1,0:T(8,128)(2,1)S(1)}, bf16[8,9600]{1,0:T(8,128)(2,1)S(1)}, u32[]{:S(2)}, u32[]{:S(2)}) %collective-permute-start.10) | collective-permute-done | bytes 153632 | tf_op jit(solution)/shard_map/ppermute | solution.py:508
  80.8 1.7 %collective-permute-done.11.got_ref = bf16[8,24960]{1,0:T(8,128)(2,1)S(1)} collective-permute-done((bf16[8,24960]{1,0:T(8,128)(2,1)S(1)}, bf16[8,24960]{1,0:T(8,128)(2,1)S(1)}, u32[]{:S(2)}, u32[]{:S(2)}) %collective-permute-start.11) | collective-permute-done | bytes 399392 | tf_op jit(solution)/shard_map/ppermute | solution.py:713
  82.5 1.4 %finish.1 = (f32[64,3072]{1,0:T(8,128)}, f32[64,3072]{1,0:T(8,128)}, f32[1,1]{1,0:T(1,128)}) custom-call(s32[1]{0:T(128)} %bitcast.where_ref.side_ref, bf16[32,3072]{1,0:T(8,128)(2,1)S(1)} %pad_maximum_fusion.a_ref, bf16[32,3072]{1,0:T(8,128)(2,1)S(1)} %pad_maximum_fusion.1.b_ref, f32[8,128]{1,0:T(8,128)S(1)} %get-tuple-element.56.sums_ref, ...), custom_call_target="tpu_custom_call" | custom-call | tf_op jit(solution)/shard_map/finish/pallas_call | solution.py:467
  (78 shorter events, 1.7 us)
Async XLA Ops:
  4.5 7.3 %collective-permute-start = (f32[2,6144]{1,0:T(2,128)S(1)}, f32[2,6144]{1,0:T(2,128)S(1)}, u32[]{:S(2)}, u32[]{:S(2)}) collective-permute-start(f32[2,6144]{1,0:T(2,128)S(1)} %modulation.1.after_ref), channel_id=1, source_target_pairs={{0,4},{4,0},{1,5},{5,1},{2,6},{6,2},{3,7},{7,3},{8,12},{12,8},{9,1... | collective-permute-start | bytes 147464 | tf_op jit(solution)/shard_map/ppermute | solution.py:482
  9.0 14.3 %collective-permute-start.1 = (bf16[80,3072]{1,0:T(8,128)(2,1)S(1)}, bf16[80,3072]{1,0:T(8,128)(2,1)S(1)}, u32[]{:S(2)}, u32[]{:S(2)}) collective-permute-start(bf16[80,3072]{1,0:T(8,128)(2,1)S(1)} %noisy.1.tokens), channel_id=1, source_target_pairs={{0,4},{4,0},{1,5},{5,1},{2,6},{6,2},{3,7},{7,3},{8,12},{12,8},{9,1... | collective-permute-start | bytes 1474568 | tf_op jit(solution)/shard_map/ppermute | solution.py:482
  9.1 20.3 %collective-permute-start.2 = (bf16[48,3072]{1,0:T(8,128)(2,1)}, bf16[48,3072]{1,0:T(8,128)(2,1)S(1)}, u32[]{:S(2)}, u32[]{:S(2)}) collective-permute-start(bf16[48,3072]{1,0:T(8,128)(2,1)} %bitcast.43), channel_id=1, source_target_pairs={{0,4},{4,0},{1,5},{5,1},{2,6},{6,2},{3,7},{7,3},{8,12},{12,8},{9,1... | collective-permute-start | bytes 884744 | tf_op jit(solution)/shard_map/ppermute | solution.py:482
  23.2 6.2 %copy-start = (bf16[1,48,3072]{2,1,0:T(8,128)(2,1)S(1)}, bf16[1,48,3072]{2,1,0:T(8,128)(2,1)}, u32[]{:S(2)}) copy-start(bf16[1,48,3072]{2,1,0:T(8,128)(2,1)} %param.14) | copy-start | bytes 884740
  40.8 1.5 %collective-permute-start.4 = (bf16[32,3072]{1,0:T(8,128)(2,1)S(1)}, bf16[32,3072]{1,0:T(8,128)(2,1)S(1)}, u32[]{:S(2)}, u32[]{:S(2)}) collective-permute-start(bf16[32,3072]{1,0:T(8,128)(2,1)S(1)} %get-tuple-element.50), channel_id=1, source_target_pairs={{0,8},{8,0},{16,24},{24,16},{1,9},{9,1},{17,25},{25,17},{2,10},{10... | collective-permute-start | bytes 589832 | tf_op jit(solution)/shard_map/ppermute | solution.py:507
  40.9 1.7 %collective-permute-start.3 = (bf16[32,3072]{1,0:T(8,128)(2,1)S(1)}, bf16[32,3072]{1,0:T(8,128)(2,1)S(1)}, u32[]{:S(2)}, u32[]{:S(2)}) collective-permute-start(bf16[32,3072]{1,0:T(8,128)(2,1)S(1)} %get-tuple-element.48), channel_id=1, source_target_pairs={{0,8},{8,0},{16,24},{24,16},{1,9},{9,1},{17,25},{25,17},{2,10},{10... | collective-permute-start | bytes 589832 | tf_op jit(solution)/shard_map/ppermute | solution.py:507
  42.7 7.1 %collective-permute-start.5 = (bf16[8,9216]{1,0:T(8,128)(2,1)S(1)}, bf16[8,9216]{1,0:T(8,128)(2,1)S(1)}, u32[]{:S(2)}, u32[]{:S(2)}) collective-permute-start(bf16[8,9216]{1,0:T(8,128)(2,1)S(1)} %pad_maximum_fusion.2), channel_id=1, source_target_pairs={{0,16},{4,20},{8,24},{12,28},{16,0},{20,4},{24,8},{28,12},{1,17},{... | collective-permute-start | bytes 442376 | tf_op jit(solution)/shard_map/ppermute | solution.py:508
  44.2 4.5 %collective-permute-start.6 = (bf16[8,3072]{1,0:T(8,128)(2,1)S(1)}, bf16[8,3072]{1,0:T(8,128)(2,1)S(1)}, u32[]{:S(2)}, u32[]{:S(2)}) collective-permute-start(bf16[8,3072]{1,0:T(8,128)(2,1)S(1)} %get-tuple-element.75), channel_id=1, source_target_pairs={{0,4},{4,0},{8,12},{12,8},{16,20},{20,16},{24,28},{28,24},{1,5},{5... | collective-permute-start | bytes 147464 | tf_op jit(solution)/shard_map/ppermute | solution.py:507
  44.7 5.0 %collective-permute-start.7 = (bf16[8,3072]{1,0:T(8,128)(2,1)S(1)}, bf16[8,3072]{1,0:T(8,128)(2,1)S(1)}, u32[]{:S(2)}, u32[]{:S(2)}) collective-permute-start(bf16[8,3072]{1,0:T(8,128)(2,1)S(1)} %get-tuple-element.74), channel_id=1, source_target_pairs={{0,20},{4,16},{8,28},{12,24},{16,4},{20,0},{24,12},{28,8},{1,21},{... | collective-permute-start | bytes 147464 | tf_op jit(solution)/shard_map/ppermute | solution.py:507
  50.6 10.8 %all-to-all-start = ((bf16[4,8,2304]{2,1,0:T(8,128)(2,1)}), bf16[4,8,2304]{2,1,0:T(8,128)(2,1)S(1)}, u32[]{:S(2)}, u32[]{:S(2)}) async-start(bf16[4,8,2304]{2,1,0:T(8,128)(2,1)} %pad_maximum_fusion.3), calls=%async_computation | async-start | bytes 294912 | tf_op jit(solution)/shard_map/all_to_all | solution.py:561
  62.6 9.4 %all-to-all-start.1 = ((bf16[4,8,2688]{2,1,0:T(8,128)(2,1)}), bf16[4,8,2688]{2,1,0:T(8,128)(2,1)S(1)}, u32[]{:S(2)}, u32[]{:S(2)}) async-start(bf16[4,8,2688]{2,1,0:T(8,128)(2,1)} %stack.27), calls=%async_computation.1 | async-start | bytes 344064 | tf_op jit(solution)/shard_map/all_to_all | solution.py:561
  72.2 6.7 %collective-permute-start.8 = (bf16[8,3456]{1,0:T(8,128)(2,1)S(1)}, bf16[8,3456]{1,0:T(8,128)(2,1)S(1)}, u32[]{:S(2)}, u32[]{:S(2)}) collective-permute-start(bf16[8,3456]{1,0:T(8,128)(2,1)S(1)} %get-tuple-element.135), channel_id=1, source_target_pairs={{0,20},{4,16},{8,28},{12,24},{16,4},{20,0},{24,12},{28,8},{1,21},{... | collective-permute-start | bytes 165896 | tf_op jit(solution)/shard_map/ppermute | solution.py:508
  74.7 4.2 %collective-permute-start.9 = (bf16[8,3456]{1,0:T(8,128)(2,1)S(1)}, bf16[8,3456]{1,0:T(8,128)(2,1)S(1)}, u32[]{:S(2)}, u32[]{:S(2)}) collective-permute-start(bf16[8,3456]{1,0:T(8,128)(2,1)S(1)} %get-tuple-element.135), channel_id=1, source_target_pairs={{0,4},{4,0},{8,12},{12,8},{16,20},{20,16},{24,28},{28,24},{1,5},{5... | collective-permute-start | bytes 165896 | tf_op jit(solution)/shard_map/ppermute | solution.py:508
  75.2 5.2 %collective-permute-start.10 = (bf16[8,9600]{1,0:T(8,128)(2,1)S(1)}, bf16[8,9600]{1,0:T(8,128)(2,1)S(1)}, u32[]{:S(2)}, u32[]{:S(2)}) collective-permute-start(bf16[8,9600]{1,0:T(8,128)(2,1)S(1)} %constant_dynamic-update-slice_fusion.13), channel_id=1, source_target_pairs={{0,16},{4,20},{8,24},{12,28},{16,0},{20,4},{24,8},{28,12},{1,17},{... | collective-permute-start | bytes 460808 | tf_op jit(solution)/shard_map/ppermute | solution.py:508
  80.7 1.8 %collective-permute-start.11 = (bf16[8,24960]{1,0:T(8,128)(2,1)S(1)}, bf16[8,24960]{1,0:T(8,128)(2,1)S(1)}, u32[]{:S(2)}, u32[]{:S(2)}) collective-permute-start(bf16[8,24960]{1,0:T(8,128)(2,1)S(1)} %constant_dynamic-update-slice_fusion.22), channel_id=1, source_target_pairs={{0,8},{8,0},{16,24},{24,16},{1,9},{9,1},{17,25},{25,17},{2,10},{10... | collective-permute-start | bytes 1198088 | tf_op jit(solution)/shard_map/ppermute | solution.py:713

commit v7 on v6

--- a/solution.py
+++ b/solution.py
@@ -161,7 +161,7 @@
 def image_kernel(pair, index, past, mod_ref, gain_ref, down_ref, up_ref, w_ref, tokens, *refs):
     first = past == 0
     q_ref, k_ref, v_ref, x_ref, low_ref, hs_ref, *rest = refs[past:]
-    weights, copies = w_ref, None
+    weights = w_ref
     if first:
         weights, *small, hi, sems, small_sems = rest
         given = (gain_ref, down_ref, up_ref)
@@ -169,8 +169,7 @@
             pltpu.make_async_copy(g, s, small_sems.at[i]) for i, (g, s) in enumerate(zip(given, small))
         ]
         gain_ref, down_ref, up_ref = small
-        copies = fetches(w_ref, weights, sems)
-        for copy in fetched + copies:
+        for copy in fetched + fetches(w_ref, weights, sems):
             copy.start()
     else:
         (hi,) = rest
@@ -183,33 +182,24 @@
     hs_ref[part, :] = hi[rows:, :]
     low_ref[part, :] = nt(hi[rows:, :], down_ref[...]).astype(BF16)
     cols = pair * 3 * HD
-    piece = 2 * HD if cols % (2 * HD) == 0 else HD
 
     def project(step):
-        for at in range(0, cols, piece):
-            columns = pl.ds(step * cols + at, piece)
-            if not isinstance(step, int):
-                columns = pl.ds(pl.multiple_of(step * cols + at, HD), piece)
-            out = nn(hi[...], weights[:, columns])
-            student = out[rows:] + nn(low_ref[part, :], up_ref[:, columns])
-            for c in range(at, at + piece, HD):
-                head, kind = step * pair + c // (3 * HD), c // HD % 3
-                for m, own in enumerate((out[:rows], student)):
-                    x = own[:, c - at : c - at + HD]
-                    if kind == 2:
-                        v_ref[head, m, part, :] = x.astype(BF16)
-                    else:
-                        dest = (q_ref, k_ref)[kind]
-                        dest[head, m, part, :] = normed(x, gain_ref[kind : kind + 1, :])
-                        if m == 1:
-                            x_ref[head, kind, part, :] = x
-
-    if copies is None:
-        pl.loop(0, w_ref.shape[1] // cols)(project)
-    else:
-        for step, copy in enumerate(copies):
-            copy.wait()
-            project(step)
+        columns = pl.ds(pl.multiple_of(step * cols, cols), cols)
+        if first:
+            pltpu.make_async_copy(w_ref.at[:, columns], weights.at[:, columns], sems.at[step]).wait()
+        out = nn(hi[...], weights[:, columns])
+        student = out[rows:] + nn(low_ref[part, :], up_ref[:, columns])
+        for j in range(pair):
+            head, c = step * pair + j, j * 3 * HD
+            for m, own in enumerate((out[:rows], student)):
+                for kind, dest in enumerate((q_ref, k_ref)):
+                    x = own[:, c + kind * HD : c + (kind + 1) * HD]
+                    dest[head, m, part, :] = normed(x, gain_ref[kind : kind + 1, :])
+                    if m == 1:
+                        x_ref[head, kind, part, :] = x
+                v_ref[head, m, part, :] = own[:, c + 2 * HD : c + 3 * HD].astype(BF16)
+
+    pl.loop(0, w_ref.shape[1] // cols)(project)
 
 
 def project_image(part, n, before, mod, gain, down, up, w, tokens):
@@ -427,7 +417,7 @@
         out_specs=tokens,
         out_shape=jax.ShapeDtypeStruct((rows, width), BF16),
         compiler_params=params(10),
-        cost_estimate=pl.CostEstimate(flops=0, bytes_accessed=6 * image.size, transcendentals=0),
+        cost_estimate=pl.CostEstimate(flops=0, bytes_accessed=0, transcendentals=0),
         name="noisy",
     )(sigma, held(image), held(noise), after)
 
@@ -554,35 +544,6 @@
         if join:
             more_sums = [t + g for t, g in zip(more_sums, got[len(sums) :])]
     return sums, dims, more_sums, more_dims
-
-
-def to_all(blocks, axis):
-    if packed(blocks[0]):
-        got = lax.all_to_all(jnp.stack([pack(b) for b in blocks]), axis, 0, 0)
-        return [unpack(got[j], blocks[0]) for j in range(len(blocks))]
-    got = [lax.all_to_all(jnp.stack(x), axis, 0, 0) for x in zip(*blocks)]
-    return [[x[j] for x in got] for j in range(len(blocks))]
-
-
-def scatter_axis(arrays, axis):
-    count, me = lax.axis_size(axis), lax.axis_index(axis)
-    dims = [cut_of(x, count) for x in arrays]
-    blocks = [[block(x, d, count, j).astype(BF16) for x, d in zip(arrays, dims)] for j in range(count)]
-    sums = [block(x, d, count, me) for x, d in zip(arrays, dims)]
-    for j, got in enumerate(to_all(blocks, axis)):
-        sums = [t + jnp.where(me == j, 0.0, g.astype(F32)) for t, g in zip(sums, got)]
-    return sums, dims
-
-
-def gather_axis(arrays, dims, sums, axis):
-    blocks = [[*arrays, pieces(sums)]] * lax.axis_size(axis)
-    *parts, others = zip(*to_all(blocks, axis))
-    others = [o.astype(F32) for o in others]
-    totals = [o[:, :HD] + o[:, HD : 2 * HD] + o[:, 2 * HD :] for o in others]
-    return (
-        [jnp.concatenate(p, d) for p, d in zip(parts, dims)],
-        functools.reduce(lambda x, y: x + y, totals),
-    )
 
 
 def ordered(parts, me):
@@ -699,11 +660,12 @@
         (grad_a,), dims[:], _, _ = scatter(([grad_a], group))
     near, across = Group(("seq", last), ("grp", 2)), Group(("grp", 2))
     (grad_a,), dims_a, (grad_b,), dims_b = scatter(([grad_a], near), ([grad_b], across))
-    (grad_a, grad_b), dims_z = scatter_axis([grad_a, grad_b], "dp")
+    line = Group(*[("dp", bit) for bit in reversed(bits("dp"))])
+    (grad_a, grad_b), dims_z, _, _ = scatter(([grad_a, grad_b], line))
     squares = fold(jnp.sum(grad_b.reshape(-1, min(grad_b.shape[0], 8), grad_b.shape[1]) ** 2, 0))
     squares = jnp.pad(squares, ((0, 8 - squares.shape[0]), (0, 0)))
     sums = jnp.concatenate([fold(loss), squares], 1)
-    grads, sums = gather_axis([grad_a.astype(BF16), grad_b.astype(BF16)], dims_z, sums, "dp")
+    grads, _, sums = gather(([grad_a.astype(BF16), grad_b.astype(BF16)], dims_z, line), sums)
     (grad_a,), (grad_b,), sums = gather(
         (grads[:1], dims_a, near), sums, (grads[1:], dims_b, across)
     )

time: 84.3 us -> 77.6 us (0.921)
  waiting for transfers between devices: 22.8 us -> 18.7 us
  Pallas kernels: 33.8 us -> 32.5 us
    all_to_all x2 -> x0, waiting for transfers between devices: 11.9 us -> none  [to_all(): got = lax.all_to_all(jnp.stack([pack(b) for b in blocks]), axis, 0, 0)]
    ppermute x4 -> x10, waiting for transfers between devices: 4.66 us -> 14.3 us  [send(): return unpack(lax.ppermute(pack(arrays), group.axes, pairs), arrays)]
    ppermute x4 -> x10, starting transfers between devices: 5.1 us -> 13.9 us  [send(): return unpack(lax.ppermute(pack(arrays), group.axes, pairs), arrays)]
    all_to_all x2 -> x0, starting transfers between devices: 8.22 us -> none  [to_all(): got = lax.all_to_all(jnp.stack([pack(b) for b in blocks]), axis, 0, 0)]
    ppermute x4, waiting for transfers between devices: 4.62 us -> 1.54 us  [send(): return [lax.ppermute(x, group.axes, pairs) for x in arrays]]
    pallas_call x2, Pallas kernels: 17.4 us -> 16.1 us  [project_image(): pl.pallas_call(functools.partial(image_kernel, pair, part, len(before)),...]
    ppermute x3, waiting for transfers between devices: 0.01 us -> 1.21 us  [shifted(): return lax.ppermute(x, axis, [(i, (i + k) % size) for i in range(size)])]
  transfers between devices with their start and end apart: 14 -> 18, of which waited for: 9 -> 12; matrix products, arithmetic and copies ran while one was open for 0% -> 1% of each run, Pallas kernels for 22% -> 23%
where the time goes in v7:
time: 77.6 us; the launch traced here: 77.4 us
  Pallas kernels  32.5 us (42%)
  starting transfers between devices  21.6 us (28%)
  waiting for transfers between devices  18.7 us (24%)
  between operations  3.09 us (4%)
  other arithmetic  1.47 us (2%)
    pallas_call x2, Pallas kernels, project_image(): pl.pallas_call(functools.partial(image_kernel, pair, part, len(before)),...  16.1 us
    ppermute x10, waiting for transfers between devices, send(): return unpack(lax.ppermute(pack(arrays), group.axes, pairs), arrays)  14.3 us
    ppermute x10, starting transfers between devices, send(): return unpack(lax.ppermute(pack(arrays), group.axes, pairs), arrays)  13.9 us
    pallas_call x1, Pallas kernels, attend(): pl.pallas_call(functools.partial(attend_kernel, steps, pair, samples), in...  5.76 us
    pallas_call x1, Pallas kernels, project_text(): pl.pallas_call(functools.partial(text_kernel, n, pair), in_specs=[VMEM, V...  5.61 us
    ppermute x3, starting transfers between devices, shifted(): return lax.ppermute(x, axis, [(i, (i + k) % size) for i in range(size)])  5.11 us
    ppermute x4, starting transfers between devices, send(): return [lax.ppermute(x, group.axes, pairs) for x in arrays]  2.53 us
    pallas_call x1, Pallas kernels, modulation(): pl.pallas_call(modulation_kernel, grid=(steps,), in_specs=[pl.BlockSpec(e...  2.2 us
  transfers between devices with their start and end apart: 18, of which 12 were waited for; matrix products, arithmetic and copies ran while one was open for 1% of the time, Pallas kernels for 23%

profile of v7, /device:TPU:0, one launch (start us, length us, event | category | flops | bytes accessed | tf_op | source)
XLA Modules:
  0.0 77.4 jit_solution(16627838696554162731)
XLA Ops:
  2.3 2.2 %modulation.1.after_ref = f32[2,6144]{1,0:T(2,128)S(1)} custom-call(bf16[16,256]{1,0:T(8,128)(2,1)S(1)} %fusion.5.emb_ref, bf16[256,6144]{1,0:T(8,128)(2,1)} %weight_ref.1), custom_call_target="tpu_custom_call" | custom-call | flops 6291456 | bytes 3145728 | tf_op jit(solution)/shard_map/modulation/pallas_call | solution.py:381
  4.5 3.0 %collective-permute-start = (f32[2,6144]{1,0:T(2,128)S(1)}, f32[2,6144]{1,0:T(2,128)S(1)}, u32[]{:S(2)}, u32[]{:S(2)}) collective-permute-start(f32[2,6144]{1,0:T(2,128)S(1)} %modulation.1.after_ref), channel_id=1, source_target_pairs={{0,4},{4,0},{1,5},{5,1},{2,6},{6,2},{3,7},{7,3},{8,12},{12,8},{9,1... | collective-permute-start | bytes 147464 | tf_op jit(solution)/shard_map/ppermute | solution.py:472
  7.5 1.4 %noisy.1.tokens = bf16[80,3072]{1,0:T(8,128)(2,1)S(1)} custom-call(f32[1]{0:T(128)} %bitcast.7.sigma_ref, bf16[80,3072]{1,0:T(8,128)(2,1)} %bitcast.21, bf16[80,3072]{1,0:T(8,128)(2,1)} %bitcast.22, f32[2,6144]{1,0:T(2,128)S(1)} %modulation.1.after_ref), custom_call_target="tpu_custom_call" | custom-call | tf_op jit(solution)/shard_map/noisy/pallas_call | solution.py:408
  9.1 2.0 %collective-permute-start.2 = (bf16[48,3072]{1,0:T(8,128)(2,1)}, bf16[48,3072]{1,0:T(8,128)(2,1)S(1)}, u32[]{:S(2)}, u32[]{:S(2)}) collective-permute-start(bf16[48,3072]{1,0:T(8,128)(2,1)} %bitcast.19), channel_id=1, source_target_pairs={{0,4},{4,0},{1,5},{5,1},{2,6},{6,2},{3,7},{7,3},{8,12},{12,8},{9,1... | collective-permute-start | bytes 884744 | tf_op jit(solution)/shard_map/ppermute | solution.py:472
  11.9 10.0 %project_image.2 = (bf16[8,2,160,128]{3,2,1,0:T(8,128)(2,1)S(1)}, bf16[8,2,160,128]{3,2,1,0:T(8,128)(2,1)S(1)}, bf16[8,2,160,128]{3,2,1,0:T(8,128)(2,1)S(1)}, f3...) custom-call(f32[2,12288]{1,0:T(2,128)S(1)} %pad_maximum_fusion.3.mod, ...), custom_call_target="tpu_custom_call" | custom-call | flops 3019898880 | bytes 18874368 | tf_op jit(solution)/shard_map/project_image/pallas_call | solution.py:218
  22.0 1.2 %collective-permute-done.1.tokens = bf16[80,3072]{1,0:T(8,128)(2,1)S(1)} collective-permute-done((bf16[80,3072]{1,0:T(8,128)(2,1)S(1)}, bf16[80,3072]{1,0:T(8,128)(2,1)S(1)}, u32[]{:S(2)}, u32[]{:S(2)}) %collective-permute-start.1) | collective-permute-done | bytes 491552 | tf_op jit(solution)/shard_map/ppermute | solution.py:472
  23.2 6.0 %project_image.3 = (bf16[8,2,160,128]{3,2,1,0:T(8,128)(2,1)S(1)}, bf16[8,2,160,128]{3,2,1,0:T(8,128)(2,1)S(1)}, bf16[8,2,160,128]{3,2,1,0:T(8,128)(2,1)S(1)}, f3...) custom-call(f32[2,12288]{1,0:T(2,128)S(1)} %pad_maximum_fusion.3.mod, ...), custom_call_target="tpu_custom_call", output_to_operand_aliasing={{0}: (6, {}), {1}: (7, {}), {2}: (8, {}), {3}: (9, {}), {4}... | custom-call | flops 3019898880 | bytes 18874368 | tf_op jit(solution)/shard_map/project_image/pallas_call | solution.py:218
  29.2 5.6 %project_text.1 = (bf16[8,2,96,128]{3,2,1,0:T(8,128)(2,1)S(1)}, bf16[8,2,96,128]{3,2,1,0:T(8,128)(2,1)S(1)}) custom-call(f32[2,12288]{1,0:T(2,128)S(1)} %pad_maximum_fusion.3.mod_ref, f32[3,128]{1,0:T(4,128)S(1)} %get-tuple-element.29.gain_ref, bf16[3072,2048]{1,0:T(8,128)(2,1)} %w_ref.3, bf16[8,2,160,128]{3,2,1,0:T(8,128)(2,1)S(1)} %get-tuple-element.39.after_ref.q_ref, ...), custom_call_target="tpu_custom_call" | custom-call | flops 2415919104 | bytes 12582912 | tf_op jit(solution)/shard_map/project_text/pallas_call | solution.py:143
  34.9 5.8 %attend.1 = (bf16[32,3072]{1,0:T(8,128)(2,1)S(1)}, f32[32,3072]{1,0:T(8,128)S(1)}, bf16[32,3072]{1,0:T(8,128)(2,1)S(1)}, f32[32,3072]{1,0:T(8,128)S(1)}, f32[8,128]{1,0:T(8,128)S(1)}) custom-call(s32[1]{0:T(128)} %bitcast.where_ref.side_ref, f32[1,256]{1,0:T(1,128)S(1)} %compare_select_fusion.bias_ref, f32[3,128]{1,0:T(4,128)S(1)} %get-tuple-element.29.gain_ref, ...), custom_call_target="tpu_custom_call" | custom-call | flops 671088640 | bytes 8000000 | tf_op jit(solution)/shard_map/attend/pallas_call | solution.py:343
  40.8 0.5 collective-permute-start.3
  41.2 0.9 %collective-permute-done.4 = bf16[32,3072]{1,0:T(8,128)(2,1)S(1)} collective-permute-done((bf16[32,3072]{1,0:T(8,128)(2,1)S(1)}, bf16[32,3072]{1,0:T(8,128)(2,1)S(1)}, u32[]{:S(2)}, u32[]{:S(2)}) %collective-permute-start.4) | collective-permute-done | bytes 196640 | tf_op jit(solution)/shard_map/ppermute | solution.py:497
  42.5 1.5 %collective-permute-start.5 = (bf16[8,9216]{1,0:T(8,128)(2,1)S(1)}, bf16[8,9216]{1,0:T(8,128)(2,1)S(1)}, u32[]{:S(2)}, u32[]{:S(2)}) collective-permute-start(bf16[8,9216]{1,0:T(8,128)(2,1)S(1)} %pad_maximum_fusion.2), channel_id=1, source_target_pairs={{0,16},{4,20},{8,24},{12,28},{16,0},{20,4},{24,8},{28,12},{1,17},{... | collective-permute-start | bytes 442376 | tf_op jit(solution)/shard_map/ppermute | solution.py:498
  44.1 0.5 collective-permute-start.6
  44.6 1.5 %collective-permute-start.7 = (bf16[8,3072]{1,0:T(8,128)(2,1)S(1)}, bf16[8,3072]{1,0:T(8,128)(2,1)S(1)}, u32[]{:S(2)}, u32[]{:S(2)}) collective-permute-start(bf16[8,3072]{1,0:T(8,128)(2,1)S(1)} %get-tuple-element.80), channel_id=1, source_target_pairs={{0,20},{4,16},{8,28},{12,24},{16,4},{20,0},{24,12},{28,8},{1,21},{... | collective-permute-start | bytes 147464 | tf_op jit(solution)/shard_map/ppermute | solution.py:497
  46.1 3.0 %collective-permute-done.5 = bf16[8,9216]{1,0:T(8,128)(2,1)S(1)} collective-permute-done((bf16[8,9216]{1,0:T(8,128)(2,1)S(1)}, bf16[8,9216]{1,0:T(8,128)(2,1)S(1)}, u32[]{:S(2)}, u32[]{:S(2)}) %collective-permute-start.5) | collective-permute-done | bytes 147488 | tf_op jit(solution)/shard_map/ppermute | solution.py:498
  49.2 0.4 collective-permute-done.7
  49.7 2.7 %collective-permute-start.9 = (bf16[8,2304]{1,0:T(8,128)(2,1)S(1)}, bf16[8,2304]{1,0:T(8,128)(2,1)S(1)}, u32[]{:S(2)}, u32[]{:S(2)}) collective-permute-start(bf16[8,2304]{1,0:T(8,128)(2,1)S(1)} %pad_maximum_fusion.8), channel_id=1, source_target_pairs={{0,2},{1,3},{2,0},{3,1},{4,6},{5,7},{6,4},{7,5},{8,10},{9,11},{10,... | collective-permute-start | bytes 110600 | tf_op jit(solution)/shard_map/ppermute | solution.py:498
  52.3 1.3 %collective-permute-start.10 = (bf16[8,2304]{1,0:T(8,128)(2,1)S(1)}, bf16[8,2304]{1,0:T(8,128)(2,1)S(1)}, u32[]{:S(2)}, u32[]{:S(2)}) collective-permute-start(bf16[8,2304]{1,0:T(8,128)(2,1)S(1)} %pad_maximum_fusion.9), channel_id=1, source_target_pairs={{0,3},{1,2},{2,1},{3,0},{4,7},{5,6},{6,5},{7,4},{8,11},{9,10},{10,... | collective-permute-start | bytes 110600 | tf_op jit(solution)/shard_map/ppermute | solution.py:498
  53.7 0.3 collective-permute-start.8
  54.1 0.5 collective-permute-done.9
  54.6 3.5 %collective-permute-done.10 = bf16[8,2304]{1,0:T(8,128)(2,1)S(1)} collective-permute-done((bf16[8,2304]{1,0:T(8,128)(2,1)S(1)}, bf16[8,2304]{1,0:T(8,128)(2,1)S(1)}, u32[]{:S(2)}, u32[]{:S(2)}) %collective-permute-start.10) | collective-permute-done | bytes 36896 | tf_op jit(solution)/shard_map/ppermute | solution.py:498
  58.4 2.1 %collective-permute-start.11 = (bf16[8,2688]{1,0:T(8,128)(2,1)S(1)}, bf16[8,2688]{1,0:T(8,128)(2,1)S(1)}, u32[]{:S(2)}, u32[]{:S(2)}) collective-permute-start(bf16[8,2688]{1,0:T(8,128)(2,1)S(1)} %constant_dynamic-update-slice_fusion), channel_id=1, source_target_pairs={{0,3},{1,2},{2,1},{3,0},{4,7},{5,6},{6,5},{7,4},{8,11},{9,10},{10,... | collective-permute-start | bytes 129032 | tf_op jit(solution)/shard_map/ppermute | solution.py:498
  60.5 2.4 %collective-permute-start.13 = (bf16[8,2688]{1,0:T(8,128)(2,1)S(1)}, bf16[8,2688]{1,0:T(8,128)(2,1)S(1)}, u32[]{:S(2)}, u32[]{:S(2)}) collective-permute-start(bf16[8,2688]{1,0:T(8,128)(2,1)S(1)} %constant_dynamic-update-slice_fusion), channel_id=1, source_target_pairs={{0,1},{1,0},{2,3},{3,2},{4,5},{5,4},{6,7},{7,6},{8,9},{9,8},{10,11... | collective-permute-start | bytes 129032 | tf_op jit(solution)/shard_map/ppermute | solution.py:498
  62.8 1.4 %collective-permute-done.11 = bf16[8,2688]{1,0:T(8,128)(2,1)S(1)} collective-permute-done((bf16[8,2688]{1,0:T(8,128)(2,1)S(1)}, bf16[8,2688]{1,0:T(8,128)(2,1)S(1)}, u32[]{:S(2)}, u32[]{:S(2)}) %collective-permute-start.11) | collective-permute-done | bytes 43040 | tf_op jit(solution)/shard_map/ppermute | solution.py:498
  64.3 1.1 %collective-permute-done.12 = bf16[8,2688]{1,0:T(8,128)(2,1)S(1)} collective-permute-done((bf16[8,2688]{1,0:T(8,128)(2,1)S(1)}, bf16[8,2688]{1,0:T(8,128)(2,1)S(1)}, u32[]{:S(2)}, u32[]{:S(2)}) %collective-permute-start.12) | collective-permute-done | bytes 43040 | tf_op jit(solution)/shard_map/ppermute | solution.py:498
  65.7 2.5 %collective-permute-start.14 = (bf16[8,3456]{1,0:T(8,128)(2,1)S(1)}, bf16[8,3456]{1,0:T(8,128)(2,1)S(1)}, u32[]{:S(2)}, u32[]{:S(2)}) collective-permute-start(bf16[8,3456]{1,0:T(8,128)(2,1)S(1)} %get-tuple-element.122), channel_id=1, source_target_pairs={{0,20},{4,16},{8,28},{12,24},{16,4},{20,0},{24,12},{28,8},{1,21},{... | collective-permute-start | bytes 165896 | tf_op jit(solution)/shard_map/ppermute | solution.py:498
  68.2 0.5 collective-permute-start.15
  68.8 0.5 collective-permute-start.16
  69.3 3.1 %collective-permute-done.15 = bf16[8,3456]{1,0:T(8,128)(2,1)S(1)} collective-permute-done((bf16[8,3456]{1,0:T(8,128)(2,1)S(1)}, bf16[8,3456]{1,0:T(8,128)(2,1)S(1)}, u32[]{:S(2)}, u32[]{:S(2)}) %collective-permute-start.15) | collective-permute-done | bytes 55328 | tf_op jit(solution)/shard_map/ppermute | solution.py:498
  72.4 1.6 %collective-permute-done.16 = bf16[8,9600]{1,0:T(8,128)(2,1)S(1)} collective-permute-done((bf16[8,9600]{1,0:T(8,128)(2,1)S(1)}, bf16[8,9600]{1,0:T(8,128)(2,1)S(1)}, u32[]{:S(2)}, u32[]{:S(2)}) %collective-permute-start.16) | collective-permute-done | bytes 153632 | tf_op jit(solution)/shard_map/ppermute | solution.py:498
  74.4 1.7 %collective-permute-done.17.got_ref = bf16[8,24960]{1,0:T(8,128)(2,1)S(1)} collective-permute-done((bf16[8,24960]{1,0:T(8,128)(2,1)S(1)}, bf16[8,24960]{1,0:T(8,128)(2,1)S(1)}, u32[]{:S(2)}, u32[]{:S(2)}) %collective-permute-start.17) | collective-permute-done | bytes 399392 | tf_op jit(solution)/shard_map/ppermute | solution.py:675
  76.1 1.4 %finish.1 = (f32[64,3072]{1,0:T(8,128)}, f32[64,3072]{1,0:T(8,128)}, f32[1,1]{1,0:T(1,128)}) custom-call(s32[1]{0:T(128)} %bitcast.where_ref.side_ref, bf16[32,3072]{1,0:T(8,128)(2,1)S(1)} %pad_maximum_fusion.a_ref, bf16[32,3072]{1,0:T(8,128)(2,1)S(1)} %pad_maximum_fusion.1.b_ref, f32[8,128]{1,0:T(8,128)S(1)} %get-tuple-element.56.sums_ref, ...), custom_call_target="tpu_custom_call" | custom-call | tf_op jit(solution)/shard_map/finish/pallas_call | solution.py:457
  (90 shorter events, 2.1 us)
Async XLA Ops:
  4.5 7.3 %collective-permute-start = (f32[2,6144]{1,0:T(2,128)S(1)}, f32[2,6144]{1,0:T(2,128)S(1)}, u32[]{:S(2)}, u32[]{:S(2)}) collective-permute-start(f32[2,6144]{1,0:T(2,128)S(1)} %modulation.1.after_ref), channel_id=1, source_target_pairs={{0,4},{4,0},{1,5},{5,1},{2,6},{6,2},{3,7},{7,3},{8,12},{12,8},{9,1... | collective-permute-start | bytes 147464 | tf_op jit(solution)/shard_map/ppermute | solution.py:472
  9.0 14.2 %collective-permute-start.1 = (bf16[80,3072]{1,0:T(8,128)(2,1)S(1)}, bf16[80,3072]{1,0:T(8,128)(2,1)S(1)}, u32[]{:S(2)}, u32[]{:S(2)}) collective-permute-start(bf16[80,3072]{1,0:T(8,128)(2,1)S(1)} %noisy.1.tokens), channel_id=1, source_target_pairs={{0,4},{4,0},{1,5},{5,1},{2,6},{6,2},{3,7},{7,3},{8,12},{12,8},{9,1... | collective-permute-start | bytes 1474568 | tf_op jit(solution)/shard_map/ppermute | solution.py:472
  9.1 20.2 %collective-permute-start.2 = (bf16[48,3072]{1,0:T(8,128)(2,1)}, bf16[48,3072]{1,0:T(8,128)(2,1)S(1)}, u32[]{:S(2)}, u32[]{:S(2)}) collective-permute-start(bf16[48,3072]{1,0:T(8,128)(2,1)} %bitcast.19), channel_id=1, source_target_pairs={{0,4},{4,0},{1,5},{5,1},{2,6},{6,2},{3,7},{7,3},{8,12},{12,8},{9,1... | collective-permute-start | bytes 884744 | tf_op jit(solution)/shard_map/ppermute | solution.py:472
  21.9 7.3 %copy-start = (bf16[1,48,3072]{2,1,0:T(8,128)(2,1)S(1)}, bf16[1,48,3072]{2,1,0:T(8,128)(2,1)}, u32[]{:S(2)}) copy-start(bf16[1,48,3072]{2,1,0:T(8,128)(2,1)} %param.14) | copy-start | bytes 884740
  40.6 1.5 %collective-permute-start.4 = (bf16[32,3072]{1,0:T(8,128)(2,1)S(1)}, bf16[32,3072]{1,0:T(8,128)(2,1)S(1)}, u32[]{:S(2)}, u32[]{:S(2)}) collective-permute-start(bf16[32,3072]{1,0:T(8,128)(2,1)S(1)} %get-tuple-element.50), channel_id=1, source_target_pairs={{0,8},{8,0},{16,24},{24,16},{1,9},{9,1},{17,25},{25,17},{2,10},{10... | collective-permute-start | bytes 589832 | tf_op jit(solution)/shard_map/ppermute | solution.py:497
  40.8 1.7 %collective-permute-start.3 = (bf16[32,3072]{1,0:T(8,128)(2,1)S(1)}, bf16[32,3072]{1,0:T(8,128)(2,1)S(1)}, u32[]{:S(2)}, u32[]{:S(2)}) collective-permute-start(bf16[32,3072]{1,0:T(8,128)(2,1)S(1)} %get-tuple-element.48), channel_id=1, source_target_pairs={{0,8},{8,0},{16,24},{24,16},{1,9},{9,1},{17,25},{25,17},{2,10},{10... | collective-permute-start | bytes 589832 | tf_op jit(solution)/shard_map/ppermute | solution.py:497
  42.5 6.6 %collective-permute-start.5 = (bf16[8,9216]{1,0:T(8,128)(2,1)S(1)}, bf16[8,9216]{1,0:T(8,128)(2,1)S(1)}, u32[]{:S(2)}, u32[]{:S(2)}) collective-permute-start(bf16[8,9216]{1,0:T(8,128)(2,1)S(1)} %pad_maximum_fusion.2), channel_id=1, source_target_pairs={{0,16},{4,20},{8,24},{12,28},{16,0},{20,4},{24,8},{28,12},{1,17},{... | collective-permute-start | bytes 442376 | tf_op jit(solution)/shard_map/ppermute | solution.py:498
  44.1 5.1 %collective-permute-start.6 = (bf16[8,3072]{1,0:T(8,128)(2,1)S(1)}, bf16[8,3072]{1,0:T(8,128)(2,1)S(1)}, u32[]{:S(2)}, u32[]{:S(2)}) collective-permute-start(bf16[8,3072]{1,0:T(8,128)(2,1)S(1)} %get-tuple-element.79), channel_id=1, source_target_pairs={{0,4},{4,0},{8,12},{12,8},{16,20},{20,16},{24,28},{28,24},{1,5},{5... | collective-permute-start | bytes 147464 | tf_op jit(solution)/shard_map/ppermute | solution.py:497
  44.6 5.0 %collective-permute-start.7 = (bf16[8,3072]{1,0:T(8,128)(2,1)S(1)}, bf16[8,3072]{1,0:T(8,128)(2,1)S(1)}, u32[]{:S(2)}, u32[]{:S(2)}) collective-permute-start(bf16[8,3072]{1,0:T(8,128)(2,1)S(1)} %get-tuple-element.80), channel_id=1, source_target_pairs={{0,20},{4,16},{8,28},{12,24},{16,4},{20,0},{24,12},{28,8},{1,21},{... | collective-permute-start | bytes 147464 | tf_op jit(solution)/shard_map/ppermute | solution.py:497
  49.7 4.9 %collective-permute-start.9 = (bf16[8,2304]{1,0:T(8,128)(2,1)S(1)}, bf16[8,2304]{1,0:T(8,128)(2,1)S(1)}, u32[]{:S(2)}, u32[]{:S(2)}) collective-permute-start(bf16[8,2304]{1,0:T(8,128)(2,1)S(1)} %pad_maximum_fusion.8), channel_id=1, source_target_pairs={{0,2},{1,3},{2,0},{3,1},{4,6},{5,7},{6,4},{7,5},{8,10},{9,11},{10,... | collective-permute-start | bytes 110600 | tf_op jit(solution)/shard_map/ppermute | solution.py:498
  52.3 5.8 %collective-permute-start.10 = (bf16[8,2304]{1,0:T(8,128)(2,1)S(1)}, bf16[8,2304]{1,0:T(8,128)(2,1)S(1)}, u32[]{:S(2)}, u32[]{:S(2)}) collective-permute-start(bf16[8,2304]{1,0:T(8,128)(2,1)S(1)} %pad_maximum_fusion.9), channel_id=1, source_target_pairs={{0,3},{1,2},{2,1},{3,0},{4,7},{5,6},{6,5},{7,4},{8,11},{9,10},{10,... | collective-permute-start | bytes 110600 | tf_op jit(solution)/shard_map/ppermute | solution.py:498
  53.7 4.4 %collective-permute-start.8 = (bf16[8,2304]{1,0:T(8,128)(2,1)S(1)}, bf16[8,2304]{1,0:T(8,128)(2,1)S(1)}, u32[]{:S(2)}, u32[]{:S(2)}) collective-permute-start(bf16[8,2304]{1,0:T(8,128)(2,1)S(1)} %pad_maximum_fusion.7), channel_id=1, source_target_pairs={{0,1},{1,0},{2,3},{3,2},{4,5},{5,4},{6,7},{7,6},{8,9},{9,8},{10,11... | collective-permute-start | bytes 110600 | tf_op jit(solution)/shard_map/ppermute | solution.py:498
  58.4 5.9 %collective-permute-start.11 = (bf16[8,2688]{1,0:T(8,128)(2,1)S(1)}, bf16[8,2688]{1,0:T(8,128)(2,1)S(1)}, u32[]{:S(2)}, u32[]{:S(2)}) collective-permute-start(bf16[8,2688]{1,0:T(8,128)(2,1)S(1)} %constant_dynamic-update-slice_fusion), channel_id=1, source_target_pairs={{0,3},{1,2},{2,1},{3,0},{4,7},{5,6},{6,5},{7,4},{8,11},{9,10},{10,... | collective-permute-start | bytes 129032 | tf_op jit(solution)/shard_map/ppermute | solution.py:498
  60.5 4.9 %collective-permute-start.12 = (bf16[8,2688]{1,0:T(8,128)(2,1)S(1)}, bf16[8,2688]{1,0:T(8,128)(2,1)S(1)}, u32[]{:S(2)}, u32[]{:S(2)}) collective-permute-start(bf16[8,2688]{1,0:T(8,128)(2,1)S(1)} %constant_dynamic-update-slice_fusion), channel_id=1, source_target_pairs={{0,2},{1,3},{2,0},{3,1},{4,6},{5,7},{6,4},{7,5},{8,10},{9,11},{10,... | collective-permute-start | bytes 129032 | tf_op jit(solution)/shard_map/ppermute | solution.py:498
  60.5 4.9 %collective-permute-start.13 = (bf16[8,2688]{1,0:T(8,128)(2,1)S(1)}, bf16[8,2688]{1,0:T(8,128)(2,1)S(1)}, u32[]{:S(2)}, u32[]{:S(2)}) collective-permute-start(bf16[8,2688]{1,0:T(8,128)(2,1)S(1)} %constant_dynamic-update-slice_fusion), channel_id=1, source_target_pairs={{0,1},{1,0},{2,3},{3,2},{4,5},{5,4},{6,7},{7,6},{8,9},{9,8},{10,11... | collective-permute-start | bytes 129032 | tf_op jit(solution)/shard_map/ppermute | solution.py:498
  65.7 6.7 %collective-permute-start.14 = (bf16[8,3456]{1,0:T(8,128)(2,1)S(1)}, bf16[8,3456]{1,0:T(8,128)(2,1)S(1)}, u32[]{:S(2)}, u32[]{:S(2)}) collective-permute-start(bf16[8,3456]{1,0:T(8,128)(2,1)S(1)} %get-tuple-element.122), channel_id=1, source_target_pairs={{0,20},{4,16},{8,28},{12,24},{16,4},{20,0},{24,12},{28,8},{1,21},{... | collective-permute-start | bytes 165896 | tf_op jit(solution)/shard_map/ppermute | solution.py:498
  68.2 4.2 %collective-permute-start.15 = (bf16[8,3456]{1,0:T(8,128)(2,1)S(1)}, bf16[8,3456]{1,0:T(8,128)(2,1)S(1)}, u32[]{:S(2)}, u32[]{:S(2)}) collective-permute-start(bf16[8,3456]{1,0:T(8,128)(2,1)S(1)} %get-tuple-element.122), channel_id=1, source_target_pairs={{0,4},{4,0},{8,12},{12,8},{16,20},{20,16},{24,28},{28,24},{1,5},{5... | collective-permute-start | bytes 165896 | tf_op jit(solution)/shard_map/ppermute | solution.py:498
  68.8 5.2 %collective-permute-start.16 = (bf16[8,9600]{1,0:T(8,128)(2,1)S(1)}, bf16[8,9600]{1,0:T(8,128)(2,1)S(1)}, u32[]{:S(2)}, u32[]{:S(2)}) collective-permute-start(bf16[8,9600]{1,0:T(8,128)(2,1)S(1)} %constant_dynamic-update-slice_fusion.13), channel_id=1, source_target_pairs={{0,16},{4,20},{8,24},{12,28},{16,0},{20,4},{24,8},{28,12},{1,17},{... | collective-permute-start | bytes 460808 | tf_op jit(solution)/shard_map/ppermute | solution.py:498
  74.3 1.8 %collective-permute-start.17 = (bf16[8,24960]{1,0:T(8,128)(2,1)S(1)}, bf16[8,24960]{1,0:T(8,128)(2,1)S(1)}, u32[]{:S(2)}, u32[]{:S(2)}) collective-permute-start(bf16[8,24960]{1,0:T(8,128)(2,1)S(1)} %constant_dynamic-update-slice_fusion.22), channel_id=1, source_target_pairs={{0,8},{8,0},{16,24},{24,16},{1,9},{9,1},{17,25},{25,17},{2,10},{10... | collective-permute-start | bytes 1198088 | tf_op jit(solution)/shard_map/ppermute | solution.py:675

commit v8 on v7

--- a/solution.py
+++ b/solution.py
@@ -17,13 +17,8 @@
 ROOT = 1.0 / math.sqrt(HD)
 LOG2E = 1.0 / math.log(2.0)
 SMALL = 10 * 1024 * 1024
-
-
-def timing(value, width):
-    count = width // 4
-    freqs = jnp.exp(-math.log(10000.0) * jnp.arange(count, dtype=F32) / count)
-    angles = 1000.0 * value * freqs
-    return jnp.concatenate([jnp.cos(angles), jnp.sin(angles)])
+VMEM = pl.BlockSpec(memory_space=pltpu.VMEM)
+HELD = pl.BlockSpec(memory_space=pltpu.HBM)
 
 
 def nn(a, b):
@@ -78,37 +73,24 @@
     return (x * inverse_rms(x) * gain).astype(BF16)
 
 
-def fetches(w_ref, out_ref, sems):
-    cols = w_ref.shape[1] // sems.shape[0]
-    return [
-        pltpu.make_async_copy(
-            w_ref.at[:, i * cols : (i + 1) * cols], out_ref.at[:, i * cols : (i + 1) * cols], sems.at[i]
-        )
-        for i in range(sems.shape[0])
-    ]
-
-
 def held(x):
     return pltpu.with_memory_space_constraint(x, pltpu.HBM)
 
 
-def text_kernel(n, pair, mod_ref, gain_ref, w_ref, after_ref, *refs):
-    parts, (k_ref, v_ref, ht, weights, sems) = refs[:n], refs[n:]
-    copies = fetches(w_ref, weights, sems)
-    for copy in copies:
-        copy.start()
+def text_kernel(n, pair, mod_ref, gain_ref, w_ref, *refs):
+    parts, (k_ref, v_ref, ht) = refs[:n], refs[n:]
     rows = n * parts[0].shape[0]
     for k in range(n):
         modulate(parts[k], mod_ref, 2, w_ref.shape[0], ht, rows, k * parts[0].shape[0])
     cols = pair * 2 * HD
     size = min(rows, 96)
-    for step, copy in enumerate(copies):
-        copy.wait()
-
-        def project(start, step=step):
+
+    @pl.loop(0, w_ref.shape[1] // cols)
+    def _(step):
+        def project(start):
             for j in range(pair):
-                head, c = step * pair + j, step * cols + j * 2 * HD
-                w = weights[:, c : c + 2 * HD]
+                head = step * pair + j
+                w = w_ref[:, pl.ds(pl.multiple_of(head * 2 * HD, 2 * HD), 2 * HD)]
                 if size == rows:
                     both = nn(ht[...], w)
                     own = [both[:rows], both[rows:]]
@@ -132,53 +114,77 @@
     )
 
 
-VMEM = pl.BlockSpec(memory_space=pltpu.VMEM)
-HELD = pl.BlockSpec(memory_space=pltpu.HBM)
-
-
-def project_text(mod, gain, w, after, parts):
+def project_text(mod, gain, w, parts):
     n, (part, width) = len(parts), parts[0].shape
     pair, steps = split(w.shape[1] // (2 * HD))
     out = pltpu.VMEM((pair * steps, 2, n * part, HD), BF16)
     return pl.pallas_call(
         functools.partial(text_kernel, n, pair),
-        in_specs=[VMEM, VMEM, HELD, pl.BlockSpec(memory_space=pl.ANY)] + [VMEM] * n,
+        in_specs=[VMEM] * (3 + n),
         out_specs=[VMEM] * 2,
         out_shape=[out, out],
-        scratch_shapes=[
-            pltpu.VMEM((2 * n * part, width), BF16),
-            pltpu.VMEM(w.shape, w.dtype),
-            pltpu.SemaphoreType.DMA((steps,)),
-        ],
-        compiler_params=pltpu.CompilerParams(vmem_limit_bytes=2 * SMALL),
+        scratch_shapes=[pltpu.VMEM((2 * n * part, width), BF16)],
+        compiler_params=pltpu.CompilerParams(vmem_limit_bytes=SMALL),
         cost_estimate=pl.CostEstimate(
             flops=4 * n * part * w.size, bytes_accessed=2 * w.size, transcendentals=0
         ),
         name="project_text",
-    )(mod, gain, w, after, *parts)
-
-
-def image_kernel(pair, index, past, mod_ref, gain_ref, down_ref, up_ref, w_ref, tokens, *refs):
-    first = past == 0
-    q_ref, k_ref, v_ref, x_ref, low_ref, hs_ref, *rest = refs[past:]
+    )(mod, gain, w, *parts)
+
+
+def chunk(w_ref, out_ref, sems, index):
+    cols = w_ref.shape[1] // sems.shape[0]
+    at = pl.ds(index * cols if isinstance(index, int) else pl.multiple_of(index * cols, cols), cols)
+    return pltpu.make_async_copy(w_ref.at[:, at], out_ref.at[:, at], sems.at[index])
+
+
+def fetch_kernel(after_ref, *refs):
+    *given, last_sems, sems = refs
+    count = len(given) // 2
+    copies = [
+        pltpu.make_async_copy(given[i], given[count + i], sems.at[i]) for i in range(count - 1)
+    ]
+    copies.append(chunk(given[count - 1], given[-1], last_sems, 0))
+    for copy in copies:
+        copy.start()
+    for copy in copies:
+        copy.wait()
+
+
+def fetch(small, w, steps, after):
+    arrays = [*small, w]
+    return pl.pallas_call(
+        fetch_kernel,
+        in_specs=[pl.BlockSpec(memory_space=pl.ANY)] + [HELD] * len(arrays),
+        out_specs=[VMEM] * len(arrays),
+        out_shape=[pltpu.VMEM(x.shape, x.dtype) for x in arrays],
+        scratch_shapes=[pltpu.SemaphoreType.DMA((steps,)), pltpu.SemaphoreType.DMA((len(small),))],
+        compiler_params=pltpu.CompilerParams(vmem_limit_bytes=SMALL),
+        cost_estimate=pl.CostEstimate(
+            flops=0, bytes_accessed=2 * w.size // steps, transcendentals=0
+        ),
+        name="fetch",
+    )(after, *[held(x) for x in arrays])
+
+
+def image_kernel(pair, index, n, mod_ref, gain_ref, down_ref, up_ref, w_ref, tokens, *refs):
+    first, last = index == 0, index == n - 1
+    refs = list(refs)
+    more = refs.pop(0) if first or last else None
+    refs = refs[1 if first else 6 :]
+    q_ref, k_ref, v_ref, x_ref, low_ref, hs_ref, *rest = refs
     weights = w_ref
-    if first:
-        weights, *small, hi, sems, small_sems = rest
-        given = (gain_ref, down_ref, up_ref)
-        fetched = [
-            pltpu.make_async_copy(g, s, small_sems.at[i]) for i, (g, s) in enumerate(zip(given, small))
-        ]
-        gain_ref, down_ref, up_ref = small
-        for copy in fetched + fetches(w_ref, weights, sems):
+    if first or last:
+        into, hi, sems = rest
+        copies = [chunk(more, into, sems, i) for i in range(1 if first else 0, sems.shape[0])]
+        for copy in copies:
             copy.start()
+        weights = into if first else w_ref
     else:
         (hi,) = rest
     rows = tokens.shape[0]
     part = slice(index * rows, (index + 1) * rows)
     modulate(tokens, mod_ref, 0, w_ref.shape[0], hi, rows, 0)
-    if first:
-        for copy in fetched:
-            copy.wait()
     hs_ref[part, :] = hi[rows:, :]
     low_ref[part, :] = nt(hi[rows:, :], down_ref[...]).astype(BF16)
     cols = pair * 3 * HD
@@ -186,7 +192,11 @@
     def project(step):
         columns = pl.ds(pl.multiple_of(step * cols, cols), cols)
         if first:
-            pltpu.make_async_copy(w_ref.at[:, columns], weights.at[:, columns], sems.at[step]).wait()
+
+            @pl.when(step > 0)
+            def _():
+                chunk(more, into, sems, step).wait()
+
         out = nn(hi[...], weights[:, columns])
         student = out[rows:] + nn(low_ref[part, :], up_ref[:, columns])
         for j in range(pair):
@@ -200,9 +210,12 @@
                 v_ref[head, m, part, :] = own[:, c + 2 * HD : c + 3 * HD].astype(BF16)
 
     pl.loop(0, w_ref.shape[1] // cols)(project)
-
-
-def project_image(part, n, before, mod, gain, down, up, w, tokens):
+    if last and not first:
+        for copy in copies:
+            copy.wait()
+
+
+def project_image(part, n, before, mod, gain, down, up, w, tokens, more):
     (rows, width), rank = tokens.shape, up.shape[0]
     pair, steps = split(w.shape[1] // (3 * HD))
     heads = (pair * steps, 2, n * rows, HD)
@@ -212,22 +225,32 @@
         pltpu.VMEM((n * rows, width), BF16),
     ]
     scratch = [pltpu.VMEM((2 * rows, width), BF16)]
-    if not before:
-        shapes += [pltpu.VMEM(x.shape, x.dtype) for x in (w, gain, down, up)]
-        scratch += [pltpu.SemaphoreType.DMA((steps,)), pltpu.SemaphoreType.DMA((3,))]
+    operands, specs, aliases = [mod, gain, down, up, w, tokens], [VMEM] * 6, {}
+    if part == 0 or part == n - 1:
+        operands.append(more)
+        specs.append(HELD)
+        shapes.append(pltpu.VMEM(more.shape, more.dtype))
+        scratch.append(pltpu.SemaphoreType.DMA((steps,)))
+    if part == 0:
+        operands[4] = more
+        specs[4] = HELD
+        aliases = {len(operands): 6}
+        before = [w]
+    else:
+        aliases = {len(operands) + i: i for i in range(len(before))}
     return pl.pallas_call(
-        functools.partial(image_kernel, pair, part, len(before)),
-        in_specs=[VMEM] + [VMEM if before else HELD] * 4 + [VMEM] * (1 + len(before)),
+        functools.partial(image_kernel, pair, part, n),
+        in_specs=specs + [VMEM] * len(before),
         out_specs=[VMEM] * len(shapes),
         out_shape=shapes,
-        input_output_aliases={6 + i: i for i in range(len(before))},
+        input_output_aliases=aliases,
         scratch_shapes=scratch,
         compiler_params=pltpu.CompilerParams(vmem_limit_bytes=SMALL),
         cost_estimate=pl.CostEstimate(
             flops=4 * rows * w.size, bytes_accessed=2 * w.size, transcendentals=0
         ),
         name="project_image",
-    )(mod, gain, down, up, w, tokens, *before)
+    )(*operands, *before)
 
 
 def attend_kernel(
@@ -371,55 +394,73 @@
     )(where, bias, gain, up, q, k, v, x, kt, vt, low, hs)
 
 
-def modulation_kernel(emb_ref, weight_ref, part_ref):
-    part_ref[...] = nn(emb_ref[...], weight_ref[...])[: part_ref.shape[0]]
-
-
-def modulation(emb, weight):
+def noise_level(step_ref, shape):
+    return (jnp.full(shape, step_ref[0], jnp.int32).astype(F32) + 1.0) / STEPS
+
+
+def embedding(value):
+    count = value.shape[1] // 2
+    lane = lax.broadcasted_iota(jnp.int32, value.shape, 1)
+    place = lax.rem(lane, count).astype(F32)
+    angles = 1000.0 * value * jnp.exp(-math.log(10000.0) * place / count)
+    wave = jnp.where(lane < count, jnp.cos(angles), jnp.sin(angles))
+    return wave / (1.0 + jnp.exp(-wave))
+
+
+def modulation_kernel(step_ref, guidance_ref, weight_ref, part_ref, emb):
+    @pl.when(pl.program_id(0) == 0)
+    def _():
+        half = emb.shape[1] // 2
+        time = embedding(noise_level(step_ref, (1, half)))
+        guide = embedding(jnp.full((1, half), guidance_ref[0], F32))
+        row = lax.broadcasted_iota(jnp.int32, (emb.shape[0], half), 0)
+        emb[:, :half] = jnp.where(row >= 0, time, 0.0).astype(BF16)
+        emb[:, half:] = jnp.where(row == 0, guide, 0.0).astype(BF16)
+
+    part_ref[...] = nn(emb[...], weight_ref[...])[: part_ref.shape[0]]
+
+
+SCALAR = pl.BlockSpec(memory_space=pltpu.SMEM)
+
+
+def modulation(timestep, guidance, weight):
     depth, cols = weight.shape
     steps = 2 if cols % 256 == 0 else 1
     return pl.pallas_call(
         modulation_kernel,
         grid=(steps,),
-        in_specs=[
-            pl.BlockSpec(emb.shape, lambda s: (0, 0)),
-            pl.BlockSpec((depth, cols // steps), lambda s: (0, s)),
-        ],
+        in_specs=[SCALAR, SCALAR, pl.BlockSpec((depth, cols // steps), lambda s: (0, s))],
         out_specs=pl.BlockSpec((2, cols // steps), lambda s: (0, s)),
         out_shape=jax.ShapeDtypeStruct((2, cols), F32),
+        scratch_shapes=[pltpu.VMEM((16, depth), BF16)],
         compiler_params=params(10),
         cost_estimate=pl.CostEstimate(
             flops=4 * depth * cols, bytes_accessed=2 * weight.size, transcendentals=0
         ),
         name="modulation",
-    )(emb, held(weight))
-
-
-def noisy_kernel(sigma_ref, image_ref, noise_ref, after_ref, noisy_ref):
-    sigma = sigma_ref[0]
+    )(timestep, guidance, held(weight))
+
+
+def noisy_kernel(step_ref, image_ref, noise_ref, after_ref, noisy_ref):
+    sigma = noise_level(step_ref, (1, image_ref.shape[1]))
     clean, noise = image_ref[...].astype(F32), noise_ref[...].astype(F32)
     noisy_ref[...] = ((1.0 - sigma) * clean + sigma * noise).astype(BF16)
 
 
-def mix(sigma, image, noise, after):
+def mix(timestep, image, noise, after):
     rows, width = image.shape
     steps = 2 if width % 256 == 0 else 1
     tokens = pl.BlockSpec((rows, width // steps), lambda s: (0, s))
     return pl.pallas_call(
         noisy_kernel,
         grid=(steps,),
-        in_specs=[
-            pl.BlockSpec(memory_space=pltpu.SMEM),
-            tokens,
-            tokens,
-            pl.BlockSpec(memory_space=pl.ANY),
-        ],
+        in_specs=[SCALAR, tokens, tokens, pl.BlockSpec(memory_space=pl.ANY)],
         out_specs=tokens,
         out_shape=jax.ShapeDtypeStruct((rows, width), BF16),
         compiler_params=params(10),
-        cost_estimate=pl.CostEstimate(flops=0, bytes_accessed=0, transcendentals=0),
+        cost_estimate=pl.CostEstimate(flops=0, bytes_accessed=6 * image.size, transcendentals=0),
         name="noisy",
-    )(sigma, held(image), held(noise), after)
+    )(timestep, held(image), held(noise), after)
 
 
 def finish_kernel(scale_a, scale_b, scale_loss, side_ref, a_ref, b_ref, sums_ref, got_ref, out_a, out_b, loss_ref):
@@ -609,16 +650,10 @@
     adapter_down_weight,
     adapter_up_weight,
 ):
-    emb_width = modulation_weight.shape[0]
     n, me = lax.axis_size("seq"), lax.axis_index("seq")
     samples = lax.axis_size("grp") * lax.axis_size("dp")
-    sigma = (timestep[0].astype(F32) + 1.0) / STEPS
-    time = timing(sigma, emb_width)
-    guide = jnp.where(jnp.arange(16)[:, None] == 0, timing(guidance[0], emb_width)[None], 0.0)
-    emb = jnp.concatenate([jnp.broadcast_to(time[None], guide.shape), guide], 1)
-    emb = jax.nn.silu(emb).astype(BF16)
-    part = modulation(emb, modulation_weight)
-    noisy = mix(sigma[None], image[0], noise[0], part)
+    part = modulation(timestep, guidance, modulation_weight)
+    noisy = mix(timestep, image[0], noise[0], part)
     mods = [part] + [shifted(part, "seq", k) for k in range(1, n)]
     noisy_parts = [noisy] + [shifted(noisy, "seq", k) for k in range(1, n)]
     words = text[0]
@@ -639,15 +674,21 @@
     bias = jnp.where(place < text_token_length[0], 0.0, -1000000000.0).astype(F32)[None]
     core = lax.rem(lax.axis_index("grp"), 2).astype(jnp.int32)
     gain = query_key_norm_gain
-    down, up = adapter_down_weight.T, adapter_up_weight
-    weights, image_heads = [held(x) for x in (image_projection_weight, gain, down, up)], []
+    steps = split(image_projection_weight.shape[1] // (3 * HD))[1]
+    gain, down, up, weights = fetch(
+        [gain, adapter_down_weight.T, adapter_up_weight], image_projection_weight, steps, noisy
+    )
+    far_weights, image_heads = held(image_projection_weight), []
     for k in range(n):
-        weight, gain, down, up = weights
-        image_heads = project_image(k, n, image_heads, mod, gain, down, up, weight, noisy_parts[k])
+        if k == n - 1:
+            far_weights = held(text_projection_weight)
+        image_heads = project_image(
+            k, n, image_heads, mod, gain, down, up, weights, noisy_parts[k], far_weights
+        )
         if k == 0:
-            image_heads, weights = image_heads[:6], image_heads[6:]
-    _, gain, _, up = weights
-    text_heads = project_text(mod, gain, held(text_projection_weight), image_heads[0], text_parts)
+            *image_heads, weights = image_heads
+    *image_heads, text_weights = image_heads
+    text_heads = project_text(mod, gain, text_weights, text_parts)
     send_a, keep_a, send_b, keep_b, loss = attend(
         core[None], bias, gain, up, image_heads, text_heads
     )

time: 77.6 us -> 79.2 us (1.021)
    select_n x1, other arithmetic: 0.04 us -> 0.84 us  [on_device(): jnp.where(origin[k] == j, mods[k], so_far)]
    pallas_call x5 -> x6, Pallas kernels: 25.3 us -> 25.9 us  [the longest x2 13.4 us: project_image(): pl.pallas_call(functools.partial(image_kernel, pair, part, n), in_specs=s...]
  transfers between devices with their start and end apart: 18 -> 18, of which waited for: 12 -> 12; matrix products, arithmetic and copies ran while one was open for 1% -> 2% of each run, Pallas kernels for 23% -> 22%
where the time goes in v8:
time: 79.2 us; the launch traced here: 78.9 us
  Pallas kernels  33.1 us (42%)
  starting transfers between devices  21.6 us (27%)
  waiting for transfers between devices  19.1 us (24%)
  between operations  3.06 us (4%)
  other arithmetic  1.92 us (2%)
    ppermute x10, waiting for transfers between devices, send(): return unpack(lax.ppermute(pack(arrays), group.axes, pairs), arrays)  14.3 us
    ppermute x10, starting transfers between devices, send(): return unpack(lax.ppermute(pack(arrays), group.axes, pairs), arrays)  13.9 us
    pallas_call x2, Pallas kernels, project_image(): pl.pallas_call(functools.partial(image_kernel, pair, part, n), in_specs=s...  13.4 us
    pallas_call x1, Pallas kernels, project_text(): pl.pallas_call(functools.partial(text_kernel, n, pair), in_specs=[VMEM] *...  6.22 us
    pallas_call x1, Pallas kernels, attend(): pl.pallas_call(functools.partial(attend_kernel, steps, pair, samples), in...  5.76 us
    ppermute x3, starting transfers between devices, shifted(): return lax.ppermute(x, axis, [(i, (i + k) % size) for i in range(size)])  5.11 us
    pallas_call x1, Pallas kernels, fetch(): pl.pallas_call(fetch_kernel, in_specs=[pl.BlockSpec(memory_space=pl.ANY)]...  2.66 us
    ppermute x4, starting transfers between devices, send(): return [lax.ppermute(x, group.axes, pairs) for x in arrays]  2.52 us
  transfers between devices with their start and end apart: 18, of which 12 were waited for; matrix products, arithmetic and copies ran while one was open for 2% of the time, Pallas kernels for 22%

profile of v8, /device:TPU:0, one launch (start us, length us, event | category | flops | bytes accessed | tf_op | source)
XLA Modules:
  0.0 78.9 jit_solution(8921683790519818330)
XLA Ops:
  1.9 2.2 %modulation.1.after_ref = f32[2,6144]{1,0:T(2,128)S(1)} custom-call(s32[1]{0:T(128)S(6)} %copy.58.step_ref, f32[1]{0:T(128)S(6)} %copy.59.guidance_ref, bf16[256,6144]{1,0:T(8,128)(2,1)} %weight_ref.1), custom_call_target="tpu_custom_call" | custom-call | flops 6291456 | bytes 3145728 | tf_op jit(solution)/shard_map/modulation/pallas_call | solution.py:429
  4.1 3.0 %collective-permute-start = (f32[2,6144]{1,0:T(2,128)S(1)}, f32[2,6144]{1,0:T(2,128)}, u32[]{:S(2)}, u32[]{:S(2)}) collective-permute-start(f32[2,6144]{1,0:T(2,128)S(1)} %modulation.1.after_ref), channel_id=1, source_target_pairs={{0,4},{4,0},{1,5},{5,1},{2,6},{6,2},{3,7},{7,3},{8,12},{12,8},{9,1... | collective-permute-start | bytes 147464 | tf_op jit(solution)/shard_map/ppermute | solution.py:513
  7.1 1.4 %noisy.1.after_ref.tokens = bf16[80,3072]{1,0:T(8,128)(2,1)S(1)} custom-call(s32[1]{0:T(128)S(6)} %copy.58.step_ref, bf16[80,3072]{1,0:T(8,128)(2,1)} %bitcast.18, bf16[80,3072]{1,0:T(8,128)(2,1)} %bitcast.19, f32[2,6144]{1,0:T(2,128)S(1)} %modulation.1.after_ref), custom_call_target="tpu_custom_call" | custom-call | bytes 1474560 | tf_op jit(solution)/shard_map/noisy/pallas_call | solution.py:454
  8.7 2.0 %collective-permute-start.2 = (bf16[48,3072]{1,0:T(8,128)(2,1)}, bf16[48,3072]{1,0:T(8,128)(2,1)}, u32[]{:S(2)}, u32[]{:S(2)}) collective-permute-start(bf16[48,3072]{1,0:T(8,128)(2,1)} %bitcast.16), channel_id=1, source_target_pairs={{0,4},{4,0},{1,5},{5,1},{2,6},{6,2},{3,7},{7,3},{8,12},{12,8},{9,1... | collective-permute-start | bytes 884744 | tf_op jit(solution)/shard_map/ppermute | solution.py:513
  11.4 2.7 %fetch.1 = (f32[3,128]{1,0:T(4,128)S(1)}, bf16[64,3072]{1,0:T(8,128)(2,1)S(1)}, bf16[64,3072]{1,0:T(8,128)(2,1)S(1)}, bf16[3072,3072]{1,0:T(8,128)(2,1)S(1)}) custom-call(bf16[80,3072]{1,0:T(8,128)(2,1)S(1)} %noisy.1.after_ref.tokens, f32[3,128]{1,0:T(4,128)} %refs_0_.3, bf16[64,3072]{1,0:T(8,128)(2,1)} %bitcast.20, bf16[64,3072]{1,0:T(8,128)(2,1)} %refs_2_.1, ...), custom_call_target="tpu_custom_call" | custom-call | bytes 4718592 | tf_op jit(solution)/shard_map/fetch/pallas_call | solution.py:156
  14.1 0.8 %broadcast_select_fusion.3 = (f32[2,6144]{1,0:T(2,128)S(1)}, f32[2,6144]{1,0:T(2,128)S(1)}) fusion(f32[2,6144]{1,0:T(2,128)} %collective-permute-done, f32[2,6144]{1,0:T(2,128)S(1)} %modulation.1.after_ref, pred[]{:T(512)S(6)} %eq.26, pred[]{:T(512)S(6)} %eq.27), kind=kLoop, calls=%fused_computation.60 | loop fusion | flops 24576 | bytes 196610 | tf_op jit(solution)/shard_map/jit(_where)/select_n | solution.py:664
  15.0 6.3 %project_image.2 = (bf16[8,2,160,128]{3,2,1,0:T(8,128)(2,1)S(1)}, bf16[8,2,160,128]{3,2,1,0:T(8,128)(2,1)S(1)}, bf16[8,2,160,128]{3,2,1,0:T(8,128)(2,1)S(1)}, f3...) custom-call(f32[2,12288]{1,0:T(2,128)S(1)} %pad_maximum_fusion.3.mod, ...), custom_call_target="tpu_custom_call", output_to_operand_aliasing={{6}: (7, {})} | custom-call | flops 3019898880 | bytes 18874368 | tf_op jit(solution)/shard_map/project_image/pallas_call | solution.py:241
  21.3 1.6 %collective-permute-done.1.tokens = bf16[80,3072]{1,0:T(8,128)(2,1)} collective-permute-done((bf16[80,3072]{1,0:T(8,128)(2,1)S(1)}, bf16[80,3072]{1,0:T(8,128)(2,1)}, u32[]{:S(2)}, u32[]{:S(2)}) %collective-permute-start.1) | collective-permute-done | bytes 491552 | tf_op jit(solution)/shard_map/ppermute | solution.py:513
  22.9 7.2 %project_image.3 = (bf16[8,2,160,128]{3,2,1,0:T(8,128)(2,1)S(1)}, bf16[8,2,160,128]{3,2,1,0:T(8,128)(2,1)S(1)}, bf16[8,2,160,128]{3,2,1,0:T(8,128)(2,1)S(1)}, f3...) custom-call(f32[2,12288]{1,0:T(2,128)S(1)} %pad_maximum_fusion.3.mod, ...), custom_call_target="tpu_custom_call", output_to_operand_aliasing={{0}: (7, {}), {1}: (8, {}), {2}: (9, {}), {3}: (10, {}), {4... | custom-call | flops 3019898880 | bytes 18874368 | tf_op jit(solution)/shard_map/project_image/pallas_call | solution.py:241
  30.1 6.2 %project_text.1 = (bf16[8,2,96,128]{3,2,1,0:T(8,128)(2,1)S(1)}, bf16[8,2,96,128]{3,2,1,0:T(8,128)(2,1)S(1)}) custom-call(f32[2,12288]{1,0:T(2,128)S(1)} %pad_maximum_fusion.3.mod_ref, f32[3,128]{1,0:T(4,128)S(1)} %get-tuple-element.31.gain_ref, bf16[3072,2048]{1,0:T(8,128)(2,1)S(1)} %get-tuple-element.46.w_ref, bf16[48,3072]{1,0:T(8,128)(2,1)S(1)} %bitcast.17, ...), custom_call_target="tpu_custom_call" | custom-call | flops 2415919104 | bytes 12582912 | tf_op jit(solution)/shard_map/project_text/pallas_call | solution.py:121
  36.3 5.8 %attend.1 = (bf16[32,3072]{1,0:T(8,128)(2,1)S(1)}, f32[32,3072]{1,0:T(8,128)S(1)}, bf16[32,3072]{1,0:T(8,128)(2,1)S(1)}, f32[32,3072]{1,0:T(8,128)S(1)}, f32[8,128]{1,0:T(8,128)S(1)}) custom-call(s32[1]{0:T(128)} %bitcast.where_ref.side_ref, f32[1,256]{1,0:T(1,128)S(1)} %compare_select_fusion.bias_ref, f32[3,128]{1,0:T(4,128)S(1)} %get-tuple-element.31.gain_ref, ...), custom_call_target="tpu_custom_call" | custom-call | flops 671088640 | bytes 8000000 | tf_op jit(solution)/shard_map/attend/pallas_call | solution.py:366
  42.2 0.5 collective-permute-start.3
  42.7 0.9 %collective-permute-done.4 = bf16[32,3072]{1,0:T(8,128)(2,1)S(1)} collective-permute-done((bf16[32,3072]{1,0:T(8,128)(2,1)S(1)}, bf16[32,3072]{1,0:T(8,128)(2,1)S(1)}, u32[]{:S(2)}, u32[]{:S(2)}) %collective-permute-start.4) | collective-permute-done | bytes 196640 | tf_op jit(solution)/shard_map/ppermute | solution.py:538
  44.0 1.6 %collective-permute-start.5 = (bf16[8,9216]{1,0:T(8,128)(2,1)S(1)}, bf16[8,9216]{1,0:T(8,128)(2,1)S(1)}, u32[]{:S(2)}, u32[]{:S(2)}) collective-permute-start(bf16[8,9216]{1,0:T(8,128)(2,1)S(1)} %pad_maximum_fusion.2), channel_id=1, source_target_pairs={{0,16},{4,20},{8,24},{12,28},{16,0},{20,4},{24,8},{28,12},{1,17},{... | collective-permute-start | bytes 442376 | tf_op jit(solution)/shard_map/ppermute | solution.py:539
  45.5 0.5 collective-permute-start.6
  46.0 1.5 %collective-permute-start.7 = (bf16[8,3072]{1,0:T(8,128)(2,1)S(1)}, bf16[8,3072]{1,0:T(8,128)(2,1)S(1)}, u32[]{:S(2)}, u32[]{:S(2)}) collective-permute-start(bf16[8,3072]{1,0:T(8,128)(2,1)S(1)} %get-tuple-element.84), channel_id=1, source_target_pairs={{0,20},{4,16},{8,28},{12,24},{16,4},{20,0},{24,12},{28,8},{1,21},{... | collective-permute-start | bytes 147464 | tf_op jit(solution)/shard_map/ppermute | solution.py:538
  47.5 3.0 %collective-permute-done.5 = bf16[8,9216]{1,0:T(8,128)(2,1)S(1)} collective-permute-done((bf16[8,9216]{1,0:T(8,128)(2,1)S(1)}, bf16[8,9216]{1,0:T(8,128)(2,1)S(1)}, u32[]{:S(2)}, u32[]{:S(2)}) %collective-permute-start.5) | collective-permute-done | bytes 147488 | tf_op jit(solution)/shard_map/ppermute | solution.py:539
  51.1 2.6 %collective-permute-start.9 = (bf16[8,2304]{1,0:T(8,128)(2,1)S(1)}, bf16[8,2304]{1,0:T(8,128)(2,1)S(1)}, u32[]{:S(2)}, u32[]{:S(2)}) collective-permute-start(bf16[8,2304]{1,0:T(8,128)(2,1)S(1)} %pad_maximum_fusion.8), channel_id=1, source_target_pairs={{0,2},{1,3},{2,0},{3,1},{4,6},{5,7},{6,4},{7,5},{8,10},{9,11},{10,... | collective-permute-start | bytes 110600 | tf_op jit(solution)/shard_map/ppermute | solution.py:539
  53.8 1.4 %collective-permute-start.10 = (bf16[8,2304]{1,0:T(8,128)(2,1)S(1)}, bf16[8,2304]{1,0:T(8,128)(2,1)S(1)}, u32[]{:S(2)}, u32[]{:S(2)}) collective-permute-start(bf16[8,2304]{1,0:T(8,128)(2,1)S(1)} %pad_maximum_fusion.9), channel_id=1, source_target_pairs={{0,3},{1,2},{2,1},{3,0},{4,7},{5,6},{6,5},{7,4},{8,11},{9,10},{10,... | collective-permute-start | bytes 110600 | tf_op jit(solution)/shard_map/ppermute | solution.py:539
  55.5 0.5 collective-permute-done.9
  56.1 3.5 %collective-permute-done.10 = bf16[8,2304]{1,0:T(8,128)(2,1)S(1)} collective-permute-done((bf16[8,2304]{1,0:T(8,128)(2,1)S(1)}, bf16[8,2304]{1,0:T(8,128)(2,1)S(1)}, u32[]{:S(2)}, u32[]{:S(2)}) %collective-permute-start.10) | collective-permute-done | bytes 36896 | tf_op jit(solution)/shard_map/ppermute | solution.py:539
  59.8 2.1 %collective-permute-start.11 = (bf16[8,2688]{1,0:T(8,128)(2,1)S(1)}, bf16[8,2688]{1,0:T(8,128)(2,1)S(1)}, u32[]{:S(2)}, u32[]{:S(2)}) collective-permute-start(bf16[8,2688]{1,0:T(8,128)(2,1)S(1)} %constant_dynamic-update-slice_fusion), channel_id=1, source_target_pairs={{0,3},{1,2},{2,1},{3,0},{4,7},{5,6},{6,5},{7,4},{8,11},{9,10},{10,... | collective-permute-start | bytes 129032 | tf_op jit(solution)/shard_map/ppermute | solution.py:539
  61.9 2.4 %collective-permute-start.13 = (bf16[8,2688]{1,0:T(8,128)(2,1)S(1)}, bf16[8,2688]{1,0:T(8,128)(2,1)S(1)}, u32[]{:S(2)}, u32[]{:S(2)}) collective-permute-start(bf16[8,2688]{1,0:T(8,128)(2,1)S(1)} %constant_dynamic-update-slice_fusion), channel_id=1, source_target_pairs={{0,1},{1,0},{2,3},{3,2},{4,5},{5,4},{6,7},{7,6},{8,9},{9,8},{10,11... | collective-permute-start | bytes 129032 | tf_op jit(solution)/shard_map/ppermute | solution.py:539
  64.3 1.4 %collective-permute-done.11 = bf16[8,2688]{1,0:T(8,128)(2,1)S(1)} collective-permute-done((bf16[8,2688]{1,0:T(8,128)(2,1)S(1)}, bf16[8,2688]{1,0:T(8,128)(2,1)S(1)}, u32[]{:S(2)}, u32[]{:S(2)}) %collective-permute-start.11) | collective-permute-done | bytes 43040 | tf_op jit(solution)/shard_map/ppermute | solution.py:539
  65.7 1.1 %collective-permute-done.12 = bf16[8,2688]{1,0:T(8,128)(2,1)S(1)} collective-permute-done((bf16[8,2688]{1,0:T(8,128)(2,1)S(1)}, bf16[8,2688]{1,0:T(8,128)(2,1)S(1)}, u32[]{:S(2)}, u32[]{:S(2)}) %collective-permute-start.12) | collective-permute-done | bytes 43040 | tf_op jit(solution)/shard_map/ppermute | solution.py:539
  67.2 2.5 %collective-permute-start.14 = (bf16[8,3456]{1,0:T(8,128)(2,1)S(1)}, bf16[8,3456]{1,0:T(8,128)(2,1)S(1)}, u32[]{:S(2)}, u32[]{:S(2)}) collective-permute-start(bf16[8,3456]{1,0:T(8,128)(2,1)S(1)} %get-tuple-element.126), channel_id=1, source_target_pairs={{0,20},{4,16},{8,28},{12,24},{16,4},{20,0},{24,12},{28,8},{1,21},{... | collective-permute-start | bytes 165896 | tf_op jit(solution)/shard_map/ppermute | solution.py:539
  69.7 0.5 collective-permute-start.15
  70.2 0.5 collective-permute-start.16
  70.7 3.1 %collective-permute-done.15 = bf16[8,3456]{1,0:T(8,128)(2,1)S(1)} collective-permute-done((bf16[8,3456]{1,0:T(8,128)(2,1)S(1)}, bf16[8,3456]{1,0:T(8,128)(2,1)S(1)}, u32[]{:S(2)}, u32[]{:S(2)}) %collective-permute-start.15) | collective-permute-done | bytes 55328 | tf_op jit(solution)/shard_map/ppermute | solution.py:539
  73.9 1.6 %collective-permute-done.16 = bf16[8,9600]{1,0:T(8,128)(2,1)S(1)} collective-permute-done((bf16[8,9600]{1,0:T(8,128)(2,1)S(1)}, bf16[8,9600]{1,0:T(8,128)(2,1)S(1)}, u32[]{:S(2)}, u32[]{:S(2)}) %collective-permute-start.16) | collective-permute-done | bytes 153632 | tf_op jit(solution)/shard_map/ppermute | solution.py:539
  75.9 1.7 %collective-permute-done.17.got_ref = bf16[8,24960]{1,0:T(8,128)(2,1)S(1)} collective-permute-done((bf16[8,24960]{1,0:T(8,128)(2,1)S(1)}, bf16[8,24960]{1,0:T(8,128)(2,1)S(1)}, u32[]{:S(2)}, u32[]{:S(2)}) %collective-permute-start.17) | collective-permute-done | bytes 399392 | tf_op jit(solution)/shard_map/ppermute | solution.py:716
  77.5 1.4 %finish.1 = (f32[64,3072]{1,0:T(8,128)}, f32[64,3072]{1,0:T(8,128)}, f32[1,1]{1,0:T(1,128)}) custom-call(s32[1]{0:T(128)} %bitcast.where_ref.side_ref, bf16[32,3072]{1,0:T(8,128)(2,1)S(1)} %pad_maximum_fusion.a_ref, bf16[32,3072]{1,0:T(8,128)(2,1)S(1)} %pad_maximum_fusion.1.b_ref, f32[8,128]{1,0:T(8,128)S(1)} %get-tuple-element.60.sums_ref, ...), custom_call_target="tpu_custom_call" | custom-call | tf_op jit(solution)/shard_map/finish/pallas_call | solution.py:498
  (84 shorter events, 2.4 us)
Async XLA Ops:
  4.1 10.0 %collective-permute-start = (f32[2,6144]{1,0:T(2,128)S(1)}, f32[2,6144]{1,0:T(2,128)}, u32[]{:S(2)}, u32[]{:S(2)}) collective-permute-start(f32[2,6144]{1,0:T(2,128)S(1)} %modulation.1.after_ref), channel_id=1, source_target_pairs={{0,4},{4,0},{1,5},{5,1},{2,6},{6,2},{3,7},{7,3},{8,12},{12,8},{9,1... | collective-permute-start | bytes 147464 | tf_op jit(solution)/shard_map/ppermute | solution.py:513
  8.6 14.3 %collective-permute-start.1 = (bf16[80,3072]{1,0:T(8,128)(2,1)S(1)}, bf16[80,3072]{1,0:T(8,128)(2,1)}, u32[]{:S(2)}, u32[]{:S(2)}) collective-permute-start(bf16[80,3072]{1,0:T(8,128)(2,1)S(1)} %noisy.1.after_ref.tokens), channel_id=1, source_target_pairs={{0,4},{4,0},{1,5},{5,1},{2,6},{6,2},{3,7},{7,3},{8,12},{12,8},{9,1... | collective-permute-start | bytes 1474568 | tf_op jit(solution)/shard_map/ppermute | solution.py:513
  8.7 21.4 %collective-permute-start.2 = (bf16[48,3072]{1,0:T(8,128)(2,1)}, bf16[48,3072]{1,0:T(8,128)(2,1)}, u32[]{:S(2)}, u32[]{:S(2)}) collective-permute-start(bf16[48,3072]{1,0:T(8,128)(2,1)} %bitcast.16), channel_id=1, source_target_pairs={{0,4},{4,0},{1,5},{5,1},{2,6},{6,2},{3,7},{7,3},{8,12},{12,8},{9,1... | collective-permute-start | bytes 884744 | tf_op jit(solution)/shard_map/ppermute | solution.py:513
  22.9 7.2 %copy-start = (bf16[1,48,3072]{2,1,0:T(8,128)(2,1)S(1)}, bf16[1,48,3072]{2,1,0:T(8,128)(2,1)}, u32[]{:S(2)}) copy-start(bf16[1,48,3072]{2,1,0:T(8,128)(2,1)} %param.14) | copy-start | bytes 884740
  42.1 1.5 %collective-permute-start.4 = (bf16[32,3072]{1,0:T(8,128)(2,1)S(1)}, bf16[32,3072]{1,0:T(8,128)(2,1)S(1)}, u32[]{:S(2)}, u32[]{:S(2)}) collective-permute-start(bf16[32,3072]{1,0:T(8,128)(2,1)S(1)} %get-tuple-element.54), channel_id=1, source_target_pairs={{0,8},{8,0},{16,24},{24,16},{1,9},{9,1},{17,25},{25,17},{2,10},{10... | collective-permute-start | bytes 589832 | tf_op jit(solution)/shard_map/ppermute | solution.py:538
  42.2 1.7 %collective-permute-start.3 = (bf16[32,3072]{1,0:T(8,128)(2,1)S(1)}, bf16[32,3072]{1,0:T(8,128)(2,1)S(1)}, u32[]{:S(2)}, u32[]{:S(2)}) collective-permute-start(bf16[32,3072]{1,0:T(8,128)(2,1)S(1)} %get-tuple-element.52), channel_id=1, source_target_pairs={{0,8},{8,0},{16,24},{24,16},{1,9},{9,1},{17,25},{25,17},{2,10},{10... | collective-permute-start | bytes 589832 | tf_op jit(solution)/shard_map/ppermute | solution.py:538
  44.0 6.6 %collective-permute-start.5 = (bf16[8,9216]{1,0:T(8,128)(2,1)S(1)}, bf16[8,9216]{1,0:T(8,128)(2,1)S(1)}, u32[]{:S(2)}, u32[]{:S(2)}) collective-permute-start(bf16[8,9216]{1,0:T(8,128)(2,1)S(1)} %pad_maximum_fusion.2), channel_id=1, source_target_pairs={{0,16},{4,20},{8,24},{12,28},{16,0},{20,4},{24,8},{28,12},{1,17},{... | collective-permute-start | bytes 442376 | tf_op jit(solution)/shard_map/ppermute | solution.py:539
  45.5 5.1 %collective-permute-start.6 = (bf16[8,3072]{1,0:T(8,128)(2,1)S(1)}, bf16[8,3072]{1,0:T(8,128)(2,1)S(1)}, u32[]{:S(2)}, u32[]{:S(2)}) collective-permute-start(bf16[8,3072]{1,0:T(8,128)(2,1)S(1)} %get-tuple-element.83), channel_id=1, source_target_pairs={{0,4},{4,0},{8,12},{12,8},{16,20},{20,16},{24,28},{28,24},{1,5},{5... | collective-permute-start | bytes 147464 | tf_op jit(solution)/shard_map/ppermute | solution.py:538
  46.0 5.0 %collective-permute-start.7 = (bf16[8,3072]{1,0:T(8,128)(2,1)S(1)}, bf16[8,3072]{1,0:T(8,128)(2,1)S(1)}, u32[]{:S(2)}, u32[]{:S(2)}) collective-permute-start(bf16[8,3072]{1,0:T(8,128)(2,1)S(1)} %get-tuple-element.84), channel_id=1, source_target_pairs={{0,20},{4,16},{8,28},{12,24},{16,4},{20,0},{24,12},{28,8},{1,21},{... | collective-permute-start | bytes 147464 | tf_op jit(solution)/shard_map/ppermute | solution.py:538
  51.1 4.9 %collective-permute-start.9 = (bf16[8,2304]{1,0:T(8,128)(2,1)S(1)}, bf16[8,2304]{1,0:T(8,128)(2,1)S(1)}, u32[]{:S(2)}, u32[]{:S(2)}) collective-permute-start(bf16[8,2304]{1,0:T(8,128)(2,1)S(1)} %pad_maximum_fusion.8), channel_id=1, source_target_pairs={{0,2},{1,3},{2,0},{3,1},{4,6},{5,7},{6,4},{7,5},{8,10},{9,11},{10,... | collective-permute-start | bytes 110600 | tf_op jit(solution)/shard_map/ppermute | solution.py:539
  53.8 5.8 %collective-permute-start.10 = (bf16[8,2304]{1,0:T(8,128)(2,1)S(1)}, bf16[8,2304]{1,0:T(8,128)(2,1)S(1)}, u32[]{:S(2)}, u32[]{:S(2)}) collective-permute-start(bf16[8,2304]{1,0:T(8,128)(2,1)S(1)} %pad_maximum_fusion.9), channel_id=1, source_target_pairs={{0,3},{1,2},{2,1},{3,0},{4,7},{5,6},{6,5},{7,4},{8,11},{9,10},{10,... | collective-permute-start | bytes 110600 | tf_op jit(solution)/shard_map/ppermute | solution.py:539
  55.2 4.4 %collective-permute-start.8 = (bf16[8,2304]{1,0:T(8,128)(2,1)S(1)}, bf16[8,2304]{1,0:T(8,128)(2,1)S(1)}, u32[]{:S(2)}, u32[]{:S(2)}) collective-permute-start(bf16[8,2304]{1,0:T(8,128)(2,1)S(1)} %pad_maximum_fusion.7), channel_id=1, source_target_pairs={{0,1},{1,0},{2,3},{3,2},{4,5},{5,4},{6,7},{7,6},{8,9},{9,8},{10,11... | collective-permute-start | bytes 110600 | tf_op jit(solution)/shard_map/ppermute | solution.py:539
  59.8 5.9 %collective-permute-start.11 = (bf16[8,2688]{1,0:T(8,128)(2,1)S(1)}, bf16[8,2688]{1,0:T(8,128)(2,1)S(1)}, u32[]{:S(2)}, u32[]{:S(2)}) collective-permute-start(bf16[8,2688]{1,0:T(8,128)(2,1)S(1)} %constant_dynamic-update-slice_fusion), channel_id=1, source_target_pairs={{0,3},{1,2},{2,1},{3,0},{4,7},{5,6},{6,5},{7,4},{8,11},{9,10},{10,... | collective-permute-start | bytes 129032 | tf_op jit(solution)/shard_map/ppermute | solution.py:539
  61.9 4.9 %collective-permute-start.12 = (bf16[8,2688]{1,0:T(8,128)(2,1)S(1)}, bf16[8,2688]{1,0:T(8,128)(2,1)S(1)}, u32[]{:S(2)}, u32[]{:S(2)}) collective-permute-start(bf16[8,2688]{1,0:T(8,128)(2,1)S(1)} %constant_dynamic-update-slice_fusion), channel_id=1, source_target_pairs={{0,2},{1,3},{2,0},{3,1},{4,6},{5,7},{6,4},{7,5},{8,10},{9,11},{10,... | collective-permute-start | bytes 129032 | tf_op jit(solution)/shard_map/ppermute | solution.py:539
  61.9 4.9 %collective-permute-start.13 = (bf16[8,2688]{1,0:T(8,128)(2,1)S(1)}, bf16[8,2688]{1,0:T(8,128)(2,1)S(1)}, u32[]{:S(2)}, u32[]{:S(2)}) collective-permute-start(bf16[8,2688]{1,0:T(8,128)(2,1)S(1)} %constant_dynamic-update-slice_fusion), channel_id=1, source_target_pairs={{0,1},{1,0},{2,3},{3,2},{4,5},{5,4},{6,7},{7,6},{8,9},{9,8},{10,11... | collective-permute-start | bytes 129032 | tf_op jit(solution)/shard_map/ppermute | solution.py:539
  67.2 6.7 %collective-permute-start.14 = (bf16[8,3456]{1,0:T(8,128)(2,1)S(1)}, bf16[8,3456]{1,0:T(8,128)(2,1)S(1)}, u32[]{:S(2)}, u32[]{:S(2)}) collective-permute-start(bf16[8,3456]{1,0:T(8,128)(2,1)S(1)} %get-tuple-element.126), channel_id=1, source_target_pairs={{0,20},{4,16},{8,28},{12,24},{16,4},{20,0},{24,12},{28,8},{1,21},{... | collective-permute-start | bytes 165896 | tf_op jit(solution)/shard_map/ppermute | solution.py:539
  69.7 4.2 %collective-permute-start.15 = (bf16[8,3456]{1,0:T(8,128)(2,1)S(1)}, bf16[8,3456]{1,0:T(8,128)(2,1)S(1)}, u32[]{:S(2)}, u32[]{:S(2)}) collective-permute-start(bf16[8,3456]{1,0:T(8,128)(2,1)S(1)} %get-tuple-element.126), channel_id=1, source_target_pairs={{0,4},{4,0},{8,12},{12,8},{16,20},{20,16},{24,28},{28,24},{1,5},{5... | collective-permute-start | bytes 165896 | tf_op jit(solution)/shard_map/ppermute | solution.py:539
  70.2 5.2 %collective-permute-start.16 = (bf16[8,9600]{1,0:T(8,128)(2,1)S(1)}, bf16[8,9600]{1,0:T(8,128)(2,1)S(1)}, u32[]{:S(2)}, u32[]{:S(2)}) collective-permute-start(bf16[8,9600]{1,0:T(8,128)(2,1)S(1)} %constant_dynamic-update-slice_fusion.13), channel_id=1, source_target_pairs={{0,16},{4,20},{8,24},{12,28},{16,0},{20,4},{24,8},{28,12},{1,17},{... | collective-permute-start | bytes 460808 | tf_op jit(solution)/shard_map/ppermute | solution.py:539
  75.7 1.8 %collective-permute-start.17 = (bf16[8,24960]{1,0:T(8,128)(2,1)S(1)}, bf16[8,24960]{1,0:T(8,128)(2,1)S(1)}, u32[]{:S(2)}, u32[]{:S(2)}) collective-permute-start(bf16[8,24960]{1,0:T(8,128)(2,1)S(1)} %constant_dynamic-update-slice_fusion.22), channel_id=1, source_target_pairs={{0,8},{8,0},{16,24},{24,16},{1,9},{9,1},{17,25},{25,17},{2,10},{10... | collective-permute-start | bytes 1198088 | tf_op jit(solution)/shard_map/ppermute | solution.py:716

commit v9 on v8

--- a/solution.py
+++ b/solution.py
@@ -77,20 +77,23 @@
     return pltpu.with_memory_space_constraint(x, pltpu.HBM)
 
 
-def text_kernel(n, pair, mod_ref, gain_ref, w_ref, *refs):
-    parts, (k_ref, v_ref, ht) = refs[:n], refs[n:]
+def text_kernel(n, pair, mod_ref, gain_ref, w_ref, after_ref, *refs):
+    parts, (k_ref, v_ref, ht, weights, sems) = refs[:n], refs[n:]
+    copies = [chunk(w_ref, weights, sems, i) for i in range(sems.shape[0])]
+    for copy in copies:
+        copy.start()
     rows = n * parts[0].shape[0]
     for k in range(n):
         modulate(parts[k], mod_ref, 2, w_ref.shape[0], ht, rows, k * parts[0].shape[0])
     cols = pair * 2 * HD
     size = min(rows, 96)
-
-    @pl.loop(0, w_ref.shape[1] // cols)
-    def _(step):
-        def project(start):
+    for step, copy in enumerate(copies):
+        copy.wait()
+
+        def project(start, step=step):
             for j in range(pair):
-                head = step * pair + j
-                w = w_ref[:, pl.ds(pl.multiple_of(head * 2 * HD, 2 * HD), 2 * HD)]
+                head, c = step * pair + j, step * cols + j * 2 * HD
+                w = weights[:, c : c + 2 * HD]
                 if size == rows:
                     both = nn(ht[...], w)
                     own = [both[:rows], both[rows:]]
@@ -114,22 +117,26 @@
     )
 
 
-def project_text(mod, gain, w, parts):
+def project_text(mod, gain, w, after, parts):
     n, (part, width) = len(parts), parts[0].shape
     pair, steps = split(w.shape[1] // (2 * HD))
     out = pltpu.VMEM((pair * steps, 2, n * part, HD), BF16)
     return pl.pallas_call(
         functools.partial(text_kernel, n, pair),
-        in_specs=[VMEM] * (3 + n),
+        in_specs=[VMEM, VMEM, HELD, pl.BlockSpec(memory_space=pl.ANY)] + [VMEM] * n,
         out_specs=[VMEM] * 2,
         out_shape=[out, out],
-        scratch_shapes=[pltpu.VMEM((2 * n * part, width), BF16)],
-        compiler_params=pltpu.CompilerParams(vmem_limit_bytes=SMALL),
+        scratch_shapes=[
+            pltpu.VMEM((2 * n * part, width), BF16),
+            pltpu.VMEM(w.shape, w.dtype),
+            pltpu.SemaphoreType.DMA((steps,)),
+        ],
+        compiler_params=pltpu.CompilerParams(vmem_limit_bytes=2 * SMALL),
         cost_estimate=pl.CostEstimate(
             flops=4 * n * part * w.size, bytes_accessed=2 * w.size, transcendentals=0
         ),
         name="project_text",
-    )(mod, gain, w, *parts)
+    )(mod, gain, w, after, *parts)
 
 
 def chunk(w_ref, out_ref, sems, index):
@@ -167,19 +174,14 @@
     )(after, *[held(x) for x in arrays])
 
 
-def image_kernel(pair, index, n, mod_ref, gain_ref, down_ref, up_ref, w_ref, tokens, *refs):
-    first, last = index == 0, index == n - 1
-    refs = list(refs)
-    more = refs.pop(0) if first or last else None
-    refs = refs[1 if first else 6 :]
-    q_ref, k_ref, v_ref, x_ref, low_ref, hs_ref, *rest = refs
+def image_kernel(pair, index, mod_ref, gain_ref, down_ref, up_ref, w_ref, tokens, *refs):
+    first = index == 0
+    q_ref, k_ref, v_ref, x_ref, low_ref, hs_ref, *rest = refs[1 if first else 6 :]
     weights = w_ref
-    if first or last:
-        into, hi, sems = rest
-        copies = [chunk(more, into, sems, i) for i in range(1 if first else 0, sems.shape[0])]
-        for copy in copies:
-            copy.start()
-        weights = into if first else w_ref
+    if first:
+        weights, hi, sems = rest
+        for i in range(1, sems.shape[0]):
+            chunk(w_ref, weights, sems, i).start()
     else:
         (hi,) = rest
     rows = tokens.shape[0]
@@ -195,7 +197,7 @@
 
             @pl.when(step > 0)
             def _():
-                chunk(more, into, sems, step).wait()
+                chunk(w_ref, weights, sems, step).wait()
 
         out = nn(hi[...], weights[:, columns])
         student = out[rows:] + nn(low_ref[part, :], up_ref[:, columns])
@@ -210,12 +212,9 @@
                 v_ref[head, m, part, :] = own[:, c + 2 * HD : c + 3 * HD].astype(BF16)
 
     pl.loop(0, w_ref.shape[1] // cols)(project)
-    if last and not first:
-        for copy in copies:
-            copy.wait()
-
-
-def project_image(part, n, before, mod, gain, down, up, w, tokens, more):
+
+
+def project_image(part, n, before, mod, gain, down, up, w, tokens, far):
     (rows, width), rank = tokens.shape, up.shape[0]
     pair, steps = split(w.shape[1] // (3 * HD))
     heads = (pair * steps, 2, n * rows, HD)
@@ -225,21 +224,15 @@
         pltpu.VMEM((n * rows, width), BF16),
     ]
     scratch = [pltpu.VMEM((2 * rows, width), BF16)]
-    operands, specs, aliases = [mod, gain, down, up, w, tokens], [VMEM] * 6, {}
-    if part == 0 or part == n - 1:
-        operands.append(more)
-        specs.append(HELD)
-        shapes.append(pltpu.VMEM(more.shape, more.dtype))
+    operands, specs = [mod, gain, down, up, w, tokens], [VMEM] * 6
+    aliases = {6 + i: i for i in range(len(before))}
+    if part == 0:
+        operands[4], specs[4] = far, HELD
+        before, aliases = [w], {6: 6}
+        shapes.append(pltpu.VMEM(w.shape, w.dtype))
         scratch.append(pltpu.SemaphoreType.DMA((steps,)))
-    if part == 0:
-        operands[4] = more
-        specs[4] = HELD
-        aliases = {len(operands): 6}
-        before = [w]
-    else:
-        aliases = {len(operands) + i: i for i in range(len(before))}
     return pl.pallas_call(
-        functools.partial(image_kernel, pair, part, n),
+        functools.partial(image_kernel, pair, part),
         in_specs=specs + [VMEM] * len(before),
         out_specs=[VMEM] * len(shapes),
         out_shape=shapes,
@@ -656,7 +649,13 @@
     noisy = mix(timestep, image[0], noise[0], part)
     mods = [part] + [shifted(part, "seq", k) for k in range(1, n)]
     noisy_parts = [noisy] + [shifted(noisy, "seq", k) for k in range(1, n)]
-    words = text[0]
+    steps = split(image_projection_weight.shape[1] // (3 * HD))[1]
+    gain, down, up, words, weights = fetch(
+        [query_key_norm_gain, adapter_down_weight.T, adapter_up_weight, text[0]],
+        image_projection_weight,
+        steps,
+        noisy,
+    )
     text_parts = [words] + [shifted(words, "seq", k) for k in range(1, n)]
     origin = [lax.rem(me + n - k, n) for k in range(n)]
     ordered = [
@@ -673,22 +672,14 @@
     )
     bias = jnp.where(place < text_token_length[0], 0.0, -1000000000.0).astype(F32)[None]
     core = lax.rem(lax.axis_index("grp"), 2).astype(jnp.int32)
-    gain = query_key_norm_gain
-    steps = split(image_projection_weight.shape[1] // (3 * HD))[1]
-    gain, down, up, weights = fetch(
-        [gain, adapter_down_weight.T, adapter_up_weight], image_projection_weight, steps, noisy
-    )
     far_weights, image_heads = held(image_projection_weight), []
     for k in range(n):
-        if k == n - 1:
-            far_weights = held(text_projection_weight)
         image_heads = project_image(
             k, n, image_heads, mod, gain, down, up, weights, noisy_parts[k], far_weights
         )
         if k == 0:
             *image_heads, weights = image_heads
-    *image_heads, text_weights = image_heads
-    text_heads = project_text(mod, gain, text_weights, text_parts)
+    text_heads = project_text(mod, gain, held(text_projection_weight), image_heads[0], text_parts)
     send_a, keep_a, send_b, keep_b, loss = attend(
         core[None], bias, gain, up, image_heads, text_heads
     )

time: 79.2 us -> 101 us (1.28)
  local copies, waits for them, and re-layouts: 0.18 us -> 25.8 us
  Pallas kernels: 33.1 us -> 31.4 us
  waiting for transfers between devices: 19.1 us -> 17.5 us
    unnamed x14 -> x20, local copies, waits for them, and re-layouts: 0.06 us -> 25.7 us
    pallas_call x3, Pallas kernels: 19.6 us -> 17.9 us  [the longest x2 12.3 us: project_image(): pl.pallas_call(functools.partial(image_kernel, pair, part), in_specs=spec...]
    ppermute x3, waiting for transfers between devices: 1.64 us -> 0.01 us  [shifted(): return lax.ppermute(x, axis, [(i, (i + k) % size) for i in range(size)])]
  transfers between devices with their start and end apart: 18 -> 18, of which waited for: 12 -> 11; matrix products, arithmetic and copies ran while one was open for 2% -> 0% of each run, Pallas kernels for 22% -> 16%
where the time goes in v9:
time: 101 us
  Pallas kernels  31.4 us (31%)
  local copies, waits for them, and re-layouts  25.8 us (26%)
  starting transfers between devices  21.6 us (21%)
  waiting for transfers between devices  17.5 us (17%)
  between operations  3.07 us (3%)
  other arithmetic  1.11 us (1%)
    unnamed x20, local copies, waits for them, and re-layouts  25.7 us
    ppermute x10, waiting for transfers between devices, send(): return unpack(lax.ppermute(pack(arrays), group.axes, pairs), arrays)  14.3 us
    ppermute x10, starting transfers between devices, send(): return unpack(lax.ppermute(pack(arrays), group.axes, pairs), arrays)  13.9 us
    pallas_call x2, Pallas kernels, project_image(): pl.pallas_call(functools.partial(image_kernel, pair, part), in_specs=spec...  12.3 us
    pallas_call x1, Pallas kernels, attend(): pl.pallas_call(functools.partial(attend_kernel, steps, pair, samples), in...  5.74 us
    pallas_call x1, Pallas kernels, project_text(): pl.pallas_call(functools.partial(text_kernel, n, pair), in_specs=[VMEM, V...  5.61 us
    ppermute x3, starting transfers between devices, shifted(): return lax.ppermute(x, axis, [(i, (i + k) % size) for i in range(size)])  5.11 us
    pallas_call x1, Pallas kernels, fetch(): pl.pallas_call(fetch_kernel, in_specs=[pl.BlockSpec(memory_space=pl.ANY)]...  2.76 us
  transfers between devices with their start and end apart: 18, of which 11 were waited for; matrix products, arithmetic and copies ran while one was open for 0% of the time, Pallas kernels for 16%

profile of v9, /device:TPU:0, one launch (start us, length us, event | category | flops | bytes accessed | tf_op | source)
XLA Modules:
  0.0 100.5 jit_solution(17596249301606575772)
XLA Ops:
  1.9 2.2 %modulation.1.after_ref = f32[2,6144]{1,0:T(2,128)S(1)} custom-call(s32[1]{0:T(128)S(6)} %copy.58.step_ref, f32[1]{0:T(128)S(6)} %copy.59.guidance_ref, bf16[256,6144]{1,0:T(8,128)(2,1)} %weight_ref.1), custom_call_target="tpu_custom_call" | custom-call | flops 6291456 | bytes 3145728 | tf_op jit(solution)/shard_map/modulation/pallas_call | solution.py:422
  4.1 3.0 %collective-permute-start = (f32[2,6144]{1,0:T(2,128)S(1)}, f32[2,6144]{1,0:T(2,128)S(1)}, u32[]{:S(2)}, u32[]{:S(2)}) collective-permute-start(f32[2,6144]{1,0:T(2,128)S(1)} %modulation.1.after_ref), channel_id=1, source_target_pairs={{0,4},{4,0},{1,5},{5,1},{2,6},{6,2},{3,7},{7,3},{8,12},{12,8},{9,1... | collective-permute-start | bytes 147464 | tf_op jit(solution)/shard_map/ppermute | solution.py:506
  7.1 1.4 %noisy.1.after_ref.tokens = bf16[80,3072]{1,0:T(8,128)(2,1)S(1)} custom-call(s32[1]{0:T(128)S(6)} %copy.58.step_ref, bf16[80,3072]{1,0:T(8,128)(2,1)} %bitcast.16, bf16[80,3072]{1,0:T(8,128)(2,1)} %bitcast.17, f32[2,6144]{1,0:T(2,128)S(1)} %modulation.1.after_ref), custom_call_target="tpu_custom_call" | custom-call | bytes 1474560 | tf_op jit(solution)/shard_map/noisy/pallas_call | solution.py:447
  8.7 2.8 %fetch.1 = (f32[3,128]{1,0:T(4,128)S(1)}, bf16[64,3072]{1,0:T(8,128)(2,1)S(1)}, bf16[64,3072]{1,0:T(8,128)(2,1)S(1)}, bf16[48,3072]{1,0:T(8,128)(2,1)S(1)}, bf16[3072,3072]{1,0:T(8,128)(2,1)S(1)}) custom-call(bf16[80,3072]{1,0:T(8,128)(2,1)S(1)} %noisy.1.after_ref.tokens, f32[3,128]{1,0:T(4,128)} %refs_0_.1, bf16[64,3072]{1,0:T(8,128)(2,1)} %bitcast.18, ...), custom_call_target="tpu_custom_call" | custom-call | bytes 4718592 | tf_op jit(solution)/shard_map/fetch/pallas_call | solution.py:163
  11.5 6.5 %copy-done = bf16[3072,3072]{1,0:T(8,128)(2,1)} copy-done((bf16[3072,3072]{1,0:T(8,128)(2,1)}, bf16[3072,3072]{1,0:T(8,128)(2,1)S(1)}, u32[]{:S(2)}) %copy-start) | copy-done | bytes 18874392
  17.9 2.0 %collective-permute-start.2 = (bf16[48,3072]{1,0:T(8,128)(2,1)S(1)}, bf16[48,3072]{1,0:T(8,128)(2,1)S(1)}, u32[]{:S(2)}, u32[]{:S(2)}) collective-permute-start(bf16[48,3072]{1,0:T(8,128)(2,1)S(1)} %get-tuple-element.46.refs_0_), channel_id=1, source_target_pairs={{0,4},{4,0},{1,5},{5,1},{2,6},{6,2},{3,7},{7,3},{8,12},{12,8},{9,1... | collective-permute-start | bytes 884744 | tf_op jit(solution)/shard_map/ppermute | solution.py:506
  20.8 6.4 %copy-done.1 = bf16[3072,3072]{1,0:T(8,128)(2,1)S(1)} copy-done((bf16[3072,3072]{1,0:T(8,128)(2,1)S(1)}, bf16[3072,3072]{1,0:T(8,128)(2,1)}, u32[]{:S(2)}) %copy-start.1) | copy-done | bytes 18874392
  27.1 6.3 %project_image.2 = (bf16[8,2,160,128]{3,2,1,0:T(8,128)(2,1)S(1)}, bf16[8,2,160,128]{3,2,1,0:T(8,128)(2,1)S(1)}, bf16[8,2,160,128]{3,2,1,0:T(8,128)(2,1)S(1)}, f3...) custom-call(f32[2,12288]{1,0:T(2,128)S(1)} %pad_maximum_fusion.3.mod, ...), custom_call_target="tpu_custom_call", output_to_operand_aliasing={{6}: (6, {})} | custom-call | flops 3019898880 | bytes 18874368 | tf_op jit(solution)/shard_map/project_image/pallas_call | solution.py:234
  33.4 6.5 %copy-done.2 = bf16[3072,3072]{1,0:T(8,128)(2,1)} copy-done((bf16[3072,3072]{1,0:T(8,128)(2,1)}, bf16[3072,3072]{1,0:T(8,128)(2,1)S(1)}, u32[]{:S(2)}) %copy-start.2) | copy-done | bytes 18874392
  39.9 6.4 %copy-done.3 = bf16[3072,3072]{1,0:T(8,128)(2,1)S(1)} copy-done((bf16[3072,3072]{1,0:T(8,128)(2,1)S(1)}, bf16[3072,3072]{1,0:T(8,128)(2,1)}, u32[]{:S(2)}) %copy-start.3) | copy-done | bytes 18874392
  46.3 6.0 %project_image.3 = (bf16[8,2,160,128]{3,2,1,0:T(8,128)(2,1)S(1)}, bf16[8,2,160,128]{3,2,1,0:T(8,128)(2,1)S(1)}, bf16[8,2,160,128]{3,2,1,0:T(8,128)(2,1)S(1)}, f3...) custom-call(f32[2,12288]{1,0:T(2,128)S(1)} %pad_maximum_fusion.3.mod, ...), custom_call_target="tpu_custom_call", output_to_operand_aliasing={{0}: (6, {}), {1}: (7, {}), {2}: (8, {}), {3}: (9, {}), {4}... | custom-call | flops 3019898880 | bytes 18874368 | tf_op jit(solution)/shard_map/project_image/pallas_call | solution.py:234
  52.3 5.6 %project_text.1 = (bf16[8,2,96,128]{3,2,1,0:T(8,128)(2,1)S(1)}, bf16[8,2,96,128]{3,2,1,0:T(8,128)(2,1)S(1)}) custom-call(f32[2,12288]{1,0:T(2,128)S(1)} %pad_maximum_fusion.3.mod_ref, f32[3,128]{1,0:T(4,128)S(1)} %get-tuple-element.31.gain_ref, bf16[3072,2048]{1,0:T(8,128)(2,1)} %w_ref.3, bf16[8,2,160,128]{3,2,1,0:T(8,128)(2,1)S(1)} %get-tuple-element.42.after_ref.q_ref, ...), custom_call_target="tpu_custom_call" | custom-call | flops 2415919104 | bytes 12582912 | tf_op jit(solution)/shard_map/project_text/pallas_call | solution.py:124
  57.9 5.7 %attend.1 = (bf16[32,3072]{1,0:T(8,128)(2,1)S(1)}, f32[32,3072]{1,0:T(8,128)S(1)}, bf16[32,3072]{1,0:T(8,128)(2,1)S(1)}, f32[32,3072]{1,0:T(8,128)S(1)}, f32[8,128]{1,0:T(8,128)S(1)}) custom-call(s32[1]{0:T(128)} %bitcast.where_ref.side_ref, f32[1,256]{1,0:T(1,128)S(1)} %compare_select_fusion.bias_ref, f32[3,128]{1,0:T(4,128)S(1)} %get-tuple-element.31.gain_ref, ...), custom_call_target="tpu_custom_call" | custom-call | flops 671088640 | bytes 8000000 | tf_op jit(solution)/shard_map/attend/pallas_call | solution.py:359
  64.3 0.9 collective-permute-done.4
  65.6 1.6 %collective-permute-start.5 = (bf16[8,9216]{1,0:T(8,128)(2,1)S(1)}, bf16[8,9216]{1,0:T(8,128)(2,1)S(1)}, u32[]{:S(2)}, u32[]{:S(2)}) collective-permute-start(bf16[8,9216]{1,0:T(8,128)(2,1)S(1)} %pad_maximum_fusion.2), channel_id=1, source_target_pairs={{0,16},{4,20},{8,24},{12,28},{16,0},{20,4},{24,8},{28,12},{1,17},{... | collective-permute-start | bytes 442376 | tf_op jit(solution)/shard_map/ppermute | solution.py:532
  67.6 1.5 %collective-permute-start.7 = (bf16[8,3072]{1,0:T(8,128)(2,1)S(1)}, bf16[8,3072]{1,0:T(8,128)(2,1)S(1)}, u32[]{:S(2)}, u32[]{:S(2)}) collective-permute-start(bf16[8,3072]{1,0:T(8,128)(2,1)S(1)} %get-tuple-element.84), channel_id=1, source_target_pairs={{0,20},{4,16},{8,28},{12,24},{16,4},{20,0},{24,12},{28,8},{1,21},{... | collective-permute-start | bytes 147464 | tf_op jit(solution)/shard_map/ppermute | solution.py:531
  69.1 3.0 %collective-permute-done.5 = bf16[8,9216]{1,0:T(8,128)(2,1)S(1)} collective-permute-done((bf16[8,9216]{1,0:T(8,128)(2,1)S(1)}, bf16[8,9216]{1,0:T(8,128)(2,1)S(1)}, u32[]{:S(2)}, u32[]{:S(2)}) %collective-permute-start.5) | collective-permute-done | bytes 147488 | tf_op jit(solution)/shard_map/ppermute | solution.py:532
  72.7 2.7 %collective-permute-start.9 = (bf16[8,2304]{1,0:T(8,128)(2,1)S(1)}, bf16[8,2304]{1,0:T(8,128)(2,1)S(1)}, u32[]{:S(2)}, u32[]{:S(2)}) collective-permute-start(bf16[8,2304]{1,0:T(8,128)(2,1)S(1)} %pad_maximum_fusion.8), channel_id=1, source_target_pairs={{0,2},{1,3},{2,0},{3,1},{4,6},{5,7},{6,4},{7,5},{8,10},{9,11},{10,... | collective-permute-start | bytes 110600 | tf_op jit(solution)/shard_map/ppermute | solution.py:532
  75.4 1.3 %collective-permute-start.10 = (bf16[8,2304]{1,0:T(8,128)(2,1)S(1)}, bf16[8,2304]{1,0:T(8,128)(2,1)S(1)}, u32[]{:S(2)}, u32[]{:S(2)}) collective-permute-start(bf16[8,2304]{1,0:T(8,128)(2,1)S(1)} %pad_maximum_fusion.9), channel_id=1, source_target_pairs={{0,3},{1,2},{2,1},{3,0},{4,7},{5,6},{6,5},{7,4},{8,11},{9,10},{10,... | collective-permute-start | bytes 110600 | tf_op jit(solution)/shard_map/ppermute | solution.py:532
  77.1 0.5 collective-permute-done.9
  77.7 3.5 %collective-permute-done.10 = bf16[8,2304]{1,0:T(8,128)(2,1)S(1)} collective-permute-done((bf16[8,2304]{1,0:T(8,128)(2,1)S(1)}, bf16[8,2304]{1,0:T(8,128)(2,1)S(1)}, u32[]{:S(2)}, u32[]{:S(2)}) %collective-permute-start.10) | collective-permute-done | bytes 36896 | tf_op jit(solution)/shard_map/ppermute | solution.py:532
  81.4 2.1 %collective-permute-start.11 = (bf16[8,2688]{1,0:T(8,128)(2,1)S(1)}, bf16[8,2688]{1,0:T(8,128)(2,1)S(1)}, u32[]{:S(2)}, u32[]{:S(2)}) collective-permute-start(bf16[8,2688]{1,0:T(8,128)(2,1)S(1)} %constant_dynamic-update-slice_fusion), channel_id=1, source_target_pairs={{0,3},{1,2},{2,1},{3,0},{4,7},{5,6},{6,5},{7,4},{8,11},{9,10},{10,... | collective-permute-start | bytes 129032 | tf_op jit(solution)/shard_map/ppermute | solution.py:532
  83.5 2.4 %collective-permute-start.13 = (bf16[8,2688]{1,0:T(8,128)(2,1)S(1)}, bf16[8,2688]{1,0:T(8,128)(2,1)S(1)}, u32[]{:S(2)}, u32[]{:S(2)}) collective-permute-start(bf16[8,2688]{1,0:T(8,128)(2,1)S(1)} %constant_dynamic-update-slice_fusion), channel_id=1, source_target_pairs={{0,1},{1,0},{2,3},{3,2},{4,5},{5,4},{6,7},{7,6},{8,9},{9,8},{10,11... | collective-permute-start | bytes 129032 | tf_op jit(solution)/shard_map/ppermute | solution.py:532
  85.9 1.4 %collective-permute-done.11 = bf16[8,2688]{1,0:T(8,128)(2,1)S(1)} collective-permute-done((bf16[8,2688]{1,0:T(8,128)(2,1)S(1)}, bf16[8,2688]{1,0:T(8,128)(2,1)S(1)}, u32[]{:S(2)}, u32[]{:S(2)}) %collective-permute-start.11) | collective-permute-done | bytes 43040 | tf_op jit(solution)/shard_map/ppermute | solution.py:532
  87.3 1.1 %collective-permute-done.12 = bf16[8,2688]{1,0:T(8,128)(2,1)S(1)} collective-permute-done((bf16[8,2688]{1,0:T(8,128)(2,1)S(1)}, bf16[8,2688]{1,0:T(8,128)(2,1)S(1)}, u32[]{:S(2)}, u32[]{:S(2)}) %collective-permute-start.12) | collective-permute-done | bytes 43040 | tf_op jit(solution)/shard_map/ppermute | solution.py:532
  88.8 2.5 %collective-permute-start.14 = (bf16[8,3456]{1,0:T(8,128)(2,1)S(1)}, bf16[8,3456]{1,0:T(8,128)(2,1)S(1)}, u32[]{:S(2)}, u32[]{:S(2)}) collective-permute-start(bf16[8,3456]{1,0:T(8,128)(2,1)S(1)} %get-tuple-element.126), channel_id=1, source_target_pairs={{0,20},{4,16},{8,28},{12,24},{16,4},{20,0},{24,12},{28,8},{1,21},{... | collective-permute-start | bytes 165896 | tf_op jit(solution)/shard_map/ppermute | solution.py:532
  91.3 0.5 collective-permute-start.15
  91.8 0.5 collective-permute-start.16
  92.4 3.1 %collective-permute-done.15 = bf16[8,3456]{1,0:T(8,128)(2,1)S(1)} collective-permute-done((bf16[8,3456]{1,0:T(8,128)(2,1)S(1)}, bf16[8,3456]{1,0:T(8,128)(2,1)S(1)}, u32[]{:S(2)}, u32[]{:S(2)}) %collective-permute-start.15) | collective-permute-done | bytes 55328 | tf_op jit(solution)/shard_map/ppermute | solution.py:532
  95.5 1.6 %collective-permute-done.16 = bf16[8,9600]{1,0:T(8,128)(2,1)S(1)} collective-permute-done((bf16[8,9600]{1,0:T(8,128)(2,1)S(1)}, bf16[8,9600]{1,0:T(8,128)(2,1)S(1)}, u32[]{:S(2)}, u32[]{:S(2)}) %collective-permute-start.16) | collective-permute-done | bytes 153632 | tf_op jit(solution)/shard_map/ppermute | solution.py:532
  97.5 1.7 %collective-permute-done.17.got_ref = bf16[8,24960]{1,0:T(8,128)(2,1)S(1)} collective-permute-done((bf16[8,24960]{1,0:T(8,128)(2,1)S(1)}, bf16[8,24960]{1,0:T(8,128)(2,1)S(1)}, u32[]{:S(2)}, u32[]{:S(2)}) %collective-permute-start.17) | collective-permute-done | bytes 399392 | tf_op jit(solution)/shard_map/ppermute | solution.py:707
  99.1 1.4 %finish.1 = (f32[64,3072]{1,0:T(8,128)}, f32[64,3072]{1,0:T(8,128)}, f32[1,1]{1,0:T(1,128)}) custom-call(s32[1]{0:T(128)} %bitcast.where_ref.side_ref, bf16[32,3072]{1,0:T(8,128)(2,1)S(1)} %pad_maximum_fusion.a_ref, bf16[32,3072]{1,0:T(8,128)(2,1)S(1)} %pad_maximum_fusion.1.b_ref, f32[8,128]{1,0:T(8,128)S(1)} %get-tuple-element.60.sums_ref, ...), custom_call_target="tpu_custom_call" | custom-call | tf_op jit(solution)/shard_map/finish/pallas_call | solution.py:491
  (90 shorter events, 3.4 us)
Async XLA Ops:
  4.1 16.5 %collective-permute-start = (f32[2,6144]{1,0:T(2,128)S(1)}, f32[2,6144]{1,0:T(2,128)S(1)}, u32[]{:S(2)}, u32[]{:S(2)}) collective-permute-start(f32[2,6144]{1,0:T(2,128)S(1)} %modulation.1.after_ref), channel_id=1, source_target_pairs={{0,4},{4,0},{1,5},{5,1},{2,6},{6,2},{3,7},{7,3},{8,12},{12,8},{9,1... | collective-permute-start | bytes 147464 | tf_op jit(solution)/shard_map/ppermute | solution.py:506
  8.6 31.3 %collective-permute-start.1 = (bf16[80,3072]{1,0:T(8,128)(2,1)S(1)}, bf16[80,3072]{1,0:T(8,128)(2,1)S(1)}, u32[]{:S(2)}, u32[]{:S(2)}) collective-permute-start(bf16[80,3072]{1,0:T(8,128)(2,1)S(1)} %noisy.1.after_ref.tokens), channel_id=1, source_target_pairs={{0,4},{4,0},{1,5},{5,1},{2,6},{6,2},{3,7},{7,3},{8,12},{12,8},{9,1... | collective-permute-start | bytes 1474568 | tf_op jit(solution)/shard_map/ppermute | solution.py:506
  11.4 6.5 %copy-start = (bf16[3072,3072]{1,0:T(8,128)(2,1)}, bf16[3072,3072]{1,0:T(8,128)(2,1)S(1)}, u32[]{:S(2)}) copy-start(bf16[3072,3072]{1,0:T(8,128)(2,1)S(1)} %get-tuple-element.34.refs_0_) | copy-start | bytes 56623108
  17.9 34.4 %collective-permute-start.2 = (bf16[48,3072]{1,0:T(8,128)(2,1)S(1)}, bf16[48,3072]{1,0:T(8,128)(2,1)S(1)}, u32[]{:S(2)}, u32[]{:S(2)}) collective-permute-start(bf16[48,3072]{1,0:T(8,128)(2,1)S(1)} %get-tuple-element.46.refs_0_), channel_id=1, source_target_pairs={{0,4},{4,0},{1,5},{5,1},{2,6},{6,2},{3,7},{7,3},{8,12},{12,8},{9,1... | collective-permute-start | bytes 884744 | tf_op jit(solution)/shard_map/ppermute | solution.py:506
  20.8 6.4 %copy-start.1 = (bf16[3072,3072]{1,0:T(8,128)(2,1)S(1)}, bf16[3072,3072]{1,0:T(8,128)(2,1)}, u32[]{:S(2)}) copy-start(bf16[3072,3072]{1,0:T(8,128)(2,1)} %copy-done) | copy-start | bytes 56623108
  33.4 6.5 %copy-start.2 = (bf16[3072,3072]{1,0:T(8,128)(2,1)}, bf16[3072,3072]{1,0:T(8,128)(2,1)S(1)}, u32[]{:S(2)}) copy-start(bf16[3072,3072]{1,0:T(8,128)(2,1)S(1)} %get-tuple-element.35.w_ref) | copy-start | bytes 56623108
  39.9 6.4 %copy-start.3 = (bf16[3072,3072]{1,0:T(8,128)(2,1)S(1)}, bf16[3072,3072]{1,0:T(8,128)(2,1)}, u32[]{:S(2)}) copy-start(bf16[3072,3072]{1,0:T(8,128)(2,1)} %copy-done.2) | copy-start | bytes 56623108
  63.7 1.5 %collective-permute-start.4 = (bf16[32,3072]{1,0:T(8,128)(2,1)S(1)}, bf16[32,3072]{1,0:T(8,128)(2,1)S(1)}, u32[]{:S(2)}, u32[]{:S(2)}) collective-permute-start(bf16[32,3072]{1,0:T(8,128)(2,1)S(1)} %get-tuple-element.54), channel_id=1, source_target_pairs={{0,8},{8,0},{16,24},{24,16},{1,9},{9,1},{17,25},{25,17},{2,10},{10... | collective-permute-start | bytes 589832 | tf_op jit(solution)/shard_map/ppermute | solution.py:531
  63.8 1.7 %collective-permute-start.3 = (bf16[32,3072]{1,0:T(8,128)(2,1)S(1)}, bf16[32,3072]{1,0:T(8,128)(2,1)S(1)}, u32[]{:S(2)}, u32[]{:S(2)}) collective-permute-start(bf16[32,3072]{1,0:T(8,128)(2,1)S(1)} %get-tuple-element.52), channel_id=1, source_target_pairs={{0,8},{8,0},{16,24},{24,16},{1,9},{9,1},{17,25},{25,17},{2,10},{10... | collective-permute-start | bytes 589832 | tf_op jit(solution)/shard_map/ppermute | solution.py:531
  65.6 6.6 %collective-permute-start.5 = (bf16[8,9216]{1,0:T(8,128)(2,1)S(1)}, bf16[8,9216]{1,0:T(8,128)(2,1)S(1)}, u32[]{:S(2)}, u32[]{:S(2)}) collective-permute-start(bf16[8,9216]{1,0:T(8,128)(2,1)S(1)} %pad_maximum_fusion.2), channel_id=1, source_target_pairs={{0,16},{4,20},{8,24},{12,28},{16,0},{20,4},{24,8},{28,12},{1,17},{... | collective-permute-start | bytes 442376 | tf_op jit(solution)/shard_map/ppermute | solution.py:532
  67.1 5.1 %collective-permute-start.6 = (bf16[8,3072]{1,0:T(8,128)(2,1)S(1)}, bf16[8,3072]{1,0:T(8,128)(2,1)S(1)}, u32[]{:S(2)}, u32[]{:S(2)}) collective-permute-start(bf16[8,3072]{1,0:T(8,128)(2,1)S(1)} %get-tuple-element.83), channel_id=1, source_target_pairs={{0,4},{4,0},{8,12},{12,8},{16,20},{20,16},{24,28},{28,24},{1,5},{5... | collective-permute-start | bytes 147464 | tf_op jit(solution)/shard_map/ppermute | solution.py:531
  67.6 5.0 %collective-permute-start.7 = (bf16[8,3072]{1,0:T(8,128)(2,1)S(1)}, bf16[8,3072]{1,0:T(8,128)(2,1)S(1)}, u32[]{:S(2)}, u32[]{:S(2)}) collective-permute-start(bf16[8,3072]{1,0:T(8,128)(2,1)S(1)} %get-tuple-element.84), channel_id=1, source_target_pairs={{0,20},{4,16},{8,28},{12,24},{16,4},{20,0},{24,12},{28,8},{1,21},{... | collective-permute-start | bytes 147464 | tf_op jit(solution)/shard_map/ppermute | solution.py:531
  72.7 4.9 %collective-permute-start.9 = (bf16[8,2304]{1,0:T(8,128)(2,1)S(1)}, bf16[8,2304]{1,0:T(8,128)(2,1)S(1)}, u32[]{:S(2)}, u32[]{:S(2)}) collective-permute-start(bf16[8,2304]{1,0:T(8,128)(2,1)S(1)} %pad_maximum_fusion.8), channel_id=1, source_target_pairs={{0,2},{1,3},{2,0},{3,1},{4,6},{5,7},{6,4},{7,5},{8,10},{9,11},{10,... | collective-permute-start | bytes 110600 | tf_op jit(solution)/shard_map/ppermute | solution.py:532
  75.4 5.8 %collective-permute-start.10 = (bf16[8,2304]{1,0:T(8,128)(2,1)S(1)}, bf16[8,2304]{1,0:T(8,128)(2,1)S(1)}, u32[]{:S(2)}, u32[]{:S(2)}) collective-permute-start(bf16[8,2304]{1,0:T(8,128)(2,1)S(1)} %pad_maximum_fusion.9), channel_id=1, source_target_pairs={{0,3},{1,2},{2,1},{3,0},{4,7},{5,6},{6,5},{7,4},{8,11},{9,10},{10,... | collective-permute-start | bytes 110600 | tf_op jit(solution)/shard_map/ppermute | solution.py:532
  76.8 4.4 %collective-permute-start.8 = (bf16[8,2304]{1,0:T(8,128)(2,1)S(1)}, bf16[8,2304]{1,0:T(8,128)(2,1)S(1)}, u32[]{:S(2)}, u32[]{:S(2)}) collective-permute-start(bf16[8,2304]{1,0:T(8,128)(2,1)S(1)} %pad_maximum_fusion.7), channel_id=1, source_target_pairs={{0,1},{1,0},{2,3},{3,2},{4,5},{5,4},{6,7},{7,6},{8,9},{9,8},{10,11... | collective-permute-start | bytes 110600 | tf_op jit(solution)/shard_map/ppermute | solution.py:532
  81.4 5.9 %collective-permute-start.11 = (bf16[8,2688]{1,0:T(8,128)(2,1)S(1)}, bf16[8,2688]{1,0:T(8,128)(2,1)S(1)}, u32[]{:S(2)}, u32[]{:S(2)}) collective-permute-start(bf16[8,2688]{1,0:T(8,128)(2,1)S(1)} %constant_dynamic-update-slice_fusion), channel_id=1, source_target_pairs={{0,3},{1,2},{2,1},{3,0},{4,7},{5,6},{6,5},{7,4},{8,11},{9,10},{10,... | collective-permute-start | bytes 129032 | tf_op jit(solution)/shard_map/ppermute | solution.py:532
  83.5 4.9 %collective-permute-start.12 = (bf16[8,2688]{1,0:T(8,128)(2,1)S(1)}, bf16[8,2688]{1,0:T(8,128)(2,1)S(1)}, u32[]{:S(2)}, u32[]{:S(2)}) collective-permute-start(bf16[8,2688]{1,0:T(8,128)(2,1)S(1)} %constant_dynamic-update-slice_fusion), channel_id=1, source_target_pairs={{0,2},{1,3},{2,0},{3,1},{4,6},{5,7},{6,4},{7,5},{8,10},{9,11},{10,... | collective-permute-start | bytes 129032 | tf_op jit(solution)/shard_map/ppermute | solution.py:532
  83.5 4.9 %collective-permute-start.13 = (bf16[8,2688]{1,0:T(8,128)(2,1)S(1)}, bf16[8,2688]{1,0:T(8,128)(2,1)S(1)}, u32[]{:S(2)}, u32[]{:S(2)}) collective-permute-start(bf16[8,2688]{1,0:T(8,128)(2,1)S(1)} %constant_dynamic-update-slice_fusion), channel_id=1, source_target_pairs={{0,1},{1,0},{2,3},{3,2},{4,5},{5,4},{6,7},{7,6},{8,9},{9,8},{10,11... | collective-permute-start | bytes 129032 | tf_op jit(solution)/shard_map/ppermute | solution.py:532
  88.8 6.7 %collective-permute-start.14 = (bf16[8,3456]{1,0:T(8,128)(2,1)S(1)}, bf16[8,3456]{1,0:T(8,128)(2,1)S(1)}, u32[]{:S(2)}, u32[]{:S(2)}) collective-permute-start(bf16[8,3456]{1,0:T(8,128)(2,1)S(1)} %get-tuple-element.126), channel_id=1, source_target_pairs={{0,20},{4,16},{8,28},{12,24},{16,4},{20,0},{24,12},{28,8},{1,21},{... | collective-permute-start | bytes 165896 | tf_op jit(solution)/shard_map/ppermute | solution.py:532
  91.3 4.2 %collective-permute-start.15 = (bf16[8,3456]{1,0:T(8,128)(2,1)S(1)}, bf16[8,3456]{1,0:T(8,128)(2,1)S(1)}, u32[]{:S(2)}, u32[]{:S(2)}) collective-permute-start(bf16[8,3456]{1,0:T(8,128)(2,1)S(1)} %get-tuple-element.126), channel_id=1, source_target_pairs={{0,4},{4,0},{8,12},{12,8},{16,20},{20,16},{24,28},{28,24},{1,5},{5... | collective-permute-start | bytes 165896 | tf_op jit(solution)/shard_map/ppermute | solution.py:532
  91.8 5.2 %collective-permute-start.16 = (bf16[8,9600]{1,0:T(8,128)(2,1)S(1)}, bf16[8,9600]{1,0:T(8,128)(2,1)S(1)}, u32[]{:S(2)}, u32[]{:S(2)}) collective-permute-start(bf16[8,9600]{1,0:T(8,128)(2,1)S(1)} %constant_dynamic-update-slice_fusion.13), channel_id=1, source_target_pairs={{0,16},{4,20},{8,24},{12,28},{16,0},{20,4},{24,8},{28,12},{1,17},{... | collective-permute-start | bytes 460808 | tf_op jit(solution)/shard_map/ppermute | solution.py:532
  97.3 1.8 %collective-permute-start.17 = (bf16[8,24960]{1,0:T(8,128)(2,1)S(1)}, bf16[8,24960]{1,0:T(8,128)(2,1)S(1)}, u32[]{:S(2)}, u32[]{:S(2)}) collective-permute-start(bf16[8,24960]{1,0:T(8,128)(2,1)S(1)} %constant_dynamic-update-slice_fusion.22), channel_id=1, source_target_pairs={{0,8},{8,0},{16,24},{24,16},{1,9},{9,1},{17,25},{25,17},{2,10},{10... | collective-permute-start | bytes 1198088 | tf_op jit(solution)/shard_map/ppermute | solution.py:707

commit v10 on v7

--- a/solution.py
+++ b/solution.py
@@ -17,13 +17,6 @@
 ROOT = 1.0 / math.sqrt(HD)
 LOG2E = 1.0 / math.log(2.0)
 SMALL = 10 * 1024 * 1024
-
-
-def timing(value, width):
-    count = width // 4
-    freqs = jnp.exp(-math.log(10000.0) * jnp.arange(count, dtype=F32) / count)
-    angles = 1000.0 * value * freqs
-    return jnp.concatenate([jnp.cos(angles), jnp.sin(angles)])
 
 
 def nn(a, b):
@@ -169,7 +162,7 @@
             pltpu.make_async_copy(g, s, small_sems.at[i]) for i, (g, s) in enumerate(zip(given, small))
         ]
         gain_ref, down_ref, up_ref = small
-        for copy in fetched + fetches(w_ref, weights, sems):
+        for copy in fetched + fetches(w_ref, weights, sems)[:2]:
             copy.start()
     else:
         (hi,) = rest
@@ -187,6 +180,12 @@
         columns = pl.ds(pl.multiple_of(step * cols, cols), cols)
         if first:
             pltpu.make_async_copy(w_ref.at[:, columns], weights.at[:, columns], sems.at[step]).wait()
+
+            @pl.when(step + 2 < w_ref.shape[1] // cols)
+            def _():
+                later = pl.ds(pl.multiple_of((step + 2) * cols, cols), cols)
+                pltpu.make_async_copy(w_ref.at[:, later], weights.at[:, later], sems.at[step + 2]).start()
+
         out = nn(hi[...], weights[:, columns])
         student = out[rows:] + nn(low_ref[part, :], up_ref[:, columns])
         for j in range(pair):
@@ -371,55 +370,73 @@
     )(where, bias, gain, up, q, k, v, x, kt, vt, low, hs)
 
 
-def modulation_kernel(emb_ref, weight_ref, part_ref):
-    part_ref[...] = nn(emb_ref[...], weight_ref[...])[: part_ref.shape[0]]
-
-
-def modulation(emb, weight):
+def noise_level(step_ref, shape):
+    return (jnp.full(shape, step_ref[0], jnp.int32).astype(F32) + 1.0) / STEPS
+
+
+def embedding(value):
+    count = value.shape[1] // 2
+    lane = lax.broadcasted_iota(jnp.int32, value.shape, 1)
+    place = lax.rem(lane, count).astype(F32)
+    angles = 1000.0 * value * jnp.exp(-math.log(10000.0) * place / count)
+    wave = jnp.where(lane < count, jnp.cos(angles), jnp.sin(angles))
+    return wave / (1.0 + jnp.exp(-wave))
+
+
+def modulation_kernel(step_ref, guidance_ref, weight_ref, part_ref, emb):
+    @pl.when(pl.program_id(0) == 0)
+    def _():
+        half = emb.shape[1] // 2
+        time = embedding(noise_level(step_ref, (1, half)))
+        guide = embedding(jnp.full((1, half), guidance_ref[0], F32))
+        row = lax.broadcasted_iota(jnp.int32, (emb.shape[0], half), 0)
+        emb[:, :half] = jnp.where(row >= 0, time, 0.0).astype(BF16)
+        emb[:, half:] = jnp.where(row == 0, guide, 0.0).astype(BF16)
+
+    part_ref[...] = nn(emb[...], weight_ref[...])[: part_ref.shape[0]]
+
+
+SCALAR = pl.BlockSpec(memory_space=pltpu.SMEM)
+
+
+def modulation(timestep, guidance, weight):
     depth, cols = weight.shape
     steps = 2 if cols % 256 == 0 else 1
     return pl.pallas_call(
         modulation_kernel,
         grid=(steps,),
-        in_specs=[
-            pl.BlockSpec(emb.shape, lambda s: (0, 0)),
-            pl.BlockSpec((depth, cols // steps), lambda s: (0, s)),
-        ],
+        in_specs=[SCALAR, SCALAR, pl.BlockSpec((depth, cols // steps), lambda s: (0, s))],
         out_specs=pl.BlockSpec((2, cols // steps), lambda s: (0, s)),
         out_shape=jax.ShapeDtypeStruct((2, cols), F32),
+        scratch_shapes=[pltpu.VMEM((16, depth), BF16)],
         compiler_params=params(10),
         cost_estimate=pl.CostEstimate(
             flops=4 * depth * cols, bytes_accessed=2 * weight.size, transcendentals=0
         ),
         name="modulation",
-    )(emb, held(weight))
-
-
-def noisy_kernel(sigma_ref, image_ref, noise_ref, after_ref, noisy_ref):
-    sigma = sigma_ref[0]
+    )(timestep, guidance, held(weight))
+
+
+def noisy_kernel(step_ref, image_ref, noise_ref, after_ref, noisy_ref):
+    sigma = noise_level(step_ref, (1, image_ref.shape[1]))
     clean, noise = image_ref[...].astype(F32), noise_ref[...].astype(F32)
     noisy_ref[...] = ((1.0 - sigma) * clean + sigma * noise).astype(BF16)
 
 
-def mix(sigma, image, noise, after):
+def mix(timestep, image, noise, after):
     rows, width = image.shape
     steps = 2 if width % 256 == 0 else 1
     tokens = pl.BlockSpec((rows, width // steps), lambda s: (0, s))
     return pl.pallas_call(
         noisy_kernel,
         grid=(steps,),
-        in_specs=[
-            pl.BlockSpec(memory_space=pltpu.SMEM),
-            tokens,
-            tokens,
-            pl.BlockSpec(memory_space=pl.ANY),
-        ],
+        in_specs=[SCALAR, tokens, tokens, pl.BlockSpec(memory_space=pl.ANY)],
         out_specs=tokens,
         out_shape=jax.ShapeDtypeStruct((rows, width), BF16),
         compiler_params=params(10),
-        cost_estimate=pl.CostEstimate(flops=0, bytes_accessed=0, transcendentals=0),
+        cost_estimate=pl.CostEstimate(flops=0, bytes_accessed=6 * image.size, transcendentals=0),
         name="noisy",
-    )(sigma, held(image), held(noise), after)
+    )(timestep, held(image), held(noise), after)
 
 
 def finish_kernel(scale_a, scale_b, scale_loss, side_ref, a_ref, b_ref, sums_ref, got_ref, out_a, out_b, loss_ref):
@@ -609,16 +626,10 @@
     adapter_down_weight,
     adapter_up_weight,
 ):
-    emb_width = modulation_weight.shape[0]
     n, me = lax.axis_size("seq"), lax.axis_index("seq")
     samples = lax.axis_size("grp") * lax.axis_size("dp")
-    sigma = (timestep[0].astype(F32) + 1.0) / STEPS
-    time = timing(sigma, emb_width)
-    guide = jnp.where(jnp.arange(16)[:, None] == 0, timing(guidance[0], emb_width)[None], 0.0)
-    emb = jnp.concatenate([jnp.broadcast_to(time[None], guide.shape), guide], 1)
-    emb = jax.nn.silu(emb).astype(BF16)
-    part = modulation(emb, modulation_weight)
-    noisy = mix(sigma[None], image[0], noise[0], part)
+    part = modulation(timestep, guidance, modulation_weight)
+    noisy = mix(timestep, image[0], noise[0], part)
     mods = [part] + [shifted(part, "seq", k) for k in range(1, n)]
     noisy_parts = [noisy] + [shifted(noisy, "seq", k) for k in range(1, n)]
     words = text[0]

time: 77.6 us -> 77.3 us (level)
  Pallas kernels: 32.5 us -> 30.5 us
  waiting for transfers between devices: 18.7 us -> 20.7 us
    pallas_call x2, Pallas kernels: 16.1 us -> 14.1 us  [project_image(): pl.pallas_call(functools.partial(image_kernel, pair, part, len(before)),...]
    ppermute x3, waiting for transfers between devices: 1.21 us -> 3.2 us  [shifted(): return lax.ppermute(x, axis, [(i, (i + k) % size) for i in range(size)])]
  transfers between devices with their start and end apart: 18 -> 18, of which waited for: 12 -> 12; matrix products, arithmetic and copies ran while one was open for 1% -> 1% of each run, Pallas kernels for 23% -> 20%
where the time goes in v10:
time: 77.3 us; the launch traced here: 77.1 us
  Pallas kernels  30.5 us (39%)
  starting transfers between devices  21.6 us (28%)
  waiting for transfers between devices  20.7 us (27%)
  between operations  3.05 us (4%)
  other arithmetic  1.12 us (1%)
    ppermute x10, waiting for transfers between devices, send(): return unpack(lax.ppermute(pack(arrays), group.axes, pairs), arrays)  14.3 us
    pallas_call x2, Pallas kernels, project_image(): pl.pallas_call(functools.partial(image_kernel, pair, part, len(before)),...  14.1 us
    ppermute x10, starting transfers between devices, send(): return unpack(lax.ppermute(pack(arrays), group.axes, pairs), arrays)  13.9 us
    pallas_call x1, Pallas kernels, attend(): pl.pallas_call(functools.partial(attend_kernel, steps, pair, samples), in...  5.76 us
    pallas_call x1, Pallas kernels, project_text(): pl.pallas_call(functools.partial(text_kernel, n, pair), in_specs=[VMEM, V...  5.61 us
    ppermute x3, starting transfers between devices, shifted(): return lax.ppermute(x, axis, [(i, (i + k) % size) for i in range(size)])  5.11 us
    ppermute x3, waiting for transfers between devices, shifted(): return lax.ppermute(x, axis, [(i, (i + k) % size) for i in range(size)])  3.2 us
    ppermute x4, starting transfers between devices, send(): return [lax.ppermute(x, group.axes, pairs) for x in arrays]  2.52 us
  transfers between devices with their start and end apart: 18, of which 12 were waited for; matrix products, arithmetic and copies ran while one was open for 1% of the time, Pallas kernels for 20%

profile of v10, /device:TPU:0, one launch (start us, length us, event | category | flops | bytes accessed | tf_op | source)
XLA Modules:
  0.0 77.1 jit_solution(14711697941209745224)
XLA Ops:
  1.9 2.2 %modulation.1.after_ref = f32[2,6144]{1,0:T(2,128)S(1)} custom-call(s32[1]{0:T(128)S(6)} %copy.56.step_ref, f32[1]{0:T(128)S(6)} %copy.57.guidance_ref, bf16[256,6144]{1,0:T(8,128)(2,1)} %weight_ref.1), custom_call_target="tpu_custom_call" | custom-call | flops 6291456 | bytes 3145728 | tf_op jit(solution)/shard_map/modulation/pallas_call | solution.py:405
  4.1 3.0 %collective-permute-start = (f32[2,6144]{1,0:T(2,128)S(1)}, f32[2,6144]{1,0:T(2,128)S(1)}, u32[]{:S(2)}, u32[]{:S(2)}) collective-permute-start(f32[2,6144]{1,0:T(2,128)S(1)} %modulation.1.after_ref), channel_id=1, source_target_pairs={{0,4},{4,0},{1,5},{5,1},{2,6},{6,2},{3,7},{7,3},{8,12},{12,8},{9,1... | collective-permute-start | bytes 147464 | tf_op jit(solution)/shard_map/ppermute | solution.py:489
  7.1 1.4 %noisy.1.tokens = bf16[80,3072]{1,0:T(8,128)(2,1)S(1)} custom-call(s32[1]{0:T(128)S(6)} %copy.56.step_ref, bf16[80,3072]{1,0:T(8,128)(2,1)} %bitcast.18, bf16[80,3072]{1,0:T(8,128)(2,1)} %bitcast.19, f32[2,6144]{1,0:T(2,128)S(1)} %modulation.1.after_ref), custom_call_target="tpu_custom_call" | custom-call | bytes 1474560 | tf_op jit(solution)/shard_map/noisy/pallas_call | solution.py:430
  8.7 2.0 %collective-permute-start.2 = (bf16[48,3072]{1,0:T(8,128)(2,1)}, bf16[48,3072]{1,0:T(8,128)(2,1)S(1)}, u32[]{:S(2)}, u32[]{:S(2)}) collective-permute-start(bf16[48,3072]{1,0:T(8,128)(2,1)} %bitcast.16), channel_id=1, source_target_pairs={{0,4},{4,0},{1,5},{5,1},{2,6},{6,2},{3,7},{7,3},{8,12},{12,8},{9,1... | collective-permute-start | bytes 884744 | tf_op jit(solution)/shard_map/ppermute | solution.py:489
  11.5 8.0 %project_image.2 = (bf16[8,2,160,128]{3,2,1,0:T(8,128)(2,1)S(1)}, bf16[8,2,160,128]{3,2,1,0:T(8,128)(2,1)S(1)}, bf16[8,2,160,128]{3,2,1,0:T(8,128)(2,1)S(1)}, f3...) custom-call(f32[2,12288]{1,0:T(2,128)S(1)} %pad_maximum_fusion.3.mod, ...), custom_call_target="tpu_custom_call" | custom-call | flops 3019898880 | bytes 18874368 | tf_op jit(solution)/shard_map/project_image/pallas_call | solution.py:217
  19.6 3.2 %collective-permute-done.1.tokens = bf16[80,3072]{1,0:T(8,128)(2,1)S(1)} collective-permute-done((bf16[80,3072]{1,0:T(8,128)(2,1)S(1)}, bf16[80,3072]{1,0:T(8,128)(2,1)S(1)}, u32[]{:S(2)}, u32[]{:S(2)}) %collective-permute-start.1) | collective-permute-done | bytes 491552 | tf_op jit(solution)/shard_map/ppermute | solution.py:489
  22.8 6.0 %project_image.3 = (bf16[8,2,160,128]{3,2,1,0:T(8,128)(2,1)S(1)}, bf16[8,2,160,128]{3,2,1,0:T(8,128)(2,1)S(1)}, bf16[8,2,160,128]{3,2,1,0:T(8,128)(2,1)S(1)}, f3...) custom-call(f32[2,12288]{1,0:T(2,128)S(1)} %pad_maximum_fusion.3.mod, ...), custom_call_target="tpu_custom_call", output_to_operand_aliasing={{0}: (6, {}), {1}: (7, {}), {2}: (8, {}), {3}: (9, {}), {4}... | custom-call | flops 3019898880 | bytes 18874368 | tf_op jit(solution)/shard_map/project_image/pallas_call | solution.py:217
  28.9 5.6 %project_text.1 = (bf16[8,2,96,128]{3,2,1,0:T(8,128)(2,1)S(1)}, bf16[8,2,96,128]{3,2,1,0:T(8,128)(2,1)S(1)}) custom-call(f32[2,12288]{1,0:T(2,128)S(1)} %pad_maximum_fusion.3.mod_ref, f32[3,128]{1,0:T(4,128)S(1)} %get-tuple-element.29.gain_ref, bf16[3072,2048]{1,0:T(8,128)(2,1)} %w_ref.3, bf16[8,2,160,128]{3,2,1,0:T(8,128)(2,1)S(1)} %get-tuple-element.39.after_ref.q_ref, ...), custom_call_target="tpu_custom_call" | custom-call | flops 2415919104 | bytes 12582912 | tf_op jit(solution)/shard_map/project_text/pallas_call | solution.py:136
  34.5 5.8 %attend.1 = (bf16[32,3072]{1,0:T(8,128)(2,1)S(1)}, f32[32,3072]{1,0:T(8,128)S(1)}, bf16[32,3072]{1,0:T(8,128)(2,1)S(1)}, f32[32,3072]{1,0:T(8,128)S(1)}, f32[8,128]{1,0:T(8,128)S(1)}) custom-call(s32[1]{0:T(128)} %bitcast.where_ref.side_ref, f32[1,256]{1,0:T(1,128)S(1)} %compare_select_fusion.bias_ref, f32[3,128]{1,0:T(4,128)S(1)} %get-tuple-element.29.gain_ref, ...), custom_call_target="tpu_custom_call" | custom-call | flops 671088640 | bytes 8000000 | tf_op jit(solution)/shard_map/attend/pallas_call | solution.py:342
  40.4 0.5 collective-permute-start.3
  40.8 0.9 %collective-permute-done.4 = bf16[32,3072]{1,0:T(8,128)(2,1)S(1)} collective-permute-done((bf16[32,3072]{1,0:T(8,128)(2,1)S(1)}, bf16[32,3072]{1,0:T(8,128)(2,1)S(1)}, u32[]{:S(2)}, u32[]{:S(2)}) %collective-permute-start.4) | collective-permute-done | bytes 196640 | tf_op jit(solution)/shard_map/ppermute | solution.py:514
  42.1 1.6 %collective-permute-start.5 = (bf16[8,9216]{1,0:T(8,128)(2,1)S(1)}, bf16[8,9216]{1,0:T(8,128)(2,1)S(1)}, u32[]{:S(2)}, u32[]{:S(2)}) collective-permute-start(bf16[8,9216]{1,0:T(8,128)(2,1)S(1)} %pad_maximum_fusion.2), channel_id=1, source_target_pairs={{0,16},{4,20},{8,24},{12,28},{16,0},{20,4},{24,8},{28,12},{1,17},{... | collective-permute-start | bytes 442376 | tf_op jit(solution)/shard_map/ppermute | solution.py:515
  43.7 0.5 collective-permute-start.6
  44.2 1.5 %collective-permute-start.7 = (bf16[8,3072]{1,0:T(8,128)(2,1)S(1)}, bf16[8,3072]{1,0:T(8,128)(2,1)S(1)}, u32[]{:S(2)}, u32[]{:S(2)}) collective-permute-start(bf16[8,3072]{1,0:T(8,128)(2,1)S(1)} %get-tuple-element.80), channel_id=1, source_target_pairs={{0,20},{4,16},{8,28},{12,24},{16,4},{20,0},{24,12},{28,8},{1,21},{... | collective-permute-start | bytes 147464 | tf_op jit(solution)/shard_map/ppermute | solution.py:514
  45.7 3.0 %collective-permute-done.5 = bf16[8,9216]{1,0:T(8,128)(2,1)S(1)} collective-permute-done((bf16[8,9216]{1,0:T(8,128)(2,1)S(1)}, bf16[8,9216]{1,0:T(8,128)(2,1)S(1)}, u32[]{:S(2)}, u32[]{:S(2)}) %collective-permute-start.5) | collective-permute-done | bytes 147488 | tf_op jit(solution)/shard_map/ppermute | solution.py:515
  48.8 0.4 collective-permute-done.7
  49.3 2.7 %collective-permute-start.9 = (bf16[8,2304]{1,0:T(8,128)(2,1)S(1)}, bf16[8,2304]{1,0:T(8,128)(2,1)S(1)}, u32[]{:S(2)}, u32[]{:S(2)}) collective-permute-start(bf16[8,2304]{1,0:T(8,128)(2,1)S(1)} %pad_maximum_fusion.8), channel_id=1, source_target_pairs={{0,2},{1,3},{2,0},{3,1},{4,6},{5,7},{6,4},{7,5},{8,10},{9,11},{10,... | collective-permute-start | bytes 110600 | tf_op jit(solution)/shard_map/ppermute | solution.py:515
  52.0 1.3 %collective-permute-start.10 = (bf16[8,2304]{1,0:T(8,128)(2,1)S(1)}, bf16[8,2304]{1,0:T(8,128)(2,1)S(1)}, u32[]{:S(2)}, u32[]{:S(2)}) collective-permute-start(bf16[8,2304]{1,0:T(8,128)(2,1)S(1)} %pad_maximum_fusion.9), channel_id=1, source_target_pairs={{0,3},{1,2},{2,1},{3,0},{4,7},{5,6},{6,5},{7,4},{8,11},{9,10},{10,... | collective-permute-start | bytes 110600 | tf_op jit(solution)/shard_map/ppermute | solution.py:515
  53.3 0.3 collective-permute-start.8
  53.7 0.5 collective-permute-done.9
  54.2 3.5 %collective-permute-done.10 = bf16[8,2304]{1,0:T(8,128)(2,1)S(1)} collective-permute-done((bf16[8,2304]{1,0:T(8,128)(2,1)S(1)}, bf16[8,2304]{1,0:T(8,128)(2,1)S(1)}, u32[]{:S(2)}, u32[]{:S(2)}) %collective-permute-start.10) | collective-permute-done | bytes 36896 | tf_op jit(solution)/shard_map/ppermute | solution.py:515
  58.0 2.1 %collective-permute-start.11 = (bf16[8,2688]{1,0:T(8,128)(2,1)S(1)}, bf16[8,2688]{1,0:T(8,128)(2,1)S(1)}, u32[]{:S(2)}, u32[]{:S(2)}) collective-permute-start(bf16[8,2688]{1,0:T(8,128)(2,1)S(1)} %constant_dynamic-update-slice_fusion), channel_id=1, source_target_pairs={{0,3},{1,2},{2,1},{3,0},{4,7},{5,6},{6,5},{7,4},{8,11},{9,10},{10,... | collective-permute-start | bytes 129032 | tf_op jit(solution)/shard_map/ppermute | solution.py:515
  60.1 2.4 %collective-permute-start.13 = (bf16[8,2688]{1,0:T(8,128)(2,1)S(1)}, bf16[8,2688]{1,0:T(8,128)(2,1)S(1)}, u32[]{:S(2)}, u32[]{:S(2)}) collective-permute-start(bf16[8,2688]{1,0:T(8,128)(2,1)S(1)} %constant_dynamic-update-slice_fusion), channel_id=1, source_target_pairs={{0,1},{1,0},{2,3},{3,2},{4,5},{5,4},{6,7},{7,6},{8,9},{9,8},{10,11... | collective-permute-start | bytes 129032 | tf_op jit(solution)/shard_map/ppermute | solution.py:515
  62.5 1.4 %collective-permute-done.11 = bf16[8,2688]{1,0:T(8,128)(2,1)S(1)} collective-permute-done((bf16[8,2688]{1,0:T(8,128)(2,1)S(1)}, bf16[8,2688]{1,0:T(8,128)(2,1)S(1)}, u32[]{:S(2)}, u32[]{:S(2)}) %collective-permute-start.11) | collective-permute-done | bytes 43040 | tf_op jit(solution)/shard_map/ppermute | solution.py:515
  63.9 1.1 %collective-permute-done.12 = bf16[8,2688]{1,0:T(8,128)(2,1)S(1)} collective-permute-done((bf16[8,2688]{1,0:T(8,128)(2,1)S(1)}, bf16[8,2688]{1,0:T(8,128)(2,1)S(1)}, u32[]{:S(2)}, u32[]{:S(2)}) %collective-permute-start.12) | collective-permute-done | bytes 43040 | tf_op jit(solution)/shard_map/ppermute | solution.py:515
  65.3 2.5 %collective-permute-start.14 = (bf16[8,3456]{1,0:T(8,128)(2,1)S(1)}, bf16[8,3456]{1,0:T(8,128)(2,1)S(1)}, u32[]{:S(2)}, u32[]{:S(2)}) collective-permute-start(bf16[8,3456]{1,0:T(8,128)(2,1)S(1)} %get-tuple-element.122), channel_id=1, source_target_pairs={{0,20},{4,16},{8,28},{12,24},{16,4},{20,0},{24,12},{28,8},{1,21},{... | collective-permute-start | bytes 165896 | tf_op jit(solution)/shard_map/ppermute | solution.py:515
  67.9 0.5 collective-permute-start.15
  68.4 0.5 collective-permute-start.16
  68.9 3.1 %collective-permute-done.15 = bf16[8,3456]{1,0:T(8,128)(2,1)S(1)} collective-permute-done((bf16[8,3456]{1,0:T(8,128)(2,1)S(1)}, bf16[8,3456]{1,0:T(8,128)(2,1)S(1)}, u32[]{:S(2)}, u32[]{:S(2)}) %collective-permute-start.15) | collective-permute-done | bytes 55328 | tf_op jit(solution)/shard_map/ppermute | solution.py:515
  72.0 1.6 %collective-permute-done.16 = bf16[8,9600]{1,0:T(8,128)(2,1)S(1)} collective-permute-done((bf16[8,9600]{1,0:T(8,128)(2,1)S(1)}, bf16[8,9600]{1,0:T(8,128)(2,1)S(1)}, u32[]{:S(2)}, u32[]{:S(2)}) %collective-permute-start.16) | collective-permute-done | bytes 153632 | tf_op jit(solution)/shard_map/ppermute | solution.py:515
  74.0 1.7 %collective-permute-done.17.got_ref = bf16[8,24960]{1,0:T(8,128)(2,1)S(1)} collective-permute-done((bf16[8,24960]{1,0:T(8,128)(2,1)S(1)}, bf16[8,24960]{1,0:T(8,128)(2,1)S(1)}, u32[]{:S(2)}, u32[]{:S(2)}) %collective-permute-start.17) | collective-permute-done | bytes 399392 | tf_op jit(solution)/shard_map/ppermute | solution.py:686
  75.7 1.4 %finish.1 = (f32[64,3072]{1,0:T(8,128)}, f32[64,3072]{1,0:T(8,128)}, f32[1,1]{1,0:T(1,128)}) custom-call(s32[1]{0:T(128)} %bitcast.where_ref.side_ref, bf16[32,3072]{1,0:T(8,128)(2,1)S(1)} %pad_maximum_fusion.a_ref, bf16[32,3072]{1,0:T(8,128)(2,1)S(1)} %pad_maximum_fusion.1.b_ref, f32[8,128]{1,0:T(8,128)S(1)} %get-tuple-element.56.sums_ref, ...), custom_call_target="tpu_custom_call" | custom-call | tf_op jit(solution)/shard_map/finish/pallas_call | solution.py:474
  (83 shorter events, 1.7 us)
Async XLA Ops:
  4.1 7.3 %collective-permute-start = (f32[2,6144]{1,0:T(2,128)S(1)}, f32[2,6144]{1,0:T(2,128)S(1)}, u32[]{:S(2)}, u32[]{:S(2)}) collective-permute-start(f32[2,6144]{1,0:T(2,128)S(1)} %modulation.1.after_ref), channel_id=1, source_target_pairs={{0,4},{4,0},{1,5},{5,1},{2,6},{6,2},{3,7},{7,3},{8,12},{12,8},{9,1... | collective-permute-start | bytes 147464 | tf_op jit(solution)/shard_map/ppermute | solution.py:489
  8.6 14.2 %collective-permute-start.1 = (bf16[80,3072]{1,0:T(8,128)(2,1)S(1)}, bf16[80,3072]{1,0:T(8,128)(2,1)S(1)}, u32[]{:S(2)}, u32[]{:S(2)}) collective-permute-start(bf16[80,3072]{1,0:T(8,128)(2,1)S(1)} %noisy.1.tokens), channel_id=1, source_target_pairs={{0,4},{4,0},{1,5},{5,1},{2,6},{6,2},{3,7},{7,3},{8,12},{12,8},{9,1... | collective-permute-start | bytes 1474568 | tf_op jit(solution)/shard_map/ppermute | solution.py:489
  8.7 20.2 %collective-permute-start.2 = (bf16[48,3072]{1,0:T(8,128)(2,1)}, bf16[48,3072]{1,0:T(8,128)(2,1)S(1)}, u32[]{:S(2)}, u32[]{:S(2)}) collective-permute-start(bf16[48,3072]{1,0:T(8,128)(2,1)} %bitcast.16), channel_id=1, source_target_pairs={{0,4},{4,0},{1,5},{5,1},{2,6},{6,2},{3,7},{7,3},{8,12},{12,8},{9,1... | collective-permute-start | bytes 884744 | tf_op jit(solution)/shard_map/ppermute | solution.py:489
  19.6 9.3 %copy-start = (bf16[1,48,3072]{2,1,0:T(8,128)(2,1)S(1)}, bf16[1,48,3072]{2,1,0:T(8,128)(2,1)}, u32[]{:S(2)}) copy-start(bf16[1,48,3072]{2,1,0:T(8,128)(2,1)} %param.14) | copy-start | bytes 884740
  40.3 1.5 %collective-permute-start.4 = (bf16[32,3072]{1,0:T(8,128)(2,1)S(1)}, bf16[32,3072]{1,0:T(8,128)(2,1)S(1)}, u32[]{:S(2)}, u32[]{:S(2)}) collective-permute-start(bf16[32,3072]{1,0:T(8,128)(2,1)S(1)} %get-tuple-element.50), channel_id=1, source_target_pairs={{0,8},{8,0},{16,24},{24,16},{1,9},{9,1},{17,25},{25,17},{2,10},{10... | collective-permute-start | bytes 589832 | tf_op jit(solution)/shard_map/ppermute | solution.py:514
  40.4 1.7 %collective-permute-start.3 = (bf16[32,3072]{1,0:T(8,128)(2,1)S(1)}, bf16[32,3072]{1,0:T(8,128)(2,1)S(1)}, u32[]{:S(2)}, u32[]{:S(2)}) collective-permute-start(bf16[32,3072]{1,0:T(8,128)(2,1)S(1)} %get-tuple-element.48), channel_id=1, source_target_pairs={{0,8},{8,0},{16,24},{24,16},{1,9},{9,1},{17,25},{25,17},{2,10},{10... | collective-permute-start | bytes 589832 | tf_op jit(solution)/shard_map/ppermute | solution.py:514
  42.1 6.6 %collective-permute-start.5 = (bf16[8,9216]{1,0:T(8,128)(2,1)S(1)}, bf16[8,9216]{1,0:T(8,128)(2,1)S(1)}, u32[]{:S(2)}, u32[]{:S(2)}) collective-permute-start(bf16[8,9216]{1,0:T(8,128)(2,1)S(1)} %pad_maximum_fusion.2), channel_id=1, source_target_pairs={{0,16},{4,20},{8,24},{12,28},{16,0},{20,4},{24,8},{28,12},{1,17},{... | collective-permute-start | bytes 442376 | tf_op jit(solution)/shard_map/ppermute | solution.py:515
  43.7 5.1 %collective-permute-start.6 = (bf16[8,3072]{1,0:T(8,128)(2,1)S(1)}, bf16[8,3072]{1,0:T(8,128)(2,1)S(1)}, u32[]{:S(2)}, u32[]{:S(2)}) collective-permute-start(bf16[8,3072]{1,0:T(8,128)(2,1)S(1)} %get-tuple-element.79), channel_id=1, source_target_pairs={{0,4},{4,0},{8,12},{12,8},{16,20},{20,16},{24,28},{28,24},{1,5},{5... | collective-permute-start | bytes 147464 | tf_op jit(solution)/shard_map/ppermute | solution.py:514
  44.2 5.0 %collective-permute-start.7 = (bf16[8,3072]{1,0:T(8,128)(2,1)S(1)}, bf16[8,3072]{1,0:T(8,128)(2,1)S(1)}, u32[]{:S(2)}, u32[]{:S(2)}) collective-permute-start(bf16[8,3072]{1,0:T(8,128)(2,1)S(1)} %get-tuple-element.80), channel_id=1, source_target_pairs={{0,20},{4,16},{8,28},{12,24},{16,4},{20,0},{24,12},{28,8},{1,21},{... | collective-permute-start | bytes 147464 | tf_op jit(solution)/shard_map/ppermute | solution.py:514
  49.3 4.9 %collective-permute-start.9 = (bf16[8,2304]{1,0:T(8,128)(2,1)S(1)}, bf16[8,2304]{1,0:T(8,128)(2,1)S(1)}, u32[]{:S(2)}, u32[]{:S(2)}) collective-permute-start(bf16[8,2304]{1,0:T(8,128)(2,1)S(1)} %pad_maximum_fusion.8), channel_id=1, source_target_pairs={{0,2},{1,3},{2,0},{3,1},{4,6},{5,7},{6,4},{7,5},{8,10},{9,11},{10,... | collective-permute-start | bytes 110600 | tf_op jit(solution)/shard_map/ppermute | solution.py:515
  52.0 5.8 %collective-permute-start.10 = (bf16[8,2304]{1,0:T(8,128)(2,1)S(1)}, bf16[8,2304]{1,0:T(8,128)(2,1)S(1)}, u32[]{:S(2)}, u32[]{:S(2)}) collective-permute-start(bf16[8,2304]{1,0:T(8,128)(2,1)S(1)} %pad_maximum_fusion.9), channel_id=1, source_target_pairs={{0,3},{1,2},{2,1},{3,0},{4,7},{5,6},{6,5},{7,4},{8,11},{9,10},{10,... | collective-permute-start | bytes 110600 | tf_op jit(solution)/shard_map/ppermute | solution.py:515
  53.3 4.4 %collective-permute-start.8 = (bf16[8,2304]{1,0:T(8,128)(2,1)S(1)}, bf16[8,2304]{1,0:T(8,128)(2,1)S(1)}, u32[]{:S(2)}, u32[]{:S(2)}) collective-permute-start(bf16[8,2304]{1,0:T(8,128)(2,1)S(1)} %pad_maximum_fusion.7), channel_id=1, source_target_pairs={{0,1},{1,0},{2,3},{3,2},{4,5},{5,4},{6,7},{7,6},{8,9},{9,8},{10,11... | collective-permute-start | bytes 110600 | tf_op jit(solution)/shard_map/ppermute | solution.py:515
  58.0 5.9 %collective-permute-start.11 = (bf16[8,2688]{1,0:T(8,128)(2,1)S(1)}, bf16[8,2688]{1,0:T(8,128)(2,1)S(1)}, u32[]{:S(2)}, u32[]{:S(2)}) collective-permute-start(bf16[8,2688]{1,0:T(8,128)(2,1)S(1)} %constant_dynamic-update-slice_fusion), channel_id=1, source_target_pairs={{0,3},{1,2},{2,1},{3,0},{4,7},{5,6},{6,5},{7,4},{8,11},{9,10},{10,... | collective-permute-start | bytes 129032 | tf_op jit(solution)/shard_map/ppermute | solution.py:515
  60.1 4.9 %collective-permute-start.12 = (bf16[8,2688]{1,0:T(8,128)(2,1)S(1)}, bf16[8,2688]{1,0:T(8,128)(2,1)S(1)}, u32[]{:S(2)}, u32[]{:S(2)}) collective-permute-start(bf16[8,2688]{1,0:T(8,128)(2,1)S(1)} %constant_dynamic-update-slice_fusion), channel_id=1, source_target_pairs={{0,2},{1,3},{2,0},{3,1},{4,6},{5,7},{6,4},{7,5},{8,10},{9,11},{10,... | collective-permute-start | bytes 129032 | tf_op jit(solution)/shard_map/ppermute | solution.py:515
  60.1 4.9 %collective-permute-start.13 = (bf16[8,2688]{1,0:T(8,128)(2,1)S(1)}, bf16[8,2688]{1,0:T(8,128)(2,1)S(1)}, u32[]{:S(2)}, u32[]{:S(2)}) collective-permute-start(bf16[8,2688]{1,0:T(8,128)(2,1)S(1)} %constant_dynamic-update-slice_fusion), channel_id=1, source_target_pairs={{0,1},{1,0},{2,3},{3,2},{4,5},{5,4},{6,7},{7,6},{8,9},{9,8},{10,11... | collective-permute-start | bytes 129032 | tf_op jit(solution)/shard_map/ppermute | solution.py:515
  65.3 6.7 %collective-permute-start.14 = (bf16[8,3456]{1,0:T(8,128)(2,1)S(1)}, bf16[8,3456]{1,0:T(8,128)(2,1)S(1)}, u32[]{:S(2)}, u32[]{:S(2)}) collective-permute-start(bf16[8,3456]{1,0:T(8,128)(2,1)S(1)} %get-tuple-element.122), channel_id=1, source_target_pairs={{0,20},{4,16},{8,28},{12,24},{16,4},{20,0},{24,12},{28,8},{1,21},{... | collective-permute-start | bytes 165896 | tf_op jit(solution)/shard_map/ppermute | solution.py:515
  67.9 4.2 %collective-permute-start.15 = (bf16[8,3456]{1,0:T(8,128)(2,1)S(1)}, bf16[8,3456]{1,0:T(8,128)(2,1)S(1)}, u32[]{:S(2)}, u32[]{:S(2)}) collective-permute-start(bf16[8,3456]{1,0:T(8,128)(2,1)S(1)} %get-tuple-element.122), channel_id=1, source_target_pairs={{0,4},{4,0},{8,12},{12,8},{16,20},{20,16},{24,28},{28,24},{1,5},{5... | collective-permute-start | bytes 165896 | tf_op jit(solution)/shard_map/ppermute | solution.py:515
  68.4 5.2 %collective-permute-start.16 = (bf16[8,9600]{1,0:T(8,128)(2,1)S(1)}, bf16[8,9600]{1,0:T(8,128)(2,1)S(1)}, u32[]{:S(2)}, u32[]{:S(2)}) collective-permute-start(bf16[8,9600]{1,0:T(8,128)(2,1)S(1)} %constant_dynamic-update-slice_fusion.13), channel_id=1, source_target_pairs={{0,16},{4,20},{8,24},{12,28},{16,0},{20,4},{24,8},{28,12},{1,17},{... | collective-permute-start | bytes 460808 | tf_op jit(solution)/shard_map/ppermute | solution.py:515
  73.9 1.8 %collective-permute-start.17 = (bf16[8,24960]{1,0:T(8,128)(2,1)S(1)}, bf16[8,24960]{1,0:T(8,128)(2,1)S(1)}, u32[]{:S(2)}, u32[]{:S(2)}) collective-permute-start(bf16[8,24960]{1,0:T(8,128)(2,1)S(1)} %constant_dynamic-update-slice_fusion.22), channel_id=1, source_target_pairs={{0,8},{8,0},{16,24},{24,16},{1,9},{9,1},{17,25},{25,17},{2,10},{10... | collective-permute-start | bytes 1198088 | tf_op jit(solution)/shard_map/ppermute | solution.py:686

commit v11 on v10

--- a/solution.py
+++ b/solution.py
@@ -633,7 +633,6 @@
     mods = [part] + [shifted(part, "seq", k) for k in range(1, n)]
     noisy_parts = [noisy] + [shifted(noisy, "seq", k) for k in range(1, n)]
     words = text[0]
-    text_parts = [words] + [shifted(words, "seq", k) for k in range(1, n)]
     origin = [lax.rem(me + n - k, n) for k in range(n)]
     ordered = [
         functools.reduce(
@@ -657,6 +656,8 @@
         image_heads = project_image(k, n, image_heads, mod, gain, down, up, weight, noisy_parts[k])
         if k == 0:
             image_heads, weights = image_heads[:6], image_heads[6:]
+            later, _ = lax.optimization_barrier((words, image_heads[4]))
+            text_parts = [words] + [shifted(later, "seq", hop) for hop in range(1, n)]
     _, gain, _, up = weights
     text_heads = project_text(mod, gain, held(text_projection_weight), image_heads[0], text_parts)
     send_a, keep_a, send_b, keep_b, loss = attend(

time: 77.3 us -> 104 us (1.35)
  local copies, waits for them, and re-layouts: 0.18 us -> 25.5 us
  waiting for transfers between devices: 20.7 us -> 17.1 us
  Pallas kernels: 30.5 us -> 32.6 us
  other arithmetic: 1.12 us -> 3.09 us
    unnamed x14 -> x54, local copies, waits for them, and re-layouts: 0.06 us -> 25.3 us
    ppermute x3, waiting for transfers between devices: 3.2 us -> 0.01 us  [shifted(): return lax.ppermute(x, axis, [(i, (i + k) % size) for i in range(size)])]
    add x2, other arithmetic: 0.09 us -> 2.06 us  [on_device(): grad_a, grad_b = (keep_a + got_a.astype(F32), keep_b + got_b.astype(F32))]
    pallas_call x2, Pallas kernels: 14.1 us -> 15.2 us  [project_image(): pl.pallas_call(functools.partial(image_kernel, pair, part, len(before)),...]
    pallas_call x1, Pallas kernels: 5.61 us -> 6.67 us  [project_text(): pl.pallas_call(functools.partial(text_kernel, n, pair), in_specs=[VMEM, V...]
  transfers between devices with their start and end apart: 18 -> 18, of which waited for: 12 -> 10; matrix products, arithmetic and copies ran while one was open for 1% -> 1% of each run, Pallas kernels for 20% -> 16%
where the time goes in v11:
time: 104 us; the launch traced here: 103 us
  Pallas kernels  32.6 us (31%)
  local copies, waits for them, and re-layouts  25.5 us (25%)
  starting transfers between devices  21.6 us (21%)
  waiting for transfers between devices  17.1 us (16%)
  other arithmetic  3.09 us (3%)
  between operations  3.08 us (3%)
    unnamed x54, local copies, waits for them, and re-layouts  25.3 us
    pallas_call x2, Pallas kernels, project_image(): pl.pallas_call(functools.partial(image_kernel, pair, part, len(before)),...  15.2 us
    ppermute x10, waiting for transfers between devices, send(): return unpack(lax.ppermute(pack(arrays), group.axes, pairs), arrays)  14.1 us
    ppermute x10, starting transfers between devices, send(): return unpack(lax.ppermute(pack(arrays), group.axes, pairs), arrays)  13.8 us
    pallas_call x1, Pallas kernels, project_text(): pl.pallas_call(functools.partial(text_kernel, n, pair), in_specs=[VMEM, V...  6.67 us
    pallas_call x1, Pallas kernels, attend(): pl.pallas_call(functools.partial(attend_kernel, steps, pair, samples), in...  5.72 us
    ppermute x3, starting transfers between devices, shifted(): return lax.ppermute(x, axis, [(i, (i + k) % size) for i in range(size)])  5.17 us
    ppermute x4, starting transfers between devices, send(): return [lax.ppermute(x, group.axes, pairs) for x in arrays]  2.59 us
  transfers between devices with their start and end apart: 18, of which 10 were waited for; matrix products, arithmetic and copies ran while one was open for 1% of the time, Pallas kernels for 16%

profile of v11, /device:TPU:0, one launch (start us, length us, event | category | flops | bytes accessed | tf_op | source)
XLA Modules:
  0.0 103.0 jit_solution(16542104746837312546)
XLA Ops:
  1.9 2.2 %modulation.1.after_ref = f32[2,6144]{1,0:T(2,128)S(1)} custom-call(s32[1]{0:T(128)S(6)} %copy.56.step_ref, f32[1]{0:T(128)S(6)} %copy.57.guidance_ref, bf16[256,6144]{1,0:T(8,128)(2,1)} %weight_ref.1), custom_call_target="tpu_custom_call" | custom-call | flops 6291456 | bytes 3145728 | tf_op jit(solution)/shard_map/modulation/pallas_call | solution.py:405
  4.1 3.0 %collective-permute-start = (f32[2,6144]{1,0:T(2,128)S(1)}, f32[2,6144]{1,0:T(2,128)S(1)}, u32[]{:S(2)}, u32[]{:S(2)}) collective-permute-start(f32[2,6144]{1,0:T(2,128)S(1)} %modulation.1.after_ref), channel_id=1, source_target_pairs={{0,4},{4,0},{1,5},{5,1},{2,6},{6,2},{3,7},{7,3},{8,12},{12,8},{9,1... | collective-permute-start | bytes 147464 | tf_op jit(solution)/shard_map/ppermute | solution.py:489
  7.1 1.4 %noisy.1.tokens = bf16[80,3072]{1,0:T(8,128)(2,1)S(1)} custom-call(s32[1]{0:T(128)S(6)} %copy.56.step_ref, bf16[80,3072]{1,0:T(8,128)(2,1)} %bitcast.18, bf16[80,3072]{1,0:T(8,128)(2,1)} %bitcast.19, f32[2,6144]{1,0:T(2,128)S(1)} %modulation.1.after_ref), custom_call_target="tpu_custom_call" | custom-call | bytes 1474560 | tf_op jit(solution)/shard_map/noisy/pallas_call | solution.py:430
  9.5 8.1 %project_image.2 = (bf16[8,2,160,128]{3,2,1,0:T(8,128)(2,1)S(1)}, bf16[8,2,160,128]{3,2,1,0:T(8,128)(2,1)S(1)}, bf16[8,2,160,128]{3,2,1,0:T(8,128)(2,1)S(1)}, f3...) custom-call(f32[2,12288]{1,0:T(2,128)S(1)} %pad_maximum_fusion.3.mod, ...), custom_call_target="tpu_custom_call" | custom-call | flops 3019898880 | bytes 18874368 | tf_op jit(solution)/shard_map/project_image/pallas_call | solution.py:217
  17.6 6.4 %copy-done = bf16[3072,3072]{1,0:T(8,128)(2,1)} copy-done((bf16[3072,3072]{1,0:T(8,128)(2,1)}, bf16[3072,3072]{1,0:T(8,128)(2,1)S(1)}, u32[]{:S(2)}) %copy-start) | copy-done | bytes 18874392
  27.8 2.1 %collective-permute-start.2 = (bf16[48,3072]{1,0:T(8,128)(2,1)}, bf16[48,3072]{1,0:T(8,128)(2,1)}, u32[]{:S(2)}, u32[]{:S(2)}) collective-permute-start(bf16[48,3072]{1,0:T(8,128)(2,1)} %bitcast.16), channel_id=1, source_target_pairs={{0,4},{4,0},{1,5},{5,1},{2,6},{6,2},{3,7},{7,3},{8,12},{12,8},{9,1... | collective-permute-start | bytes 884744 | tf_op jit(solution)/shard_map/ppermute | solution.py:489
  29.9 6.4 %copy-done.1 = bf16[3072,3072]{1,0:T(8,128)(2,1)S(1)} copy-done((bf16[3072,3072]{1,0:T(8,128)(2,1)S(1)}, bf16[3072,3072]{1,0:T(8,128)(2,1)}, u32[]{:S(2)}) %copy-start.1) | copy-done | bytes 18874392
  36.3 1.1 %copy-done.3 = bf16[8,2,160,128]{3,2,1,0:T(8,128)(2,1)S(1)} copy-done((bf16[8,2,160,128]{3,2,1,0:T(8,128)(2,1)S(1)}, bf16[8,2,160,128]{3,2,1,0:T(8,128)(2,1)}, u32[]{:S(2)}) %copy-start.3) | copy-done | bytes 655384
  37.4 1.1 %copy-done.7 = bf16[8,2,160,128]{3,2,1,0:T(8,128)(2,1)S(1)} copy-done((bf16[8,2,160,128]{3,2,1,0:T(8,128)(2,1)S(1)}, bf16[8,2,160,128]{3,2,1,0:T(8,128)(2,1)}, u32[]{:S(2)}) %copy-start.7) | copy-done | bytes 655384
  38.5 1.0 copy-done.11
  39.5 1.0 copy-done.15
  41.2 7.1 %project_image.3 = (bf16[8,2,160,128]{3,2,1,0:T(8,128)(2,1)S(1)}, bf16[8,2,160,128]{3,2,1,0:T(8,128)(2,1)S(1)}, bf16[8,2,160,128]{3,2,1,0:T(8,128)(2,1)S(1)}, f3...) custom-call(f32[2,12288]{1,0:T(2,128)S(1)} %pad_maximum_fusion.3.mod, ...), custom_call_target="tpu_custom_call", output_to_operand_aliasing={{0}: (6, {}), {1}: (7, {}), {2}: (8, {}), {3}: (9, {}), {4}... | custom-call | flops 3019898880 | bytes 18874368 | tf_op jit(solution)/shard_map/project_image/pallas_call | solution.py:217
  50.6 6.7 %project_text.1 = (bf16[8,2,96,128]{3,2,1,0:T(8,128)(2,1)S(1)}, bf16[8,2,96,128]{3,2,1,0:T(8,128)(2,1)S(1)}) custom-call(f32[2,12288]{1,0:T(2,128)S(1)} %pad_maximum_fusion.3.mod_ref, f32[3,128]{1,0:T(4,128)S(1)} %get-tuple-element.30.gain_ref, bf16[3072,2048]{1,0:T(8,128)(2,1)} %w_ref.3, bf16[8,2,160,128]{3,2,1,0:T(8,128)(2,1)S(1)} %get-tuple-element.40.after_ref.q_ref, ...), custom_call_target="tpu_custom_call" | custom-call | flops 2415919104 | bytes 12582912 | tf_op jit(solution)/shard_map/project_text/pallas_call | solution.py:136
  57.3 5.7 %attend.1 = (bf16[32,3072]{1,0:T(8,128)(2,1)S(1)}, f32[32,3072]{1,0:T(8,128)S(1)}, bf16[32,3072]{1,0:T(8,128)(2,1)S(1)}, f32[32,3072]{1,0:T(8,128)S(1)}, f32[8,128]{1,0:T(8,128)S(1)}) custom-call(s32[1]{0:T(128)} %bitcast.where_ref.side_ref, f32[1,256]{1,0:T(1,128)S(1)} %compare_select_fusion.bias_ref, f32[3,128]{1,0:T(4,128)S(1)} %get-tuple-element.30.gain_ref, ...), custom_call_target="tpu_custom_call" | custom-call | flops 671088640 | bytes 8000000 | tf_op jit(solution)/shard_map/attend/pallas_call | solution.py:342
  65.1 0.9 collective-permute-done.4
  66.0 1.0 %convert_add_fusion = f32[32,3072]{1,0:T(8,128)S(1)} fusion(f32[32,3072]{1,0:T(8,128)} %copy-done.13, bf16[32,3072]{1,0:T(8,128)(2,1)S(1)} %collective-permute-done.4), kind=kLoop, calls=%fused_computation | loop fusion | flops 196608 | bytes 983040 | tf_op jit(solution)/shard_map/add | solution.py:668
  67.1 1.0 %convert_add_fusion.1 = f32[32,3072]{1,0:T(8,128)S(1)} fusion(f32[32,3072]{1,0:T(8,128)} %copy-done.12, bf16[32,3072]{1,0:T(8,128)(2,1)S(1)} %collective-permute-done.3), kind=kLoop, calls=%fused_computation.1 | loop fusion | flops 196608 | bytes 983040 | tf_op jit(solution)/shard_map/add | solution.py:668
  68.2 1.5 %collective-permute-start.5 = (bf16[8,9216]{1,0:T(8,128)(2,1)S(1)}, bf16[8,9216]{1,0:T(8,128)(2,1)S(1)}, u32[]{:S(2)}, u32[]{:S(2)}) collective-permute-start(bf16[8,9216]{1,0:T(8,128)(2,1)S(1)} %pad_maximum_fusion.2), channel_id=1, source_target_pairs={{0,16},{4,20},{8,24},{12,28},{16,0},{20,4},{24,8},{28,12},{1,17},{... | collective-permute-start | bytes 442376 | tf_op jit(solution)/shard_map/ppermute | solution.py:515
  70.2 1.6 %collective-permute-start.7 = (bf16[8,3072]{1,0:T(8,128)(2,1)S(1)}, bf16[8,3072]{1,0:T(8,128)(2,1)S(1)}, u32[]{:S(2)}, u32[]{:S(2)}) collective-permute-start(bf16[8,3072]{1,0:T(8,128)(2,1)S(1)} %get-tuple-element.82), channel_id=1, source_target_pairs={{0,20},{4,16},{8,28},{12,24},{16,4},{20,0},{24,12},{28,8},{1,21},{... | collective-permute-start | bytes 147464 | tf_op jit(solution)/shard_map/ppermute | solution.py:514
  71.7 2.9 %collective-permute-done.5 = bf16[8,9216]{1,0:T(8,128)(2,1)S(1)} collective-permute-done((bf16[8,9216]{1,0:T(8,128)(2,1)S(1)}, bf16[8,9216]{1,0:T(8,128)(2,1)S(1)}, u32[]{:S(2)}, u32[]{:S(2)}) %collective-permute-start.5) | collective-permute-done | bytes 147488 | tf_op jit(solution)/shard_map/ppermute | solution.py:515
  75.3 2.7 %collective-permute-start.9 = (bf16[8,2304]{1,0:T(8,128)(2,1)S(1)}, bf16[8,2304]{1,0:T(8,128)(2,1)S(1)}, u32[]{:S(2)}, u32[]{:S(2)}) collective-permute-start(bf16[8,2304]{1,0:T(8,128)(2,1)S(1)} %pad_maximum_fusion.8), channel_id=1, source_target_pairs={{0,2},{1,3},{2,0},{3,1},{4,6},{5,7},{6,4},{7,5},{8,10},{9,11},{10,... | collective-permute-start | bytes 110600 | tf_op jit(solution)/shard_map/ppermute | solution.py:515
  77.9 1.3 %collective-permute-start.10 = (bf16[8,2304]{1,0:T(8,128)(2,1)S(1)}, bf16[8,2304]{1,0:T(8,128)(2,1)S(1)}, u32[]{:S(2)}, u32[]{:S(2)}) collective-permute-start(bf16[8,2304]{1,0:T(8,128)(2,1)S(1)} %pad_maximum_fusion.9), channel_id=1, source_target_pairs={{0,3},{1,2},{2,1},{3,0},{4,7},{5,6},{6,5},{7,4},{8,11},{9,10},{10,... | collective-permute-start | bytes 110600 | tf_op jit(solution)/shard_map/ppermute | solution.py:515
  80.2 3.5 %collective-permute-done.10 = bf16[8,2304]{1,0:T(8,128)(2,1)S(1)} collective-permute-done((bf16[8,2304]{1,0:T(8,128)(2,1)S(1)}, bf16[8,2304]{1,0:T(8,128)(2,1)S(1)}, u32[]{:S(2)}, u32[]{:S(2)}) %collective-permute-start.10) | collective-permute-done | bytes 36896 | tf_op jit(solution)/shard_map/ppermute | solution.py:515
  84.0 2.1 %collective-permute-start.11 = (bf16[8,2688]{1,0:T(8,128)(2,1)S(1)}, bf16[8,2688]{1,0:T(8,128)(2,1)S(1)}, u32[]{:S(2)}, u32[]{:S(2)}) collective-permute-start(bf16[8,2688]{1,0:T(8,128)(2,1)S(1)} %constant_dynamic-update-slice_fusion), channel_id=1, source_target_pairs={{0,3},{1,2},{2,1},{3,0},{4,7},{5,6},{6,5},{7,4},{8,11},{9,10},{10,... | collective-permute-start | bytes 129032 | tf_op jit(solution)/shard_map/ppermute | solution.py:515
  86.1 2.4 %collective-permute-start.13 = (bf16[8,2688]{1,0:T(8,128)(2,1)S(1)}, bf16[8,2688]{1,0:T(8,128)(2,1)S(1)}, u32[]{:S(2)}, u32[]{:S(2)}) collective-permute-start(bf16[8,2688]{1,0:T(8,128)(2,1)S(1)} %constant_dynamic-update-slice_fusion), channel_id=1, source_target_pairs={{0,1},{1,0},{2,3},{3,2},{4,5},{5,4},{6,7},{7,6},{8,9},{9,8},{10,11... | collective-permute-start | bytes 129032 | tf_op jit(solution)/shard_map/ppermute | solution.py:515
  88.4 1.4 %collective-permute-done.11 = bf16[8,2688]{1,0:T(8,128)(2,1)S(1)} collective-permute-done((bf16[8,2688]{1,0:T(8,128)(2,1)S(1)}, bf16[8,2688]{1,0:T(8,128)(2,1)S(1)}, u32[]{:S(2)}, u32[]{:S(2)}) %collective-permute-start.11) | collective-permute-done | bytes 43040 | tf_op jit(solution)/shard_map/ppermute | solution.py:515
  89.9 1.1 %collective-permute-done.12 = bf16[8,2688]{1,0:T(8,128)(2,1)S(1)} collective-permute-done((bf16[8,2688]{1,0:T(8,128)(2,1)S(1)}, bf16[8,2688]{1,0:T(8,128)(2,1)S(1)}, u32[]{:S(2)}, u32[]{:S(2)}) %collective-permute-start.12) | collective-permute-done | bytes 43040 | tf_op jit(solution)/shard_map/ppermute | solution.py:515
  91.3 2.4 %collective-permute-start.14 = (bf16[8,3456]{1,0:T(8,128)(2,1)S(1)}, bf16[8,3456]{1,0:T(8,128)(2,1)S(1)}, u32[]{:S(2)}, u32[]{:S(2)}) collective-permute-start(bf16[8,3456]{1,0:T(8,128)(2,1)S(1)} %get-tuple-element.124), channel_id=1, source_target_pairs={{0,20},{4,16},{8,28},{12,24},{16,4},{20,0},{24,12},{28,8},{1,21},{... | collective-permute-start | bytes 165896 | tf_op jit(solution)/shard_map/ppermute | solution.py:515
  94.9 3.0 %collective-permute-done.15 = bf16[8,3456]{1,0:T(8,128)(2,1)S(1)} collective-permute-done((bf16[8,3456]{1,0:T(8,128)(2,1)S(1)}, bf16[8,3456]{1,0:T(8,128)(2,1)S(1)}, u32[]{:S(2)}, u32[]{:S(2)}) %collective-permute-start.15) | collective-permute-done | bytes 55328 | tf_op jit(solution)/shard_map/ppermute | solution.py:515
  97.9 1.6 %collective-permute-done.16 = bf16[8,9600]{1,0:T(8,128)(2,1)S(1)} collective-permute-done((bf16[8,9600]{1,0:T(8,128)(2,1)S(1)}, bf16[8,9600]{1,0:T(8,128)(2,1)S(1)}, u32[]{:S(2)}, u32[]{:S(2)}) %collective-permute-start.16) | collective-permute-done | bytes 153632 | tf_op jit(solution)/shard_map/ppermute | solution.py:515
  99.9 1.7 %collective-permute-done.17.got_ref = bf16[8,24960]{1,0:T(8,128)(2,1)S(1)} collective-permute-done((bf16[8,24960]{1,0:T(8,128)(2,1)S(1)}, bf16[8,24960]{1,0:T(8,128)(2,1)S(1)}, u32[]{:S(2)}, u32[]{:S(2)}) %collective-permute-start.17) | collective-permute-done | bytes 399392 | tf_op jit(solution)/shard_map/ppermute | solution.py:687
  101.6 1.4 %finish.1 = (f32[64,3072]{1,0:T(8,128)}, f32[64,3072]{1,0:T(8,128)}, f32[1,1]{1,0:T(1,128)}) custom-call(s32[1]{0:T(128)} %bitcast.where_ref.side_ref, bf16[32,3072]{1,0:T(8,128)(2,1)S(1)} %pad_maximum_fusion.a_ref, bf16[32,3072]{1,0:T(8,128)(2,1)S(1)} %pad_maximum_fusion.1.b_ref, f32[8,128]{1,0:T(8,128)S(1)} %get-tuple-element.58.sums_ref, ...), custom_call_target="tpu_custom_call" | custom-call | tf_op jit(solution)/shard_map/finish/pallas_call | solution.py:474
  (123 shorter events, 13.2 us)
Async XLA Ops:
  4.1 5.2 %collective-permute-start = (f32[2,6144]{1,0:T(2,128)S(1)}, f32[2,6144]{1,0:T(2,128)S(1)}, u32[]{:S(2)}, u32[]{:S(2)}) collective-permute-start(f32[2,6144]{1,0:T(2,128)S(1)} %modulation.1.after_ref), channel_id=1, source_target_pairs={{0,4},{4,0},{1,5},{5,1},{2,6},{6,2},{3,7},{7,3},{8,12},{12,8},{9,1... | collective-permute-start | bytes 147464 | tf_op jit(solution)/shard_map/ppermute | solution.py:489
  8.6 21.3 %collective-permute-start.1 = (bf16[80,3072]{1,0:T(8,128)(2,1)S(1)}, bf16[80,3072]{1,0:T(8,128)(2,1)}, u32[]{:S(2)}, u32[]{:S(2)}) collective-permute-start(bf16[80,3072]{1,0:T(8,128)(2,1)S(1)} %noisy.1.tokens), channel_id=1, source_target_pairs={{0,4},{4,0},{1,5},{5,1},{2,6},{6,2},{3,7},{7,3},{8,12},{12,8},{9,1... | collective-permute-start | bytes 1474568 | tf_op jit(solution)/shard_map/ppermute | solution.py:489
  17.6 6.4 %copy-start = (bf16[3072,3072]{1,0:T(8,128)(2,1)}, bf16[3072,3072]{1,0:T(8,128)(2,1)S(1)}, u32[]{:S(2)}) copy-start(bf16[3072,3072]{1,0:T(8,128)(2,1)S(1)} %get-tuple-element.33.w_ref) | copy-start | bytes 56623108
  24.0 0.8 copy-start.2
  24.8 0.8 copy-start.6
  27.8 22.9 %collective-permute-start.2 = (bf16[48,3072]{1,0:T(8,128)(2,1)}, bf16[48,3072]{1,0:T(8,128)(2,1)}, u32[]{:S(2)}, u32[]{:S(2)}) collective-permute-start(bf16[48,3072]{1,0:T(8,128)(2,1)} %bitcast.16), channel_id=1, source_target_pairs={{0,4},{4,0},{1,5},{5,1},{2,6},{6,2},{3,7},{7,3},{8,12},{12,8},{9,1... | collective-permute-start | bytes 884744 | tf_op jit(solution)/shard_map/ppermute | solution.py:489
  29.9 6.4 %copy-start.1 = (bf16[3072,3072]{1,0:T(8,128)(2,1)S(1)}, bf16[3072,3072]{1,0:T(8,128)(2,1)}, u32[]{:S(2)}) copy-start(bf16[3072,3072]{1,0:T(8,128)(2,1)} %copy-done) | copy-start | bytes 56623108
  36.3 1.1 %copy-start.3 = (bf16[8,2,160,128]{3,2,1,0:T(8,128)(2,1)S(1)}, bf16[8,2,160,128]{3,2,1,0:T(8,128)(2,1)}, u32[]{:S(2)}) copy-start(bf16[8,2,160,128]{3,2,1,0:T(8,128)(2,1)} %copy-done.2) | copy-start | bytes 1966084
  37.4 1.1 %copy-start.7 = (bf16[8,2,160,128]{3,2,1,0:T(8,128)(2,1)S(1)}, bf16[8,2,160,128]{3,2,1,0:T(8,128)(2,1)}, u32[]{:S(2)}) copy-start(bf16[8,2,160,128]{3,2,1,0:T(8,128)(2,1)} %copy-done.6) | copy-start | bytes 1966084
  38.5 1.0 copy-start.11
  39.4 1.0 copy-start.15
  41.2 9.4 %copy-start.16 = (bf16[1,48,3072]{2,1,0:T(8,128)(2,1)S(1)}, bf16[1,48,3072]{2,1,0:T(8,128)(2,1)}, u32[]{:S(2)}) copy-start(bf16[1,48,3072]{2,1,0:T(8,128)(2,1)} %param.14) | copy-start | bytes 884740
  48.3 0.8 copy-start.4
  49.2 0.8 copy-start.8
  50.6 6.7 %copy-start.5 = (bf16[8,2,160,128]{3,2,1,0:T(8,128)(2,1)S(1)}, bf16[8,2,160,128]{3,2,1,0:T(8,128)(2,1)}, u32[]{:S(2)}) copy-start(bf16[8,2,160,128]{3,2,1,0:T(8,128)(2,1)} %copy-done.4) | copy-start | bytes 1966084
  50.6 6.7 %copy-start.9 = (bf16[8,2,160,128]{3,2,1,0:T(8,128)(2,1)S(1)}, bf16[8,2,160,128]{3,2,1,0:T(8,128)(2,1)}, u32[]{:S(2)}) copy-start(bf16[8,2,160,128]{3,2,1,0:T(8,128)(2,1)} %copy-done.8) | copy-start | bytes 1966084
  50.6 6.7 %copy-start.20 = (bf16[160,64]{1,0:T(8,128)(2,1)S(1)}, bf16[160,64]{1,0:T(8,128)(2,1)}, u32[]{:S(2)}) copy-start(bf16[160,64]{1,0:T(8,128)(2,1)} %copy-done.19) | copy-start | bytes 61444
  64.6 1.4 %collective-permute-start.4 = (bf16[32,3072]{1,0:T(8,128)(2,1)S(1)}, bf16[32,3072]{1,0:T(8,128)(2,1)S(1)}, u32[]{:S(2)}, u32[]{:S(2)}) collective-permute-start(bf16[32,3072]{1,0:T(8,128)(2,1)S(1)} %get-tuple-element.52), channel_id=1, source_target_pairs={{0,8},{8,0},{16,24},{24,16},{1,9},{9,1},{17,25},{25,17},{2,10},{10... | collective-permute-start | bytes 589832 | tf_op jit(solution)/shard_map/ppermute | solution.py:514
  64.6 2.5 %collective-permute-start.3 = (bf16[32,3072]{1,0:T(8,128)(2,1)S(1)}, bf16[32,3072]{1,0:T(8,128)(2,1)S(1)}, u32[]{:S(2)}, u32[]{:S(2)}) collective-permute-start(bf16[32,3072]{1,0:T(8,128)(2,1)S(1)} %get-tuple-element.50), channel_id=1, source_target_pairs={{0,8},{8,0},{16,24},{24,16},{1,9},{9,1},{17,25},{25,17},{2,10},{10... | collective-permute-start | bytes 589832 | tf_op jit(solution)/shard_map/ppermute | solution.py:514
  68.2 6.5 %collective-permute-start.5 = (bf16[8,9216]{1,0:T(8,128)(2,1)S(1)}, bf16[8,9216]{1,0:T(8,128)(2,1)S(1)}, u32[]{:S(2)}, u32[]{:S(2)}) collective-permute-start(bf16[8,9216]{1,0:T(8,128)(2,1)S(1)} %pad_maximum_fusion.2), channel_id=1, source_target_pairs={{0,16},{4,20},{8,24},{12,28},{16,0},{20,4},{24,8},{28,12},{1,17},{... | collective-permute-start | bytes 442376 | tf_op jit(solution)/shard_map/ppermute | solution.py:515
  69.7 5.1 %collective-permute-start.6 = (bf16[8,3072]{1,0:T(8,128)(2,1)S(1)}, bf16[8,3072]{1,0:T(8,128)(2,1)S(1)}, u32[]{:S(2)}, u32[]{:S(2)}) collective-permute-start(bf16[8,3072]{1,0:T(8,128)(2,1)S(1)} %get-tuple-element.81), channel_id=1, source_target_pairs={{0,4},{4,0},{8,12},{12,8},{16,20},{20,16},{24,28},{28,24},{1,5},{5... | collective-permute-start | bytes 147464 | tf_op jit(solution)/shard_map/ppermute | solution.py:514
  70.2 5.0 %collective-permute-start.7 = (bf16[8,3072]{1,0:T(8,128)(2,1)S(1)}, bf16[8,3072]{1,0:T(8,128)(2,1)S(1)}, u32[]{:S(2)}, u32[]{:S(2)}) collective-permute-start(bf16[8,3072]{1,0:T(8,128)(2,1)S(1)} %get-tuple-element.82), channel_id=1, source_target_pairs={{0,20},{4,16},{8,28},{12,24},{16,4},{20,0},{24,12},{28,8},{1,21},{... | collective-permute-start | bytes 147464 | tf_op jit(solution)/shard_map/ppermute | solution.py:514
  75.3 4.9 %collective-permute-start.9 = (bf16[8,2304]{1,0:T(8,128)(2,1)S(1)}, bf16[8,2304]{1,0:T(8,128)(2,1)S(1)}, u32[]{:S(2)}, u32[]{:S(2)}) collective-permute-start(bf16[8,2304]{1,0:T(8,128)(2,1)S(1)} %pad_maximum_fusion.8), channel_id=1, source_target_pairs={{0,2},{1,3},{2,0},{3,1},{4,6},{5,7},{6,4},{7,5},{8,10},{9,11},{10,... | collective-permute-start | bytes 110600 | tf_op jit(solution)/shard_map/ppermute | solution.py:515
  77.9 5.8 %collective-permute-start.10 = (bf16[8,2304]{1,0:T(8,128)(2,1)S(1)}, bf16[8,2304]{1,0:T(8,128)(2,1)S(1)}, u32[]{:S(2)}, u32[]{:S(2)}) collective-permute-start(bf16[8,2304]{1,0:T(8,128)(2,1)S(1)} %pad_maximum_fusion.9), channel_id=1, source_target_pairs={{0,3},{1,2},{2,1},{3,0},{4,7},{5,6},{6,5},{7,4},{8,11},{9,10},{10,... | collective-permute-start | bytes 110600 | tf_op jit(solution)/shard_map/ppermute | solution.py:515
  79.3 4.4 %collective-permute-start.8 = (bf16[8,2304]{1,0:T(8,128)(2,1)S(1)}, bf16[8,2304]{1,0:T(8,128)(2,1)S(1)}, u32[]{:S(2)}, u32[]{:S(2)}) collective-permute-start(bf16[8,2304]{1,0:T(8,128)(2,1)S(1)} %pad_maximum_fusion.7), channel_id=1, source_target_pairs={{0,1},{1,0},{2,3},{3,2},{4,5},{5,4},{6,7},{7,6},{8,9},{9,8},{10,11... | collective-permute-start | bytes 110600 | tf_op jit(solution)/shard_map/ppermute | solution.py:515
  84.0 5.9 %collective-permute-start.11 = (bf16[8,2688]{1,0:T(8,128)(2,1)S(1)}, bf16[8,2688]{1,0:T(8,128)(2,1)S(1)}, u32[]{:S(2)}, u32[]{:S(2)}) collective-permute-start(bf16[8,2688]{1,0:T(8,128)(2,1)S(1)} %constant_dynamic-update-slice_fusion), channel_id=1, source_target_pairs={{0,3},{1,2},{2,1},{3,0},{4,7},{5,6},{6,5},{7,4},{8,11},{9,10},{10,... | collective-permute-start | bytes 129032 | tf_op jit(solution)/shard_map/ppermute | solution.py:515
  86.1 4.9 %collective-permute-start.12 = (bf16[8,2688]{1,0:T(8,128)(2,1)S(1)}, bf16[8,2688]{1,0:T(8,128)(2,1)S(1)}, u32[]{:S(2)}, u32[]{:S(2)}) collective-permute-start(bf16[8,2688]{1,0:T(8,128)(2,1)S(1)} %constant_dynamic-update-slice_fusion), channel_id=1, source_target_pairs={{0,2},{1,3},{2,0},{3,1},{4,6},{5,7},{6,4},{7,5},{8,10},{9,11},{10,... | collective-permute-start | bytes 129032 | tf_op jit(solution)/shard_map/ppermute | solution.py:515
  86.1 4.9 %collective-permute-start.13 = (bf16[8,2688]{1,0:T(8,128)(2,1)S(1)}, bf16[8,2688]{1,0:T(8,128)(2,1)S(1)}, u32[]{:S(2)}, u32[]{:S(2)}) collective-permute-start(bf16[8,2688]{1,0:T(8,128)(2,1)S(1)} %constant_dynamic-update-slice_fusion), channel_id=1, source_target_pairs={{0,1},{1,0},{2,3},{3,2},{4,5},{5,4},{6,7},{7,6},{8,9},{9,8},{10,11... | collective-permute-start | bytes 129032 | tf_op jit(solution)/shard_map/ppermute | solution.py:515
  91.3 6.6 %collective-permute-start.14 = (bf16[8,3456]{1,0:T(8,128)(2,1)S(1)}, bf16[8,3456]{1,0:T(8,128)(2,1)S(1)}, u32[]{:S(2)}, u32[]{:S(2)}) collective-permute-start(bf16[8,3456]{1,0:T(8,128)(2,1)S(1)} %get-tuple-element.124), channel_id=1, source_target_pairs={{0,20},{4,16},{8,28},{12,24},{16,4},{20,0},{24,12},{28,8},{1,21},{... | collective-permute-start | bytes 165896 | tf_op jit(solution)/shard_map/ppermute | solution.py:515
  93.7 4.2 %collective-permute-start.15 = (bf16[8,3456]{1,0:T(8,128)(2,1)S(1)}, bf16[8,3456]{1,0:T(8,128)(2,1)S(1)}, u32[]{:S(2)}, u32[]{:S(2)}) collective-permute-start(bf16[8,3456]{1,0:T(8,128)(2,1)S(1)} %get-tuple-element.124), channel_id=1, source_target_pairs={{0,4},{4,0},{8,12},{12,8},{16,20},{20,16},{24,28},{28,24},{1,5},{5... | collective-permute-start | bytes 165896 | tf_op jit(solution)/shard_map/ppermute | solution.py:515
  94.3 5.2 %collective-permute-start.16 = (bf16[8,9600]{1,0:T(8,128)(2,1)S(1)}, bf16[8,9600]{1,0:T(8,128)(2,1)S(1)}, u32[]{:S(2)}, u32[]{:S(2)}) collective-permute-start(bf16[8,9600]{1,0:T(8,128)(2,1)S(1)} %constant_dynamic-update-slice_fusion.13), channel_id=1, source_target_pairs={{0,16},{4,20},{8,24},{12,28},{16,0},{20,4},{24,8},{28,12},{1,17},{... | collective-permute-start | bytes 460808 | tf_op jit(solution)/shard_map/ppermute | solution.py:515
  99.8 1.8 %collective-permute-start.17 = (bf16[8,24960]{1,0:T(8,128)(2,1)S(1)}, bf16[8,24960]{1,0:T(8,128)(2,1)S(1)}, u32[]{:S(2)}, u32[]{:S(2)}) collective-permute-start(bf16[8,24960]{1,0:T(8,128)(2,1)S(1)} %constant_dynamic-update-slice_fusion.22), channel_id=1, source_target_pairs={{0,8},{8,0},{16,24},{24,16},{1,9},{9,1},{17,25},{25,17},{2,10},{10... | collective-permute-start | bytes 1198088 | tf_op jit(solution)/shard_map/ppermute | solution.py:687
  (7 other events, 5.0 us)
